TPU v7x, 32 devices: a whole 2x2x4 slice. The times are simulated.
32 devices in a mesh: groups: 2 (over y), blk: 4 (over z), leaf: 2 (over x), rhs: 2 (over core).
Axes of the slice: x: 2, y: 2, z: 4, core: 2. Of those that a mesh axis runs over, the one named last changes fastest.
Arguments:
- points: float32 [3, 32768], P(None, 'groups'), parts along dimension 1, may hold values from -1 to 1
- charges: bfloat16 [32768, 64], P(('groups', 'blk'), 'rhs'), parts along dimension 0, may hold values from -6 to 6
- basis: bfloat16 [32, 32768], P(None, ('groups', 'blk')), parts along dimension 1, may hold values from -0.5 to 0.5
- couplings: bfloat16 [256, 32, 32, 32], P(('groups', 'blk', 'leaf')), parts along dimension 0, may hold values from -0.1875 to 0.1875
- near_src: int32 [256, 27], P(('groups', 'blk', 'leaf')), parts along dimension 0, may hold values from 0 to 127, as said below
- far_src: int32 [256, 32], P('groups'), parts along dimension 0, may hold values from 0 to 127, as said below
Outputs:
- potential: bfloat16 [32768, 64], P(('groups', 'blk', 'leaf'), 'rhs'), parts along dimension 0
There are 2 independent parts, one for each index of `groups`. A program takes and returns all parts, laid end to end along the dimension named above; each array names one. Nothing has to cross between parts.
Inputs may be any that keep to these rules, and one draw needn't show every extreme that they name: `near_src`: target cluster t lies in segment t // 32; every near cluster of t lies in that segment or in the one before or after it, cyclically over the 4 segments. `far_src`: the target clusters 16 * d to 16 * d + 15 form one group; among that group's 16 * 32 list entries at most 128 name clusters of one segment, and in every group some segment is named exactly 128 times.
All inputs are finite; a program needn't handle non-finite values.
Results may differ from a plain program's by a relative error of at most 0.0055.
Values may be sent and summed in bfloat16 or wider, within the bound.
No kernel may reach another device: no remote copies, remote signals or barrier semaphores. Data moves between devices by JAX's collectives and lax.ppermute only.
A program may use at most 128 MiB of HBM per device.

v0:
```python
import functools

import jax
import jax.numpy as jnp
from jax import lax
from jax.experimental import pallas as pl
from jax.experimental.pallas import tpu as pltpu
from jax.sharding import PartitionSpec as P

LEAF = 128
BATCH = 12
DEPTH = 48

kernel_scale = 0.0625 / (4.0 * 3.141592653589793)
soften = 0.001
inverse_sq = 1.0 / (kernel_scale * kernel_scale)

bf16 = jnp.bfloat16
f32 = jnp.float32
VMEM = pl.BlockSpec(memory_space=pltpu.VMEM)
SMEM = pl.BlockSpec(memory_space=pltpu.SMEM)
PARAMS = pltpu.CompilerParams(vmem_limit_bytes=48 * 2**20)


def shifted(block, axis, shift):
    count = lax.axis_size(axis)
    return lax.ppermute(block, axis, [(i, (i + shift) % count) for i in range(count)])


def cluster(index):
    return pl.ds(pl.multiple_of(index * LEAF, LEAF), LEAF)


def list_kernel(seg_size, near_ref, basis_ref, charges_ref, own_ref, prev_ref, next_ref, skel_ref):
    targets = near_ref.shape[0] // 2
    near_count = near_ref.shape[1]
    blk_count = lax.axis_size("blk")
    blk = lax.axis_index("blk")
    before = lax.rem(blk + blk_count - 1, blk_count)
    row = lax.axis_index("rhs") * targets
    last = own_ref.shape[0] - 1
    zero = jnp.int32(0)

    def one_target(target, counts):
        own, prev, after = counts
        for j in range(near_count):
            source = near_ref[row + target, j]
            segment = lax.div(source, seg_size)
            code = target * 256 + (source - segment * seg_size)
            is_own = (segment == blk).astype(jnp.int32)
            is_prev = (segment == before).astype(jnp.int32) * (1 - is_own)
            own_ref[own] = code
            prev_ref[prev] = code
            next_ref[after] = code
            own = own + is_own
            prev = prev + is_prev
            after = after + (1 - is_own - is_prev)
        return own, prev, after

    own, prev, after = lax.fori_loop(0, targets, one_target, (zero, zero, zero))
    own_ref[last] = own
    prev_ref[last] = prev
    next_ref[last] = after

    columns = charges_ref.shape[0]
    rank = basis_ref.shape[0]
    pack = LEAF // columns
    for group in range(seg_size // pack):
        rows = []
        for i in range(pack):
            at = (group * pack + i) * LEAF
            parts = [jnp.zeros((columns, LEAF), bf16)] * pack
            parts[i] = charges_ref[:, at : at + LEAF]
            rows.append(jnp.concatenate(parts, axis=1))
        spread = jnp.concatenate(rows, axis=0)
        at = group * pack * LEAF
        block = lax.dot_general(
            basis_ref[:, at : at + pack * LEAF],
            spread,
            (((1,), (1,)), ((), ())),
            preferred_element_type=f32,
        )
        skel_ref[group * rank : (group + 1) * rank, :] = block.astype(bf16)


def split(value):
    high = value.astype(bf16).astype(f32)
    rest = value - high
    middle = rest.astype(bf16).astype(f32)
    return high, middle, rest - middle


def coords_of(points_ref, at):
    block = points_ref[:, cluster(at)]
    zero, one, two = block[0:1, :], block[1:2, :], block[2:3, :]
    return zero, one, two, zero * zero + one * one + two * two


def rows_of(values):
    row = lax.broadcasted_iota(jnp.int32, (8, LEAF), 0)
    out = jnp.zeros((8, LEAF), f32)
    for i, value in enumerate(values):
        out = jnp.where(row == i, value, out)
    return out


def target_features(points_ref, at):
    zero, one, two, norm = coords_of(points_ref, at)
    slope = -2.0 * inverse_sq
    rows = rows_of((zero * slope, one * slope, two * slope, (norm + soften) * inverse_sq, 1.0))
    high, middle, low = split(rows)
    return jnp.concatenate([high, high, middle, middle, high, low], axis=0).astype(bf16)


def source_features(points_ref, at):
    zero, one, two, norm = coords_of(points_ref, at)
    rows = rows_of((zero, one, two, 1.0, norm * inverse_sq))
    high, middle, low = split(rows)
    stacked = jnp.concatenate([high, middle, high, middle, low, high], axis=0)
    return jnp.transpose(stacked).astype(bf16)


def feature_kernel(seg_size, targets, leaf_clusters, points_ref, target_ref, source_ref):
    blk_count = lax.axis_size("blk")
    blk = lax.axis_index("blk")
    first = lax.axis_index("leaf") * leaf_clusters + lax.axis_index("rhs") * targets
    for which in range(3):
        segment = lax.rem(blk + which + blk_count - 1, blk_count)
        for i in range(targets):
            target_ref[which * targets + i] = target_features(
                points_ref, segment * seg_size + first + i
            )
    target_ref[3 * targets] = jnp.zeros((DEPTH, LEAF), bf16)

    def some_sources(step, carry):
        for u in range(8):
            at = step * 8 + u
            source_ref[at] = source_features(points_ref, blk * seg_size + at)
        return carry

    lax.fori_loop(0, seg_size // 8, some_sources, 0)


def near_kernel(base, list_ref, target_ref, source_ref, mine_ref, other_ref, out_ref, total, even, odd):
    targets = total.shape[0] - 1
    length = list_ref[list_ref.shape[0] - 1]
    batches = lax.div(length + (BATCH - 1), BATCH)
    total[...] = jnp.zeros_like(total)

    def pair(batch, u):
        at = batch * BATCH + u
        code = jnp.where(at < length, list_ref[at], targets * 256)
        return lax.shift_right_logical(code, 8), lax.bitwise_and(code, 255)

    def make(batch, slot):
        for u in range(BATCH):
            target, source = pair(batch, u)
            square = jnp.dot(source_ref[source], target_ref[base + target], preferred_element_type=f32)
            slot[u] = lax.rsqrt(square).astype(bf16)

    def use(batch, slot):
        sums = []
        for u in range(BATCH):
            target, source = pair(batch, u)
            charges = jnp.concatenate([mine_ref[:, cluster(source)], other_ref[:, cluster(source)]], axis=0)
            sums.append((target, jnp.dot(charges, slot[u], preferred_element_type=f32)))
        for target, value in sums:
            total[target] += value

    make(0, even)

    def body(step, carry):
        make(2 * step + 1, odd)
        use(2 * step, even)
        make(2 * step + 2, even)
        use(2 * step + 1, odd)
        return carry

    lax.fori_loop(0, lax.div(batches + 1, 2), body, 0)
    for i in range(targets):
        out_ref[:, i * LEAF : (i + 1) * LEAF] = total[i].astype(out_ref.dtype)


def near_sum(base, targets, pairs, target_rows, source_rows, mine, other, dtype):
    columns = 2 * mine.shape[0]
    return pl.pallas_call(
        functools.partial(near_kernel, base),
        out_shape=jax.ShapeDtypeStruct((columns, targets * LEAF), dtype),
        in_specs=[SMEM] + [VMEM] * 4,
        out_specs=VMEM,
        scratch_shapes=[
            pltpu.VMEM((targets + 1, columns, LEAF), f32),
            pltpu.VMEM((BATCH, LEAF, LEAF), bf16),
            pltpu.VMEM((BATCH, LEAF, LEAF), bf16),
        ],
        compiler_params=PARAMS,
    )(pairs, target_rows, source_rows, mine, other)


def far_kernel(seg_size, far_ref, couplings_ref, basis_ref, *refs):
    parts, (out_ref, skel) = refs[:-2], refs[-2:]
    clusters = couplings_ref.shape[0]
    far_count = couplings_ref.shape[1]
    rank = couplings_ref.shape[2]
    columns = out_ref.shape[0]
    pack = LEAF // columns
    leaf = lax.axis_index("leaf") * clusters
    for order, part in enumerate(parts):
        def unpack(group, carry, order=order, part=part):
            block = part[pl.ds(pl.multiple_of(group * rank, rank), rank), :]
            for i in range(pack):
                skel[order * seg_size + group * pack + i] = block[:, i * columns : (i + 1) * columns]
            return carry
        groups = part.shape[0] // rank
        lax.fori_loop(0, groups, unpack, 0)

    for target in range(clusters):
        coefficient = jnp.zeros((rank, columns), f32)
        step = 256 // rank
        for at in range(0, far_count, step):
            left = jnp.concatenate([couplings_ref[target, at + i] for i in range(step)], axis=1)
            rows = []
            for i in range(step):
                rows.append(skel[far_ref[target, at + i]])
            coefficient = coefficient + jnp.dot(
                left, jnp.concatenate(rows, axis=0), preferred_element_type=f32
            )
        own_basis = basis_ref[:, cluster(leaf + target)]
        out_ref[:, target * LEAF : (target + 1) * LEAF] = lax.dot_general(
            coefficient.astype(bf16),
            own_basis,
            (((0,), (0,)), ((), ())),
            preferred_element_type=f32,
        )


def on_device(points, charges, basis, couplings, near_src, far_src):
    blk_count = lax.axis_size("blk")
    mine = charges.T
    columns, seg_rows = mine.shape
    seg_size = seg_rows // LEAF
    rank = basis.shape[0]
    own_clusters, near_count = near_src.shape
    targets = own_clusters // 2
    cluster_total = seg_size * blk_count
    other = shifted(mine, "rhs", 1)

    list_size = -(-(targets * near_count + 4 * BATCH + 1) // 128) * 128
    pack = LEAF // columns
    own_list, prev_list, next_list, skeleton = pl.pallas_call(
        functools.partial(list_kernel, seg_size),
        out_shape=[jax.ShapeDtypeStruct((list_size,), jnp.int32)] * 3
        + [jax.ShapeDtypeStruct((seg_size // pack * rank, LEAF), bf16)],
        in_specs=[SMEM, VMEM, VMEM],
        out_specs=[SMEM, SMEM, SMEM, VMEM],
        compiler_params=PARAMS,
    )(near_src, basis, mine)

    after_list = shifted(prev_list, "blk", -1)
    before_list = shifted(next_list, "blk", 1)
    if blk_count == 4:
        skeletons = [skeleton] + [shifted(skeleton, "blk", -i) for i in range(1, blk_count)]
    else:
        skeletons = [lax.all_gather(skeleton, "blk", axis=0, tiled=True)]

    target_rows, source_rows = pl.pallas_call(
        functools.partial(feature_kernel, seg_size, targets, own_clusters),
        out_shape=[
            jax.ShapeDtypeStruct((3 * targets + 1, DEPTH, LEAF), bf16),
            jax.ShapeDtypeStruct((seg_size, LEAF, DEPTH), bf16),
        ],
        in_specs=[VMEM],
        out_specs=[VMEM, VMEM],
        compiler_params=PARAMS,
    )(points)
    own_near = near_sum(targets, targets, own_list, target_rows, source_rows, mine, other, f32)
    to_before = near_sum(0, targets, before_list, target_rows, source_rows, mine, other, bf16)
    from_after = shifted(to_before, "blk", -1)
    to_after = near_sum(2 * targets, targets, after_list, target_rows, source_rows, mine, other, bf16)
    from_before = shifted(to_after, "blk", 1)

    blk = lax.axis_index("blk")
    first = blk * seg_size + lax.axis_index("leaf") * own_clusters
    entries = lax.dynamic_slice_in_dim(far_src, first, own_clusters, 0)
    if len(skeletons) > 1:
        entries = lax.rem(entries + (blk_count - blk) * seg_size, cluster_total)
    far = pl.pallas_call(
        functools.partial(far_kernel, seg_size),
        out_shape=jax.ShapeDtypeStruct((columns, own_clusters * LEAF), f32),
        in_specs=[SMEM] + [VMEM] * (2 + len(skeletons)),
        out_specs=VMEM,
        scratch_shapes=[pltpu.VMEM((cluster_total, rank, columns), bf16)],
        compiler_params=PARAMS,
    )(entries, couplings, basis, *skeletons)

    near = own_near + from_before.astype(f32) + from_after.astype(f32)
    keep = near[:columns]
    got = shifted(near[columns:], "rhs", 1)
    even = lax.axis_index("rhs") == 0
    whole = jnp.concatenate([jnp.where(even, keep, got), jnp.where(even, got, keep)], axis=1)
    return (whole + far).astype(bf16).T


def solution(mesh):
    in_specs = (
        P(None, "groups"),
        P(("groups", "blk"), "rhs"),
        P(None, ("groups", "blk")),
        P(("groups", "blk", "leaf"), None, None, None),
        P(("groups", "blk", "leaf"), None),
        P("groups", None),
    )
    out_specs = P(("groups", "blk", "leaf"), "rhs")
    return jax.shard_map(
        on_device, mesh=mesh, in_specs=in_specs, out_specs=out_specs, check_vma=False
    )
```

profile of v0, /device:TPU:0, one launch (start us, length us, event | category | flops | bytes accessed | tf_op | source)
XLA Modules:
  0.0 42.2 jit_solution(467973974128942736)
XLA Ops:
  0.0 0.5 %collective-permute-start = (bf16[32,4096]{1,0:T(8,128)(2,1)}, bf16[32,4096]{1,0:T(8,128)(2,1)S(1)}, u32[]{:S(2)}, u32[]{:S(2)}) collective-permute-start(bf16[32,4096]{1,0:T(8,128)(2,1)} %bitcast.3), channel_id=1, source_target_pairs={{0,1},{1,0},{2,3},{3,2},{4,5},{5,4},{6,7},{7,6},{8,9},{9,8},{10,11... | collective-permute-start | bytes 786440 | tf_op jit(solution)/shard_map/ppermute | solution.py:27
  0.5 0.9 %copy-done.1 = bf16[4096,32]{0,1:T(8,128)(2,1)S(1)} copy-done((bf16[4096,32]{0,1:T(8,128)(2,1)S(1)}, bf16[4096,32]{0,1:T(8,128)(2,1)}, u32[]{:S(2)}) %copy-start.1) | copy-done | bytes 262168
  1.4 0.9 %copy-done.5 = bf16[32,4096]{1,0:T(8,128)(2,1)S(1)} copy-done((bf16[32,4096]{1,0:T(8,128)(2,1)S(1)}, bf16[32,4096]{1,0:T(8,128)(2,1)}, u32[]{:S(2)}) %copy-start.5) | copy-done | bytes 262168
  2.4 0.7 %copy-done.8 = s32[16,27]{1,0:T(8,128)S(1)} copy-done((s32[16,27]{1,0:T(8,128)S(1)}, s32[16,27]{1,0:T(8,128)}, u32[]{:S(2)}) %copy-start.8) | copy-done | bytes 1752
  3.1 3.1 %shard_map.64 = (s32[384]{0:T(512)S(1)}, s32[384]{0:T(512)S(1)}, s32[384]{0:T(512)S(1)}, bf16[256,128]{1,0:T(8,128)(2,1)S(1)}) custom-call(s32[16,27]{1,0:T(8,128)S(1)} %copy-done.8, bf16[32,4096]{1,0:T(8,128)(2,1)S(1)} %copy-done.5, bf16[32,4096]{1,0:T(8,128)(2,1)S(1)} %bitcast.4), custom_call_target="tpu_custom_call" | custom-call | tf_op jit(solution)/shard_map/pallas_call | solution.py:250
  6.1 4.7 %collective-permute-start.1 = (s32[384]{0:T(512)S(1)}, s32[384]{0:T(512)S(1)}, u32[]{:S(2)}, u32[]{:S(2)}) collective-permute-start(s32[384]{0:T(512)S(1)} %get-tuple-element.14), channel_id=1, source_target_pairs={{0,12},{4,0},{8,4},{12,8},{1,13},{5,1},{9,5},{13,9},{2,14},{6,2},{... | collective-permute-start | bytes 4616 | tf_op jit(solution)/shard_map/ppermute | solution.py:27
  10.8 0.9 %copy-done.7 = f32[3,16384]{1,0:T(4,128)S(1)} copy-done((f32[3,16384]{1,0:T(4,128)S(1)}, f32[3,16384]{1,0:T(4,128)}, u32[]{:S(2)}) %copy-start.7) | copy-done | bytes 196632
  11.8 0.7 %shard_map.65 = (bf16[25,48,128]{2,1,0:T(8,128)(2,1)S(1)}, bf16[32,128,48]{2,1,0:T(8,128)(2,1)S(1)}) custom-call(f32[3,16384]{1,0:T(4,128)S(1)} %copy-done.7), custom_call_target="tpu_custom_call" | custom-call | tf_op jit(solution)/shard_map/pallas_call | solution.py:266
  12.5 0.0 copy-start.2
  12.5 0.9 %copy-done.2 = bf16[4096,32]{0,1:T(8,128)(2,1)S(1)} copy-done((bf16[4096,32]{0,1:T(8,128)(2,1)S(1)}, bf16[4096,32]{0,1:T(8,128)(2,1)}, u32[]{:S(2)}) %copy-start.2) | copy-done | bytes 262168
  13.4 2.5 %shard_map.67 = bf16[64,1024]{1,0:T(8,128)(2,1)S(1)} custom-call(s32[384]{0:T(512)S(1)} %collective-permute-done.1.list_ref, bf16[25,48,128]{2,1,0:T(8,128)(2,1)S(1)} %get-tuple-element.12.target_ref, bf16[32,128,48]{2,1,0:T(8,128)(2,1)S(1)} %get-tuple-element.13.source_ref, bf16[32,4096]{1,0:T(8,128)(2,1)S(1)} %bitcast.5, ...), custom_call_target="tpu_custom_call" | custom-call | tf_op jit(solution)/shard_map/pallas_call | solution.py:186
  16.0 0.6 %collective-permute-start.2 = (bf16[64,1024]{1,0:T(8,128)(2,1)S(1)}, bf16[64,1024]{1,0:T(8,128)(2,1)S(1)}, u32[]{:S(2)}, u32[]{:S(2)}) collective-permute-start(bf16[64,1024]{1,0:T(8,128)(2,1)S(1)} %shard_map.67), channel_id=1, source_target_pairs={{0,4},{4,8},{8,12},{12,0},{1,5},{5,9},{9,13},{13,1},{2,6},{6,10},{... | collective-permute-start | bytes 393224 | tf_op jit(solution)/shard_map/ppermute | solution.py:27
  16.6 3.1 %shard_map.68 = bf16[64,1024]{1,0:T(8,128)(2,1)S(1)} custom-call(s32[384]{0:T(512)S(1)} %collective-permute-done.3.list_ref, bf16[25,48,128]{2,1,0:T(8,128)(2,1)S(1)} %get-tuple-element.12.target_ref, bf16[32,128,48]{2,1,0:T(8,128)(2,1)S(1)} %get-tuple-element.13.source_ref, bf16[32,4096]{1,0:T(8,128)(2,1)S(1)} %bitcast.6, ...), custom_call_target="tpu_custom_call" | custom-call | tf_op jit(solution)/shard_map/pallas_call | solution.py:186
  19.7 3.9 %collective-permute-start.4 = (bf16[64,1024]{1,0:T(8,128)(2,1)S(1)}, bf16[64,1024]{1,0:T(8,128)(2,1)S(1)}, u32[]{:S(2)}, u32[]{:S(2)}) collective-permute-start(bf16[64,1024]{1,0:T(8,128)(2,1)S(1)} %shard_map.68), channel_id=1, source_target_pairs={{0,12},{4,0},{8,4},{12,8},{1,13},{5,1},{9,5},{13,9},{2,14},{6,2},{... | collective-permute-start | bytes 393224 | tf_op jit(solution)/shard_map/ppermute | solution.py:27
  23.6 2.0 %collective-permute-start.6 = (bf16[256,128]{1,0:T(8,128)(2,1)S(1)}, bf16[256,128]{1,0:T(8,128)(2,1)S(1)}, u32[]{:S(2)}, u32[]{:S(2)}) collective-permute-start(bf16[256,128]{1,0:T(8,128)(2,1)S(1)} %get-tuple-element.16.refs_0_), channel_id=1, source_target_pairs={{0,12},{4,0},{8,4},{12,8},{1,13},{5,1},{9,5},{13,9},{2,14},{6,2},{... | collective-permute-start | bytes 196616 | tf_op jit(solution)/shard_map/ppermute | solution.py:27
  25.6 0.6 %collective-permute-start.8 = (bf16[256,128]{1,0:T(8,128)(2,1)S(1)}, bf16[256,128]{1,0:T(8,128)(2,1)S(1)}, u32[]{:S(2)}, u32[]{:S(2)}) collective-permute-start(bf16[256,128]{1,0:T(8,128)(2,1)S(1)} %get-tuple-element.16.refs_0_), channel_id=1, source_target_pairs={{0,4},{4,8},{8,12},{12,0},{1,5},{5,9},{9,13},{13,1},{2,6},{6,10},{... | collective-permute-start | bytes 196616 | tf_op jit(solution)/shard_map/ppermute | solution.py:27
  26.2 0.1 constant_dynamic-slice_fusion
  26.3 0.1 copy.8
  26.4 2.5 %shard_map.66 = f32[64,1024]{1,0:T(8,128)S(1)} custom-call(s32[384]{0:T(512)S(1)} %get-tuple-element.11.list_ref, bf16[25,48,128]{2,1,0:T(8,128)(2,1)S(1)} %get-tuple-element.12.target_ref, bf16[32,128,48]{2,1,0:T(8,128)(2,1)S(1)} %get-tuple-element.13.source_ref, bf16[32,4096]{1,0:T(8,128)(2,1)S(1)} %bitcast.7, ...), custom_call_target="tpu_custom_call" | custom-call | tf_op jit(solution)/shard_map/pallas_call | solution.py:186
  29.0 0.1 collective-permute-start.5
  29.1 3.4 %collective-permute-done.7.refs_2_ = bf16[256,128]{1,0:T(8,128)(2,1)S(1)} collective-permute-done((bf16[256,128]{1,0:T(8,128)(2,1)S(1)}, bf16[256,128]{1,0:T(8,128)(2,1)S(1)}, u32[]{:S(2)}, u32[]{:S(2)}) %collective-permute-start.7) | collective-permute-done | bytes 65568 | tf_op jit(solution)/shard_map/ppermute | solution.py:27
  32.5 2.2 %copy-done.4 = bf16[16,32,32,32]{3,2,1,0:T(8,128)(2,1)S(1)} copy-done((bf16[16,32,32,32]{3,2,1,0:T(8,128)(2,1)S(1)}, bf16[16,32,32,32]{3,2,1,0:T(8,128)(2,1)}, u32[]{:S(2)}) %copy-start.4) | copy-done | bytes 1048600
  34.7 6.7 %shard_map.69 = f32[32,2048]{1,0:T(8,128)S(1)} custom-call(s32[16,32]{1,0:T(8,128)S(1)} %negate_select_fusion.far_ref, bf16[16,32,32,32]{3,2,1,0:T(8,128)(2,1)S(1)} %copy-done.4, bf16[32,4096]{1,0:T(8,128)(2,1)S(1)} %copy-done.6, bf16[256,128]{1,0:T(8,128)(2,1)S(1)} %get-tuple-element.16.refs_0_, bf16[256,128]{1,0:T(8,128)(2,1)S(1)} %collective-permute-done.6.refs_1_, ...), custom_call_target="tpu_custom_call" | custom-call | tf_op jit(solution)/shard_map/pallas_call | solution.py:287
  41.5 0.7 %fusion.1 = bf16[2048,32]{0,1:T(8,128)(2,1)} fusion(f32[32,2048]{1,0:T(8,128)S(1)} %shard_map.69, f32[32,1024]{1,0:T(8,128)S(1)} %get-tuple-element.18, f32[32,1024]{1,0:T(8,128)S(1)} %get-tuple-element.17), kind=kLoop, calls=%fused_computation.3 | loop fusion | flops 196608 | bytes 655360 | tf_op jit(solution)/shard_map/transpose | solution.py:301
  (25 shorter events, 0.1 us)
Async XLA Ops:
  0.0 26.2 %copy-start = (s32[128,32]{0,1:T(8,128)S(1)}, s32[128,32]{0,1:T(8,128)}, u32[]{:S(2)}) copy-start(s32[128,32]{0,1:T(8,128)} %param.11) | copy-start | bytes 49156
  0.0 12.5 %collective-permute-start = (bf16[32,4096]{1,0:T(8,128)(2,1)}, bf16[32,4096]{1,0:T(8,128)(2,1)S(1)}, u32[]{:S(2)}, u32[]{:S(2)}) collective-permute-start(bf16[32,4096]{1,0:T(8,128)(2,1)} %bitcast.3), channel_id=1, source_target_pairs={{0,1},{1,0},{2,3},{3,2},{4,5},{5,4},{6,7},{7,6},{8,9},{9,8},{10,11... | collective-permute-start | bytes 786440 | tf_op jit(solution)/shard_map/ppermute | solution.py:27
  0.5 0.9 %copy-start.1 = (bf16[4096,32]{0,1:T(8,128)(2,1)S(1)}, bf16[4096,32]{0,1:T(8,128)(2,1)}, u32[]{:S(2)}) copy-start(bf16[4096,32]{0,1:T(8,128)(2,1)} %param.7) | copy-start | bytes 786436
  1.4 0.9 %copy-start.5 = (bf16[32,4096]{1,0:T(8,128)(2,1)S(1)}, bf16[32,4096]{1,0:T(8,128)(2,1)}, u32[]{:S(2)}) copy-start(bf16[32,4096]{1,0:T(8,128)(2,1)} %basis_ref.3) | copy-start | bytes 786436
  2.4 0.7 %copy-start.8 = (s32[16,27]{1,0:T(8,128)S(1)}, s32[16,27]{1,0:T(8,128)}, u32[]{:S(2)}) copy-start(s32[16,27]{1,0:T(8,128)} %near_ref.1) | copy-start | bytes 5188
  3.1 23.3 %copy-start.3 = (bf16[4096,32]{0,1:T(8,128)(2,1)S(1)}, bf16[4096,32]{0,1:T(8,128)(2,1)}, u32[]{:S(2)}) copy-start(bf16[4096,32]{0,1:T(8,128)(2,1)} %param.7) | copy-start | bytes 786436
  3.1 29.5 %copy-start.6 = (bf16[32,4096]{1,0:T(8,128)(2,1)S(1)}, bf16[32,4096]{1,0:T(8,128)(2,1)}, u32[]{:S(2)}) copy-start(bf16[32,4096]{1,0:T(8,128)(2,1)} %basis_ref.3) | copy-start | bytes 786436
  6.1 6.3 %collective-permute-start.1 = (s32[384]{0:T(512)S(1)}, s32[384]{0:T(512)S(1)}, u32[]{:S(2)}, u32[]{:S(2)}) collective-permute-start(s32[384]{0:T(512)S(1)} %get-tuple-element.14), channel_id=1, source_target_pairs={{0,12},{4,0},{8,4},{12,8},{1,13},{5,1},{9,5},{13,9},{2,14},{6,2},{... | collective-permute-start | bytes 4616 | tf_op jit(solution)/shard_map/ppermute | solution.py:27
  10.8 5.8 %collective-permute-start.3 = (s32[384]{0:T(512)S(1)}, s32[384]{0:T(512)S(1)}, u32[]{:S(2)}, u32[]{:S(2)}) collective-permute-start(s32[384]{0:T(512)S(1)} %get-tuple-element.15), channel_id=1, source_target_pairs={{0,4},{4,8},{8,12},{12,0},{1,5},{5,9},{9,13},{13,1},{2,6},{6,10},{... | collective-permute-start | bytes 4616 | tf_op jit(solution)/shard_map/ppermute | solution.py:27
  10.8 1.0 %copy-start.7 = (f32[3,16384]{1,0:T(4,128)S(1)}, f32[3,16384]{1,0:T(4,128)}, u32[]{:S(2)}) copy-start(f32[3,16384]{1,0:T(4,128)} %points_ref.1) | copy-start | bytes 589828
  12.5 1.0 %copy-start.2 = (bf16[4096,32]{0,1:T(8,128)(2,1)S(1)}, bf16[4096,32]{0,1:T(8,128)(2,1)}, u32[]{:S(2)}) copy-start(bf16[4096,32]{0,1:T(8,128)(2,1)} %param.7) | copy-start | bytes 786436
  16.0 13.0 %collective-permute-start.2 = (bf16[64,1024]{1,0:T(8,128)(2,1)S(1)}, bf16[64,1024]{1,0:T(8,128)(2,1)S(1)}, u32[]{:S(2)}, u32[]{:S(2)}) collective-permute-start(bf16[64,1024]{1,0:T(8,128)(2,1)S(1)} %shard_map.67), channel_id=1, source_target_pairs={{0,4},{4,8},{8,12},{12,0},{1,5},{5,9},{9,13},{13,1},{2,6},{6,10},{... | collective-permute-start | bytes 393224 | tf_op jit(solution)/shard_map/ppermute | solution.py:27
  19.7 9.2 %collective-permute-start.4 = (bf16[64,1024]{1,0:T(8,128)(2,1)S(1)}, bf16[64,1024]{1,0:T(8,128)(2,1)S(1)}, u32[]{:S(2)}, u32[]{:S(2)}) collective-permute-start(bf16[64,1024]{1,0:T(8,128)(2,1)S(1)} %shard_map.68), channel_id=1, source_target_pairs={{0,12},{4,0},{8,4},{12,8},{1,13},{5,1},{9,5},{13,9},{2,14},{6,2},{... | collective-permute-start | bytes 393224 | tf_op jit(solution)/shard_map/ppermute | solution.py:27
  23.6 5.5 %collective-permute-start.6 = (bf16[256,128]{1,0:T(8,128)(2,1)S(1)}, bf16[256,128]{1,0:T(8,128)(2,1)S(1)}, u32[]{:S(2)}, u32[]{:S(2)}) collective-permute-start(bf16[256,128]{1,0:T(8,128)(2,1)S(1)} %get-tuple-element.16.refs_0_), channel_id=1, source_target_pairs={{0,12},{4,0},{8,4},{12,8},{1,13},{5,1},{9,5},{13,9},{2,14},{6,2},{... | collective-permute-start | bytes 196616 | tf_op jit(solution)/shard_map/ppermute | solution.py:27
  25.6 6.9 %collective-permute-start.7 = (bf16[256,128]{1,0:T(8,128)(2,1)S(1)}, bf16[256,128]{1,0:T(8,128)(2,1)S(1)}, u32[]{:S(2)}, u32[]{:S(2)}) collective-permute-start(bf16[256,128]{1,0:T(8,128)(2,1)S(1)} %get-tuple-element.16.refs_0_), channel_id=1, source_target_pairs={{0,8},{4,12},{8,0},{12,4},{1,9},{5,13},{9,1},{13,5},{2,10},{6,14},... | collective-permute-start | bytes 196616 | tf_op jit(solution)/shard_map/ppermute | solution.py:27
  25.6 6.9 %collective-permute-start.8 = (bf16[256,128]{1,0:T(8,128)(2,1)S(1)}, bf16[256,128]{1,0:T(8,128)(2,1)S(1)}, u32[]{:S(2)}, u32[]{:S(2)}) collective-permute-start(bf16[256,128]{1,0:T(8,128)(2,1)S(1)} %get-tuple-element.16.refs_0_), channel_id=1, source_target_pairs={{0,4},{4,8},{8,12},{12,0},{1,5},{5,9},{9,13},{13,1},{2,6},{6,10},{... | collective-permute-start | bytes 196616 | tf_op jit(solution)/shard_map/ppermute | solution.py:27
  29.0 12.4 %collective-permute-start.5 = (f32[32,1024]{1,0:T(8,128)S(1)}, f32[32,1024]{1,0:T(8,128)S(1)}, u32[]{:S(2)}, u32[]{:S(2)}) collective-permute-start(f32[32,1024]{1,0:T(8,128)S(1)} %slice.9), channel_id=1, source_target_pairs={{0,1},{1,0},{2,3},{3,2},{4,5},{5,4},{6,7},{7,6},{8,9},{9,8},{10,11... | collective-permute-start | bytes 393224 | tf_op jit(solution)/shard_map/ppermute | solution.py:27
  32.5 2.2 %copy-start.4 = (bf16[16,32,32,32]{3,2,1,0:T(8,128)(2,1)S(1)}, bf16[16,32,32,32]{3,2,1,0:T(8,128)(2,1)}, u32[]{:S(2)}) copy-start(bf16[16,32,32,32]{3,2,1,0:T(8,128)(2,1)} %couplings_ref.1) | copy-start | bytes 3145732
where the time goes:
time: 42.5 us; the launch traced here: 42.2 us
  Pallas kernels  18.7 us (44%)
  starting transfers between devices  12.3 us (29%)
  local copies, waits for them, and re-layouts  6.84 us (16%)
  waiting for transfers between devices  3.42 us (8%)
  other arithmetic  0.76 us (2%)
    ppermute x9, starting transfers between devices, shifted(): lax.ppermute(block, axis, [(i, (i + shift) % count) for i in range(count)])  12.3 us
    pallas_call x3, Pallas kernels, near_sum(): pl.pallas_call(functools.partial(near_kernel, base), out_shape=jax.ShapeD...  8.15 us
    unnamed x19, local copies, waits for them, and re-layouts  6.76 us
    pallas_call x1, Pallas kernels, on_device(): pl.pallas_call(functools.partial(far_kernel, seg_size), out_shape=jax.Sha...  6.75 us
    ppermute x9, waiting for transfers between devices, shifted(): lax.ppermute(block, axis, [(i, (i + shift) % count) for i in range(count)])  3.42 us
    pallas_call x1, Pallas kernels, on_device(): pl.pallas_call(functools.partial(list_kernel, seg_size), out_shape=[jax.S...  3.07 us
  transfers between devices with their start and end apart: 9, of which 1 were waited for; matrix products, arithmetic and copies ran while one was open for 0% of the time, Pallas kernels for 44%

commit v1 on v0

v1 whole, which is shorter than its diff:
```python
import functools

import jax
import jax.numpy as jnp
from jax import lax
from jax.experimental import pallas as pl
from jax.experimental.pallas import tpu as pltpu
from jax.sharding import PartitionSpec as P

LEAF = 128
BATCH = 12
DEPTH = 48

kernel_scale = 0.0625 / (4.0 * 3.141592653589793)
soften = 0.001
inverse_sq = 1.0 / (kernel_scale * kernel_scale)

bf16 = jnp.bfloat16
f32 = jnp.float32
VMEM = pl.BlockSpec(memory_space=pltpu.VMEM)
ANY = pl.BlockSpec(memory_space=pl.ANY)
SMEM = pl.BlockSpec(memory_space=pltpu.SMEM)
PARAMS = pltpu.CompilerParams(vmem_limit_bytes=48 * 2**20)


def cost(microseconds):
    return pl.CostEstimate(flops=int(microseconds * 1e9), bytes_accessed=0, transcendentals=0)


def shifted(block, axis, shift):
    count = lax.axis_size(axis)
    return lax.ppermute(block, axis, [(i, (i + shift) % count) for i in range(count)])


def cluster(index):
    return pl.ds(pl.multiple_of(index * LEAF, LEAF), LEAF)


def list_kernel(seg_size, near_hbm, basis_hbm, charges_hbm, own_ref, prev_ref, next_ref, near_ref, basis_ref, charges_ref, sems):
    copies = [
        pltpu.make_async_copy(near_hbm, near_ref, sems.at[0]),
        pltpu.make_async_copy(basis_hbm, basis_ref, sems.at[1]),
        pltpu.make_async_copy(charges_hbm, charges_ref, sems.at[2]),
    ]
    for copy in copies:
        copy.start()
    targets = near_ref.shape[0] // 2
    near_count = near_ref.shape[1]
    blk_count = lax.axis_size("blk")
    blk = lax.axis_index("blk")
    before = lax.rem(blk + blk_count - 1, blk_count)
    row = lax.axis_index("rhs") * targets
    place = lax.broadcasted_iota(jnp.int32, (8, LEAF), 0) * LEAF + lax.broadcasted_iota(jnp.int32, (8, LEAF), 1)
    zero = jnp.int32(0)
    blank = jnp.zeros((8, LEAF), jnp.int32)
    copies[0].wait()

    def one_target(target, carry):
        own, prev, after, prev_list, next_list = carry
        for j in range(near_count):
            source = near_ref[row + target, j]
            segment = lax.div(source, seg_size)
            code = target * 256 + (source - segment * seg_size)
            is_own = segment == blk
            is_prev = jnp.logical_and(segment == before, jnp.logical_not(is_own))
            is_next = jnp.logical_not(jnp.logical_or(is_own, is_prev))
            own_ref[lax.shift_right_logical(own, 7), lax.bitwise_and(own, 127)] = code
            prev_list = jnp.where(place == jnp.where(is_prev, prev, -1), code, prev_list)
            next_list = jnp.where(place == jnp.where(is_next, after, -1), code, next_list)
            own = own + is_own.astype(jnp.int32)
            prev = prev + is_prev.astype(jnp.int32)
            after = after + is_next.astype(jnp.int32)
        return own, prev, after, prev_list, next_list

    own, prev, after, prev_list, next_list = lax.fori_loop(
        0, targets, one_target, (zero, zero, zero, blank, blank)
    )
    own_ref[7, LEAF - 1] = own
    columns = charges_ref.shape[0]
    rank = basis_ref.shape[0]
    pack = LEAF // columns
    rows_end = seg_size // pack * rank
    for out, count, entries in ((prev_ref, prev, prev_list), (next_ref, after, next_list)):
        entries = jnp.where(place == 8 * LEAF - 1, count, entries)
        both = jnp.concatenate([lax.bitwise_and(entries, 255), lax.shift_right_logical(entries, 8)], axis=0)
        out[rows_end : rows_end + 16, :] = both.astype(f32).astype(bf16)

    copies[1].wait()
    copies[2].wait()
    for group in range(seg_size // pack):
        rows = []
        for i in range(pack):
            at = (group * pack + i) * LEAF
            parts = [jnp.zeros((columns, LEAF), bf16)] * pack
            parts[i] = charges_ref[:, at : at + LEAF]
            rows.append(jnp.concatenate(parts, axis=1))
        spread = jnp.concatenate(rows, axis=0)
        at = group * pack * LEAF
        block = lax.dot_general(
            basis_ref[:, at : at + pack * LEAF],
            spread,
            (((1,), (1,)), ((), ())),
            preferred_element_type=f32,
        ).astype(bf16)
        prev_ref[group * rank : (group + 1) * rank, :] = block
        next_ref[group * rank : (group + 1) * rank, :] = block


def split(value):
    high = value.astype(bf16).astype(f32)
    rest = value - high
    middle = rest.astype(bf16).astype(f32)
    return high, middle, rest - middle


def coords_of(points_ref, at):
    block = points_ref[:, cluster(at)]
    zero, one, two = block[0:1, :], block[1:2, :], block[2:3, :]
    return zero, one, two, zero * zero + one * one + two * two


def rows_of(values):
    row = lax.broadcasted_iota(jnp.int32, (8, LEAF), 0)
    out = jnp.zeros((8, LEAF), f32)
    for i, value in enumerate(values):
        out = jnp.where(row == i, value, out)
    return out


def target_features(points_ref, at):
    zero, one, two, norm = coords_of(points_ref, at)
    slope = -2.0 * inverse_sq
    rows = rows_of((zero * slope, one * slope, two * slope, (norm + soften) * inverse_sq, 1.0))
    high, middle, low = split(rows)
    return jnp.concatenate([high, high, middle, middle, high, low], axis=0).astype(bf16)


def source_features(points_ref, at):
    zero, one, two, norm = coords_of(points_ref, at)
    rows = rows_of((zero, one, two, 1.0, norm * inverse_sq))
    high, middle, low = split(rows)
    stacked = jnp.concatenate([high, middle, high, middle, low, high], axis=0)
    return jnp.transpose(stacked).astype(bf16)


def feature_kernel(seg_size, targets, leaf_clusters, points_ref, target_ref, source_ref):
    blk_count = lax.axis_size("blk")
    blk = lax.axis_index("blk")
    first = lax.axis_index("leaf") * leaf_clusters + lax.axis_index("rhs") * targets
    for which in range(3):
        segment = lax.rem(blk + which + blk_count - 1, blk_count)
        for i in range(targets):
            target_ref[which * targets + i] = target_features(
                points_ref, segment * seg_size + first + i
            )
    target_ref[3 * targets] = jnp.zeros((DEPTH, LEAF), bf16)

    def some_sources(step, carry):
        for u in range(8):
            at = step * 8 + u
            source_ref[at] = source_features(points_ref, blk * seg_size + at)
        return carry

    lax.fori_loop(0, seg_size // 8, some_sources, 0)


def near_kernel(base, list_ref, target_ref, source_ref, mine_ref, other_ref, out_ref, total, held):
    targets = total.shape[0] - 1
    length = list_ref[7, LEAF - 1]
    batches = lax.div(length + (BATCH - 1), BATCH)
    total[...] = jnp.zeros_like(total)

    def pair(batch, u):
        at = batch * BATCH + u
        code = list_ref[lax.shift_right_logical(at, 7), lax.bitwise_and(at, 127)]
        code = jnp.where(at < length, code, targets * 256)
        return lax.shift_right_logical(code, 8), lax.bitwise_and(code, 255)

    def make(batch, u):
        target, source = pair(batch, u)
        square = jnp.dot(source_ref[source], target_ref[base + target], preferred_element_type=f32)
        held[u] = lax.rsqrt(square).astype(bf16)

    def use(batch, u):
        target, source = pair(batch, u)
        charges = jnp.concatenate([mine_ref[:, cluster(source)], other_ref[:, cluster(source)]], axis=0)
        return target, jnp.dot(charges, held[u], preferred_element_type=f32)

    def body(batch, carry):
        values = []
        for u in range(BATCH):
            values.append(use(batch, u))
            make(batch + 1, u)
        for target, value in values:
            total[target] += value
        return carry

    for u in range(BATCH):
        make(0, u)
    lax.fori_loop(0, batches - 1, body, 0)
    final = jnp.maximum(batches - 1, 0)
    values = [use(final, u) for u in range(BATCH)]
    for target, value in values:
        total[target] += value
    for i in range(targets):
        out_ref[:, i * LEAF : (i + 1) * LEAF] = total[i].astype(out_ref.dtype)


def near_sum(base, targets, pairs, target_rows, source_rows, mine, other, dtype):
    columns = 2 * mine.shape[0]
    return pl.pallas_call(
        functools.partial(near_kernel, base),
        out_shape=jax.ShapeDtypeStruct((columns, targets * LEAF), dtype),
        in_specs=[SMEM] + [VMEM] * 4,
        out_specs=VMEM,
        scratch_shapes=[
            pltpu.VMEM((targets + 1, columns, LEAF), f32),
            pltpu.VMEM((BATCH, LEAF, LEAF), bf16),
        ],
        compiler_params=PARAMS,
        cost_estimate=cost(2.5),
    )(pairs, target_rows, source_rows, mine, other)


def far_sum(out_ref, basis_ref, target, at, coefficient):
    out_ref[:, target * LEAF : (target + 1) * LEAF] = lax.dot_general(
        coefficient.astype(bf16),
        basis_ref[:, cluster(at)],
        (((0,), (0,)), ((), ())),
        preferred_element_type=f32,
    )


def far_kernel(seg_size, far_ref, couplings_ref, basis_ref, part, out_ref, skel):
    leaf = lax.axis_index("leaf") * couplings_ref.shape[0]
    clusters, far_count, rank, _ = couplings_ref.shape
    columns = out_ref.shape[0]
    pack = LEAF // columns

    def unpack(group, carry):
        block = part[pl.ds(pl.multiple_of(group * rank, rank), rank), :]
        for i in range(pack):
            skel[group * pack + i] = block[:, i * columns : (i + 1) * columns]
        return carry

    lax.fori_loop(0, part.shape[0] // rank, unpack, 0)
    for target in range(clusters):
        coefficient = jnp.zeros((rank, columns), f32)
        step = 256 // rank
        for at in range(0, far_count, step):
            left = jnp.concatenate([couplings_ref[target, at + i] for i in range(step)], axis=1)
            rows = [skel[far_ref[target, at + i]] for i in range(step)]
            coefficient = coefficient + jnp.dot(
                left, jnp.concatenate(rows, axis=0), preferred_element_type=f32
            )
        far_sum(out_ref, basis_ref, target, leaf + target, coefficient)


def far_kernel_wide(seg_size, far_ref, couplings_hbm, basis_ref, *refs):
    parts, (out_ref, skel, couplings_ref, sems) = refs[:-4], refs[-4:]
    clusters, far_count, rank, _ = couplings_ref.shape
    columns = out_ref.shape[0]
    pack = LEAF // columns
    leaf = lax.axis_index("leaf") * clusters
    copies = [
        pltpu.make_async_copy(couplings_hbm.at[t], couplings_ref.at[t], sems.at[t]) for t in range(clusters)
    ]
    for copy in copies:
        copy.start()
    lane_block = lax.broadcasted_iota(jnp.int32, (rank, LEAF), 1) // columns
    for order, part in enumerate(parts):
        def unpack(group, carry, order=order, part=part):
            block = part[pl.ds(pl.multiple_of(group * rank, rank), rank), :].astype(f32)
            turned = [block] + [pltpu.roll(block, k * columns, 1) for k in range(1, pack)]
            for i in range(pack):
                for j in range(pack):
                    value = jnp.where(lane_block == j, turned[(j - i) % pack], 0.0)
                    skel[j, order * seg_size + group * pack + i] = value.astype(bf16)
            return carry
        lax.fori_loop(0, seg_size // pack, unpack, 0, unroll=2)

    for target in range(clusters):
        copies[target].wait()
        wide = jnp.zeros((rank, LEAF), f32)
        for at in range(0, far_count, pack):
            right = skel[0, far_ref[target, at]]
            for i in range(1, pack):
                right = right + skel[i, far_ref[target, at + i]]
            left = couplings_ref[target, at : at + pack].reshape(pack * rank, rank)
            product = jnp.dot(left, right, preferred_element_type=f32)
            chosen = product[:rank]
            for i in range(1, pack):
                chosen = jnp.where(lane_block == i, product[i * rank : (i + 1) * rank], chosen)
            wide = wide + chosen
        turn = columns
        while turn < LEAF:
            wide = wide + pltpu.roll(wide, turn, 1)
            turn *= 2
        far_sum(out_ref, basis_ref, target, leaf + target, wide[:, :columns])


def on_device(points, charges, basis, couplings, near_src, far_src):
    blk_count = lax.axis_size("blk")
    mine = charges.T
    columns, seg_rows = mine.shape
    seg_size = seg_rows // LEAF
    rank = basis.shape[0]
    own_clusters, near_count = near_src.shape
    targets = own_clusters // 2
    cluster_total = seg_size * blk_count
    pack = LEAF // columns
    skel_rows = seg_size // pack * rank
    other = shifted(mine, "rhs", 1)

    own_list, prev_load, next_load = pl.pallas_call(
        functools.partial(list_kernel, seg_size),
        out_shape=[jax.ShapeDtypeStruct((8, LEAF), jnp.int32)]
        + [jax.ShapeDtypeStruct((skel_rows + 16, LEAF), bf16)] * 2,
        in_specs=[ANY] * 3,
        out_specs=[SMEM, VMEM, VMEM],
        scratch_shapes=[
            pltpu.SMEM(near_src.shape, jnp.int32),
            pltpu.VMEM(basis.shape, bf16),
            pltpu.VMEM(mine.shape, bf16),
            pltpu.SemaphoreType.DMA((3,)),
        ],
        compiler_params=PARAMS,
        cost_estimate=cost(3.0),
    )(near_src, basis, mine)

    after_load = shifted(prev_load, "blk", -1)
    before_load = shifted(next_load, "blk", 1)

    def list_of(load):
        entries = load[skel_rows:].astype(jnp.int32)
        return entries[:8] + 256 * entries[8:]

    target_rows, source_rows = pl.pallas_call(
        functools.partial(feature_kernel, seg_size, targets, own_clusters),
        out_shape=[
            jax.ShapeDtypeStruct((3 * targets + 1, DEPTH, LEAF), bf16),
            jax.ShapeDtypeStruct((seg_size, LEAF, DEPTH), bf16),
        ],
        in_specs=[VMEM],
        out_specs=[VMEM, VMEM],
        compiler_params=PARAMS,
        cost_estimate=cost(0.7),
    )(points)
    args = (target_rows, source_rows, mine, other)
    own_near = near_sum(targets, targets, own_list, *args, f32)
    to_before = near_sum(0, targets, list_of(before_load), *args, bf16)
    from_after = shifted(to_before, "blk", -1)
    to_after = near_sum(2 * targets, targets, list_of(after_load), *args, bf16)
    from_before = shifted(to_after, "blk", 1)

    blk = lax.axis_index("blk")
    first = blk * seg_size + lax.axis_index("leaf") * own_clusters
    entries = lax.dynamic_slice_in_dim(far_src, first, own_clusters, 0)
    far_shape = jax.ShapeDtypeStruct((columns, own_clusters * LEAF), f32)
    if blk_count == 4 and cluster_total <= 256:
        middle_load = shifted(prev_load, "blk", 2)
        entries = lax.rem(entries + (blk_count - blk) * seg_size, cluster_total)
        far = pl.pallas_call(
            functools.partial(far_kernel_wide, seg_size),
            out_shape=far_shape,
            in_specs=[SMEM, ANY] + [VMEM] * 5,
            out_specs=VMEM,
            scratch_shapes=[
                pltpu.VMEM((pack, cluster_total, rank, LEAF), bf16),
                pltpu.VMEM(couplings.shape, bf16),
                pltpu.SemaphoreType.DMA((own_clusters,)),
            ],
            compiler_params=PARAMS,
            cost_estimate=cost(3.0),
        )(entries, couplings, basis, prev_load, after_load, middle_load, before_load)
    else:
        far = pl.pallas_call(
            functools.partial(far_kernel, seg_size),
            out_shape=far_shape,
            in_specs=[SMEM] + [VMEM] * 3,
            out_specs=VMEM,
            scratch_shapes=[pltpu.VMEM((cluster_total, rank, columns), bf16)],
            compiler_params=PARAMS,
        )(entries, couplings, basis, lax.all_gather(prev_load[:skel_rows], "blk", axis=0, tiled=True))

    near = own_near + from_before.astype(f32) + from_after.astype(f32)
    keep = near[:columns]
    got = shifted(near[columns:], "rhs", 1)
    even = lax.axis_index("rhs") == 0
    whole = jnp.concatenate([jnp.where(even, keep, got), jnp.where(even, got, keep)], axis=1)
    return (whole + far).astype(bf16).T


def solution(mesh):
    in_specs = (
        P(None, "groups"),
        P(("groups", "blk"), "rhs"),
        P(None, ("groups", "blk")),
        P(("groups", "blk", "leaf"), None, None, None),
        P(("groups", "blk", "leaf"), None),
        P("groups", None),
    )
    out_specs = P(("groups", "blk", "leaf"), "rhs")
    return jax.shard_map(
        on_device, mesh=mesh, in_specs=in_specs, out_specs=out_specs, check_vma=False
    )
```

time: 42.5 us -> 43 us (1.012)
  Pallas kernels: 18.7 us -> 24.8 us
  local copies, waits for them, and re-layouts: 6.84 us -> 2.77 us
  starting transfers between devices: 12.3 us -> 10.2 us
  waiting for transfers between devices: 3.42 us -> 4.23 us
    pallas_call x1, Pallas kernels: 6.75 us -> 11.1 us  [on_device(): pl.pallas_call(functools.partial(far_kernel_wide, seg_size), out_shape=fa...]
    unnamed x19 -> x17, local copies, waits for them, and re-layouts: 6.76 us -> 2.68 us
    ppermute x9 -> x7, starting transfers between devices: 12.3 us -> 10.2 us  [shifted(): lax.ppermute(block, axis, [(i, (i + shift) % count) for i in range(count)])]
    pallas_call x3, Pallas kernels: 8.15 us -> 9.45 us  [near_sum(): pl.pallas_call(functools.partial(near_kernel, base), out_shape=jax.ShapeD...]
    ppermute x9 -> x7, waiting for transfers between devices: 3.42 us -> 4.23 us  [shifted(): lax.ppermute(block, axis, [(i, (i + shift) % count) for i in range(count)])]
    pallas_call x1, Pallas kernels: 3.07 us -> 3.56 us  [on_device(): pl.pallas_call(functools.partial(list_kernel, seg_size), out_shape=[jax.S...]
  transfers between devices with their start and end apart: 9 -> 7, of which waited for: 1 -> 2; matrix products, arithmetic and copies ran while one was open for 0% -> 1% of each run, Pallas kernels for 44% -> 58%
where the time goes in v1:
time: 43 us; the launch traced here: 42.9 us
  Pallas kernels  24.8 us (58%)
  starting transfers between devices  10.2 us (24%)
  waiting for transfers between devices  4.23 us (10%)
  local copies, waits for them, and re-layouts  2.77 us (6%)
  other arithmetic  0.78 us (2%)
    pallas_call x1, Pallas kernels, on_device(): pl.pallas_call(functools.partial(far_kernel_wide, seg_size), out_shape=fa...  11.1 us
    ppermute x7, starting transfers between devices, shifted(): lax.ppermute(block, axis, [(i, (i + shift) % count) for i in range(count)])  10.2 us
    pallas_call x3, Pallas kernels, near_sum(): pl.pallas_call(functools.partial(near_kernel, base), out_shape=jax.ShapeD...  9.45 us
    ppermute x7, waiting for transfers between devices, shifted(): lax.ppermute(block, axis, [(i, (i + shift) % count) for i in range(count)])  4.23 us
    pallas_call x1, Pallas kernels, on_device(): pl.pallas_call(functools.partial(list_kernel, seg_size), out_shape=[jax.S...  3.56 us
    unnamed x17, local copies, waits for them, and re-layouts  2.68 us
  transfers between devices with their start and end apart: 7, of which 2 were waited for; matrix products, arithmetic and copies ran while one was open for 1% of the time, Pallas kernels for 58%

profile of v1, /device:TPU:0, one launch (start us, length us, event | category | flops | bytes accessed | tf_op | source)
XLA Modules:
  0.0 42.9 jit_solution(13193366189312356106)
XLA Ops:
  0.0 0.5 %collective-permute-start = (bf16[32,4096]{1,0:T(8,128)(2,1)}, bf16[32,4096]{1,0:T(8,128)(2,1)S(1)}, u32[]{:S(2)}, u32[]{:S(2)}) collective-permute-start(bf16[32,4096]{1,0:T(8,128)(2,1)} %bitcast.3), channel_id=1, source_target_pairs={{0,1},{1,0},{2,3},{3,2},{4,5},{5,4},{6,7},{7,6},{8,9},{9,8},{10,11... | collective-permute-start | bytes 786440 | tf_op jit(solution)/shard_map/ppermute | solution.py:32
  0.5 0.9 %copy-done.3 = bf16[4096,32]{0,1:T(8,128)(2,1)S(1)} copy-done((bf16[4096,32]{0,1:T(8,128)(2,1)S(1)}, bf16[4096,32]{0,1:T(8,128)(2,1)}, u32[]{:S(2)}) %copy-start.3) | copy-done | bytes 262168
  1.4 0.9 %copy-done.5 = bf16[32,4096]{1,0:T(8,128)(2,1)S(1)} copy-done((bf16[32,4096]{1,0:T(8,128)(2,1)S(1)}, bf16[32,4096]{1,0:T(8,128)(2,1)}, u32[]{:S(2)}) %copy-start.5) | copy-done | bytes 262168
  2.4 0.7 %copy-done.7 = s32[16,27]{1,0:T(8,128)S(1)} copy-done((s32[16,27]{1,0:T(8,128)S(1)}, s32[16,27]{1,0:T(8,128)}, u32[]{:S(2)}) %copy-start.7) | copy-done | bytes 1752
  3.1 3.6 %shard_map.64 = (s32[8,128]{1,0:T(8,128)S(1)}, bf16[272,128]{1,0:T(8,128)(2,1)S(1)}, bf16[272,128]{1,0:T(8,128)(2,1)S(1)}) custom-call(s32[16,27]{1,0:T(8,128)S(1)} %copy-done.7, bf16[32,4096]{1,0:T(8,128)(2,1)S(1)} %copy-done.5, bf16[32,4096]{1,0:T(8,128)(2,1)S(1)} %bitcast.4), custom_call_target="tpu_custom_call" | custom-call | flops 3000000000 | tf_op jit(solution)/shard_map/pallas_call | solution.py:315
  6.6 4.7 %collective-permute-start.1 = (bf16[272,128]{1,0:T(8,128)(2,1)S(1)}, bf16[272,128]{1,0:T(8,128)(2,1)S(1)}, u32[]{:S(2)}, u32[]{:S(2)}) collective-permute-start(bf16[272,128]{1,0:T(8,128)(2,1)S(1)} %get-tuple-element.13.refs_0_), channel_id=1, source_target_pairs={{0,12},{4,0},{8,4},{12,8},{1,13},{5,1},{9,5},{13,9},{2,14},{6,2},{... | collective-permute-start | bytes 208904 | tf_op jit(solution)/shard_map/ppermute | solution.py:32
  11.3 0.0 collective-permute-start.6
  11.3 1.0 %collective-permute-start.3 = (bf16[272,128]{1,0:T(8,128)(2,1)S(1)}, bf16[272,128]{1,0:T(8,128)(2,1)S(1)}, u32[]{:S(2)}, u32[]{:S(2)}) collective-permute-start(bf16[272,128]{1,0:T(8,128)(2,1)S(1)} %get-tuple-element.14), channel_id=1, source_target_pairs={{0,4},{4,8},{8,12},{12,0},{1,5},{5,9},{9,13},{13,1},{2,6},{6,10},{... | collective-permute-start | bytes 208904 | tf_op jit(solution)/shard_map/ppermute | solution.py:32
  12.3 0.1 constant_dynamic-slice_fusion
  12.4 0.1 copy.8
  12.5 0.7 %shard_map.65 = (bf16[25,48,128]{2,1,0:T(8,128)(2,1)S(1)}, bf16[32,128,48]{2,1,0:T(8,128)(2,1)S(1)}) custom-call(f32[3,16384]{1,0:T(4,128)S(1)} %copy-done.2), custom_call_target="tpu_custom_call" | custom-call | flops 700000000 | tf_op jit(solution)/shard_map/pallas_call | solution.py:338
  13.2 0.6 %collective-permute-done.1.refs_1_ = bf16[272,128]{1,0:T(8,128)(2,1)S(1)} collective-permute-done((bf16[272,128]{1,0:T(8,128)(2,1)S(1)}, bf16[272,128]{1,0:T(8,128)(2,1)S(1)}, u32[]{:S(2)}, u32[]{:S(2)}) %collective-permute-start.1) | collective-permute-done | bytes 69664 | tf_op jit(solution)/shard_map/ppermute | solution.py:32
  13.9 3.6 %collective-permute-done.3.refs_3_ = bf16[272,128]{1,0:T(8,128)(2,1)S(1)} collective-permute-done((bf16[272,128]{1,0:T(8,128)(2,1)S(1)}, bf16[272,128]{1,0:T(8,128)(2,1)S(1)}, u32[]{:S(2)}, u32[]{:S(2)}) %collective-permute-start.3) | collective-permute-done | bytes 69664 | tf_op jit(solution)/shard_map/ppermute | solution.py:32
  17.5 0.0 collective-permute-done.other_ref
  17.5 2.9 %shard_map.67 = bf16[64,1024]{1,0:T(8,128)(2,1)S(1)} custom-call(s32[8,128]{1,0:T(8,128)S(1)} %fusion.4.list_ref, bf16[25,48,128]{2,1,0:T(8,128)(2,1)S(1)} %get-tuple-element.11.target_ref, bf16[32,128,48]{2,1,0:T(8,128)(2,1)S(1)} %get-tuple-element.12.source_ref, bf16[32,4096]{1,0:T(8,128)(2,1)S(1)} %bitcast.5, ...), custom_call_target="tpu_custom_call" | custom-call | flops 2500000000 | tf_op jit(solution)/shard_map/pallas_call | solution.py:211
  20.4 1.5 %collective-permute-start.2 = (bf16[64,1024]{1,0:T(8,128)(2,1)S(1)}, bf16[64,1024]{1,0:T(8,128)(2,1)S(1)}, u32[]{:S(2)}, u32[]{:S(2)}) collective-permute-start(bf16[64,1024]{1,0:T(8,128)(2,1)S(1)} %shard_map.67), channel_id=1, source_target_pairs={{0,4},{4,8},{8,12},{12,0},{1,5},{5,9},{9,13},{13,1},{2,6},{6,10},{... | collective-permute-start | bytes 393224 | tf_op jit(solution)/shard_map/ppermute | solution.py:32
  21.9 3.3 %shard_map.68 = bf16[64,1024]{1,0:T(8,128)(2,1)S(1)} custom-call(s32[8,128]{1,0:T(8,128)S(1)} %fusion.3.list_ref, bf16[25,48,128]{2,1,0:T(8,128)(2,1)S(1)} %get-tuple-element.11.target_ref, bf16[32,128,48]{2,1,0:T(8,128)(2,1)S(1)} %get-tuple-element.12.source_ref, bf16[32,4096]{1,0:T(8,128)(2,1)S(1)} %bitcast.6, ...), custom_call_target="tpu_custom_call" | custom-call | flops 2500000000 | tf_op jit(solution)/shard_map/pallas_call | solution.py:211
  25.2 2.4 %collective-permute-start.4 = (bf16[64,1024]{1,0:T(8,128)(2,1)S(1)}, bf16[64,1024]{1,0:T(8,128)(2,1)S(1)}, u32[]{:S(2)}, u32[]{:S(2)}) collective-permute-start(bf16[64,1024]{1,0:T(8,128)(2,1)S(1)} %shard_map.68), channel_id=1, source_target_pairs={{0,12},{4,0},{8,4},{12,8},{1,13},{5,1},{9,5},{13,9},{2,14},{6,2},{... | collective-permute-start | bytes 393224 | tf_op jit(solution)/shard_map/ppermute | solution.py:32
  27.6 3.3 %shard_map.66 = f32[64,1024]{1,0:T(8,128)S(1)} custom-call(s32[8,128]{1,0:T(8,128)S(1)} %get-tuple-element.10.list_ref, bf16[25,48,128]{2,1,0:T(8,128)(2,1)S(1)} %get-tuple-element.11.target_ref, bf16[32,128,48]{2,1,0:T(8,128)(2,1)S(1)} %get-tuple-element.12.source_ref, bf16[32,4096]{1,0:T(8,128)(2,1)S(1)} %bitcast.7, ...), custom_call_target="tpu_custom_call" | custom-call | flops 2500000000 | tf_op jit(solution)/shard_map/pallas_call | solution.py:211
  30.9 0.0 collective-permute-done.2
  30.9 0.0 collective-permute-done.4
  31.0 0.1 collective-permute-start.5
  31.1 11.1 %shard_map.69 = f32[32,2048]{1,0:T(8,128)S(1)} custom-call(s32[16,32]{1,0:T(8,128)S(1)} %negate_select_fusion.far_ref, bf16[16,32,32,32]{3,2,1,0:T(8,128)(2,1)S(1)} %copy-done.1, bf16[32,4096]{1,0:T(8,128)(2,1)S(1)} %copy-done.6, bf16[272,128]{1,0:T(8,128)(2,1)S(1)} %get-tuple-element.13.refs_0_, bf16[272,128]{1,0:T(8,128)(2,1)S(1)} %collective-permute-done.1.refs_1_, ...), custom_call_target="tpu_custom_call" | custom-call | flops 3000000000 | tf_op jit(solution)/shard_map/pallas_call | solution.py:363
  42.2 0.7 %fusion.1 = bf16[2048,32]{0,1:T(8,128)(2,1)} fusion(f32[32,2048]{1,0:T(8,128)S(1)} %shard_map.69, f32[32,1024]{1,0:T(8,128)S(1)} %get-tuple-element.16, f32[32,1024]{1,0:T(8,128)S(1)} %get-tuple-element.15), kind=kLoop, calls=%fused_computation.3 | loop fusion | flops 196608 | bytes 655360 | tf_op jit(solution)/shard_map/transpose | solution.py:391
  (23 shorter events, 0.1 us)
Async XLA Ops:
  0.0 12.3 %copy-start = (s32[128,32]{0,1:T(8,128)S(1)}, s32[128,32]{0,1:T(8,128)}, u32[]{:S(2)}) copy-start(s32[128,32]{0,1:T(8,128)} %param.11) | copy-start | bytes 49156
  0.0 12.5 %copy-start.2 = (f32[3,16384]{1,0:T(4,128)S(1)}, f32[3,16384]{1,0:T(4,128)}, u32[]{:S(2)}) copy-start(f32[3,16384]{1,0:T(4,128)} %points_ref.1) | copy-start | bytes 589828
  0.0 17.5 %collective-permute-start = (bf16[32,4096]{1,0:T(8,128)(2,1)}, bf16[32,4096]{1,0:T(8,128)(2,1)S(1)}, u32[]{:S(2)}, u32[]{:S(2)}) collective-permute-start(bf16[32,4096]{1,0:T(8,128)(2,1)} %bitcast.3), channel_id=1, source_target_pairs={{0,1},{1,0},{2,3},{3,2},{4,5},{5,4},{6,7},{7,6},{8,9},{9,8},{10,11... | collective-permute-start | bytes 786440 | tf_op jit(solution)/shard_map/ppermute | solution.py:32
  0.5 0.9 %copy-start.3 = (bf16[4096,32]{0,1:T(8,128)(2,1)S(1)}, bf16[4096,32]{0,1:T(8,128)(2,1)}, u32[]{:S(2)}) copy-start(bf16[4096,32]{0,1:T(8,128)(2,1)} %param.7) | copy-start | bytes 786436
  1.4 0.9 %copy-start.5 = (bf16[32,4096]{1,0:T(8,128)(2,1)S(1)}, bf16[32,4096]{1,0:T(8,128)(2,1)}, u32[]{:S(2)}) copy-start(bf16[32,4096]{1,0:T(8,128)(2,1)} %basis_ref.1) | copy-start | bytes 786436
  2.4 0.7 %copy-start.7 = (s32[16,27]{1,0:T(8,128)S(1)}, s32[16,27]{1,0:T(8,128)}, u32[]{:S(2)}) copy-start(s32[16,27]{1,0:T(8,128)} %near_hbm.1) | copy-start | bytes 5188
  3.1 14.4 %copy-start.4 = (bf16[4096,32]{0,1:T(8,128)(2,1)S(1)}, bf16[4096,32]{0,1:T(8,128)(2,1)}, u32[]{:S(2)}) copy-start(bf16[4096,32]{0,1:T(8,128)(2,1)} %param.7) | copy-start | bytes 786436
  6.6 7.2 %collective-permute-start.1 = (bf16[272,128]{1,0:T(8,128)(2,1)S(1)}, bf16[272,128]{1,0:T(8,128)(2,1)S(1)}, u32[]{:S(2)}, u32[]{:S(2)}) collective-permute-start(bf16[272,128]{1,0:T(8,128)(2,1)S(1)} %get-tuple-element.13.refs_0_), channel_id=1, source_target_pairs={{0,12},{4,0},{8,4},{12,8},{1,13},{5,1},{9,5},{13,9},{2,14},{6,2},{... | collective-permute-start | bytes 208904 | tf_op jit(solution)/shard_map/ppermute | solution.py:32
  11.3 19.7 %collective-permute-start.6 = (bf16[272,128]{1,0:T(8,128)(2,1)S(1)}, bf16[272,128]{1,0:T(8,128)(2,1)S(1)}, u32[]{:S(2)}, u32[]{:S(2)}) collective-permute-start(bf16[272,128]{1,0:T(8,128)(2,1)S(1)} %get-tuple-element.13.refs_0_), channel_id=1, source_target_pairs={{0,8},{4,12},{8,0},{12,4},{1,9},{5,13},{9,1},{13,5},{2,10},{6,14},... | collective-permute-start | bytes 208904 | tf_op jit(solution)/shard_map/ppermute | solution.py:32
  11.3 6.1 %collective-permute-start.3 = (bf16[272,128]{1,0:T(8,128)(2,1)S(1)}, bf16[272,128]{1,0:T(8,128)(2,1)S(1)}, u32[]{:S(2)}, u32[]{:S(2)}) collective-permute-start(bf16[272,128]{1,0:T(8,128)(2,1)S(1)} %get-tuple-element.14), channel_id=1, source_target_pairs={{0,4},{4,8},{8,12},{12,0},{1,5},{5,9},{9,13},{13,1},{2,6},{6,10},{... | collective-permute-start | bytes 208904 | tf_op jit(solution)/shard_map/ppermute | solution.py:32
  20.4 10.5 %collective-permute-start.2 = (bf16[64,1024]{1,0:T(8,128)(2,1)S(1)}, bf16[64,1024]{1,0:T(8,128)(2,1)S(1)}, u32[]{:S(2)}, u32[]{:S(2)}) collective-permute-start(bf16[64,1024]{1,0:T(8,128)(2,1)S(1)} %shard_map.67), channel_id=1, source_target_pairs={{0,4},{4,8},{8,12},{12,0},{1,5},{5,9},{9,13},{13,1},{2,6},{6,10},{... | collective-permute-start | bytes 393224 | tf_op jit(solution)/shard_map/ppermute | solution.py:32
  25.2 5.7 %collective-permute-start.4 = (bf16[64,1024]{1,0:T(8,128)(2,1)S(1)}, bf16[64,1024]{1,0:T(8,128)(2,1)S(1)}, u32[]{:S(2)}, u32[]{:S(2)}) collective-permute-start(bf16[64,1024]{1,0:T(8,128)(2,1)S(1)} %shard_map.68), channel_id=1, source_target_pairs={{0,12},{4,0},{8,4},{12,8},{1,13},{5,1},{9,5},{13,9},{2,14},{6,2},{... | collective-permute-start | bytes 393224 | tf_op jit(solution)/shard_map/ppermute | solution.py:32
  27.6 3.5 %copy-start.1 = (bf16[16,32,32,32]{3,2,1,0:T(8,128)(2,1)S(1)}, bf16[16,32,32,32]{3,2,1,0:T(8,128)(2,1)}, u32[]{:S(2)}) copy-start(bf16[16,32,32,32]{3,2,1,0:T(8,128)(2,1)} %couplings_hbm.1) | copy-start | bytes 3145732
  27.6 3.5 %copy-start.6 = (bf16[32,4096]{1,0:T(8,128)(2,1)S(1)}, bf16[32,4096]{1,0:T(8,128)(2,1)}, u32[]{:S(2)}) copy-start(bf16[32,4096]{1,0:T(8,128)(2,1)} %basis_ref.1) | copy-start | bytes 786436
  31.0 11.2 %collective-permute-start.5 = (f32[32,1024]{1,0:T(8,128)S(1)}, f32[32,1024]{1,0:T(8,128)S(1)}, u32[]{:S(2)}, u32[]{:S(2)}) collective-permute-start(f32[32,1024]{1,0:T(8,128)S(1)} %slice.39), channel_id=1, source_target_pairs={{0,1},{1,0},{2,3},{3,2},{4,5},{5,4},{6,7},{7,6},{8,9},{9,8},{10,11... | collective-permute-start | bytes 393224 | tf_op jit(solution)/shard_map/ppermute | solution.py:32

commit v2 on v1

v2 whole, which is shorter than its diff:
```python
import functools

import jax
import jax.numpy as jnp
from jax import lax
from jax.experimental import pallas as pl
from jax.experimental.pallas import tpu as pltpu
from jax.sharding import PartitionSpec as P

LEAF = 128
BATCH = 12
DEPTH = 48

kernel_scale = 0.0625 / (4.0 * 3.141592653589793)
soften = 0.001
inverse_sq = 1.0 / (kernel_scale * kernel_scale)

bf16 = jnp.bfloat16
f32 = jnp.float32
VMEM = pl.BlockSpec(memory_space=pltpu.VMEM)
HBM = pl.BlockSpec(memory_space=pltpu.HBM)
SMEM = pl.BlockSpec(memory_space=pltpu.SMEM)
PARAMS = pltpu.CompilerParams(vmem_limit_bytes=48 * 2**20)


def cost(microseconds):
    return pl.CostEstimate(flops=int(microseconds * 1e9), bytes_accessed=0, transcendentals=0)


def shifted(block, axis, shift):
    count = lax.axis_size(axis)
    return lax.ppermute(block, axis, [(i, (i + shift) % count) for i in range(count)])


def cluster(index):
    return pl.ds(pl.multiple_of(index * LEAF, LEAF), LEAF)


def list_kernel(seg_size, near_hbm, basis_hbm, charges_hbm, own_ref, prev_ref, next_ref, near_ref, basis_ref, charges_ref, sems):
    copies = [
        pltpu.make_async_copy(near_hbm, near_ref, sems.at[0]),
        pltpu.make_async_copy(basis_hbm, basis_ref, sems.at[1]),
        pltpu.make_async_copy(charges_hbm, charges_ref, sems.at[2]),
    ]
    for copy in copies:
        copy.start()
    targets = near_ref.shape[0] // 2
    near_count = near_ref.shape[1]
    blk_count = lax.axis_size("blk")
    blk = lax.axis_index("blk")
    before = lax.rem(blk + blk_count - 1, blk_count)
    half = lax.axis_index("rhs")
    columns = charges_ref.shape[0]
    rank = basis_ref.shape[0]
    pack = LEAF // columns
    rows_end = seg_size // pack * rank

    def iota(shape, dim):
        return lax.broadcasted_iota(jnp.int32, shape, dim)

    def ones(condition):
        return jnp.where(condition, 1.0, 0.0).astype(bf16)

    lane = iota((targets, LEAF), 1)
    earlier = ones(iota((LEAF, LEAF), 0) < iota((LEAF, LEAF), 1))
    above = ones(iota((targets, targets), 1) < iota((targets, targets), 0))
    row = iota((8, LEAF), 0)
    lower = iota((LEAF, LEAF), 0)
    copies[0].wait()
    sources = jnp.where(half == 0, near_ref[:targets, :], near_ref[targets:, :])
    sources = jnp.concatenate(
        [sources, jnp.full((targets, LEAF - near_count), -1, jnp.int32)], axis=1
    )
    segment = jnp.zeros((targets, LEAF), jnp.int32)
    if seg_size & (seg_size - 1) == 0:
        segment = lax.shift_right_arithmetic(sources, seg_size.bit_length() - 1)
    else:
        segment = lax.div(sources, seg_size)
    local = (sources - segment * seg_size).astype(f32)
    is_own = segment == blk
    is_prev = jnp.logical_and(segment == before, jnp.logical_not(is_own))
    is_next = jnp.logical_and(lane < near_count, jnp.logical_not(jnp.logical_or(is_own, is_prev)))
    masks = (is_own, is_prev, is_next)
    place = jnp.zeros((targets, LEAF), f32)
    totals = []
    for mask in masks:
        within = jnp.dot(ones(mask), earlier, preferred_element_type=f32)
        count = jnp.broadcast_to(within[:, LEAF - 1 :], (targets, LEAF))
        start = jnp.dot(above, count.astype(bf16), preferred_element_type=f32)
        place = jnp.where(mask, start + within, place)
        totals.append(start[targets - 1 :, :] + count[targets - 1 :, :])
    place = place.astype(jnp.int32)
    left, right = [], []
    for target in range(targets):
        at = place[target : target + 1, :]
        here = lax.shift_right_logical(at, 7) == row
        rows = []
        for mask in masks:
            chosen = jnp.logical_and(here, jnp.where(mask[target : target + 1, :], 1, 0) == 1)
            rows.append(jnp.where(chosen, local[target : target + 1, :], 0.0))
            rows.append(jnp.where(chosen, float(target), 0.0))
        left.append(jnp.concatenate(rows, axis=0).astype(bf16))
        right.append(ones(lax.bitwise_and(at, LEAF - 1) == lower))
    lists = lax.dot_general(
        jnp.concatenate(left, axis=1),
        jnp.concatenate(right, axis=1),
        (((1,), (1,)), ((), ())),
        preferred_element_type=f32,
    )
    last = row * LEAF + iota((8, LEAF), 1) == 8 * LEAF - 1
    finished = []
    for i, total in enumerate(totals):
        high = jnp.floor(total * (1.0 / 256.0))
        finished.append(jnp.where(last, total - 256.0 * high, lists[16 * i : 16 * i + 8]))
        finished.append(jnp.where(last, high, lists[16 * i + 8 : 16 * i + 16]))
    own_ref[...] = finished[0].astype(jnp.int32) + 256 * finished[1].astype(jnp.int32)
    prev_ref[rows_end : rows_end + 16, :] = jnp.concatenate(finished[2:4], axis=0).astype(bf16)
    next_ref[rows_end : rows_end + 16, :] = jnp.concatenate(finished[4:6], axis=0).astype(bf16)

    copies[1].wait()
    copies[2].wait()
    blocks = []
    for group in range(seg_size // pack):
        rows = []
        for i in range(pack):
            at = (group * pack + i) * LEAF
            parts = [jnp.zeros((columns, LEAF), bf16)] * pack
            parts[i] = charges_ref[:, at : at + LEAF]
            rows.append(jnp.concatenate(parts, axis=1))
        at = group * pack * LEAF
        blocks.append(
            lax.dot_general(
                basis_ref[:, at : at + pack * LEAF],
                jnp.concatenate(rows, axis=0),
                (((1,), (1,)), ((), ())),
                preferred_element_type=f32,
            )
        )
    for group, block in enumerate(blocks):
        prev_ref[group * rank : (group + 1) * rank, :] = block.astype(bf16)
        next_ref[group * rank : (group + 1) * rank, :] = block.astype(bf16)


def split(value):
    high = value.astype(bf16).astype(f32)
    rest = value - high
    middle = rest.astype(bf16).astype(f32)
    return high, middle, rest - middle


def coords_of(points_ref, at):
    block = points_ref[:, cluster(at)]
    zero, one, two = block[0:1, :], block[1:2, :], block[2:3, :]
    return zero, one, two, zero * zero + one * one + two * two


def rows_of(values):
    row = lax.broadcasted_iota(jnp.int32, (8, LEAF), 0)
    out = jnp.zeros((8, LEAF), f32)
    for i, value in enumerate(values):
        out = jnp.where(row == i, value, out)
    return out


def target_features(points_ref, at):
    zero, one, two, norm = coords_of(points_ref, at)
    slope = -2.0 * inverse_sq
    rows = rows_of((zero * slope, one * slope, two * slope, (norm + soften) * inverse_sq, 1.0))
    high, middle, low = split(rows)
    return jnp.concatenate([high, high, middle, middle, high, low], axis=0).astype(bf16)


def source_features(points_ref, at):
    zero, one, two, norm = coords_of(points_ref, at)
    rows = rows_of((zero, one, two, 1.0, norm * inverse_sq))
    high, middle, low = split(rows)
    stacked = jnp.concatenate([high, middle, high, middle, low, high], axis=0)
    return jnp.transpose(stacked).astype(bf16)


def feature_kernel(seg_size, targets, leaf_clusters, points_ref, target_ref, source_ref):
    blk_count = lax.axis_size("blk")
    blk = lax.axis_index("blk")
    first = lax.axis_index("leaf") * leaf_clusters + lax.axis_index("rhs") * targets
    for which in range(3):
        segment = lax.rem(blk + which + blk_count - 1, blk_count)
        for i in range(targets):
            target_ref[which * targets + i] = target_features(
                points_ref, segment * seg_size + first + i
            )
    target_ref[3 * targets] = jnp.zeros((DEPTH, LEAF), bf16)

    def some_sources(step, carry):
        for u in range(8):
            at = step * 8 + u
            source_ref[at] = source_features(points_ref, blk * seg_size + at)
        return carry

    lax.fori_loop(0, seg_size // 8, some_sources, 0)


def near_kernel(bases, targets, *refs):
    count = len(bases)
    lists = refs[:count]
    target_ref, source_ref, mine_ref, other_ref = refs[count : count + 4]
    outs = refs[count + 4 : 2 * count + 4]
    total, even, odd = refs[2 * count + 4 :]
    lengths = [ref[7, LEAF - 1] for ref in lists]
    length = sum(lengths)
    batches = lax.div(length + (BATCH - 1), BATCH)
    total[...] = jnp.zeros_like(total)

    def pair(batch, u):
        at = batch * BATCH + u
        code = jnp.int32(3 * targets * 256)
        for i in reversed(range(count)):
            start = sum(lengths[:i])
            place = jnp.maximum(at - start, 0)
            entry = lists[i][lax.shift_right_logical(place, 7), lax.bitwise_and(place, 127)]
            code = jnp.where(at < start + lengths[i], entry + bases[i] * 256, code)
        return lax.shift_right_logical(code, 8), lax.bitwise_and(code, 255)

    def make(batch, slot):
        for u in range(BATCH):
            target, source = pair(batch, u)
            square = jnp.dot(source_ref[source], target_ref[target], preferred_element_type=f32)
            slot[u] = lax.rsqrt(square).astype(bf16)

    def use(batch, slot):
        sums = []
        for u in range(BATCH):
            target, source = pair(batch, u)
            charges = jnp.concatenate([mine_ref[:, cluster(source)], other_ref[:, cluster(source)]], axis=0)
            sums.append((target, jnp.dot(charges, slot[u], preferred_element_type=f32)))
        for target, value in sums:
            total[target] += value

    make(0, even)

    def body(step, carry):
        make(2 * step + 1, odd)
        use(2 * step, even)
        make(2 * step + 2, even)
        use(2 * step + 1, odd)
        return carry

    lax.fori_loop(0, lax.div(batches + 1, 2), body, 0)
    for base, out in zip(bases, outs):
        for i in range(targets):
            out[:, i * LEAF : (i + 1) * LEAF] = total[base + i].astype(out.dtype)


def near_sums(bases, targets, lists, target_rows, source_rows, mine, other, dtype, microseconds):
    columns = 2 * mine.shape[0]
    return pl.pallas_call(
        functools.partial(near_kernel, bases, targets),
        out_shape=[jax.ShapeDtypeStruct((columns, targets * LEAF), dtype)] * len(bases),
        in_specs=[SMEM] * len(bases) + [VMEM] * 4,
        out_specs=[VMEM] * len(bases),
        scratch_shapes=[
            pltpu.VMEM((3 * targets + 1, columns, LEAF), f32),
            pltpu.VMEM((BATCH, LEAF, LEAF), bf16),
            pltpu.VMEM((BATCH, LEAF, LEAF), bf16),
        ],
        compiler_params=PARAMS,
        cost_estimate=cost(microseconds),
    )(*lists, target_rows, source_rows, mine, other)


def far_sum(out_ref, basis_ref, target, at, coefficient):
    out_ref[:, target * LEAF : (target + 1) * LEAF] = lax.dot_general(
        coefficient.astype(bf16),
        basis_ref[:, cluster(at)],
        (((0,), (0,)), ((), ())),
        preferred_element_type=f32,
    )


def far_kernel(seg_size, far_ref, couplings_ref, basis_ref, part, out_ref, skel):
    leaf = lax.axis_index("leaf") * couplings_ref.shape[0]
    clusters, far_count, rank, _ = couplings_ref.shape
    columns = out_ref.shape[0]
    pack = LEAF // columns

    def unpack(group, carry):
        block = part[pl.ds(pl.multiple_of(group * rank, rank), rank), :]
        for i in range(pack):
            skel[group * pack + i] = block[:, i * columns : (i + 1) * columns]
        return carry

    lax.fori_loop(0, part.shape[0] // rank, unpack, 0)
    for target in range(clusters):
        coefficient = jnp.zeros((rank, columns), f32)
        step = 256 // rank
        for at in range(0, far_count, step):
            left = jnp.concatenate([couplings_ref[target, at + i] for i in range(step)], axis=1)
            rows = [skel[far_ref[target, at + i]] for i in range(step)]
            coefficient = coefficient + jnp.dot(
                left, jnp.concatenate(rows, axis=0), preferred_element_type=f32
            )
        far_sum(out_ref, basis_ref, target, leaf + target, coefficient)


def far_kernel_phased(seg_size, far_ref, couplings_ref, basis_ref, *refs):
    parts, (out_ref, skel, side, held) = refs[:-4], refs[-4:]
    clusters, far_count, rank, _ = couplings_ref.shape
    columns = out_ref.shape[0]
    pack = LEAF // columns
    leaf = lax.axis_index("leaf") * clusters
    for target in range(clusters):
        for at in range(0, far_count, pack):
            side[target, :, at * rank : (at + pack) * rank] = jnp.concatenate(
                [couplings_ref[target, at + i] for i in range(pack)], axis=1
            )
    for order, part in enumerate(parts):
        for group in range(seg_size // pack):
            block = part[group * rank : (group + 1) * rank, :]
            for i in range(pack):
                skel[order * seg_size + group * pack + i] = block[:, i * columns : (i + 1) * columns]
    step = 256 // rank
    for target in range(clusters):
        coefficient = jnp.zeros((rank, columns), f32)
        for at in range(0, far_count, step):
            rows = [skel[far_ref[target, at + i]] for i in range(step)]
            coefficient = coefficient + jnp.dot(
                side[target, :, at * rank : (at + step) * rank],
                jnp.concatenate(rows, axis=0),
                preferred_element_type=f32,
            )
        held[target] = coefficient.astype(bf16)
    for target in range(clusters):
        far_sum(out_ref, basis_ref, target, leaf + target, held[target])


def on_device(points, charges, basis, couplings, near_src, far_src):
    blk_count = lax.axis_size("blk")
    mine = charges.T
    columns, seg_rows = mine.shape
    seg_size = seg_rows // LEAF
    rank = basis.shape[0]
    own_clusters, near_count = near_src.shape
    targets = own_clusters // 2
    cluster_total = seg_size * blk_count
    pack = LEAF // columns
    skel_rows = seg_size // pack * rank
    other = shifted(mine, "rhs", 1)

    own_list, prev_load, next_load = pl.pallas_call(
        functools.partial(list_kernel, seg_size),
        out_shape=[jax.ShapeDtypeStruct((8, LEAF), jnp.int32)]
        + [jax.ShapeDtypeStruct((skel_rows + 16, LEAF), bf16)] * 2,
        in_specs=[HBM] * 3,
        out_specs=[VMEM] * 3,
        scratch_shapes=[
            pltpu.VMEM(near_src.shape, jnp.int32),
            pltpu.VMEM(basis.shape, bf16),
            pltpu.VMEM(mine.shape, bf16),
            pltpu.SemaphoreType.DMA((3,)),
        ],
        compiler_params=pltpu.CompilerParams(vmem_limit_bytes=63 * 2**20),
        cost_estimate=cost(3.0),
    )(near_src, basis, mine)

    after_load = shifted(prev_load, "blk", -1)
    before_load = shifted(next_load, "blk", 1)

    def list_of(load):
        entries = load[skel_rows:].astype(jnp.int32)
        return entries[:8] + 256 * entries[8:]

    target_rows, source_rows = pl.pallas_call(
        functools.partial(feature_kernel, seg_size, targets, own_clusters),
        out_shape=[
            jax.ShapeDtypeStruct((3 * targets + 1, DEPTH, LEAF), bf16),
            jax.ShapeDtypeStruct((seg_size, LEAF, DEPTH), bf16),
        ],
        in_specs=[VMEM],
        out_specs=[VMEM, VMEM],
        compiler_params=PARAMS,
        cost_estimate=cost(0.7),
    )(points)
    args = (target_rows, source_rows, mine, other)
    (own_near,) = near_sums((targets,), targets, (own_list,), *args, f32, 2.6)
    own_near, before_load, after_load = lax.optimization_barrier((own_near, before_load, after_load))
    lists = (list_of(before_load), list_of(after_load))
    to_before, to_after = near_sums((0, 2 * targets), targets, lists, *args, bf16, 4.0)
    from_after = shifted(to_before, "blk", -1)
    from_before = shifted(to_after, "blk", 1)

    blk = lax.axis_index("blk")
    first = blk * seg_size + lax.axis_index("leaf") * own_clusters
    entries = lax.dynamic_slice_in_dim(far_src, first, own_clusters, 0)
    far_shape = jax.ShapeDtypeStruct((columns, own_clusters * LEAF), f32)
    if blk_count == 4 and cluster_total <= 256:
        middle_load = shifted(prev_load, "blk", 2)
        entries = lax.rem(entries + (blk_count - blk) * seg_size, cluster_total)
        far = pl.pallas_call(
            functools.partial(far_kernel_phased, seg_size),
            out_shape=far_shape,
            in_specs=[SMEM] + [VMEM] * 6,
            out_specs=VMEM,
            scratch_shapes=[
                pltpu.VMEM((cluster_total, rank, columns), bf16),
                pltpu.VMEM((own_clusters, rank, far_src.shape[1] * rank), bf16),
                pltpu.VMEM((own_clusters, rank, columns), bf16),
            ],
            compiler_params=PARAMS,
            cost_estimate=cost(3.0),
        )(entries, couplings, basis, prev_load, after_load, middle_load, before_load)
    else:
        far = pl.pallas_call(
            functools.partial(far_kernel, seg_size),
            out_shape=far_shape,
            in_specs=[SMEM] + [VMEM] * 3,
            out_specs=VMEM,
            scratch_shapes=[pltpu.VMEM((cluster_total, rank, columns), bf16)],
            compiler_params=PARAMS,
        )(entries, couplings, basis, lax.all_gather(prev_load[:skel_rows], "blk", axis=0, tiled=True))

    far, from_before, from_after = lax.optimization_barrier((far, from_before, from_after))
    near = own_near + from_before.astype(f32) + from_after.astype(f32)
    keep = near[:columns]
    got = shifted(near[columns:], "rhs", 1)
    even = lax.axis_index("rhs") == 0
    whole = jnp.concatenate([jnp.where(even, keep, got), jnp.where(even, got, keep)], axis=1)
    return (whole + far).astype(bf16).T


def solution(mesh):
    in_specs = (
        P(None, "groups"),
        P(("groups", "blk"), "rhs"),
        P(None, ("groups", "blk")),
        P(("groups", "blk", "leaf"), None, None, None),
        P(("groups", "blk", "leaf"), None),
        P("groups", None),
    )
    out_specs = P(("groups", "blk", "leaf"), "rhs")
    return jax.shard_map(
        on_device, mesh=mesh, in_specs=in_specs, out_specs=out_specs, check_vma=False
    )
```

time: 43 us -> 30.7 us (0.71)
  Pallas kernels: 24.8 us -> 13.5 us
  local copies, waits for them, and re-layouts: 2.77 us -> 0.85 us
  waiting for transfers between devices: 4.23 us -> 5 us
    pallas_call x4 -> x3, Pallas kernels: 20.5 us -> 10.4 us  [the longest x2 7.77 us: near_sums(): pl.pallas_call(functools.partial(near_kernel, bases, targets), out_shape=...]
    unnamed x17 -> x15, local copies, waits for them, and re-layouts: 2.68 us -> 0.77 us
    pallas_call x1, Pallas kernels: 3.56 us -> 2.38 us  [on_device(): pl.pallas_call(functools.partial(list_kernel, seg_size), out_shape=[jax.S...]
    ppermute x7, waiting for transfers between devices: 4.23 us -> 5 us  [shifted(): lax.ppermute(block, axis, [(i, (i + shift) % count) for i in range(count)])]
  transfers between devices with their start and end apart: 7 -> 7, of which waited for: 2 -> 4; matrix products, arithmetic and copies ran while one was open for 1% -> 1% of each run, Pallas kernels for 58% -> 44%
where the time goes in v2:
time: 30.7 us; the launch traced here: 30.5 us
  Pallas kernels  13.5 us (44%)
  starting transfers between devices  10.2 us (33%)
  waiting for transfers between devices  5 us (16%)
  local copies, waits for them, and re-layouts  0.85 us (3%)
  other arithmetic  0.78 us (3%)
    ppermute x7, starting transfers between devices, shifted(): lax.ppermute(block, axis, [(i, (i + shift) % count) for i in range(count)])  10.2 us
    pallas_call x2, Pallas kernels, near_sums(): pl.pallas_call(functools.partial(near_kernel, bases, targets), out_shape=...  7.77 us
    ppermute x7, waiting for transfers between devices, shifted(): lax.ppermute(block, axis, [(i, (i + shift) % count) for i in range(count)])  5 us
    pallas_call x1, Pallas kernels, on_device(): pl.pallas_call(functools.partial(far_kernel_phased, seg_size), out_shape=...  2.64 us
    pallas_call x1, Pallas kernels, on_device(): pl.pallas_call(functools.partial(list_kernel, seg_size), out_shape=[jax.S...  2.38 us
    unnamed x15, local copies, waits for them, and re-layouts  0.77 us
    pallas_call x1, Pallas kernels, on_device(): pl.pallas_call(functools.partial(feature_kernel, seg_size, targets, own_c...  0.7 us
    transpose x1, other arithmetic, on_device(): return (whole + far).astype(bf16).T  0.68 us
  transfers between devices with their start and end apart: 7, of which 4 were waited for; matrix products, arithmetic and copies ran while one was open for 1% of the time, Pallas kernels for 44%

profile of v2, /device:TPU:0, one launch (start us, length us, event | category | flops | bytes accessed | tf_op | source)
XLA Modules:
  0.0 30.5 jit_solution(12173932962180532909)
XLA Ops:
  0.0 0.5 %collective-permute-start = (bf16[32,4096]{1,0:T(8,128)(2,1)}, bf16[32,4096]{1,0:T(8,128)(2,1)S(1)}, u32[]{:S(2)}, u32[]{:S(2)}) collective-permute-start(bf16[32,4096]{1,0:T(8,128)(2,1)} %bitcast.3), channel_id=1, source_target_pairs={{0,1},{1,0},{2,3},{3,2},{4,5},{5,4},{6,7},{7,6},{8,9},{9,8},{10,11... | collective-permute-start | bytes 786440 | tf_op jit(solution)/shard_map/ppermute | solution.py:32
  0.5 2.4 %shard_map.64 = (s32[8,128]{1,0:T(8,128)}, bf16[272,128]{1,0:T(8,128)(2,1)}, bf16[272,128]{1,0:T(8,128)(2,1)}) custom-call(s32[16,27]{1,0:T(8,128)} %near_hbm.1, bf16[32,4096]{1,0:T(8,128)(2,1)} %basis_ref.1, bf16[32,4096]{1,0:T(8,128)(2,1)} %bitcast.4), custom_call_target="tpu_custom_call" | custom-call | flops 3000000000 | tf_op jit(solution)/shard_map/pallas_call | solution.py:348
  2.9 4.7 %collective-permute-start.2 = (bf16[272,128]{1,0:T(8,128)(2,1)}, bf16[272,128]{1,0:T(8,128)(2,1)S(1)}, u32[]{:S(2)}, u32[]{:S(2)}) collective-permute-start(bf16[272,128]{1,0:T(8,128)(2,1)} %get-tuple-element.22.refs_0_), channel_id=1, source_target_pairs={{0,12},{4,0},{8,4},{12,8},{1,13},{5,1},{9,5},{13,9},{2,14},{6,2},{... | collective-permute-start | bytes 208904 | tf_op jit(solution)/shard_map/ppermute | solution.py:32
  7.6 1.0 %collective-permute-start.1 = (bf16[272,128]{1,0:T(8,128)(2,1)}, bf16[272,128]{1,0:T(8,128)(2,1)S(1)}, u32[]{:S(2)}, u32[]{:S(2)}) collective-permute-start(bf16[272,128]{1,0:T(8,128)(2,1)} %get-tuple-element.21), channel_id=1, source_target_pairs={{0,4},{4,8},{8,12},{12,0},{1,5},{5,9},{9,13},{13,1},{2,6},{6,10},{... | collective-permute-start | bytes 208904 | tf_op jit(solution)/shard_map/ppermute | solution.py:32
  8.7 0.1 constant_dynamic-slice_fusion
  8.7 0.1 copy.8
  8.8 0.7 %shard_map.65 = (bf16[25,48,128]{2,1,0:T(8,128)(2,1)S(1)}, bf16[32,128,48]{2,1,0:T(8,128)(2,1)S(1)}) custom-call(f32[3,16384]{1,0:T(4,128)S(1)} %copy-done.2), custom_call_target="tpu_custom_call" | custom-call | flops 700000000 | tf_op jit(solution)/shard_map/pallas_call | solution.py:371
  9.5 0.0 collective-permute-done.refs_4_.refs_5_
  9.6 0.7 %copy-done.6 = s32[8,128]{1,0:T(8,128)S(1)} copy-done((s32[8,128]{1,0:T(8,128)S(1)}, s32[8,128]{1,0:T(8,128)}, u32[]{:S(2)}) %copy-start.6) | copy-done | bytes 4120
  10.2 3.2 %shard_map.66 = f32[64,1024]{1,0:T(8,128)S(1)} custom-call(s32[8,128]{1,0:T(8,128)S(1)} %copy-done.6, bf16[25,48,128]{2,1,0:T(8,128)(2,1)S(1)} %get-tuple-element.19.refs_1_.refs_2_, bf16[32,128,48]{2,1,0:T(8,128)(2,1)S(1)} %get-tuple-element.20.refs_2_.refs_3_, bf16[32,4096]{1,0:T(8,128)(2,1)S(1)} %bitcast.5, ...), custom_call_target="tpu_custom_call" | custom-call | flops 2600000000 | tf_op jit(solution)/shard_map/pallas_call | solution.py:255
  13.4 0.6 %collective-permute-done.1.refs_3_ = bf16[272,128]{1,0:T(8,128)(2,1)S(1)} collective-permute-done((bf16[272,128]{1,0:T(8,128)(2,1)}, bf16[272,128]{1,0:T(8,128)(2,1)S(1)}, u32[]{:S(2)}, u32[]{:S(2)}) %collective-permute-start.1) | collective-permute-done | bytes 69664 | tf_op jit(solution)/shard_map/ppermute | solution.py:32
  14.0 0.0 copy-start.1
  14.0 0.0 copy-start.4
  14.0 0.0 copy-start.5
  14.0 4.6 %shard_map.68 = (bf16[64,1024]{1,0:T(8,128)(2,1)S(1)}, bf16[64,1024]{1,0:T(8,128)(2,1)S(1)}) custom-call(s32[8,128]{1,0:T(8,128)S(1)} %fusion.4.refs_0_, s32[8,128]{1,0:T(8,128)S(1)} %fusion.3.refs_1_, bf16[25,48,128]{2,1,0:T(8,128)(2,1)S(1)} %get-tuple-element.19.refs_1_.refs_2_, bf16[32,128,48]{2,1,0:T(8,128)(2,1)S(1)} %get-tuple-element.20.refs_2_.refs_3_, ...), custom_call_target="tpu_custom_call" | custom-call | flops 4000000000 | tf_op jit(solution)/shard_map/pallas_call | solution.py:255
  18.6 1.5 %collective-permute-start.4 = (bf16[64,1024]{1,0:T(8,128)(2,1)S(1)}, bf16[64,1024]{1,0:T(8,128)(2,1)S(1)}, u32[]{:S(2)}, u32[]{:S(2)}) collective-permute-start(bf16[64,1024]{1,0:T(8,128)(2,1)S(1)} %get-tuple-element.26), channel_id=1, source_target_pairs={{0,4},{4,8},{8,12},{12,0},{1,5},{5,9},{9,13},{13,1},{2,6},{6,10},{... | collective-permute-start | bytes 393224 | tf_op jit(solution)/shard_map/ppermute | solution.py:32
  20.1 2.4 %collective-permute-start.5 = (bf16[64,1024]{1,0:T(8,128)(2,1)S(1)}, bf16[64,1024]{1,0:T(8,128)(2,1)S(1)}, u32[]{:S(2)}, u32[]{:S(2)}) collective-permute-start(bf16[64,1024]{1,0:T(8,128)(2,1)S(1)} %get-tuple-element.27), channel_id=1, source_target_pairs={{0,12},{4,0},{8,4},{12,8},{1,13},{5,1},{9,5},{13,9},{2,14},{6,2},{... | collective-permute-start | bytes 393224 | tf_op jit(solution)/shard_map/ppermute | solution.py:32
  22.5 2.6 %shard_map.67 = f32[32,2048]{1,0:T(8,128)S(1)} custom-call(s32[16,32]{1,0:T(8,128)S(1)} %negate_select_fusion.far_ref, bf16[16,32,32,32]{3,2,1,0:T(8,128)(2,1)S(1)} %copy-done.1, bf16[32,4096]{1,0:T(8,128)(2,1)S(1)} %copy-done.4, bf16[272,128]{1,0:T(8,128)(2,1)S(1)} %copy-done.5, bf16[272,128]{1,0:T(8,128)(2,1)S(1)} %collective-permute-done.2.refs_1_, ...), custom_call_target="tpu_custom_call" | custom-call | flops 3000000000 | tf_op jit(solution)/shard_map/pallas_call | solution.py:397
  25.2 1.8 %collective-permute-done.4 = bf16[64,1024]{1,0:T(8,128)(2,1)S(1)} collective-permute-done((bf16[64,1024]{1,0:T(8,128)(2,1)S(1)}, bf16[64,1024]{1,0:T(8,128)(2,1)S(1)}, u32[]{:S(2)}, u32[]{:S(2)}) %collective-permute-start.4) | collective-permute-done | bytes 131104 | tf_op jit(solution)/shard_map/ppermute | solution.py:32
  27.0 1.3 %collective-permute-done.5 = bf16[64,1024]{1,0:T(8,128)(2,1)S(1)} collective-permute-done((bf16[64,1024]{1,0:T(8,128)(2,1)S(1)}, bf16[64,1024]{1,0:T(8,128)(2,1)S(1)}, u32[]{:S(2)}, u32[]{:S(2)}) %collective-permute-start.5) | collective-permute-done | bytes 131104 | tf_op jit(solution)/shard_map/ppermute | solution.py:32
  28.3 0.1 convert_add_fusion
  28.4 0.1 collective-permute-start.6
  28.4 1.3 %collective-permute-done.6 = f32[32,1024]{1,0:T(8,128)S(1)} collective-permute-done((f32[32,1024]{1,0:T(8,128)S(1)}, f32[32,1024]{1,0:T(8,128)S(1)}, u32[]{:S(2)}, u32[]{:S(2)}) %collective-permute-start.6) | collective-permute-done | bytes 131104 | tf_op jit(solution)/shard_map/ppermute | solution.py:32
  29.8 0.7 %fusion.1 = bf16[2048,32]{0,1:T(8,128)(2,1)} fusion(f32[32,2048]{1,0:T(8,128)S(1)} %shard_map.67, f32[32,1024]{1,0:T(8,128)S(1)} %get-tuple-element.32, f32[32,1024]{1,0:T(8,128)S(1)} %get-tuple-element.31), kind=kLoop, calls=%fused_computation.3 | loop fusion | flops 196608 | bytes 655360 | tf_op jit(solution)/shard_map/transpose | solution.py:426
  (19 shorter events, 0.1 us)
Async XLA Ops:
  0.0 8.7 %copy-start = (s32[128,32]{0,1:T(8,128)S(1)}, s32[128,32]{0,1:T(8,128)}, u32[]{:S(2)}) copy-start(s32[128,32]{0,1:T(8,128)} %param.11) | copy-start | bytes 49156
  0.0 8.8 %copy-start.2 = (f32[3,16384]{1,0:T(4,128)S(1)}, f32[3,16384]{1,0:T(4,128)}, u32[]{:S(2)}) copy-start(f32[3,16384]{1,0:T(4,128)} %points_ref.1) | copy-start | bytes 589828
  0.0 9.5 %copy-start.3 = (bf16[4096,32]{0,1:T(8,128)(2,1)S(1)}, bf16[4096,32]{0,1:T(8,128)(2,1)}, u32[]{:S(2)}) copy-start(bf16[4096,32]{0,1:T(8,128)(2,1)} %param.7) | copy-start | bytes 786436
  0.0 9.5 %collective-permute-start = (bf16[32,4096]{1,0:T(8,128)(2,1)}, bf16[32,4096]{1,0:T(8,128)(2,1)S(1)}, u32[]{:S(2)}, u32[]{:S(2)}) collective-permute-start(bf16[32,4096]{1,0:T(8,128)(2,1)} %bitcast.3), channel_id=1, source_target_pairs={{0,1},{1,0},{2,3},{3,2},{4,5},{5,4},{6,7},{7,6},{8,9},{9,8},{10,11... | collective-permute-start | bytes 786440 | tf_op jit(solution)/shard_map/ppermute | solution.py:32
  2.9 10.5 %collective-permute-start.2 = (bf16[272,128]{1,0:T(8,128)(2,1)}, bf16[272,128]{1,0:T(8,128)(2,1)S(1)}, u32[]{:S(2)}, u32[]{:S(2)}) collective-permute-start(bf16[272,128]{1,0:T(8,128)(2,1)} %get-tuple-element.22.refs_0_), channel_id=1, source_target_pairs={{0,12},{4,0},{8,4},{12,8},{1,13},{5,1},{9,5},{13,9},{2,14},{6,2},{... | collective-permute-start | bytes 208904 | tf_op jit(solution)/shard_map/ppermute | solution.py:32
  7.6 14.9 %collective-permute-start.3 = (bf16[272,128]{1,0:T(8,128)(2,1)}, bf16[272,128]{1,0:T(8,128)(2,1)S(1)}, u32[]{:S(2)}, u32[]{:S(2)}) collective-permute-start(bf16[272,128]{1,0:T(8,128)(2,1)} %get-tuple-element.22.refs_0_), channel_id=1, source_target_pairs={{0,8},{4,12},{8,0},{12,4},{1,9},{5,13},{9,1},{13,5},{2,10},{6,14},... | collective-permute-start | bytes 208904 | tf_op jit(solution)/shard_map/ppermute | solution.py:32
  7.6 6.3 %collective-permute-start.1 = (bf16[272,128]{1,0:T(8,128)(2,1)}, bf16[272,128]{1,0:T(8,128)(2,1)S(1)}, u32[]{:S(2)}, u32[]{:S(2)}) collective-permute-start(bf16[272,128]{1,0:T(8,128)(2,1)} %get-tuple-element.21), channel_id=1, source_target_pairs={{0,4},{4,8},{8,12},{12,0},{1,5},{5,9},{9,13},{13,1},{2,6},{6,10},{... | collective-permute-start | bytes 208904 | tf_op jit(solution)/shard_map/ppermute | solution.py:32
  9.5 0.7 %copy-start.6 = (s32[8,128]{1,0:T(8,128)S(1)}, s32[8,128]{1,0:T(8,128)}, u32[]{:S(2)}) copy-start(s32[8,128]{1,0:T(8,128)} %get-tuple-element.18.refs_0_) | copy-start | bytes 12292
  14.0 8.5 %copy-start.1 = (bf16[16,32,32,32]{3,2,1,0:T(8,128)(2,1)S(1)}, bf16[16,32,32,32]{3,2,1,0:T(8,128)(2,1)}, u32[]{:S(2)}) copy-start(bf16[16,32,32,32]{3,2,1,0:T(8,128)(2,1)} %couplings_ref.1) | copy-start | bytes 3145732
  14.0 8.5 %copy-start.4 = (bf16[32,4096]{1,0:T(8,128)(2,1)S(1)}, bf16[32,4096]{1,0:T(8,128)(2,1)}, u32[]{:S(2)}) copy-start(bf16[32,4096]{1,0:T(8,128)(2,1)} %basis_ref.1) | copy-start | bytes 786436
  14.0 8.5 %copy-start.5 = (bf16[272,128]{1,0:T(8,128)(2,1)S(1)}, bf16[272,128]{1,0:T(8,128)(2,1)}, u32[]{:S(2)}) copy-start(bf16[272,128]{1,0:T(8,128)(2,1)} %get-tuple-element.22.refs_0_) | copy-start | bytes 208900
  18.6 8.4 %collective-permute-start.4 = (bf16[64,1024]{1,0:T(8,128)(2,1)S(1)}, bf16[64,1024]{1,0:T(8,128)(2,1)S(1)}, u32[]{:S(2)}, u32[]{:S(2)}) collective-permute-start(bf16[64,1024]{1,0:T(8,128)(2,1)S(1)} %get-tuple-element.26), channel_id=1, source_target_pairs={{0,4},{4,8},{8,12},{12,0},{1,5},{5,9},{9,13},{13,1},{2,6},{6,10},{... | collective-permute-start | bytes 393224 | tf_op jit(solution)/shard_map/ppermute | solution.py:32
  20.1 8.2 %collective-permute-start.5 = (bf16[64,1024]{1,0:T(8,128)(2,1)S(1)}, bf16[64,1024]{1,0:T(8,128)(2,1)S(1)}, u32[]{:S(2)}, u32[]{:S(2)}) collective-permute-start(bf16[64,1024]{1,0:T(8,128)(2,1)S(1)} %get-tuple-element.27), channel_id=1, source_target_pairs={{0,12},{4,0},{8,4},{12,8},{1,13},{5,1},{9,5},{13,9},{2,14},{6,2},{... | collective-permute-start | bytes 393224 | tf_op jit(solution)/shard_map/ppermute | solution.py:32
  28.4 1.4 %collective-permute-start.6 = (f32[32,1024]{1,0:T(8,128)S(1)}, f32[32,1024]{1,0:T(8,128)S(1)}, u32[]{:S(2)}, u32[]{:S(2)}) collective-permute-start(f32[32,1024]{1,0:T(8,128)S(1)} %slice.37), channel_id=1, source_target_pairs={{0,1},{1,0},{2,3},{3,2},{4,5},{5,4},{6,7},{7,6},{8,9},{9,8},{10,11... | collective-permute-start | bytes 393224 | tf_op jit(solution)/shard_map/ppermute | solution.py:32

commit v3 on v2

--- a/solution.py
+++ b/solution.py
@@ -244,7 +244,12 @@
         use(2 * step + 1, odd)
         return carry
 
-    lax.fori_loop(0, lax.div(batches + 1, 2), body, 0)
+    lax.fori_loop(0, lax.div(batches, 2), body, 0)
+
+    @pl.when(lax.rem(batches, 2) == 1)
+    def _():
+        use(batches - 1, even)
+
     for base, out in zip(bases, outs):
         for i in range(targets):
             out[:, i * LEAF : (i + 1) * LEAF] = total[base + i].astype(out.dtype)
@@ -381,7 +386,9 @@
     )(points)
     args = (target_rows, source_rows, mine, other)
     (own_near,) = near_sums((targets,), targets, (own_list,), *args, f32, 2.6)
-    own_near, before_load, after_load = lax.optimization_barrier((own_near, before_load, after_load))
+    own_near, before_load, after_load, later_load = lax.optimization_barrier(
+        (own_near, before_load, after_load, prev_load)
+    )
     lists = (list_of(before_load), list_of(after_load))
     to_before, to_after = near_sums((0, 2 * targets), targets, lists, *args, bf16, 4.0)
     from_after = shifted(to_before, "blk", -1)
@@ -392,7 +399,7 @@
     entries = lax.dynamic_slice_in_dim(far_src, first, own_clusters, 0)
     far_shape = jax.ShapeDtypeStruct((columns, own_clusters * LEAF), f32)
     if blk_count == 4 and cluster_total <= 256:
-        middle_load = shifted(prev_load, "blk", 2)
+        middle_load = shifted(later_load, "blk", 2)
         entries = lax.rem(entries + (blk_count - blk) * seg_size, cluster_total)
         far = pl.pallas_call(
             functools.partial(far_kernel_phased, seg_size),

time: 30.7 us -> 30.6 us (level)
  waiting for transfers between devices: 5 us -> 6.48 us
  starting transfers between devices: 10.2 us -> 9.26 us
    ppermute x7, waiting for transfers between devices: 5 us -> 6.48 us  [shifted(): lax.ppermute(block, axis, [(i, (i + shift) % count) for i in range(count)])]
    ppermute x7, starting transfers between devices: 10.2 us -> 9.26 us  [shifted(): lax.ppermute(block, axis, [(i, (i + shift) % count) for i in range(count)])]
    pallas_call x2, Pallas kernels: 7.77 us -> 7.44 us  [near_sums(): pl.pallas_call(functools.partial(near_kernel, bases, targets), out_shape=...]
  transfers between devices with their start and end apart: 7 -> 7, of which waited for: 4 -> 4; matrix products, arithmetic and copies ran while one was open for 1% -> 0% of each run, Pallas kernels for 44% -> 43%
where the time goes in v3:
time: 30.6 us; the launch traced here: 30.7 us
  Pallas kernels  13.2 us (43%)
  starting transfers between devices  9.26 us (30%)
  waiting for transfers between devices  6.48 us (21%)
  local copies, waits for them, and re-layouts  0.85 us (3%)
  other arithmetic  0.78 us (3%)
    ppermute x7, starting transfers between devices, shifted(): lax.ppermute(block, axis, [(i, (i + shift) % count) for i in range(count)])  9.26 us
    pallas_call x2, Pallas kernels, near_sums(): pl.pallas_call(functools.partial(near_kernel, bases, targets), out_shape=...  7.44 us
    ppermute x7, waiting for transfers between devices, shifted(): lax.ppermute(block, axis, [(i, (i + shift) % count) for i in range(count)])  6.48 us
    pallas_call x1, Pallas kernels, on_device(): pl.pallas_call(functools.partial(far_kernel_phased, seg_size), out_shape=...  2.63 us
    pallas_call x1, Pallas kernels, on_device(): pl.pallas_call(functools.partial(list_kernel, seg_size), out_shape=[jax.S...  2.38 us
    unnamed x15, local copies, waits for them, and re-layouts  0.77 us
    pallas_call x1, Pallas kernels, on_device(): pl.pallas_call(functools.partial(feature_kernel, seg_size, targets, own_c...  0.7 us
    transpose x1, other arithmetic, on_device(): return (whole + far).astype(bf16).T  0.68 us
  transfers between devices with their start and end apart: 7, of which 4 were waited for; matrix products, arithmetic and copies ran while one was open for 0% of the time, Pallas kernels for 43%

profile of v3, /device:TPU:0, one launch (start us, length us, event | category | flops | bytes accessed | tf_op | source)
XLA Modules:
  0.0 30.7 jit_solution(13390361210032433901)
XLA Ops:
  0.0 0.5 %collective-permute-start = (bf16[32,4096]{1,0:T(8,128)(2,1)}, bf16[32,4096]{1,0:T(8,128)(2,1)S(1)}, u32[]{:S(2)}, u32[]{:S(2)}) collective-permute-start(bf16[32,4096]{1,0:T(8,128)(2,1)} %bitcast.3), channel_id=1, source_target_pairs={{0,1},{1,0},{2,3},{3,2},{4,5},{5,4},{6,7},{7,6},{8,9},{9,8},{10,11... | collective-permute-start | bytes 786440 | tf_op jit(solution)/shard_map/ppermute | solution.py:32
  0.5 2.4 %shard_map.64 = (s32[8,128]{1,0:T(8,128)}, bf16[272,128]{1,0:T(8,128)(2,1)}, bf16[272,128]{1,0:T(8,128)(2,1)}) custom-call(s32[16,27]{1,0:T(8,128)} %near_hbm.1, bf16[32,4096]{1,0:T(8,128)(2,1)} %basis_ref.1, bf16[32,4096]{1,0:T(8,128)(2,1)} %bitcast.4), custom_call_target="tpu_custom_call" | custom-call | flops 3000000000 | tf_op jit(solution)/shard_map/pallas_call | solution.py:353
  2.9 4.7 %collective-permute-start.2 = (bf16[272,128]{1,0:T(8,128)(2,1)}, bf16[272,128]{1,0:T(8,128)(2,1)S(1)}, u32[]{:S(2)}, u32[]{:S(2)}) collective-permute-start(bf16[272,128]{1,0:T(8,128)(2,1)} %get-tuple-element.26.refs_0_), channel_id=1, source_target_pairs={{0,12},{4,0},{8,4},{12,8},{1,13},{5,1},{9,5},{13,9},{2,14},{6,2},{... | collective-permute-start | bytes 208904 | tf_op jit(solution)/shard_map/ppermute | solution.py:32
  7.6 0.0 collective-permute-start.1
  7.6 0.1 constant_dynamic-slice_fusion
  7.7 0.1 copy.8
  7.8 0.7 %shard_map.65 = (bf16[25,48,128]{2,1,0:T(8,128)(2,1)S(1)}, bf16[32,128,48]{2,1,0:T(8,128)(2,1)S(1)}) custom-call(f32[3,16384]{1,0:T(4,128)S(1)} %copy-done.2), custom_call_target="tpu_custom_call" | custom-call | flops 700000000 | tf_op jit(solution)/shard_map/pallas_call | solution.py:376
  8.5 0.0 collective-permute-done.refs_4_.refs_5_
  8.5 0.7 %copy-done.6 = s32[8,128]{1,0:T(8,128)S(1)} copy-done((s32[8,128]{1,0:T(8,128)S(1)}, s32[8,128]{1,0:T(8,128)}, u32[]{:S(2)}) %copy-start.6) | copy-done | bytes 4120
  9.2 2.6 %shard_map.66 = f32[64,1024]{1,0:T(8,128)S(1)} custom-call(s32[8,128]{1,0:T(8,128)S(1)} %copy-done.6, bf16[25,48,128]{2,1,0:T(8,128)(2,1)S(1)} %get-tuple-element.20.refs_1_.refs_2_, bf16[32,128,48]{2,1,0:T(8,128)(2,1)S(1)} %get-tuple-element.21.refs_2_.refs_3_, bf16[32,4096]{1,0:T(8,128)(2,1)S(1)} %bitcast.5, ...), custom_call_target="tpu_custom_call" | custom-call | flops 2600000000 | tf_op jit(solution)/shard_map/pallas_call | solution.py:260
  11.8 2.1 %collective-permute-done.1.refs_3_ = bf16[272,128]{1,0:T(8,128)(2,1)S(1)} collective-permute-done((bf16[272,128]{1,0:T(8,128)(2,1)}, bf16[272,128]{1,0:T(8,128)(2,1)S(1)}, u32[]{:S(2)}, u32[]{:S(2)}) %collective-permute-start.1) | collective-permute-done | bytes 69664 | tf_op jit(solution)/shard_map/ppermute | solution.py:32
  14.0 0.0 copy-start.1
  14.0 0.0 copy-start.4
  14.0 0.1 collective-permute-start.3
  14.1 4.8 %shard_map.68 = (bf16[64,1024]{1,0:T(8,128)(2,1)S(1)}, bf16[64,1024]{1,0:T(8,128)(2,1)S(1)}) custom-call(s32[8,128]{1,0:T(8,128)S(1)} %fusion.4.refs_0_, s32[8,128]{1,0:T(8,128)S(1)} %fusion.3.refs_1_, bf16[25,48,128]{2,1,0:T(8,128)(2,1)S(1)} %get-tuple-element.20.refs_1_.refs_2_, bf16[32,128,48]{2,1,0:T(8,128)(2,1)S(1)} %get-tuple-element.21.refs_2_.refs_3_, ...), custom_call_target="tpu_custom_call" | custom-call | flops 4000000000 | tf_op jit(solution)/shard_map/pallas_call | solution.py:260
  18.9 2.5 %collective-permute-start.4 = (bf16[64,1024]{1,0:T(8,128)(2,1)S(1)}, bf16[64,1024]{1,0:T(8,128)(2,1)S(1)}, u32[]{:S(2)}, u32[]{:S(2)}) collective-permute-start(bf16[64,1024]{1,0:T(8,128)(2,1)S(1)} %get-tuple-element.28), channel_id=1, source_target_pairs={{0,4},{4,8},{8,12},{12,0},{1,5},{5,9},{9,13},{13,1},{2,6},{6,10},{... | collective-permute-start | bytes 393224 | tf_op jit(solution)/shard_map/ppermute | solution.py:32
  21.5 1.3 %collective-permute-start.5 = (bf16[64,1024]{1,0:T(8,128)(2,1)S(1)}, bf16[64,1024]{1,0:T(8,128)(2,1)S(1)}, u32[]{:S(2)}, u32[]{:S(2)}) collective-permute-start(bf16[64,1024]{1,0:T(8,128)(2,1)S(1)} %get-tuple-element.29), channel_id=1, source_target_pairs={{0,12},{4,0},{8,4},{12,8},{1,13},{5,1},{9,5},{13,9},{2,14},{6,2},{... | collective-permute-start | bytes 393224 | tf_op jit(solution)/shard_map/ppermute | solution.py:32
  22.8 2.6 %shard_map.67 = f32[32,2048]{1,0:T(8,128)S(1)} custom-call(s32[16,32]{1,0:T(8,128)S(1)} %negate_select_fusion.far_ref, bf16[16,32,32,32]{3,2,1,0:T(8,128)(2,1)S(1)} %copy-done.1, bf16[32,4096]{1,0:T(8,128)(2,1)S(1)} %copy-done.4, bf16[272,128]{1,0:T(8,128)(2,1)S(1)} %copy-done.5, bf16[272,128]{1,0:T(8,128)(2,1)S(1)} %collective-permute-done.2.refs_1_, ...), custom_call_target="tpu_custom_call" | custom-call | flops 3000000000 | tf_op jit(solution)/shard_map/pallas_call | solution.py:404
  25.5 1.6 %collective-permute-done.4 = bf16[64,1024]{1,0:T(8,128)(2,1)S(1)} collective-permute-done((bf16[64,1024]{1,0:T(8,128)(2,1)S(1)}, bf16[64,1024]{1,0:T(8,128)(2,1)S(1)}, u32[]{:S(2)}, u32[]{:S(2)}) %collective-permute-start.4) | collective-permute-done | bytes 131104 | tf_op jit(solution)/shard_map/ppermute | solution.py:32
  27.0 1.4 %collective-permute-done.5 = bf16[64,1024]{1,0:T(8,128)(2,1)S(1)} collective-permute-done((bf16[64,1024]{1,0:T(8,128)(2,1)S(1)}, bf16[64,1024]{1,0:T(8,128)(2,1)S(1)}, u32[]{:S(2)}, u32[]{:S(2)}) %collective-permute-start.5) | collective-permute-done | bytes 131104 | tf_op jit(solution)/shard_map/ppermute | solution.py:32
  28.5 0.1 convert_add_fusion
  28.6 0.1 collective-permute-start.6
  28.6 1.3 %collective-permute-done.6 = f32[32,1024]{1,0:T(8,128)S(1)} collective-permute-done((f32[32,1024]{1,0:T(8,128)S(1)}, f32[32,1024]{1,0:T(8,128)S(1)}, u32[]{:S(2)}, u32[]{:S(2)}) %collective-permute-start.6) | collective-permute-done | bytes 131104 | tf_op jit(solution)/shard_map/ppermute | solution.py:32
  30.0 0.7 %fusion.1 = bf16[2048,32]{0,1:T(8,128)(2,1)} fusion(f32[32,2048]{1,0:T(8,128)S(1)} %shard_map.67, f32[32,1024]{1,0:T(8,128)S(1)} %get-tuple-element.34, f32[32,1024]{1,0:T(8,128)S(1)} %get-tuple-element.33), kind=kLoop, calls=%fused_computation.3 | loop fusion | flops 196608 | bytes 655360 | tf_op jit(solution)/shard_map/transpose | solution.py:433
  (19 shorter events, 0.1 us)
Async XLA Ops:
  0.0 7.6 %copy-start = (s32[128,32]{0,1:T(8,128)S(1)}, s32[128,32]{0,1:T(8,128)}, u32[]{:S(2)}) copy-start(s32[128,32]{0,1:T(8,128)} %param.11) | copy-start | bytes 49156
  0.0 7.8 %copy-start.2 = (f32[3,16384]{1,0:T(4,128)S(1)}, f32[3,16384]{1,0:T(4,128)}, u32[]{:S(2)}) copy-start(f32[3,16384]{1,0:T(4,128)} %points_ref.1) | copy-start | bytes 589828
  0.0 8.5 %copy-start.3 = (bf16[4096,32]{0,1:T(8,128)(2,1)S(1)}, bf16[4096,32]{0,1:T(8,128)(2,1)}, u32[]{:S(2)}) copy-start(bf16[4096,32]{0,1:T(8,128)(2,1)} %param.7) | copy-start | bytes 786436
  0.0 8.5 %collective-permute-start = (bf16[32,4096]{1,0:T(8,128)(2,1)}, bf16[32,4096]{1,0:T(8,128)(2,1)S(1)}, u32[]{:S(2)}, u32[]{:S(2)}) collective-permute-start(bf16[32,4096]{1,0:T(8,128)(2,1)} %bitcast.3), channel_id=1, source_target_pairs={{0,1},{1,0},{2,3},{3,2},{4,5},{5,4},{6,7},{7,6},{8,9},{9,8},{10,11... | collective-permute-start | bytes 786440 | tf_op jit(solution)/shard_map/ppermute | solution.py:32
  2.9 8.9 %collective-permute-start.2 = (bf16[272,128]{1,0:T(8,128)(2,1)}, bf16[272,128]{1,0:T(8,128)(2,1)S(1)}, u32[]{:S(2)}, u32[]{:S(2)}) collective-permute-start(bf16[272,128]{1,0:T(8,128)(2,1)} %get-tuple-element.26.refs_0_), channel_id=1, source_target_pairs={{0,12},{4,0},{8,4},{12,8},{1,13},{5,1},{9,5},{13,9},{2,14},{6,2},{... | collective-permute-start | bytes 208904 | tf_op jit(solution)/shard_map/ppermute | solution.py:32
  7.6 6.3 %collective-permute-start.1 = (bf16[272,128]{1,0:T(8,128)(2,1)}, bf16[272,128]{1,0:T(8,128)(2,1)S(1)}, u32[]{:S(2)}, u32[]{:S(2)}) collective-permute-start(bf16[272,128]{1,0:T(8,128)(2,1)} %get-tuple-element.22), channel_id=1, source_target_pairs={{0,4},{4,8},{8,12},{12,0},{1,5},{5,9},{9,13},{13,1},{2,6},{6,10},{... | collective-permute-start | bytes 208904 | tf_op jit(solution)/shard_map/ppermute | solution.py:32
  8.5 0.7 %copy-start.6 = (s32[8,128]{1,0:T(8,128)S(1)}, s32[8,128]{1,0:T(8,128)}, u32[]{:S(2)}) copy-start(s32[8,128]{1,0:T(8,128)} %get-tuple-element.19.refs_0_) | copy-start | bytes 12292
  9.2 4.8 %copy-start.5 = (bf16[272,128]{1,0:T(8,128)(2,1)S(1)}, bf16[272,128]{1,0:T(8,128)(2,1)}, u32[]{:S(2)}) copy-start(bf16[272,128]{1,0:T(8,128)(2,1)} %get-tuple-element.26.refs_0_) | copy-start | bytes 208900
  14.0 8.8 %copy-start.1 = (bf16[16,32,32,32]{3,2,1,0:T(8,128)(2,1)S(1)}, bf16[16,32,32,32]{3,2,1,0:T(8,128)(2,1)}, u32[]{:S(2)}) copy-start(bf16[16,32,32,32]{3,2,1,0:T(8,128)(2,1)} %couplings_ref.1) | copy-start | bytes 3145732
  14.0 8.8 %copy-start.4 = (bf16[32,4096]{1,0:T(8,128)(2,1)S(1)}, bf16[32,4096]{1,0:T(8,128)(2,1)}, u32[]{:S(2)}) copy-start(bf16[32,4096]{1,0:T(8,128)(2,1)} %basis_ref.1) | copy-start | bytes 786436
  14.0 8.8 %collective-permute-start.3 = (bf16[272,128]{1,0:T(8,128)(2,1)S(1)}, bf16[272,128]{1,0:T(8,128)(2,1)S(1)}, u32[]{:S(2)}, u32[]{:S(2)}) collective-permute-start(bf16[272,128]{1,0:T(8,128)(2,1)S(1)} %copy-done.5), channel_id=1, source_target_pairs={{0,8},{4,12},{8,0},{12,4},{1,9},{5,13},{9,1},{13,5},{2,10},{6,14},... | collective-permute-start | bytes 208904 | tf_op jit(solution)/shard_map/ppermute | solution.py:32
  18.9 8.1 %collective-permute-start.4 = (bf16[64,1024]{1,0:T(8,128)(2,1)S(1)}, bf16[64,1024]{1,0:T(8,128)(2,1)S(1)}, u32[]{:S(2)}, u32[]{:S(2)}) collective-permute-start(bf16[64,1024]{1,0:T(8,128)(2,1)S(1)} %get-tuple-element.28), channel_id=1, source_target_pairs={{0,4},{4,8},{8,12},{12,0},{1,5},{5,9},{9,13},{13,1},{2,6},{6,10},{... | collective-permute-start | bytes 393224 | tf_op jit(solution)/shard_map/ppermute | solution.py:32
  21.5 7.0 %collective-permute-start.5 = (bf16[64,1024]{1,0:T(8,128)(2,1)S(1)}, bf16[64,1024]{1,0:T(8,128)(2,1)S(1)}, u32[]{:S(2)}, u32[]{:S(2)}) collective-permute-start(bf16[64,1024]{1,0:T(8,128)(2,1)S(1)} %get-tuple-element.29), channel_id=1, source_target_pairs={{0,12},{4,0},{8,4},{12,8},{1,13},{5,1},{9,5},{13,9},{2,14},{6,2},{... | collective-permute-start | bytes 393224 | tf_op jit(solution)/shard_map/ppermute | solution.py:32
  28.6 1.4 %collective-permute-start.6 = (f32[32,1024]{1,0:T(8,128)S(1)}, f32[32,1024]{1,0:T(8,128)S(1)}, u32[]{:S(2)}, u32[]{:S(2)}) collective-permute-start(f32[32,1024]{1,0:T(8,128)S(1)} %slice.37), channel_id=1, source_target_pairs={{0,1},{1,0},{2,3},{3,2},{4,5},{5,4},{6,7},{7,6},{8,9},{9,8},{10,11... | collective-permute-start | bytes 393224 | tf_op jit(solution)/shard_map/ppermute | solution.py:32

commit v4 on v3

--- a/solution.py
+++ b/solution.py
@@ -348,8 +348,6 @@
     cluster_total = seg_size * blk_count
     pack = LEAF // columns
     skel_rows = seg_size // pack * rank
-    other = shifted(mine, "rhs", 1)
-
     own_list, prev_load, next_load = pl.pallas_call(
         functools.partial(list_kernel, seg_size),
         out_shape=[jax.ShapeDtypeStruct((8, LEAF), jnp.int32)]
@@ -366,6 +364,8 @@
         cost_estimate=cost(3.0),
     )(near_src, basis, mine)
 
+    later_charges, prev_load = lax.optimization_barrier((mine, prev_load))
+    other = shifted(later_charges, "rhs", 1)
     after_load = shifted(prev_load, "blk", -1)
     before_load = shifted(next_load, "blk", 1)
 
@@ -384,13 +384,12 @@
         compiler_params=PARAMS,
         cost_estimate=cost(0.7),
     )(points)
+    target_rows, later_load = lax.optimization_barrier((target_rows, prev_load))
     args = (target_rows, source_rows, mine, other)
     (own_near,) = near_sums((targets,), targets, (own_list,), *args, f32, 2.6)
-    own_near, before_load, after_load, later_load = lax.optimization_barrier(
-        (own_near, before_load, after_load, prev_load)
-    )
+    own_near, before_load, after_load = lax.optimization_barrier((own_near, before_load, after_load))
     lists = (list_of(before_load), list_of(after_load))
-    to_before, to_after = near_sums((0, 2 * targets), targets, lists, *args, bf16, 4.0)
+    to_before, to_after = near_sums((0, 2 * targets), targets, lists, *args, bf16, 0.2)
     from_after = shifted(to_before, "blk", -1)
     from_before = shifted(to_after, "blk", 1)
 

time: 30.6 us -> 30.4 us (level)
  waiting for transfers between devices: 6.48 us -> 5.03 us
  starting transfers between devices: 9.26 us -> 10.2 us
    ppermute x7, waiting for transfers between devices: 6.48 us -> 5.03 us  [shifted(): lax.ppermute(block, axis, [(i, (i + shift) % count) for i in range(count)])]
    ppermute x7, starting transfers between devices: 9.26 us -> 10.2 us  [shifted(): lax.ppermute(block, axis, [(i, (i + shift) % count) for i in range(count)])]
  transfers between devices with their start and end apart: 7 -> 7, of which waited for: 4 -> 4; matrix products, arithmetic and copies ran while one was open for 0% -> 1% of each run, Pallas kernels for 43% -> 36%
where the time goes in v4:
time: 30.4 us; the launch traced here: 30.2 us
  Pallas kernels  13.2 us (43%)
  starting transfers between devices  10.2 us (34%)
  waiting for transfers between devices  5.03 us (17%)
  local copies, waits for them, and re-layouts  0.85 us (3%)
  other arithmetic  0.79 us (3%)
    ppermute x7, starting transfers between devices, shifted(): lax.ppermute(block, axis, [(i, (i + shift) % count) for i in range(count)])  10.2 us
    pallas_call x2, Pallas kernels, near_sums(): pl.pallas_call(functools.partial(near_kernel, bases, targets), out_shape=...  7.43 us
    ppermute x7, waiting for transfers between devices, shifted(): lax.ppermute(block, axis, [(i, (i + shift) % count) for i in range(count)])  5.03 us
    pallas_call x1, Pallas kernels, on_device(): pl.pallas_call(functools.partial(far_kernel_phased, seg_size), out_shape=...  2.67 us
    pallas_call x1, Pallas kernels, on_device(): pl.pallas_call(functools.partial(list_kernel, seg_size), out_shape=[jax.S...  2.44 us
    unnamed x15, local copies, waits for them, and re-layouts  0.77 us
    pallas_call x1, Pallas kernels, on_device(): pl.pallas_call(functools.partial(feature_kernel, seg_size, targets, own_c...  0.7 us
    transpose x1, other arithmetic, on_device(): return (whole + far).astype(bf16).T  0.69 us
  transfers between devices with their start and end apart: 7, of which 4 were waited for; matrix products, arithmetic and copies ran while one was open for 1% of the time, Pallas kernels for 36%

profile of v4, /device:TPU:0, one launch (start us, length us, event | category | flops | bytes accessed | tf_op | source)
XLA Modules:
  0.0 30.2 jit_solution(1925064907494733690)
XLA Ops:
  0.0 0.0 copy-start
  0.0 2.4 %shard_map.64 = (s32[8,128]{1,0:T(8,128)}, bf16[272,128]{1,0:T(8,128)(2,1)}, bf16[272,128]{1,0:T(8,128)(2,1)}) custom-call(s32[16,27]{1,0:T(8,128)} %near_hbm.1, bf16[32,4096]{1,0:T(8,128)(2,1)} %basis_ref.1, bf16[32,4096]{1,0:T(8,128)(2,1)} %bitcast.3), custom_call_target="tpu_custom_call" | custom-call | flops 3000000000 | tf_op jit(solution)/shard_map/pallas_call | solution.py:351
  2.5 0.5 %collective-permute-start = (bf16[32,4096]{1,0:T(8,128)(2,1)S(1)}, bf16[32,4096]{1,0:T(8,128)(2,1)S(1)}, u32[]{:S(2)}, u32[]{:S(2)}) collective-permute-start(bf16[32,4096]{1,0:T(8,128)(2,1)S(1)} %bitcast.4), channel_id=1, source_target_pairs={{0,1},{1,0},{2,3},{3,2},{4,5},{5,4},{6,7},{7,6},{8,9},{9,8},{10,11... | collective-permute-start | bytes 786440 | tf_op jit(solution)/shard_map/ppermute | solution.py:32
  3.0 4.7 %collective-permute-start.2 = (bf16[272,128]{1,0:T(8,128)(2,1)}, bf16[272,128]{1,0:T(8,128)(2,1)S(1)}, u32[]{:S(2)}, u32[]{:S(2)}) collective-permute-start(bf16[272,128]{1,0:T(8,128)(2,1)} %get-tuple-element.32.refs_0_), channel_id=1, source_target_pairs={{0,12},{4,0},{8,4},{12,8},{1,13},{5,1},{9,5},{13,9},{2,14},{6,2},{... | collective-permute-start | bytes 208904 | tf_op jit(solution)/shard_map/ppermute | solution.py:32
  7.6 0.0 collective-permute-start.1
  7.7 0.7 %shard_map.65 = (bf16[25,48,128]{2,1,0:T(8,128)(2,1)S(1)}, bf16[32,128,48]{2,1,0:T(8,128)(2,1)S(1)}) custom-call(f32[3,16384]{1,0:T(4,128)S(1)} %copy-done.3), custom_call_target="tpu_custom_call" | custom-call | flops 700000000 | tf_op jit(solution)/shard_map/pallas_call | solution.py:376
  8.4 1.1 %collective-permute-start.3 = (bf16[272,128]{1,0:T(8,128)(2,1)}, bf16[272,128]{1,0:T(8,128)(2,1)S(1)}, u32[]{:S(2)}, u32[]{:S(2)}) collective-permute-start(bf16[272,128]{1,0:T(8,128)(2,1)} %get-tuple-element.32.refs_0_), channel_id=1, source_target_pairs={{0,8},{4,12},{8,0},{12,4},{1,9},{5,13},{9,1},{13,5},{2,10},{6,14},... | collective-permute-start | bytes 208904 | tf_op jit(solution)/shard_map/ppermute | solution.py:32
  9.4 0.1 constant_dynamic-slice_fusion
  9.5 0.1 copy.8
  9.6 0.0 collective-permute-done.refs_4_.refs_5_
  9.6 0.7 %copy-done.6 = s32[8,128]{1,0:T(8,128)S(1)} copy-done((s32[8,128]{1,0:T(8,128)S(1)}, s32[8,128]{1,0:T(8,128)}, u32[]{:S(2)}) %copy-start.6) | copy-done | bytes 4120
  10.3 2.8 %shard_map.66 = f32[64,1024]{1,0:T(8,128)S(1)} custom-call(s32[8,128]{1,0:T(8,128)S(1)} %copy-done.6, bf16[25,48,128]{2,1,0:T(8,128)(2,1)S(1)} %get-tuple-element.26.refs_1_.refs_2_, bf16[32,128,48]{2,1,0:T(8,128)(2,1)S(1)} %get-tuple-element.27.refs_2_.refs_3_, bf16[32,4096]{1,0:T(8,128)(2,1)S(1)} %bitcast.5, ...), custom_call_target="tpu_custom_call" | custom-call | flops 2600000000 | tf_op jit(solution)/shard_map/pallas_call | solution.py:260
  13.1 0.0 collective-permute-done.2.refs_1_
  13.1 1.6 %collective-permute-done.1.refs_3_ = bf16[272,128]{1,0:T(8,128)(2,1)S(1)} collective-permute-done((bf16[272,128]{1,0:T(8,128)(2,1)}, bf16[272,128]{1,0:T(8,128)(2,1)S(1)}, u32[]{:S(2)}, u32[]{:S(2)}) %collective-permute-start.1) | collective-permute-done | bytes 69664 | tf_op jit(solution)/shard_map/ppermute | solution.py:32
  14.8 4.6 %shard_map.68 = (bf16[64,1024]{1,0:T(8,128)(2,1)S(1)}, bf16[64,1024]{1,0:T(8,128)(2,1)S(1)}) custom-call(s32[8,128]{1,0:T(8,128)S(1)} %fusion.4.refs_0_, s32[8,128]{1,0:T(8,128)S(1)} %fusion.3.refs_1_, bf16[25,48,128]{2,1,0:T(8,128)(2,1)S(1)} %get-tuple-element.26.refs_1_.refs_2_, bf16[32,128,48]{2,1,0:T(8,128)(2,1)S(1)} %get-tuple-element.27.refs_2_.refs_3_, ...), custom_call_target="tpu_custom_call" | custom-call | flops 200000000 | tf_op jit(solution)/shard_map/pallas_call | solution.py:260
  19.4 1.5 %collective-permute-start.4 = (bf16[64,1024]{1,0:T(8,128)(2,1)S(1)}, bf16[64,1024]{1,0:T(8,128)(2,1)S(1)}, u32[]{:S(2)}, u32[]{:S(2)}) collective-permute-start(bf16[64,1024]{1,0:T(8,128)(2,1)S(1)} %get-tuple-element.34), channel_id=1, source_target_pairs={{0,4},{4,8},{8,12},{12,0},{1,5},{5,9},{9,13},{13,1},{2,6},{6,10},{... | collective-permute-start | bytes 393224 | tf_op jit(solution)/shard_map/ppermute | solution.py:32
  20.9 2.4 %collective-permute-start.5 = (bf16[64,1024]{1,0:T(8,128)(2,1)S(1)}, bf16[64,1024]{1,0:T(8,128)(2,1)S(1)}, u32[]{:S(2)}, u32[]{:S(2)}) collective-permute-start(bf16[64,1024]{1,0:T(8,128)(2,1)S(1)} %get-tuple-element.35), channel_id=1, source_target_pairs={{0,12},{4,0},{8,4},{12,8},{1,13},{5,1},{9,5},{13,9},{2,14},{6,2},{... | collective-permute-start | bytes 393224 | tf_op jit(solution)/shard_map/ppermute | solution.py:32
  23.3 0.0 collective-permute-done.3.refs_2_
  23.3 2.7 %shard_map.67 = f32[32,2048]{1,0:T(8,128)S(1)} custom-call(s32[16,32]{1,0:T(8,128)S(1)} %negate_select_fusion.far_ref, bf16[16,32,32,32]{3,2,1,0:T(8,128)(2,1)S(1)} %copy-done.2, bf16[32,4096]{1,0:T(8,128)(2,1)S(1)} %copy-done.4, bf16[272,128]{1,0:T(8,128)(2,1)S(1)} %copy-done.5, bf16[272,128]{1,0:T(8,128)(2,1)S(1)} %collective-permute-done.2.refs_1_, ...), custom_call_target="tpu_custom_call" | custom-call | flops 3000000000 | tf_op jit(solution)/shard_map/pallas_call | solution.py:403
  26.0 0.8 %collective-permute-done.4 = bf16[64,1024]{1,0:T(8,128)(2,1)S(1)} collective-permute-done((bf16[64,1024]{1,0:T(8,128)(2,1)S(1)}, bf16[64,1024]{1,0:T(8,128)(2,1)S(1)}, u32[]{:S(2)}, u32[]{:S(2)}) %collective-permute-start.4) | collective-permute-done | bytes 131104 | tf_op jit(solution)/shard_map/ppermute | solution.py:32
  26.8 1.3 %collective-permute-done.5 = bf16[64,1024]{1,0:T(8,128)(2,1)S(1)} collective-permute-done((bf16[64,1024]{1,0:T(8,128)(2,1)S(1)}, bf16[64,1024]{1,0:T(8,128)(2,1)S(1)}, u32[]{:S(2)}, u32[]{:S(2)}) %collective-permute-start.5) | collective-permute-done | bytes 131104 | tf_op jit(solution)/shard_map/ppermute | solution.py:32
  28.1 0.1 collective-permute-start.6
  28.2 1.3 %collective-permute-done.6 = f32[32,1024]{1,0:T(8,128)S(1)} collective-permute-done((f32[32,1024]{1,0:T(8,128)S(1)}, f32[32,1024]{1,0:T(8,128)S(1)}, u32[]{:S(2)}, u32[]{:S(2)}) %collective-permute-start.6) | collective-permute-done | bytes 131104 | tf_op jit(solution)/shard_map/ppermute | solution.py:32
  29.5 0.7 %fusion.1 = bf16[2048,32]{0,1:T(8,128)(2,1)} fusion(f32[32,2048]{1,0:T(8,128)S(1)} %shard_map.67, f32[32,1024]{1,0:T(8,128)S(1)} %get-tuple-element.40, f32[32,1024]{1,0:T(8,128)S(1)} %get-tuple-element.39), kind=kLoop, calls=%fused_computation.3 | loop fusion | flops 196608 | bytes 655360 | tf_op jit(solution)/shard_map/transpose | solution.py:432
  (19 shorter events, 0.1 us)
Async XLA Ops:
  0.0 9.4 %copy-start = (s32[128,32]{0,1:T(8,128)S(1)}, s32[128,32]{0,1:T(8,128)}, u32[]{:S(2)}) copy-start(s32[128,32]{0,1:T(8,128)} %param.11) | copy-start | bytes 49156
  0.0 2.5 %copy-start.1 = (bf16[4096,32]{0,1:T(8,128)(2,1)S(1)}, bf16[4096,32]{0,1:T(8,128)(2,1)}, u32[]{:S(2)}) copy-start(bf16[4096,32]{0,1:T(8,128)(2,1)} %param.7) | copy-start | bytes 786436
  0.0 7.6 %copy-start.3 = (f32[3,16384]{1,0:T(4,128)S(1)}, f32[3,16384]{1,0:T(4,128)}, u32[]{:S(2)}) copy-start(f32[3,16384]{1,0:T(4,128)} %points_ref.1) | copy-start | bytes 589828
  2.5 7.1 %collective-permute-start = (bf16[32,4096]{1,0:T(8,128)(2,1)S(1)}, bf16[32,4096]{1,0:T(8,128)(2,1)S(1)}, u32[]{:S(2)}, u32[]{:S(2)}) collective-permute-start(bf16[32,4096]{1,0:T(8,128)(2,1)S(1)} %bitcast.4), channel_id=1, source_target_pairs={{0,1},{1,0},{2,3},{3,2},{4,5},{5,4},{6,7},{7,6},{8,9},{9,8},{10,11... | collective-permute-start | bytes 786440 | tf_op jit(solution)/shard_map/ppermute | solution.py:32
  3.0 10.1 %collective-permute-start.2 = (bf16[272,128]{1,0:T(8,128)(2,1)}, bf16[272,128]{1,0:T(8,128)(2,1)S(1)}, u32[]{:S(2)}, u32[]{:S(2)}) collective-permute-start(bf16[272,128]{1,0:T(8,128)(2,1)} %get-tuple-element.32.refs_0_), channel_id=1, source_target_pairs={{0,12},{4,0},{8,4},{12,8},{1,13},{5,1},{9,5},{13,9},{2,14},{6,2},{... | collective-permute-start | bytes 208904 | tf_op jit(solution)/shard_map/ppermute | solution.py:32
  7.6 7.1 %collective-permute-start.1 = (bf16[272,128]{1,0:T(8,128)(2,1)}, bf16[272,128]{1,0:T(8,128)(2,1)S(1)}, u32[]{:S(2)}, u32[]{:S(2)}) collective-permute-start(bf16[272,128]{1,0:T(8,128)(2,1)} %get-tuple-element.29), channel_id=1, source_target_pairs={{0,4},{4,8},{8,12},{12,0},{1,5},{5,9},{9,13},{13,1},{2,6},{6,10},{... | collective-permute-start | bytes 208904 | tf_op jit(solution)/shard_map/ppermute | solution.py:32
  8.4 14.9 %collective-permute-start.3 = (bf16[272,128]{1,0:T(8,128)(2,1)}, bf16[272,128]{1,0:T(8,128)(2,1)S(1)}, u32[]{:S(2)}, u32[]{:S(2)}) collective-permute-start(bf16[272,128]{1,0:T(8,128)(2,1)} %get-tuple-element.32.refs_0_), channel_id=1, source_target_pairs={{0,8},{4,12},{8,0},{12,4},{1,9},{5,13},{9,1},{13,5},{2,10},{6,14},... | collective-permute-start | bytes 208904 | tf_op jit(solution)/shard_map/ppermute | solution.py:32
  9.6 0.7 %copy-start.6 = (s32[8,128]{1,0:T(8,128)S(1)}, s32[8,128]{1,0:T(8,128)}, u32[]{:S(2)}) copy-start(s32[8,128]{1,0:T(8,128)} %get-tuple-element.22.refs_0_) | copy-start | bytes 12292
  10.3 13.0 %copy-start.2 = (bf16[16,32,32,32]{3,2,1,0:T(8,128)(2,1)S(1)}, bf16[16,32,32,32]{3,2,1,0:T(8,128)(2,1)}, u32[]{:S(2)}) copy-start(bf16[16,32,32,32]{3,2,1,0:T(8,128)(2,1)} %couplings_ref.1) | copy-start | bytes 3145732
  10.3 13.0 %copy-start.4 = (bf16[32,4096]{1,0:T(8,128)(2,1)S(1)}, bf16[32,4096]{1,0:T(8,128)(2,1)}, u32[]{:S(2)}) copy-start(bf16[32,4096]{1,0:T(8,128)(2,1)} %basis_ref.1) | copy-start | bytes 786436
  10.3 13.0 %copy-start.5 = (bf16[272,128]{1,0:T(8,128)(2,1)S(1)}, bf16[272,128]{1,0:T(8,128)(2,1)}, u32[]{:S(2)}) copy-start(bf16[272,128]{1,0:T(8,128)(2,1)} %get-tuple-element.32.refs_0_) | copy-start | bytes 208900
  19.4 7.4 %collective-permute-start.4 = (bf16[64,1024]{1,0:T(8,128)(2,1)S(1)}, bf16[64,1024]{1,0:T(8,128)(2,1)S(1)}, u32[]{:S(2)}, u32[]{:S(2)}) collective-permute-start(bf16[64,1024]{1,0:T(8,128)(2,1)S(1)} %get-tuple-element.34), channel_id=1, source_target_pairs={{0,4},{4,8},{8,12},{12,0},{1,5},{5,9},{9,13},{13,1},{2,6},{6,10},{... | collective-permute-start | bytes 393224 | tf_op jit(solution)/shard_map/ppermute | solution.py:32
  20.9 7.2 %collective-permute-start.5 = (bf16[64,1024]{1,0:T(8,128)(2,1)S(1)}, bf16[64,1024]{1,0:T(8,128)(2,1)S(1)}, u32[]{:S(2)}, u32[]{:S(2)}) collective-permute-start(bf16[64,1024]{1,0:T(8,128)(2,1)S(1)} %get-tuple-element.35), channel_id=1, source_target_pairs={{0,12},{4,0},{8,4},{12,8},{1,13},{5,1},{9,5},{13,9},{2,14},{6,2},{... | collective-permute-start | bytes 393224 | tf_op jit(solution)/shard_map/ppermute | solution.py:32
  28.1 1.4 %collective-permute-start.6 = (f32[32,1024]{1,0:T(8,128)S(1)}, f32[32,1024]{1,0:T(8,128)S(1)}, u32[]{:S(2)}, u32[]{:S(2)}) collective-permute-start(f32[32,1024]{1,0:T(8,128)S(1)} %slice.37), channel_id=1, source_target_pairs={{0,1},{1,0},{2,3},{3,2},{4,5},{5,4},{6,7},{7,6},{8,9},{9,8},{10,11... | collective-permute-start | bytes 393224 | tf_op jit(solution)/shard_map/ppermute | solution.py:32

commit v5 on v4

--- a/solution.py
+++ b/solution.py
@@ -36,7 +36,7 @@
     return pl.ds(pl.multiple_of(index * LEAF, LEAF), LEAF)
 
 
-def list_kernel(seg_size, near_hbm, basis_hbm, charges_hbm, own_ref, prev_ref, next_ref, near_ref, basis_ref, charges_ref, sems):
+def list_kernel(seg_size, near_hbm, basis_hbm, charges_hbm, own_ref, prev_ref, next_ref, skel_ref, near_ref, basis_ref, charges_ref, sems):
     copies = [
         pltpu.make_async_copy(near_hbm, near_ref, sems.at[0]),
         pltpu.make_async_copy(basis_hbm, basis_ref, sems.at[1]),
@@ -53,7 +53,6 @@
     columns = charges_ref.shape[0]
     rank = basis_ref.shape[0]
     pack = LEAF // columns
-    rows_end = seg_size // pack * rank
 
     def iota(shape, dim):
         return lax.broadcasted_iota(jnp.int32, shape, dim)
@@ -108,14 +107,9 @@
         preferred_element_type=f32,
     )
     last = row * LEAF + iota((8, LEAF), 1) == 8 * LEAF - 1
-    finished = []
-    for i, total in enumerate(totals):
-        high = jnp.floor(total * (1.0 / 256.0))
-        finished.append(jnp.where(last, total - 256.0 * high, lists[16 * i : 16 * i + 8]))
-        finished.append(jnp.where(last, high, lists[16 * i + 8 : 16 * i + 16]))
-    own_ref[...] = finished[0].astype(jnp.int32) + 256 * finished[1].astype(jnp.int32)
-    prev_ref[rows_end : rows_end + 16, :] = jnp.concatenate(finished[2:4], axis=0).astype(bf16)
-    next_ref[rows_end : rows_end + 16, :] = jnp.concatenate(finished[4:6], axis=0).astype(bf16)
+    for i, out in enumerate((own_ref, prev_ref, next_ref)):
+        codes = lists[16 * i : 16 * i + 8] + 256.0 * lists[16 * i + 8 : 16 * i + 16]
+        out[...] = jnp.where(last, totals[i], codes).astype(jnp.int32)
 
     copies[1].wait()
     copies[2].wait()
@@ -137,8 +131,7 @@
             )
         )
     for group, block in enumerate(blocks):
-        prev_ref[group * rank : (group + 1) * rank, :] = block.astype(bf16)
-        next_ref[group * rank : (group + 1) * rank, :] = block.astype(bf16)
+        skel_ref[group * rank : (group + 1) * rank, :] = block.astype(bf16)
 
 
 def split(value):
@@ -347,13 +340,12 @@
     targets = own_clusters // 2
     cluster_total = seg_size * blk_count
     pack = LEAF // columns
-    skel_rows = seg_size // pack * rank
-    own_list, prev_load, next_load = pl.pallas_call(
+    own_list, prev_list, next_list, skeleton = pl.pallas_call(
         functools.partial(list_kernel, seg_size),
-        out_shape=[jax.ShapeDtypeStruct((8, LEAF), jnp.int32)]
-        + [jax.ShapeDtypeStruct((skel_rows + 16, LEAF), bf16)] * 2,
+        out_shape=[jax.ShapeDtypeStruct((8, LEAF), jnp.int32)] * 3
+        + [jax.ShapeDtypeStruct((seg_size // pack * rank, LEAF), bf16)],
         in_specs=[HBM] * 3,
-        out_specs=[VMEM] * 3,
+        out_specs=[VMEM] * 4,
         scratch_shapes=[
             pltpu.VMEM(near_src.shape, jnp.int32),
             pltpu.VMEM(basis.shape, bf16),
@@ -361,18 +353,12 @@
             pltpu.SemaphoreType.DMA((3,)),
         ],
         compiler_params=pltpu.CompilerParams(vmem_limit_bytes=63 * 2**20),
-        cost_estimate=cost(3.0),
+        cost_estimate=cost(0.01),
     )(near_src, basis, mine)
 
-    later_charges, prev_load = lax.optimization_barrier((mine, prev_load))
-    other = shifted(later_charges, "rhs", 1)
-    after_load = shifted(prev_load, "blk", -1)
-    before_load = shifted(next_load, "blk", 1)
-
-    def list_of(load):
-        entries = load[skel_rows:].astype(jnp.int32)
-        return entries[:8] + 256 * entries[8:]
-
+    points, prev_list, next_list = lax.optimization_barrier((points, prev_list, next_list))
+    after_list = shifted(prev_list, "blk", -1)
+    before_list = shifted(next_list, "blk", 1)
     target_rows, source_rows = pl.pallas_call(
         functools.partial(feature_kernel, seg_size, targets, own_clusters),
         out_shape=[
@@ -382,23 +368,29 @@
         in_specs=[VMEM],
         out_specs=[VMEM, VMEM],
         compiler_params=PARAMS,
-        cost_estimate=cost(0.7),
+        cost_estimate=cost(0.01),
     )(points)
-    target_rows, later_load = lax.optimization_barrier((target_rows, prev_load))
+    later_charges, skeleton = lax.optimization_barrier((mine, skeleton))
+    other = shifted(later_charges, "rhs", 1)
+    narrow = blk_count == 4 and cluster_total <= 256
+    if narrow:
+        skeletons = [skeleton] + [shifted(skeleton, "blk", -i) for i in range(1, blk_count)]
+    else:
+        skeletons = [lax.all_gather(skeleton, "blk", axis=0, tiled=True)]
     args = (target_rows, source_rows, mine, other)
-    (own_near,) = near_sums((targets,), targets, (own_list,), *args, f32, 2.6)
-    own_near, before_load, after_load = lax.optimization_barrier((own_near, before_load, after_load))
-    lists = (list_of(before_load), list_of(after_load))
-    to_before, to_after = near_sums((0, 2 * targets), targets, lists, *args, bf16, 0.2)
+    lists = (before_list, after_list)
+    to_before, to_after = near_sums((0, 2 * targets), targets, lists, *args, bf16, 20.0)
+    to_before, to_after, own_list = lax.optimization_barrier((to_before, to_after, own_list))
     from_after = shifted(to_before, "blk", -1)
     from_before = shifted(to_after, "blk", 1)
+    (own_near,) = near_sums((targets,), targets, (own_list,), *args, f32, 20.0)
+    own_near, skeletons = lax.optimization_barrier((own_near, skeletons))
 
     blk = lax.axis_index("blk")
     first = blk * seg_size + lax.axis_index("leaf") * own_clusters
     entries = lax.dynamic_slice_in_dim(far_src, first, own_clusters, 0)
     far_shape = jax.ShapeDtypeStruct((columns, own_clusters * LEAF), f32)
-    if blk_count == 4 and cluster_total <= 256:
-        middle_load = shifted(later_load, "blk", 2)
+    if narrow:
         entries = lax.rem(entries + (blk_count - blk) * seg_size, cluster_total)
         far = pl.pallas_call(
             functools.partial(far_kernel_phased, seg_size),
@@ -411,8 +403,8 @@
                 pltpu.VMEM((own_clusters, rank, columns), bf16),
             ],
             compiler_params=PARAMS,
-            cost_estimate=cost(3.0),
-        )(entries, couplings, basis, prev_load, after_load, middle_load, before_load)
+            cost_estimate=cost(0.01),
+        )(entries, couplings, basis, *skeletons)
     else:
         far = pl.pallas_call(
             functools.partial(far_kernel, seg_size),
@@ -421,7 +413,7 @@
             out_specs=VMEM,
             scratch_shapes=[pltpu.VMEM((cluster_total, rank, columns), bf16)],
             compiler_params=PARAMS,
-        )(entries, couplings, basis, lax.all_gather(prev_load[:skel_rows], "blk", axis=0, tiled=True))
+        )(entries, couplings, basis, *skeletons)
 
     far, from_before, from_after = lax.optimization_barrier((far, from_before, from_after))
     near = own_near + from_before.astype(f32) + from_after.astype(f32)

time: 30.4 us -> 31.1 us (1.023)
  waiting for transfers between devices: 5.03 us -> 2.01 us
  starting transfers between devices: 10.2 us -> 13 us
  local copies, waits for them, and re-layouts: 0.85 us -> 2.08 us
    ppermute x7 -> x9, waiting for transfers between devices: 5.03 us -> 2.01 us  [shifted(): lax.ppermute(block, axis, [(i, (i + shift) % count) for i in range(count)])]
    ppermute x7 -> x9, starting transfers between devices: 10.2 us -> 13 us  [shifted(): lax.ppermute(block, axis, [(i, (i + shift) % count) for i in range(count)])]
    unnamed x15, local copies, waits for them, and re-layouts: 0.77 us -> 2 us
  transfers between devices with their start and end apart: 7 -> 9, of which waited for: 4 -> 2; matrix products, arithmetic and copies ran while one was open for 1% -> 0% of each run, Pallas kernels for 36% -> 35%
where the time goes in v5:
time: 31.1 us; the launch traced here: 31 us
  Pallas kernels  13 us (42%)
  starting transfers between devices  13 us (42%)
  local copies, waits for them, and re-layouts  2.08 us (7%)
  waiting for transfers between devices  2.01 us (6%)
  other arithmetic  0.76 us (2%)
    ppermute x9, starting transfers between devices, shifted(): lax.ppermute(block, axis, [(i, (i + shift) % count) for i in range(count)])  13 us
    pallas_call x2, Pallas kernels, near_sums(): pl.pallas_call(functools.partial(near_kernel, bases, targets), out_shape=...  7.42 us
    pallas_call x1, Pallas kernels, on_device(): pl.pallas_call(functools.partial(far_kernel_phased, seg_size), out_shape=...  2.63 us
    pallas_call x1, Pallas kernels, on_device(): pl.pallas_call(functools.partial(list_kernel, seg_size), out_shape=[jax.S...  2.27 us
    ppermute x9, waiting for transfers between devices, shifted(): lax.ppermute(block, axis, [(i, (i + shift) % count) for i in range(count)])  2.01 us
    unnamed x15, local copies, waits for them, and re-layouts  2 us
    pallas_call x1, Pallas kernels, on_device(): pl.pallas_call(functools.partial(feature_kernel, seg_size, targets, own_c...  0.69 us
    transpose x1, other arithmetic, on_device(): return (whole + far).astype(bf16).T  0.68 us
  transfers between devices with their start and end apart: 9, of which 2 were waited for; matrix products, arithmetic and copies ran while one was open for 0% of the time, Pallas kernels for 35%

profile of v5, /device:TPU:0, one launch (start us, length us, event | category | flops | bytes accessed | tf_op | source)
XLA Modules:
  0.0 31.0 jit_solution(7653361861068797335)
XLA Ops:
  0.0 2.3 %shard_map.64 = (s32[8,128]{1,0:T(8,128)}, s32[8,128]{1,0:T(8,128)}, s32[8,128]{1,0:T(8,128)}, bf16[256,128]{1,0:T(8,128)(2,1)}) custom-call(s32[16,27]{1,0:T(8,128)} %near_hbm.1, bf16[32,4096]{1,0:T(8,128)(2,1)} %basis_ref.1, bf16[32,4096]{1,0:T(8,128)(2,1)} %bitcast.3), custom_call_target="tpu_custom_call" | custom-call | flops 10000000 | tf_op jit(solution)/shard_map/pallas_call | solution.py:343
  2.3 5.1 %collective-permute-start.3 = (bf16[256,128]{1,0:T(8,128)(2,1)}, bf16[256,128]{1,0:T(8,128)(2,1)S(1)}, u32[]{:S(2)}, u32[]{:S(2)}) collective-permute-start(bf16[256,128]{1,0:T(8,128)(2,1)} %get-tuple-element.44.refs_0_), channel_id=1, source_target_pairs={{0,12},{4,0},{8,4},{12,8},{1,13},{5,1},{9,5},{13,9},{2,14},{6,2},{... | collective-permute-start | bytes 196616 | tf_op jit(solution)/shard_map/ppermute | solution.py:32
  7.4 0.0 collective-permute-start.4
  7.4 1.0 %collective-permute-start = (s32[8,128]{1,0:T(8,128)}, s32[8,128]{1,0:T(8,128)S(1)}, u32[]{:S(2)}, u32[]{:S(2)}) collective-permute-start(s32[8,128]{1,0:T(8,128)} %get-tuple-element.31), channel_id=1, source_target_pairs={{0,4},{4,8},{8,12},{12,0},{1,5},{5,9},{9,13},{13,1},{2,6},{6,10},{... | collective-permute-start | bytes 12296 | tf_op jit(solution)/shard_map/ppermute | solution.py:32
  8.4 2.8 %collective-permute-start.1 = (s32[8,128]{1,0:T(8,128)}, s32[8,128]{1,0:T(8,128)S(1)}, u32[]{:S(2)}, u32[]{:S(2)}) collective-permute-start(s32[8,128]{1,0:T(8,128)} %get-tuple-element.32), channel_id=1, source_target_pairs={{0,12},{4,0},{8,4},{12,8},{1,13},{5,1},{9,5},{13,9},{2,14},{6,2},{... | collective-permute-start | bytes 12296 | tf_op jit(solution)/shard_map/ppermute | solution.py:32
  11.2 0.1 constant_dynamic-slice_fusion
  11.3 0.1 copy.8
  11.4 1.0 %copy-done.3 = f32[3,16384]{1,0:T(4,128)S(1)} copy-done((f32[3,16384]{1,0:T(4,128)S(1)}, f32[3,16384]{1,0:T(4,128)}, u32[]{:S(2)}) %copy-start.3) | copy-done | bytes 196632
  12.3 0.7 %shard_map.65 = (bf16[25,48,128]{2,1,0:T(8,128)(2,1)S(1)}, bf16[32,128,48]{2,1,0:T(8,128)(2,1)S(1)}) custom-call(f32[3,16384]{1,0:T(4,128)S(1)} %copy-done.3), custom_call_target="tpu_custom_call" | custom-call | flops 10000000 | tf_op jit(solution)/shard_map/pallas_call | solution.py:362
  13.0 0.1 collective-permute-start.5
  13.1 0.0 copy-start.4
  13.1 0.9 %copy-done.4 = bf16[4096,32]{0,1:T(8,128)(2,1)S(1)} copy-done((bf16[4096,32]{0,1:T(8,128)(2,1)S(1)}, bf16[4096,32]{0,1:T(8,128)(2,1)}, u32[]{:S(2)}) %copy-start.4) | copy-done | bytes 262168
  14.1 4.8 %shard_map.66 = (bf16[64,1024]{1,0:T(8,128)(2,1)S(1)}, bf16[64,1024]{1,0:T(8,128)(2,1)S(1)}) custom-call(s32[8,128]{1,0:T(8,128)S(1)} %collective-permute-done.refs_0_, s32[8,128]{1,0:T(8,128)S(1)} %collective-permute-done.1.refs_1_, bf16[25,48,128]{2,1,0:T(8,128)(2,1)S(1)} %get-tuple-element.34.refs_2_.refs_1_, ...), custom_call_target="tpu_custom_call" | custom-call | flops 20000000000 | tf_op jit(solution)/shard_map/pallas_call | solution.py:253
  18.9 0.0 copy-start.1
  18.9 0.0 copy-start.2
  18.9 0.0 copy-start.5
  18.9 1.8 %collective-permute-start.6 = (bf16[64,1024]{1,0:T(8,128)(2,1)S(1)}, bf16[64,1024]{1,0:T(8,128)(2,1)S(1)}, u32[]{:S(2)}, u32[]{:S(2)}) collective-permute-start(bf16[64,1024]{1,0:T(8,128)(2,1)S(1)} %get-tuple-element.48), channel_id=1, source_target_pairs={{0,4},{4,8},{8,12},{12,0},{1,5},{5,9},{9,13},{13,1},{2,6},{6,10},{... | collective-permute-start | bytes 393224 | tf_op jit(solution)/shard_map/ppermute | solution.py:32
  20.8 2.1 %collective-permute-start.7 = (bf16[64,1024]{1,0:T(8,128)(2,1)S(1)}, bf16[64,1024]{1,0:T(8,128)(2,1)S(1)}, u32[]{:S(2)}, u32[]{:S(2)}) collective-permute-start(bf16[64,1024]{1,0:T(8,128)(2,1)S(1)} %get-tuple-element.49), channel_id=1, source_target_pairs={{0,12},{4,0},{8,4},{12,8},{1,13},{5,1},{9,5},{13,9},{2,14},{6,2},{... | collective-permute-start | bytes 393224 | tf_op jit(solution)/shard_map/ppermute | solution.py:32
  22.9 2.6 %shard_map.67 = f32[64,1024]{1,0:T(8,128)S(1)} custom-call(s32[8,128]{1,0:T(8,128)S(1)} %copy-done.6, bf16[25,48,128]{2,1,0:T(8,128)(2,1)S(1)} %get-tuple-element.34.refs_2_.refs_1_, bf16[32,128,48]{2,1,0:T(8,128)(2,1)S(1)} %get-tuple-element.35.refs_3_.refs_2_, bf16[32,4096]{1,0:T(8,128)(2,1)S(1)} %bitcast.6, ...), custom_call_target="tpu_custom_call" | custom-call | flops 20000000000 | tf_op jit(solution)/shard_map/pallas_call | solution.py:253
  25.5 2.6 %shard_map.68 = f32[32,2048]{1,0:T(8,128)S(1)} custom-call(s32[16,32]{1,0:T(8,128)S(1)} %negate_select_fusion.far_ref, bf16[16,32,32,32]{3,2,1,0:T(8,128)(2,1)S(1)} %copy-done.1, bf16[32,4096]{1,0:T(8,128)(2,1)S(1)} %copy-done.2, bf16[256,128]{1,0:T(8,128)(2,1)S(1)} %copy-done.5, bf16[256,128]{1,0:T(8,128)(2,1)S(1)} %collective-permute-done.3.refs_1_, ...), custom_call_target="tpu_custom_call" | custom-call | flops 10000000 | tf_op jit(solution)/shard_map/pallas_call | solution.py:395
  28.2 0.7 %collective-permute-done.7 = bf16[64,1024]{1,0:T(8,128)(2,1)S(1)} collective-permute-done((bf16[64,1024]{1,0:T(8,128)(2,1)S(1)}, bf16[64,1024]{1,0:T(8,128)(2,1)S(1)}, u32[]{:S(2)}, u32[]{:S(2)}) %collective-permute-start.7) | collective-permute-done | bytes 131104 | tf_op jit(solution)/shard_map/ppermute | solution.py:32
  28.9 0.1 collective-permute-start.8
  29.0 1.3 %collective-permute-done.8 = f32[32,1024]{1,0:T(8,128)S(1)} collective-permute-done((f32[32,1024]{1,0:T(8,128)S(1)}, f32[32,1024]{1,0:T(8,128)S(1)}, u32[]{:S(2)}, u32[]{:S(2)}) %collective-permute-start.8) | collective-permute-done | bytes 131104 | tf_op jit(solution)/shard_map/ppermute | solution.py:32
  30.3 0.7 %fusion.1 = bf16[2048,32]{0,1:T(8,128)(2,1)} fusion(f32[32,2048]{1,0:T(8,128)S(1)} %shard_map.68, f32[32,1024]{1,0:T(8,128)S(1)} %get-tuple-element.54, f32[32,1024]{1,0:T(8,128)S(1)} %get-tuple-element.53), kind=kLoop, calls=%fused_computation.3 | loop fusion | flops 196608 | bytes 655360 | tf_op jit(solution)/shard_map/transpose | solution.py:424
  (20 shorter events, 0.1 us)
Async XLA Ops:
  0.0 11.2 %copy-start = (s32[128,32]{0,1:T(8,128)S(1)}, s32[128,32]{0,1:T(8,128)}, u32[]{:S(2)}) copy-start(s32[128,32]{0,1:T(8,128)} %param.11) | copy-start | bytes 49156
  2.3 23.2 %collective-permute-start.3 = (bf16[256,128]{1,0:T(8,128)(2,1)}, bf16[256,128]{1,0:T(8,128)(2,1)S(1)}, u32[]{:S(2)}, u32[]{:S(2)}) collective-permute-start(bf16[256,128]{1,0:T(8,128)(2,1)} %get-tuple-element.44.refs_0_), channel_id=1, source_target_pairs={{0,12},{4,0},{8,4},{12,8},{1,13},{5,1},{9,5},{13,9},{2,14},{6,2},{... | collective-permute-start | bytes 196616 | tf_op jit(solution)/shard_map/ppermute | solution.py:32
  7.4 18.1 %collective-permute-start.4 = (bf16[256,128]{1,0:T(8,128)(2,1)}, bf16[256,128]{1,0:T(8,128)(2,1)S(1)}, u32[]{:S(2)}, u32[]{:S(2)}) collective-permute-start(bf16[256,128]{1,0:T(8,128)(2,1)} %get-tuple-element.44.refs_0_), channel_id=1, source_target_pairs={{0,8},{4,12},{8,0},{12,4},{1,9},{5,13},{9,1},{13,5},{2,10},{6,14},... | collective-permute-start | bytes 196616 | tf_op jit(solution)/shard_map/ppermute | solution.py:32
  7.4 5.6 %collective-permute-start = (s32[8,128]{1,0:T(8,128)}, s32[8,128]{1,0:T(8,128)S(1)}, u32[]{:S(2)}, u32[]{:S(2)}) collective-permute-start(s32[8,128]{1,0:T(8,128)} %get-tuple-element.31), channel_id=1, source_target_pairs={{0,4},{4,8},{8,12},{12,0},{1,5},{5,9},{9,13},{13,1},{2,6},{6,10},{... | collective-permute-start | bytes 12296 | tf_op jit(solution)/shard_map/ppermute | solution.py:32
  8.4 4.7 %collective-permute-start.1 = (s32[8,128]{1,0:T(8,128)}, s32[8,128]{1,0:T(8,128)S(1)}, u32[]{:S(2)}, u32[]{:S(2)}) collective-permute-start(s32[8,128]{1,0:T(8,128)} %get-tuple-element.32), channel_id=1, source_target_pairs={{0,12},{4,0},{8,4},{12,8},{1,13},{5,1},{9,5},{13,9},{2,14},{6,2},{... | collective-permute-start | bytes 12296 | tf_op jit(solution)/shard_map/ppermute | solution.py:32
  11.2 1.9 %collective-permute-start.2 = (bf16[32,4096]{1,0:T(8,128)(2,1)}, bf16[32,4096]{1,0:T(8,128)(2,1)S(1)}, u32[]{:S(2)}, u32[]{:S(2)}) collective-permute-start(bf16[32,4096]{1,0:T(8,128)(2,1)} %bitcast.4), channel_id=1, source_target_pairs={{0,1},{1,0},{2,3},{3,2},{4,5},{5,4},{6,7},{7,6},{8,9},{9,8},{10,11... | collective-permute-start | bytes 786440 | tf_op jit(solution)/shard_map/ppermute | solution.py:32
  11.4 1.0 %copy-start.3 = (f32[3,16384]{1,0:T(4,128)S(1)}, f32[3,16384]{1,0:T(4,128)}, u32[]{:S(2)}) copy-start(f32[3,16384]{1,0:T(4,128)} %points_ref) | copy-start | bytes 589828
  13.0 12.5 %collective-permute-start.5 = (bf16[256,128]{1,0:T(8,128)(2,1)}, bf16[256,128]{1,0:T(8,128)(2,1)S(1)}, u32[]{:S(2)}, u32[]{:S(2)}) collective-permute-start(bf16[256,128]{1,0:T(8,128)(2,1)} %get-tuple-element.44.refs_0_), channel_id=1, source_target_pairs={{0,4},{4,8},{8,12},{12,0},{1,5},{5,9},{9,13},{13,1},{2,6},{6,10},{... | collective-permute-start | bytes 196616 | tf_op jit(solution)/shard_map/ppermute | solution.py:32
  13.1 1.0 %copy-start.4 = (bf16[4096,32]{0,1:T(8,128)(2,1)S(1)}, bf16[4096,32]{0,1:T(8,128)(2,1)}, u32[]{:S(2)}) copy-start(bf16[4096,32]{0,1:T(8,128)(2,1)} %param.7) | copy-start | bytes 786436
  14.1 8.8 %copy-start.6 = (s32[8,128]{1,0:T(8,128)S(1)}, s32[8,128]{1,0:T(8,128)}, u32[]{:S(2)}) copy-start(s32[8,128]{1,0:T(8,128)} %get-tuple-element.41.refs_0_) | copy-start | bytes 12292
  18.9 6.6 %copy-start.1 = (bf16[16,32,32,32]{3,2,1,0:T(8,128)(2,1)S(1)}, bf16[16,32,32,32]{3,2,1,0:T(8,128)(2,1)}, u32[]{:S(2)}) copy-start(bf16[16,32,32,32]{3,2,1,0:T(8,128)(2,1)} %couplings_ref.1) | copy-start | bytes 3145732
  18.9 6.6 %copy-start.2 = (bf16[32,4096]{1,0:T(8,128)(2,1)S(1)}, bf16[32,4096]{1,0:T(8,128)(2,1)}, u32[]{:S(2)}) copy-start(bf16[32,4096]{1,0:T(8,128)(2,1)} %basis_ref.1) | copy-start | bytes 786436
  18.9 6.6 %copy-start.5 = (bf16[256,128]{1,0:T(8,128)(2,1)S(1)}, bf16[256,128]{1,0:T(8,128)(2,1)}, u32[]{:S(2)}) copy-start(bf16[256,128]{1,0:T(8,128)(2,1)} %get-tuple-element.44.refs_0_) | copy-start | bytes 196612
  18.9 9.2 %collective-permute-start.6 = (bf16[64,1024]{1,0:T(8,128)(2,1)S(1)}, bf16[64,1024]{1,0:T(8,128)(2,1)S(1)}, u32[]{:S(2)}, u32[]{:S(2)}) collective-permute-start(bf16[64,1024]{1,0:T(8,128)(2,1)S(1)} %get-tuple-element.48), channel_id=1, source_target_pairs={{0,4},{4,8},{8,12},{12,0},{1,5},{5,9},{9,13},{13,1},{2,6},{6,10},{... | collective-permute-start | bytes 393224 | tf_op jit(solution)/shard_map/ppermute | solution.py:32
  20.8 8.1 %collective-permute-start.7 = (bf16[64,1024]{1,0:T(8,128)(2,1)S(1)}, bf16[64,1024]{1,0:T(8,128)(2,1)S(1)}, u32[]{:S(2)}, u32[]{:S(2)}) collective-permute-start(bf16[64,1024]{1,0:T(8,128)(2,1)S(1)} %get-tuple-element.49), channel_id=1, source_target_pairs={{0,12},{4,0},{8,4},{12,8},{1,13},{5,1},{9,5},{13,9},{2,14},{6,2},{... | collective-permute-start | bytes 393224 | tf_op jit(solution)/shard_map/ppermute | solution.py:32
  28.9 1.4 %collective-permute-start.8 = (f32[32,1024]{1,0:T(8,128)S(1)}, f32[32,1024]{1,0:T(8,128)S(1)}, u32[]{:S(2)}, u32[]{:S(2)}) collective-permute-start(f32[32,1024]{1,0:T(8,128)S(1)} %slice.9), channel_id=1, source_target_pairs={{0,1},{1,0},{2,3},{3,2},{4,5},{5,4},{6,7},{7,6},{8,9},{9,8},{10,11... | collective-permute-start | bytes 393224 | tf_op jit(solution)/shard_map/ppermute | solution.py:32

commit v6 on v5

--- a/solution.py
+++ b/solution.py
@@ -32,11 +32,20 @@
     return lax.ppermute(block, axis, [(i, (i + shift) % count) for i in range(count)])
 
 
+def crossed(block, shift):
+    count = lax.axis_size("blk")
+    pairs = []
+    for i in range(count):
+        pairs.append((2 * i, (i + shift) % count * 2))
+        pairs.append((2 * i + 1, (i - shift) % count * 2 + 1))
+    return lax.ppermute(block, ("blk", "rhs"), pairs)
+
+
 def cluster(index):
     return pl.ds(pl.multiple_of(index * LEAF, LEAF), LEAF)
 
 
-def list_kernel(seg_size, near_hbm, basis_hbm, charges_hbm, own_ref, prev_ref, next_ref, skel_ref, near_ref, basis_ref, charges_ref, sems):
+def list_kernel(seg_size, near_hbm, basis_hbm, charges_hbm, own_ref, away_ref, skel_ref, near_ref, basis_ref, charges_ref, sems):
     copies = [
         pltpu.make_async_copy(near_hbm, near_ref, sems.at[0]),
         pltpu.make_async_copy(basis_hbm, basis_ref, sems.at[1]),
@@ -44,8 +53,7 @@
     ]
     for copy in copies:
         copy.start()
-    targets = near_ref.shape[0] // 2
-    near_count = near_ref.shape[1]
+    targets, near_count = near_ref.shape
     blk_count = lax.axis_size("blk")
     blk = lax.axis_index("blk")
     before = lax.rem(blk + blk_count - 1, blk_count)
@@ -61,14 +69,14 @@
         return jnp.where(condition, 1.0, 0.0).astype(bf16)
 
     lane = iota((targets, LEAF), 1)
+    in_half = iota((targets, LEAF), 0) // (targets // 2) == half
     earlier = ones(iota((LEAF, LEAF), 0) < iota((LEAF, LEAF), 1))
     above = ones(iota((targets, targets), 1) < iota((targets, targets), 0))
     row = iota((8, LEAF), 0)
     lower = iota((LEAF, LEAF), 0)
     copies[0].wait()
-    sources = jnp.where(half == 0, near_ref[:targets, :], near_ref[targets:, :])
     sources = jnp.concatenate(
-        [sources, jnp.full((targets, LEAF - near_count), -1, jnp.int32)], axis=1
+        [near_ref[...], jnp.full((targets, LEAF - near_count), -1, jnp.int32)], axis=1
     )
     segment = jnp.zeros((targets, LEAF), jnp.int32)
     if seg_size & (seg_size - 1) == 0:
@@ -79,7 +87,8 @@
     is_own = segment == blk
     is_prev = jnp.logical_and(segment == before, jnp.logical_not(is_own))
     is_next = jnp.logical_and(lane < near_count, jnp.logical_not(jnp.logical_or(is_own, is_prev)))
-    masks = (is_own, is_prev, is_next)
+    away = jnp.where(half == 0, jnp.where(is_next, 1, 0), jnp.where(is_prev, 1, 0))
+    masks = (jnp.logical_and(is_own, in_half), away == 1)
     place = jnp.zeros((targets, LEAF), f32)
     totals = []
     for mask in masks:
@@ -107,7 +116,7 @@
         preferred_element_type=f32,
     )
     last = row * LEAF + iota((8, LEAF), 1) == 8 * LEAF - 1
-    for i, out in enumerate((own_ref, prev_ref, next_ref)):
+    for i, out in enumerate((own_ref, away_ref)):
         codes = lists[16 * i : 16 * i + 8] + 256.0 * lists[16 * i + 8 : 16 * i + 16]
         out[...] = jnp.where(last, totals[i], codes).astype(jnp.int32)
 
@@ -171,17 +180,15 @@
     return jnp.transpose(stacked).astype(bf16)
 
 
-def feature_kernel(seg_size, targets, leaf_clusters, points_ref, target_ref, source_ref):
+def feature_kernel(seg_size, targets, points_ref, target_ref, source_ref):
     blk_count = lax.axis_size("blk")
     blk = lax.axis_index("blk")
-    first = lax.axis_index("leaf") * leaf_clusters + lax.axis_index("rhs") * targets
-    for which in range(3):
-        segment = lax.rem(blk + which + blk_count - 1, blk_count)
+    first = lax.axis_index("leaf") * targets
+    away = lax.rem(blk + 2 * lax.axis_index("rhs") + blk_count - 1, blk_count)
+    for which, segment in enumerate((away, blk)):
         for i in range(targets):
-            target_ref[which * targets + i] = target_features(
-                points_ref, segment * seg_size + first + i
-            )
-    target_ref[3 * targets] = jnp.zeros((DEPTH, LEAF), bf16)
+            target_ref[which * targets + i] = target_features(points_ref, segment * seg_size + first + i)
+    target_ref[2 * targets] = jnp.zeros((DEPTH, LEAF), bf16)
 
     def some_sources(step, carry):
         for u in range(8):
@@ -192,31 +199,23 @@
     lax.fori_loop(0, seg_size // 8, some_sources, 0)
 
 
-def near_kernel(bases, targets, *refs):
-    count = len(bases)
-    lists = refs[:count]
-    target_ref, source_ref, mine_ref, other_ref = refs[count : count + 4]
-    outs = refs[count + 4 : 2 * count + 4]
-    total, even, odd = refs[2 * count + 4 :]
-    lengths = [ref[7, LEAF - 1] for ref in lists]
-    length = sum(lengths)
+def near_kernel(base, list_ref, target_ref, source_ref, mine_ref, other_ref, out_ref, total, even, odd):
+    targets = total.shape[0] - 1
+    blank = target_ref.shape[0] - 1
+    length = list_ref[7, LEAF - 1]
     batches = lax.div(length + (BATCH - 1), BATCH)
     total[...] = jnp.zeros_like(total)
 
     def pair(batch, u):
         at = batch * BATCH + u
-        code = jnp.int32(3 * targets * 256)
-        for i in reversed(range(count)):
-            start = sum(lengths[:i])
-            place = jnp.maximum(at - start, 0)
-            entry = lists[i][lax.shift_right_logical(place, 7), lax.bitwise_and(place, 127)]
-            code = jnp.where(at < start + lengths[i], entry + bases[i] * 256, code)
+        code = list_ref[lax.shift_right_logical(at, 7), lax.bitwise_and(at, 127)]
+        code = jnp.where(at < length, code, targets * 256)
         return lax.shift_right_logical(code, 8), lax.bitwise_and(code, 255)
 
     def make(batch, slot):
         for u in range(BATCH):
             target, source = pair(batch, u)
-            square = jnp.dot(source_ref[source], target_ref[target], preferred_element_type=f32)
+            square = jnp.dot(source_ref[source], target_ref[jnp.minimum(base + target, blank)], preferred_element_type=f32)
             slot[u] = lax.rsqrt(square).astype(bf16)
 
     def use(batch, slot):
@@ -243,26 +242,25 @@
     def _():
         use(batches - 1, even)
 
-    for base, out in zip(bases, outs):
-        for i in range(targets):
-            out[:, i * LEAF : (i + 1) * LEAF] = total[base + i].astype(out.dtype)
-
-
-def near_sums(bases, targets, lists, target_rows, source_rows, mine, other, dtype, microseconds):
+    for i in range(targets):
+        out_ref[:, i * LEAF : (i + 1) * LEAF] = total[i].astype(out_ref.dtype)
+
+
+def near_sum(base, targets, pairs, target_rows, source_rows, mine, other, dtype):
     columns = 2 * mine.shape[0]
     return pl.pallas_call(
-        functools.partial(near_kernel, bases, targets),
-        out_shape=[jax.ShapeDtypeStruct((columns, targets * LEAF), dtype)] * len(bases),
-        in_specs=[SMEM] * len(bases) + [VMEM] * 4,
-        out_specs=[VMEM] * len(bases),
+        functools.partial(near_kernel, base),
+        out_shape=jax.ShapeDtypeStruct((columns, targets * LEAF), dtype),
+        in_specs=[SMEM] + [VMEM] * 4,
+        out_specs=VMEM,
         scratch_shapes=[
-            pltpu.VMEM((3 * targets + 1, columns, LEAF), f32),
+            pltpu.VMEM((targets + 1, columns, LEAF), f32),
             pltpu.VMEM((BATCH, LEAF, LEAF), bf16),
             pltpu.VMEM((BATCH, LEAF, LEAF), bf16),
         ],
         compiler_params=PARAMS,
-        cost_estimate=cost(microseconds),
-    )(*lists, target_rows, source_rows, mine, other)
+        cost_estimate=cost(20.0),
+    )(pairs, target_rows, source_rows, mine, other)
 
 
 def far_sum(out_ref, basis_ref, target, at, coefficient):
@@ -337,15 +335,14 @@
     seg_size = seg_rows // LEAF
     rank = basis.shape[0]
     own_clusters, near_count = near_src.shape
-    targets = own_clusters // 2
     cluster_total = seg_size * blk_count
     pack = LEAF // columns
-    own_list, prev_list, next_list, skeleton = pl.pallas_call(
+    own_list, away_list, skeleton = pl.pallas_call(
         functools.partial(list_kernel, seg_size),
-        out_shape=[jax.ShapeDtypeStruct((8, LEAF), jnp.int32)] * 3
+        out_shape=[jax.ShapeDtypeStruct((8, LEAF), jnp.int32)] * 2
         + [jax.ShapeDtypeStruct((seg_size // pack * rank, LEAF), bf16)],
         in_specs=[HBM] * 3,
-        out_specs=[VMEM] * 4,
+        out_specs=[VMEM] * 3,
         scratch_shapes=[
             pltpu.VMEM(near_src.shape, jnp.int32),
             pltpu.VMEM(basis.shape, bf16),
@@ -353,22 +350,21 @@
             pltpu.SemaphoreType.DMA((3,)),
         ],
         compiler_params=pltpu.CompilerParams(vmem_limit_bytes=63 * 2**20),
-        cost_estimate=cost(0.01),
+        cost_estimate=cost(3.0),
     )(near_src, basis, mine)
 
-    points, prev_list, next_list = lax.optimization_barrier((points, prev_list, next_list))
-    after_list = shifted(prev_list, "blk", -1)
-    before_list = shifted(next_list, "blk", 1)
+    points, away_list = lax.optimization_barrier((points, away_list))
+    pairs = crossed(away_list, 1)
     target_rows, source_rows = pl.pallas_call(
-        functools.partial(feature_kernel, seg_size, targets, own_clusters),
+        functools.partial(feature_kernel, seg_size, own_clusters),
         out_shape=[
-            jax.ShapeDtypeStruct((3 * targets + 1, DEPTH, LEAF), bf16),
+            jax.ShapeDtypeStruct((2 * own_clusters + 1, DEPTH, LEAF), bf16),
             jax.ShapeDtypeStruct((seg_size, LEAF, DEPTH), bf16),
         ],
         in_specs=[VMEM],
         out_specs=[VMEM, VMEM],
         compiler_params=PARAMS,
-        cost_estimate=cost(0.01),
+        cost_estimate=cost(0.7),
     )(points)
     later_charges, skeleton = lax.optimization_barrier((mine, skeleton))
     other = shifted(later_charges, "rhs", 1)
@@ -378,12 +374,10 @@
     else:
         skeletons = [lax.all_gather(skeleton, "blk", axis=0, tiled=True)]
     args = (target_rows, source_rows, mine, other)
-    lists = (before_list, after_list)
-    to_before, to_after = near_sums((0, 2 * targets), targets, lists, *args, bf16, 20.0)
-    to_before, to_after, own_list = lax.optimization_barrier((to_before, to_after, own_list))
-    from_after = shifted(to_before, "blk", -1)
-    from_before = shifted(to_after, "blk", 1)
-    (own_near,) = near_sums((targets,), targets, (own_list,), *args, f32, 20.0)
+    partial = near_sum(0, own_clusters, pairs, *args, bf16)
+    partial, own_list = lax.optimization_barrier((partial, own_list))
+    returned = crossed(partial, -1)
+    own_near = near_sum(own_clusters, own_clusters, own_list, *args, f32)
     own_near, skeletons = lax.optimization_barrier((own_near, skeletons))
 
     blk = lax.axis_index("blk")
@@ -415,13 +409,10 @@
             compiler_params=PARAMS,
         )(entries, couplings, basis, *skeletons)
 
-    far, from_before, from_after = lax.optimization_barrier((far, from_before, from_after))
-    near = own_near + from_before.astype(f32) + from_after.astype(f32)
-    keep = near[:columns]
-    got = shifted(near[columns:], "rhs", 1)
-    even = lax.axis_index("rhs") == 0
-    whole = jnp.concatenate([jnp.where(even, keep, got), jnp.where(even, got, keep)], axis=1)
-    return (whole + far).astype(bf16).T
+    far, returned = lax.optimization_barrier((far, returned))
+    near = own_near + returned.astype(f32)
+    got = shifted(near[columns:].astype(bf16), "rhs", 1)
+    return (near[:columns] + got.astype(f32) + far).astype(bf16).T
 
 
 def solution(mesh):

time: 31.1 us -> 30.1 us (0.968)
  waiting for transfers between devices: 2.01 us -> 6.05 us
  starting transfers between devices: 13 us -> 10.1 us
  local copies, waits for them, and re-layouts: 2.08 us -> 0.19 us
  Pallas kernels: 13 us -> 12.6 us
    ppermute x9 -> x5, starting transfers between devices: 13 us -> 6.19 us  [shifted(): lax.ppermute(block, axis, [(i, (i + shift) % count) for i in range(count)])]
    ppermute x0 -> x2, waiting for transfers between devices: none -> 4.7 us  [crossed(): return lax.ppermute(block, ('blk', 'rhs'), pairs)]
    ppermute x0 -> x2, starting transfers between devices: none -> 3.9 us  [crossed(): return lax.ppermute(block, ('blk', 'rhs'), pairs)]
    unnamed x15, local copies, waits for them, and re-layouts: 2 us -> 0.1 us
    pallas_call x3, Pallas kernels: 8.11 us -> 7.39 us  [the longest x2 6.65 us: near_sum(): pl.pallas_call(functools.partial(near_kernel, base), out_shape=jax.ShapeD...]
    ppermute x9 -> x5, waiting for transfers between devices: 2.01 us -> 1.35 us  [shifted(): lax.ppermute(block, axis, [(i, (i + shift) % count) for i in range(count)])]
    pallas_call x1, Pallas kernels: 2.27 us -> 2.59 us  [on_device(): pl.pallas_call(functools.partial(list_kernel, seg_size), out_shape=[jax.S...]
  transfers between devices with their start and end apart: 9 -> 7, of which waited for: 2 -> 3; matrix products, arithmetic and copies ran while one was open for 0% -> 1% of each run, Pallas kernels for 35% -> 34%
where the time goes in v6:
time: 30.1 us; the launch traced here: 29.8 us
  Pallas kernels  12.6 us (42%)
  starting transfers between devices  10.1 us (34%)
  waiting for transfers between devices  6.05 us (20%)
  other arithmetic  0.76 us (3%)
    pallas_call x2, Pallas kernels, near_sum(): pl.pallas_call(functools.partial(near_kernel, base), out_shape=jax.ShapeD...  6.65 us
    ppermute x5, starting transfers between devices, shifted(): lax.ppermute(block, axis, [(i, (i + shift) % count) for i in range(count)])  6.19 us
    ppermute x2, waiting for transfers between devices, crossed(): return lax.ppermute(block, ('blk', 'rhs'), pairs)  4.7 us
    ppermute x2, starting transfers between devices, crossed(): return lax.ppermute(block, ('blk', 'rhs'), pairs)  3.9 us
    pallas_call x1, Pallas kernels, on_device(): pl.pallas_call(functools.partial(far_kernel_phased, seg_size), out_shape=...  2.64 us
    pallas_call x1, Pallas kernels, on_device(): pl.pallas_call(functools.partial(list_kernel, seg_size), out_shape=[jax.S...  2.59 us
    ppermute x5, waiting for transfers between devices, shifted(): lax.ppermute(block, axis, [(i, (i + shift) % count) for i in range(count)])  1.35 us
    pallas_call x1, Pallas kernels, on_device(): pl.pallas_call(functools.partial(feature_kernel, seg_size, own_clusters),...  0.73 us
  transfers between devices with their start and end apart: 7, of which 3 were waited for; matrix products, arithmetic and copies ran while one was open for 1% of the time, Pallas kernels for 34%

profile of v6, /device:TPU:0, one launch (start us, length us, event | category | flops | bytes accessed | tf_op | source)
XLA Modules:
  0.0 29.8 jit_solution(18121038923152915938)
XLA Ops:
  0.0 2.6 %shard_map.64 = (s32[8,128]{1,0:T(8,128)}, s32[8,128]{1,0:T(8,128)}, bf16[256,128]{1,0:T(8,128)(2,1)}) custom-call(s32[16,27]{1,0:T(8,128)} %near_hbm.1, bf16[32,4096]{1,0:T(8,128)(2,1)} %basis_ref.1, bf16[32,4096]{1,0:T(8,128)(2,1)} %bitcast.3), custom_call_target="tpu_custom_call" | custom-call | flops 3000000000 | tf_op jit(solution)/shard_map/pallas_call | solution.py:340
  2.6 5.1 %collective-permute-start.2 = (bf16[256,128]{1,0:T(8,128)(2,1)}, bf16[256,128]{1,0:T(8,128)(2,1)S(1)}, u32[]{:S(2)}, u32[]{:S(2)}) collective-permute-start(bf16[256,128]{1,0:T(8,128)(2,1)} %get-tuple-element.34.refs_0_), channel_id=1, source_target_pairs={{0,12},{4,0},{8,4},{12,8},{1,13},{5,1},{9,5},{13,9},{2,14},{6,2},{... | collective-permute-start | bytes 196616 | tf_op jit(solution)/shard_map/ppermute | solution.py:32
  7.7 0.0 collective-permute-start.3
  7.7 1.0 %collective-permute-start.4 = (bf16[256,128]{1,0:T(8,128)(2,1)}, bf16[256,128]{1,0:T(8,128)(2,1)S(1)}, u32[]{:S(2)}, u32[]{:S(2)}) collective-permute-start(bf16[256,128]{1,0:T(8,128)(2,1)} %get-tuple-element.34.refs_0_), channel_id=1, source_target_pairs={{0,4},{4,8},{8,12},{12,0},{1,5},{5,9},{9,13},{13,1},{2,6},{6,10},{... | collective-permute-start | bytes 196616 | tf_op jit(solution)/shard_map/ppermute | solution.py:32
  8.7 0.0 collective-permute-start.1
  8.7 2.5 %collective-permute-start = (s32[8,128]{1,0:T(8,128)}, s32[8,128]{1,0:T(8,128)S(1)}, u32[]{:S(2)}, u32[]{:S(2)}) collective-permute-start(s32[8,128]{1,0:T(8,128)} %get-tuple-element.24), channel_id=1, source_target_pairs={{0,4},{1,13},{4,8},{5,1},{8,12},{9,5},{12,0},{13,9},{2,6},{3,15},{... | collective-permute-start | bytes 12296 | tf_op jit(solution)/shard_map/ppermute | solution.py:41
  11.2 0.1 constant_dynamic-slice_fusion
  11.3 0.1 copy.8
  11.4 0.7 %shard_map.65 = (bf16[33,48,128]{2,1,0:T(8,128)(2,1)S(1)}, bf16[32,128,48]{2,1,0:T(8,128)(2,1)S(1)}) custom-call(f32[3,16384]{1,0:T(4,128)S(1)} %copy-done.4), custom_call_target="tpu_custom_call" | custom-call | flops 700000000 | tf_op jit(solution)/shard_map/pallas_call | solution.py:358
  12.1 2.2 %collective-permute-done.list_ref = s32[8,128]{1,0:T(8,128)S(1)} collective-permute-done((s32[8,128]{1,0:T(8,128)}, s32[8,128]{1,0:T(8,128)S(1)}, u32[]{:S(2)}, u32[]{:S(2)}) %collective-permute-start) | collective-permute-done | bytes 4128 | tf_op jit(solution)/shard_map/ppermute | solution.py:41
  14.3 0.0 collective-permute-done.1.other_ref
  14.4 4.0 %shard_map.66 = bf16[64,2048]{1,0:T(8,128)(2,1)S(1)} custom-call(s32[8,128]{1,0:T(8,128)S(1)} %collective-permute-done.list_ref, bf16[33,48,128]{2,1,0:T(8,128)(2,1)S(1)} %get-tuple-element.26.target_ref, bf16[32,128,48]{2,1,0:T(8,128)(2,1)S(1)} %get-tuple-element.27.source_ref, bf16[32,4096]{1,0:T(8,128)(2,1)S(1)} %bitcast.5, ...), custom_call_target="tpu_custom_call" | custom-call | flops 20000000000 | tf_op jit(solution)/shard_map/pallas_call | solution.py:251
  18.4 0.0 copy-start.1
  18.4 0.0 copy-start.2
  18.4 0.0 copy-start.3
  18.4 1.4 %collective-permute-start.5 = (bf16[64,2048]{1,0:T(8,128)(2,1)S(1)}, bf16[64,2048]{1,0:T(8,128)(2,1)S(1)}, u32[]{:S(2)}, u32[]{:S(2)}) collective-permute-start(bf16[64,2048]{1,0:T(8,128)(2,1)S(1)} %shard_map.66), channel_id=1, source_target_pairs={{0,12},{1,5},{4,0},{5,9},{8,4},{9,13},{12,8},{13,1},{2,14},{3,7},{... | collective-permute-start | bytes 786440 | tf_op jit(solution)/shard_map/ppermute | solution.py:41
  19.8 2.6 %shard_map.67 = f32[64,2048]{1,0:T(8,128)S(1)} custom-call(s32[8,128]{1,0:T(8,128)S(1)} %copy-done.6, bf16[33,48,128]{2,1,0:T(8,128)(2,1)S(1)} %get-tuple-element.26.target_ref, bf16[32,128,48]{2,1,0:T(8,128)(2,1)S(1)} %get-tuple-element.27.source_ref, bf16[32,4096]{1,0:T(8,128)(2,1)S(1)} %bitcast.6, bf16[32,4096]{1,0:T(8,128)(2,1)S(1)} %collective-permute-done.1.other_ref), custom_call_target="tpu_custom_call" | custom-call | flops 20000000000 | tf_op jit(solution)/shard_map/pallas_call | solution.py:251
  22.5 0.0 collective-permute-done.2.refs_1_
  22.5 0.0 collective-permute-done.4.refs_3_
  22.5 2.6 %shard_map.68 = f32[32,2048]{1,0:T(8,128)S(1)} custom-call(s32[16,32]{1,0:T(8,128)S(1)} %negate_select_fusion.far_ref, bf16[16,32,32,32]{3,2,1,0:T(8,128)(2,1)S(1)} %copy-done.1, bf16[32,4096]{1,0:T(8,128)(2,1)S(1)} %copy-done.2, bf16[256,128]{1,0:T(8,128)(2,1)S(1)} %copy-done.3, bf16[256,128]{1,0:T(8,128)(2,1)S(1)} %collective-permute-done.2.refs_1_, ...), custom_call_target="tpu_custom_call" | custom-call | flops 10000000 | tf_op jit(solution)/shard_map/pallas_call | solution.py:389
  25.2 2.5 %collective-permute-done.5 = bf16[64,2048]{1,0:T(8,128)(2,1)S(1)} collective-permute-done((bf16[64,2048]{1,0:T(8,128)(2,1)S(1)}, bf16[64,2048]{1,0:T(8,128)(2,1)S(1)}, u32[]{:S(2)}, u32[]{:S(2)}) %collective-permute-start.5) | collective-permute-done | bytes 262176 | tf_op jit(solution)/shard_map/ppermute | solution.py:41
  27.7 0.1 collective-permute-start.6
  27.8 1.3 %collective-permute-done.6 = bf16[32,2048]{1,0:T(8,128)(2,1)S(1)} collective-permute-done((bf16[32,2048]{1,0:T(8,128)(2,1)S(1)}, bf16[32,2048]{1,0:T(8,128)(2,1)S(1)}, u32[]{:S(2)}, u32[]{:S(2)}) %collective-permute-start.6) | collective-permute-done | bytes 131104 | tf_op jit(solution)/shard_map/ppermute | solution.py:32
  29.1 0.7 %fusion.2 = bf16[2048,32]{0,1:T(8,128)(2,1)} fusion(f32[32,2048]{1,0:T(8,128)S(1)} %shard_map.68, bf16[32,2048]{1,0:T(8,128)(2,1)S(1)} %collective-permute-done.6, f32[64,2048]{1,0:T(8,128)S(1)} %convert_add_fusion), kind=kLoop, calls=%fused_computation.5 | loop fusion | flops 262144 | bytes 786432 | tf_op jit(solution)/shard_map/transpose | solution.py:415
  (15 shorter events, 0.1 us)
Async XLA Ops:
  0.0 11.2 %copy-start = (s32[128,32]{0,1:T(8,128)S(1)}, s32[128,32]{0,1:T(8,128)}, u32[]{:S(2)}) copy-start(s32[128,32]{0,1:T(8,128)} %param.11) | copy-start | bytes 49156
  0.0 8.7 %copy-start.5 = (bf16[4096,32]{0,1:T(8,128)(2,1)S(1)}, bf16[4096,32]{0,1:T(8,128)(2,1)}, u32[]{:S(2)}) copy-start(bf16[4096,32]{0,1:T(8,128)(2,1)} %param.7) | copy-start | bytes 786436
  0.0 11.4 %copy-start.4 = (f32[3,16384]{1,0:T(4,128)S(1)}, f32[3,16384]{1,0:T(4,128)}, u32[]{:S(2)}) copy-start(f32[3,16384]{1,0:T(4,128)} %points_ref) | copy-start | bytes 589828
  2.6 19.9 %collective-permute-start.2 = (bf16[256,128]{1,0:T(8,128)(2,1)}, bf16[256,128]{1,0:T(8,128)(2,1)S(1)}, u32[]{:S(2)}, u32[]{:S(2)}) collective-permute-start(bf16[256,128]{1,0:T(8,128)(2,1)} %get-tuple-element.34.refs_0_), channel_id=1, source_target_pairs={{0,12},{4,0},{8,4},{12,8},{1,13},{5,1},{9,5},{13,9},{2,14},{6,2},{... | collective-permute-start | bytes 196616 | tf_op jit(solution)/shard_map/ppermute | solution.py:32
  7.7 14.8 %collective-permute-start.3 = (bf16[256,128]{1,0:T(8,128)(2,1)}, bf16[256,128]{1,0:T(8,128)(2,1)S(1)}, u32[]{:S(2)}, u32[]{:S(2)}) collective-permute-start(bf16[256,128]{1,0:T(8,128)(2,1)} %get-tuple-element.34.refs_0_), channel_id=1, source_target_pairs={{0,8},{4,12},{8,0},{12,4},{1,9},{5,13},{9,1},{13,5},{2,10},{6,14},... | collective-permute-start | bytes 196616 | tf_op jit(solution)/shard_map/ppermute | solution.py:32
  7.7 14.8 %collective-permute-start.4 = (bf16[256,128]{1,0:T(8,128)(2,1)}, bf16[256,128]{1,0:T(8,128)(2,1)S(1)}, u32[]{:S(2)}, u32[]{:S(2)}) collective-permute-start(bf16[256,128]{1,0:T(8,128)(2,1)} %get-tuple-element.34.refs_0_), channel_id=1, source_target_pairs={{0,4},{4,8},{8,12},{12,0},{1,5},{5,9},{9,13},{13,1},{2,6},{6,10},{... | collective-permute-start | bytes 196616 | tf_op jit(solution)/shard_map/ppermute | solution.py:32
  8.7 5.6 %collective-permute-start.1 = (bf16[32,4096]{1,0:T(8,128)(2,1)S(1)}, bf16[32,4096]{1,0:T(8,128)(2,1)S(1)}, u32[]{:S(2)}, u32[]{:S(2)}) collective-permute-start(bf16[32,4096]{1,0:T(8,128)(2,1)S(1)} %bitcast.4), channel_id=1, source_target_pairs={{0,1},{1,0},{2,3},{3,2},{4,5},{5,4},{6,7},{7,6},{8,9},{9,8},{10,11... | collective-permute-start | bytes 786440 | tf_op jit(solution)/shard_map/ppermute | solution.py:32
  8.7 5.6 %collective-permute-start = (s32[8,128]{1,0:T(8,128)}, s32[8,128]{1,0:T(8,128)S(1)}, u32[]{:S(2)}, u32[]{:S(2)}) collective-permute-start(s32[8,128]{1,0:T(8,128)} %get-tuple-element.24), channel_id=1, source_target_pairs={{0,4},{1,13},{4,8},{5,1},{8,12},{9,5},{12,0},{13,9},{2,6},{3,15},{... | collective-permute-start | bytes 12296 | tf_op jit(solution)/shard_map/ppermute | solution.py:41
  14.4 5.5 %copy-start.6 = (s32[8,128]{1,0:T(8,128)S(1)}, s32[8,128]{1,0:T(8,128)}, u32[]{:S(2)}) copy-start(s32[8,128]{1,0:T(8,128)} %get-tuple-element.31.list_ref) | copy-start | bytes 12292
  18.4 4.1 %copy-start.1 = (bf16[16,32,32,32]{3,2,1,0:T(8,128)(2,1)S(1)}, bf16[16,32,32,32]{3,2,1,0:T(8,128)(2,1)}, u32[]{:S(2)}) copy-start(bf16[16,32,32,32]{3,2,1,0:T(8,128)(2,1)} %couplings_ref.1) | copy-start | bytes 3145732
  18.4 4.1 %copy-start.2 = (bf16[32,4096]{1,0:T(8,128)(2,1)S(1)}, bf16[32,4096]{1,0:T(8,128)(2,1)}, u32[]{:S(2)}) copy-start(bf16[32,4096]{1,0:T(8,128)(2,1)} %basis_ref.1) | copy-start | bytes 786436
  18.4 4.1 %copy-start.3 = (bf16[256,128]{1,0:T(8,128)(2,1)S(1)}, bf16[256,128]{1,0:T(8,128)(2,1)}, u32[]{:S(2)}) copy-start(bf16[256,128]{1,0:T(8,128)(2,1)} %get-tuple-element.34.refs_0_) | copy-start | bytes 196612
  18.4 9.2 %collective-permute-start.5 = (bf16[64,2048]{1,0:T(8,128)(2,1)S(1)}, bf16[64,2048]{1,0:T(8,128)(2,1)S(1)}, u32[]{:S(2)}, u32[]{:S(2)}) collective-permute-start(bf16[64,2048]{1,0:T(8,128)(2,1)S(1)} %shard_map.66), channel_id=1, source_target_pairs={{0,12},{1,5},{4,0},{5,9},{8,4},{9,13},{12,8},{13,1},{2,14},{3,7},{... | collective-permute-start | bytes 786440 | tf_op jit(solution)/shard_map/ppermute | solution.py:41
  27.7 1.4 %collective-permute-start.6 = (bf16[32,2048]{1,0:T(8,128)(2,1)S(1)}, bf16[32,2048]{1,0:T(8,128)(2,1)S(1)}, u32[]{:S(2)}, u32[]{:S(2)}) collective-permute-start(bf16[32,2048]{1,0:T(8,128)(2,1)S(1)} %slice.19), channel_id=1, source_target_pairs={{0,1},{1,0},{2,3},{3,2},{4,5},{5,4},{6,7},{7,6},{8,9},{9,8},{10,11... | collective-permute-start | bytes 393224 | tf_op jit(solution)/shard_map/ppermute | solution.py:32

commit v7 on v6

--- a/solution.py
+++ b/solution.py
@@ -45,7 +45,7 @@
     return pl.ds(pl.multiple_of(index * LEAF, LEAF), LEAF)
 
 
-def list_kernel(seg_size, near_hbm, basis_hbm, charges_hbm, own_ref, away_ref, skel_ref, near_ref, basis_ref, charges_ref, sems):
+def list_kernel(seg_size, near_hbm, basis_hbm, charges_hbm, own_ref, load_ref, near_ref, basis_ref, charges_ref, sems):
     copies = [
         pltpu.make_async_copy(near_hbm, near_ref, sems.at[0]),
         pltpu.make_async_copy(basis_hbm, basis_ref, sems.at[1]),
@@ -87,8 +87,8 @@
     is_own = segment == blk
     is_prev = jnp.logical_and(segment == before, jnp.logical_not(is_own))
     is_next = jnp.logical_and(lane < near_count, jnp.logical_not(jnp.logical_or(is_own, is_prev)))
-    away = jnp.where(half == 0, jnp.where(is_next, 1, 0), jnp.where(is_prev, 1, 0))
-    masks = (jnp.logical_and(is_own, in_half), away == 1)
+    leaving = jnp.where(half == 0, jnp.where(is_next, 1, 0), jnp.where(is_prev, 1, 0))
+    masks = (jnp.logical_and(is_own, in_half), leaving == 1)
     place = jnp.zeros((targets, LEAF), f32)
     totals = []
     for mask in masks:
@@ -116,9 +116,14 @@
         preferred_element_type=f32,
     )
     last = row * LEAF + iota((8, LEAF), 1) == 8 * LEAF - 1
-    for i, out in enumerate((own_ref, away_ref)):
-        codes = lists[16 * i : 16 * i + 8] + 256.0 * lists[16 * i + 8 : 16 * i + 16]
-        out[...] = jnp.where(last, totals[i], codes).astype(jnp.int32)
+    own = lists[:8] + 256.0 * lists[8:16]
+    own_ref[...] = jnp.where(last, totals[0], own).astype(jnp.int32)
+    high = jnp.floor(totals[1] * (1.0 / 256.0))
+    away = jnp.concatenate(
+        [jnp.where(last, totals[1] - 256.0 * high, lists[16:24]), jnp.where(last, high, lists[24:32])], axis=0
+    )
+    rows_end = seg_size // pack * rank
+    load_ref[rows_end : rows_end + 16, :] = away.astype(bf16)
 
     copies[1].wait()
     copies[2].wait()
@@ -140,7 +145,7 @@
             )
         )
     for group, block in enumerate(blocks):
-        skel_ref[group * rank : (group + 1) * rank, :] = block.astype(bf16)
+        load_ref[group * rank : (group + 1) * rank, :] = block.astype(bf16)
 
 
 def split(value):
@@ -337,12 +342,15 @@
     own_clusters, near_count = near_src.shape
     cluster_total = seg_size * blk_count
     pack = LEAF // columns
-    own_list, away_list, skeleton = pl.pallas_call(
+    skel_rows = seg_size // pack * rank
+    own_list, load = pl.pallas_call(
         functools.partial(list_kernel, seg_size),
-        out_shape=[jax.ShapeDtypeStruct((8, LEAF), jnp.int32)] * 2
-        + [jax.ShapeDtypeStruct((seg_size // pack * rank, LEAF), bf16)],
+        out_shape=[
+            jax.ShapeDtypeStruct((8, LEAF), jnp.int32),
+            jax.ShapeDtypeStruct((skel_rows + 16, LEAF), bf16),
+        ],
         in_specs=[HBM] * 3,
-        out_specs=[VMEM] * 3,
+        out_specs=[VMEM] * 2,
         scratch_shapes=[
             pltpu.VMEM(near_src.shape, jnp.int32),
             pltpu.VMEM(basis.shape, bf16),
@@ -353,8 +361,8 @@
         cost_estimate=cost(3.0),
     )(near_src, basis, mine)
 
-    points, away_list = lax.optimization_barrier((points, away_list))
-    pairs = crossed(away_list, 1)
+    points, load = lax.optimization_barrier((points, load))
+    first_load = crossed(load, 1)
     target_rows, source_rows = pl.pallas_call(
         functools.partial(feature_kernel, seg_size, own_clusters),
         out_shape=[
@@ -366,26 +374,31 @@
         compiler_params=PARAMS,
         cost_estimate=cost(0.7),
     )(points)
-    later_charges, skeleton = lax.optimization_barrier((mine, skeleton))
+    target_rows, later_charges, later_load = lax.optimization_barrier((target_rows, mine, load))
     other = shifted(later_charges, "rhs", 1)
     narrow = blk_count == 4 and cluster_total <= 256
     if narrow:
-        skeletons = [skeleton] + [shifted(skeleton, "blk", -i) for i in range(1, blk_count)]
+        loads = [load, crossed(later_load, -1), shifted(later_load, "blk", 2), first_load]
     else:
-        skeletons = [lax.all_gather(skeleton, "blk", axis=0, tiled=True)]
+        loads = [lax.all_gather(later_load[:skel_rows], "blk", axis=0, tiled=True)]
     args = (target_rows, source_rows, mine, other)
+    codes = first_load[skel_rows:].astype(jnp.int32)
+    pairs = codes[:8] + 256 * codes[8:]
     partial = near_sum(0, own_clusters, pairs, *args, bf16)
     partial, own_list = lax.optimization_barrier((partial, own_list))
     returned = crossed(partial, -1)
     own_near = near_sum(own_clusters, own_clusters, own_list, *args, f32)
-    own_near, skeletons = lax.optimization_barrier((own_near, skeletons))
+    own_near, loads = lax.optimization_barrier((own_near, loads))
 
     blk = lax.axis_index("blk")
     first = blk * seg_size + lax.axis_index("leaf") * own_clusters
     entries = lax.dynamic_slice_in_dim(far_src, first, own_clusters, 0)
     far_shape = jax.ShapeDtypeStruct((columns, own_clusters * LEAF), f32)
     if narrow:
-        entries = lax.rem(entries + (blk_count - blk) * seg_size, cluster_total)
+        segment = lax.div(entries, seg_size)
+        ahead = jnp.where(lax.axis_index("rhs") == 0, segment - blk, blk - segment)
+        order = lax.rem(ahead + blk_count, blk_count)
+        entries = entries + (order - segment) * seg_size
         far = pl.pallas_call(
             functools.partial(far_kernel_phased, seg_size),
             out_shape=far_shape,
@@ -398,7 +411,7 @@
             ],
             compiler_params=PARAMS,
             cost_estimate=cost(0.01),
-        )(entries, couplings, basis, *skeletons)
+        )(entries, couplings, basis, *loads)
     else:
         far = pl.pallas_call(
             functools.partial(far_kernel, seg_size),
@@ -407,7 +420,7 @@
             out_specs=VMEM,
             scratch_shapes=[pltpu.VMEM((cluster_total, rank, columns), bf16)],
             compiler_params=PARAMS,
-        )(entries, couplings, basis, *skeletons)
+        )(entries, couplings, basis, *loads)
 
     far, returned = lax.optimization_barrier((far, returned))
     near = own_near + returned.astype(f32)

time: 30.1 us -> 27.3 us (0.907)
  waiting for transfers between devices: 6.05 us -> 3.23 us
  Pallas kernels: 12.6 us -> 13.6 us
  starting transfers between devices: 10.1 us -> 9.24 us
    ppermute x5 -> x3, starting transfers between devices: 6.19 us -> 1.72 us  [shifted(): lax.ppermute(block, axis, [(i, (i + shift) % count) for i in range(count)])]
    ppermute x2 -> x3, starting transfers between devices: 3.9 us -> 7.52 us  [crossed(): return lax.ppermute(block, ('blk', 'rhs'), pairs)]
    ppermute x2 -> x3, waiting for transfers between devices: 4.7 us -> 1.47 us  [crossed(): return lax.ppermute(block, ('blk', 'rhs'), pairs)]
    pallas_call x2, Pallas kernels: 6.65 us -> 7.47 us  [near_sum(): pl.pallas_call(functools.partial(near_kernel, base), out_shape=jax.ShapeD...]
    ppermute x5 -> x3, waiting for transfers between devices: 1.35 us -> 1.76 us  [shifted(): lax.ppermute(block, axis, [(i, (i + shift) % count) for i in range(count)])]
  transfers between devices with their start and end apart: 7 -> 6, of which waited for: 3 -> 4; matrix products, arithmetic and copies ran while one was open for 1% -> 1% of each run, Pallas kernels for 34% -> 40%
where the time goes in v7:
time: 27.3 us; the launch traced here: 27.2 us
  Pallas kernels  13.6 us (50%)
  starting transfers between devices  9.24 us (34%)
  waiting for transfers between devices  3.23 us (12%)
  other arithmetic  0.8 us (3%)
    ppermute x3, starting transfers between devices, crossed(): return lax.ppermute(block, ('blk', 'rhs'), pairs)  7.52 us
    pallas_call x2, Pallas kernels, near_sum(): pl.pallas_call(functools.partial(near_kernel, base), out_shape=jax.ShapeD...  7.47 us
    pallas_call x1, Pallas kernels, on_device(): pl.pallas_call(functools.partial(list_kernel, seg_size), out_shape=[jax.S...  2.8 us
    pallas_call x1, Pallas kernels, on_device(): pl.pallas_call(functools.partial(far_kernel_phased, seg_size), out_shape=...  2.64 us
    ppermute x3, waiting for transfers between devices, shifted(): lax.ppermute(block, axis, [(i, (i + shift) % count) for i in range(count)])  1.76 us
    ppermute x3, starting transfers between devices, shifted(): lax.ppermute(block, axis, [(i, (i + shift) % count) for i in range(count)])  1.72 us
    ppermute x3, waiting for transfers between devices, crossed(): return lax.ppermute(block, ('blk', 'rhs'), pairs)  1.47 us
    pallas_call x1, Pallas kernels, on_device(): pl.pallas_call(functools.partial(feature_kernel, seg_size, own_clusters),...  0.72 us
  transfers between devices with their start and end apart: 6, of which 4 were waited for; matrix products, arithmetic and copies ran while one was open for 1% of the time, Pallas kernels for 40%

profile of v7, /device:TPU:0, one launch (start us, length us, event | category | flops | bytes accessed | tf_op | source)
XLA Modules:
  0.0 27.2 jit_solution(15366457568594673194)
XLA Ops:
  0.0 2.8 %shard_map.64 = (s32[8,128]{1,0:T(8,128)}, bf16[272,128]{1,0:T(8,128)(2,1)}) custom-call(s32[16,27]{1,0:T(8,128)} %near_hbm.1, bf16[32,4096]{1,0:T(8,128)(2,1)} %basis_ref.1, bf16[32,4096]{1,0:T(8,128)(2,1)} %bitcast.3), custom_call_target="tpu_custom_call" | custom-call | flops 3000000000 | tf_op jit(solution)/shard_map/pallas_call | solution.py:346
  2.8 3.1 %collective-permute-start = (bf16[272,128]{1,0:T(8,128)(2,1)}, bf16[272,128]{1,0:T(8,128)(2,1)S(1)}, u32[]{:S(2)}, u32[]{:S(2)}) collective-permute-start(bf16[272,128]{1,0:T(8,128)(2,1)} %get-tuple-element.34.refs_0_), channel_id=1, source_target_pairs={{0,4},{1,13},{4,8},{5,1},{8,12},{9,5},{12,0},{13,9},{2,6},{3,15},{... | collective-permute-start | bytes 208904 | tf_op jit(solution)/shard_map/ppermute | solution.py:41
  5.9 0.7 %shard_map.65 = (bf16[33,48,128]{2,1,0:T(8,128)(2,1)S(1)}, bf16[32,128,48]{2,1,0:T(8,128)(2,1)S(1)}) custom-call(f32[3,16384]{1,0:T(4,128)S(1)} %copy-done.4), custom_call_target="tpu_custom_call" | custom-call | flops 700000000 | tf_op jit(solution)/shard_map/pallas_call | solution.py:366
  6.6 2.1 %collective-permute-start.2 = (bf16[272,128]{1,0:T(8,128)(2,1)}, bf16[272,128]{1,0:T(8,128)(2,1)S(1)}, u32[]{:S(2)}, u32[]{:S(2)}) collective-permute-start(bf16[272,128]{1,0:T(8,128)(2,1)} %get-tuple-element.34.refs_0_), channel_id=1, source_target_pairs={{0,12},{1,5},{4,0},{5,9},{8,4},{9,13},{12,8},{13,1},{2,14},{3,7},{... | collective-permute-start | bytes 208904 | tf_op jit(solution)/shard_map/ppermute | solution.py:41
  8.7 1.0 %collective-permute-start.3 = (bf16[272,128]{1,0:T(8,128)(2,1)}, bf16[272,128]{1,0:T(8,128)(2,1)S(1)}, u32[]{:S(2)}, u32[]{:S(2)}) collective-permute-start(bf16[272,128]{1,0:T(8,128)(2,1)} %get-tuple-element.34.refs_0_), channel_id=1, source_target_pairs={{0,8},{4,12},{8,0},{12,4},{1,9},{5,13},{9,1},{13,5},{2,10},{6,14},... | collective-permute-start | bytes 208904 | tf_op jit(solution)/shard_map/ppermute | solution.py:32
  9.7 0.0 collective-permute-start.1
  9.7 0.1 constant_dynamic-slice_fusion
  9.8 0.1 copy.8
  9.9 0.6 %collective-permute-done.refs_3_ = bf16[272,128]{1,0:T(8,128)(2,1)S(1)} collective-permute-done((bf16[272,128]{1,0:T(8,128)(2,1)}, bf16[272,128]{1,0:T(8,128)(2,1)S(1)}, u32[]{:S(2)}, u32[]{:S(2)}) %collective-permute-start) | collective-permute-done | bytes 69664 | tf_op jit(solution)/shard_map/ppermute | solution.py:41
  10.5 0.8 %collective-permute-done.1.other_ref = bf16[32,4096]{1,0:T(8,128)(2,1)S(1)} collective-permute-done((bf16[32,4096]{1,0:T(8,128)(2,1)S(1)}, bf16[32,4096]{1,0:T(8,128)(2,1)S(1)}, u32[]{:S(2)}, u32[]{:S(2)}) %collective-permute-start.1) | collective-permute-done | bytes 262176 | tf_op jit(solution)/shard_map/ppermute | solution.py:32
  11.3 4.6 %shard_map.66 = bf16[64,2048]{1,0:T(8,128)(2,1)S(1)} custom-call(s32[8,128]{1,0:T(8,128)S(1)} %fusion.9.list_ref, bf16[33,48,128]{2,1,0:T(8,128)(2,1)S(1)} %get-tuple-element.27.target_ref, bf16[32,128,48]{2,1,0:T(8,128)(2,1)S(1)} %get-tuple-element.28.source_ref, bf16[32,4096]{1,0:T(8,128)(2,1)S(1)} %bitcast.5, ...), custom_call_target="tpu_custom_call" | custom-call | flops 20000000000 | tf_op jit(solution)/shard_map/pallas_call | solution.py:256
  15.9 0.0 copy-start.1
  15.9 0.0 copy-start.2
  15.9 0.0 copy-start.3
  15.9 2.3 %collective-permute-start.4 = (bf16[64,2048]{1,0:T(8,128)(2,1)S(1)}, bf16[64,2048]{1,0:T(8,128)(2,1)S(1)}, u32[]{:S(2)}, u32[]{:S(2)}) collective-permute-start(bf16[64,2048]{1,0:T(8,128)(2,1)S(1)} %shard_map.66), channel_id=1, source_target_pairs={{0,12},{1,5},{4,0},{5,9},{8,4},{9,13},{12,8},{13,1},{2,14},{3,7},{... | collective-permute-start | bytes 786440 | tf_op jit(solution)/shard_map/ppermute | solution.py:41
  18.2 2.9 %shard_map.67 = f32[64,2048]{1,0:T(8,128)S(1)} custom-call(s32[8,128]{1,0:T(8,128)S(1)} %copy-done.6, bf16[33,48,128]{2,1,0:T(8,128)(2,1)S(1)} %get-tuple-element.27.target_ref, bf16[32,128,48]{2,1,0:T(8,128)(2,1)S(1)} %get-tuple-element.28.source_ref, bf16[32,4096]{1,0:T(8,128)(2,1)S(1)} %bitcast.6, bf16[32,4096]{1,0:T(8,128)(2,1)S(1)} %collective-permute-done.1.other_ref), custom_call_target="tpu_custom_call" | custom-call | flops 20000000000 | tf_op jit(solution)/shard_map/pallas_call | solution.py:256
  21.1 0.0 collective-permute-done.2.refs_1_
  21.1 0.0 collective-permute-done.3.refs_2_
  21.2 2.6 %shard_map.68 = f32[32,2048]{1,0:T(8,128)S(1)} custom-call(s32[16,32]{1,0:T(8,128)S(1)} %fusion.7.far_ref, bf16[16,32,32,32]{3,2,1,0:T(8,128)(2,1)S(1)} %copy-done.1, bf16[32,4096]{1,0:T(8,128)(2,1)S(1)} %copy-done.2, bf16[272,128]{1,0:T(8,128)(2,1)S(1)} %copy-done.3, bf16[272,128]{1,0:T(8,128)(2,1)S(1)} %collective-permute-done.2.refs_1_, ...), custom_call_target="tpu_custom_call" | custom-call | flops 10000000 | tf_op jit(solution)/shard_map/pallas_call | solution.py:402
  23.8 0.9 %collective-permute-done.4 = bf16[64,2048]{1,0:T(8,128)(2,1)S(1)} collective-permute-done((bf16[64,2048]{1,0:T(8,128)(2,1)S(1)}, bf16[64,2048]{1,0:T(8,128)(2,1)S(1)}, u32[]{:S(2)}, u32[]{:S(2)}) %collective-permute-start.4) | collective-permute-done | bytes 262176 | tf_op jit(solution)/shard_map/ppermute | solution.py:41
  24.7 0.1 convert_add_fusion
  24.8 0.7 %collective-permute-start.5 = (bf16[32,2048]{1,0:T(8,128)(2,1)S(1)}, bf16[32,2048]{1,0:T(8,128)(2,1)S(1)}, u32[]{:S(2)}, u32[]{:S(2)}) collective-permute-start(bf16[32,2048]{1,0:T(8,128)(2,1)S(1)} %slice.39), channel_id=1, source_target_pairs={{0,1},{1,0},{2,3},{3,2},{4,5},{5,4},{6,7},{7,6},{8,9},{9,8},{10,11... | collective-permute-start | bytes 393224 | tf_op jit(solution)/shard_map/ppermute | solution.py:32
  25.5 1.0 %collective-permute-done.5 = bf16[32,2048]{1,0:T(8,128)(2,1)S(1)} collective-permute-done((bf16[32,2048]{1,0:T(8,128)(2,1)S(1)}, bf16[32,2048]{1,0:T(8,128)(2,1)S(1)}, u32[]{:S(2)}, u32[]{:S(2)}) %collective-permute-start.5) | collective-permute-done | bytes 131104 | tf_op jit(solution)/shard_map/ppermute | solution.py:32
  26.5 0.7 %fusion.2 = bf16[2048,32]{0,1:T(8,128)(2,1)} fusion(f32[32,2048]{1,0:T(8,128)S(1)} %shard_map.68, bf16[32,2048]{1,0:T(8,128)(2,1)S(1)} %collective-permute-done.5, f32[64,2048]{1,0:T(8,128)S(1)} %convert_add_fusion), kind=kLoop, calls=%fused_computation.5 | loop fusion | flops 262144 | bytes 786432 | tf_op jit(solution)/shard_map/transpose | solution.py:428
  (15 shorter events, 0.1 us)
Async XLA Ops:
  0.0 9.7 %copy-start = (s32[128,32]{0,1:T(8,128)S(1)}, s32[128,32]{0,1:T(8,128)}, u32[]{:S(2)}) copy-start(s32[128,32]{0,1:T(8,128)} %param.11) | copy-start | bytes 49156
  0.0 5.9 %copy-start.4 = (f32[3,16384]{1,0:T(4,128)S(1)}, f32[3,16384]{1,0:T(4,128)}, u32[]{:S(2)}) copy-start(f32[3,16384]{1,0:T(4,128)} %points_ref) | copy-start | bytes 589828
  0.0 9.7 %copy-start.5 = (bf16[4096,32]{0,1:T(8,128)(2,1)S(1)}, bf16[4096,32]{0,1:T(8,128)(2,1)}, u32[]{:S(2)}) copy-start(bf16[4096,32]{0,1:T(8,128)(2,1)} %param.7) | copy-start | bytes 786436
  2.8 7.7 %collective-permute-start = (bf16[272,128]{1,0:T(8,128)(2,1)}, bf16[272,128]{1,0:T(8,128)(2,1)S(1)}, u32[]{:S(2)}, u32[]{:S(2)}) collective-permute-start(bf16[272,128]{1,0:T(8,128)(2,1)} %get-tuple-element.34.refs_0_), channel_id=1, source_target_pairs={{0,4},{1,13},{4,8},{5,1},{8,12},{9,5},{12,0},{13,9},{2,6},{3,15},{... | collective-permute-start | bytes 208904 | tf_op jit(solution)/shard_map/ppermute | solution.py:41
  6.6 14.5 %collective-permute-start.2 = (bf16[272,128]{1,0:T(8,128)(2,1)}, bf16[272,128]{1,0:T(8,128)(2,1)S(1)}, u32[]{:S(2)}, u32[]{:S(2)}) collective-permute-start(bf16[272,128]{1,0:T(8,128)(2,1)} %get-tuple-element.34.refs_0_), channel_id=1, source_target_pairs={{0,12},{1,5},{4,0},{5,9},{8,4},{9,13},{12,8},{13,1},{2,14},{3,7},{... | collective-permute-start | bytes 208904 | tf_op jit(solution)/shard_map/ppermute | solution.py:41
  8.7 12.4 %collective-permute-start.3 = (bf16[272,128]{1,0:T(8,128)(2,1)}, bf16[272,128]{1,0:T(8,128)(2,1)S(1)}, u32[]{:S(2)}, u32[]{:S(2)}) collective-permute-start(bf16[272,128]{1,0:T(8,128)(2,1)} %get-tuple-element.34.refs_0_), channel_id=1, source_target_pairs={{0,8},{4,12},{8,0},{12,4},{1,9},{5,13},{9,1},{13,5},{2,10},{6,14},... | collective-permute-start | bytes 208904 | tf_op jit(solution)/shard_map/ppermute | solution.py:32
  9.7 1.5 %collective-permute-start.1 = (bf16[32,4096]{1,0:T(8,128)(2,1)S(1)}, bf16[32,4096]{1,0:T(8,128)(2,1)S(1)}, u32[]{:S(2)}, u32[]{:S(2)}) collective-permute-start(bf16[32,4096]{1,0:T(8,128)(2,1)S(1)} %bitcast.4), channel_id=1, source_target_pairs={{0,1},{1,0},{2,3},{3,2},{4,5},{5,4},{6,7},{7,6},{8,9},{9,8},{10,11... | collective-permute-start | bytes 786440 | tf_op jit(solution)/shard_map/ppermute | solution.py:32
  11.3 7.0 %copy-start.6 = (s32[8,128]{1,0:T(8,128)S(1)}, s32[8,128]{1,0:T(8,128)}, u32[]{:S(2)}) copy-start(s32[8,128]{1,0:T(8,128)} %get-tuple-element.31.list_ref) | copy-start | bytes 12292
  15.9 5.3 %copy-start.1 = (bf16[16,32,32,32]{3,2,1,0:T(8,128)(2,1)S(1)}, bf16[16,32,32,32]{3,2,1,0:T(8,128)(2,1)}, u32[]{:S(2)}) copy-start(bf16[16,32,32,32]{3,2,1,0:T(8,128)(2,1)} %couplings_ref.1) | copy-start | bytes 3145732
  15.9 5.3 %copy-start.2 = (bf16[32,4096]{1,0:T(8,128)(2,1)S(1)}, bf16[32,4096]{1,0:T(8,128)(2,1)}, u32[]{:S(2)}) copy-start(bf16[32,4096]{1,0:T(8,128)(2,1)} %basis_ref.1) | copy-start | bytes 786436
  15.9 5.3 %copy-start.3 = (bf16[272,128]{1,0:T(8,128)(2,1)S(1)}, bf16[272,128]{1,0:T(8,128)(2,1)}, u32[]{:S(2)}) copy-start(bf16[272,128]{1,0:T(8,128)(2,1)} %get-tuple-element.34.refs_0_) | copy-start | bytes 208900
  15.9 8.8 %collective-permute-start.4 = (bf16[64,2048]{1,0:T(8,128)(2,1)S(1)}, bf16[64,2048]{1,0:T(8,128)(2,1)S(1)}, u32[]{:S(2)}, u32[]{:S(2)}) collective-permute-start(bf16[64,2048]{1,0:T(8,128)(2,1)S(1)} %shard_map.66), channel_id=1, source_target_pairs={{0,12},{1,5},{4,0},{5,9},{8,4},{9,13},{12,8},{13,1},{2,14},{3,7},{... | collective-permute-start | bytes 786440 | tf_op jit(solution)/shard_map/ppermute | solution.py:41
  24.8 1.7 %collective-permute-start.5 = (bf16[32,2048]{1,0:T(8,128)(2,1)S(1)}, bf16[32,2048]{1,0:T(8,128)(2,1)S(1)}, u32[]{:S(2)}, u32[]{:S(2)}) collective-permute-start(bf16[32,2048]{1,0:T(8,128)(2,1)S(1)} %slice.39), channel_id=1, source_target_pairs={{0,1},{1,0},{2,3},{3,2},{4,5},{5,4},{6,7},{7,6},{8,9},{9,8},{10,11... | collective-permute-start | bytes 393224 | tf_op jit(solution)/shard_map/ppermute | solution.py:32

commit v8 on v7

--- a/solution.py
+++ b/solution.py
@@ -61,6 +61,9 @@
     columns = charges_ref.shape[0]
     rank = basis_ref.shape[0]
     pack = LEAF // columns
+    slots = 4 if near_count <= LEAF // 4 and targets % 4 == 0 else 1
+    width = LEAF // slots
+    lines = targets // slots
 
     def iota(shape, dim):
         return lax.broadcasted_iota(jnp.int32, shape, dim)
@@ -68,17 +71,25 @@
     def ones(condition):
         return jnp.where(condition, 1.0, 0.0).astype(bf16)
 
-    lane = iota((targets, LEAF), 1)
-    in_half = iota((targets, LEAF), 0) // (targets // 2) == half
+    lane = iota((lines, LEAF), 1)
+    target = iota((lines, LEAF), 0) * slots + lane // width
+    in_half = target // (targets // 2) == half
     earlier = ones(iota((LEAF, LEAF), 0) < iota((LEAF, LEAF), 1))
-    above = ones(iota((targets, targets), 1) < iota((targets, targets), 0))
+    whole = jnp.ones((LEAF, LEAF), bf16)
+    above = ones(iota((lines, lines), 1) < iota((lines, lines), 0))
     row = iota((8, LEAF), 0)
     lower = iota((LEAF, LEAF), 0)
-    copies[0].wait()
-    sources = jnp.concatenate(
-        [near_ref[...], jnp.full((targets, LEAF - near_count), -1, jnp.int32)], axis=1
-    )
-    segment = jnp.zeros((targets, LEAF), jnp.int32)
+    filler = jnp.full((1, width - near_count), -1, jnp.int32)
+    for copy in copies:
+        copy.wait()
+    packed = []
+    for line in range(lines):
+        pieces = []
+        for i in range(slots):
+            at = line * slots + i
+            pieces += [near_ref[at : at + 1, :], filler]
+        packed.append(jnp.concatenate(pieces, axis=1))
+    sources = jnp.concatenate(packed, axis=0)
     if seg_size & (seg_size - 1) == 0:
         segment = lax.shift_right_arithmetic(sources, seg_size.bit_length() - 1)
     else:
@@ -86,27 +97,30 @@
     local = (sources - segment * seg_size).astype(f32)
     is_own = segment == blk
     is_prev = jnp.logical_and(segment == before, jnp.logical_not(is_own))
-    is_next = jnp.logical_and(lane < near_count, jnp.logical_not(jnp.logical_or(is_own, is_prev)))
+    is_next = jnp.logical_and(sources >= 0, jnp.logical_not(jnp.logical_or(is_own, is_prev)))
+    is_own = jnp.logical_and(jnp.logical_and(is_own, in_half), sources >= 0)
+    is_prev = jnp.logical_and(is_prev, sources >= 0)
     leaving = jnp.where(half == 0, jnp.where(is_next, 1, 0), jnp.where(is_prev, 1, 0))
-    masks = (jnp.logical_and(is_own, in_half), leaving == 1)
-    place = jnp.zeros((targets, LEAF), f32)
+    masks = (is_own, leaving == 1)
+    place = jnp.zeros((lines, LEAF), f32)
     totals = []
     for mask in masks:
         within = jnp.dot(ones(mask), earlier, preferred_element_type=f32)
-        count = jnp.broadcast_to(within[:, LEAF - 1 :], (targets, LEAF))
+        count = jnp.dot(ones(mask), whole, preferred_element_type=f32)
         start = jnp.dot(above, count.astype(bf16), preferred_element_type=f32)
         place = jnp.where(mask, start + within, place)
-        totals.append(start[targets - 1 :, :] + count[targets - 1 :, :])
+        totals.append(start[lines - 1 :, :] + count[lines - 1 :, :])
     place = place.astype(jnp.int32)
+    target = target.astype(f32)
     left, right = [], []
-    for target in range(targets):
-        at = place[target : target + 1, :]
+    for line in range(lines):
+        at = place[line : line + 1, :]
         here = lax.shift_right_logical(at, 7) == row
         rows = []
         for mask in masks:
-            chosen = jnp.logical_and(here, jnp.where(mask[target : target + 1, :], 1, 0) == 1)
-            rows.append(jnp.where(chosen, local[target : target + 1, :], 0.0))
-            rows.append(jnp.where(chosen, float(target), 0.0))
+            chosen = jnp.logical_and(here, jnp.where(mask[line : line + 1, :], 1, 0) == 1)
+            rows.append(jnp.where(chosen, local[line : line + 1, :], 0.0))
+            rows.append(jnp.where(chosen, target[line : line + 1, :], 0.0))
         left.append(jnp.concatenate(rows, axis=0).astype(bf16))
         right.append(ones(lax.bitwise_and(at, LEAF - 1) == lower))
     lists = lax.dot_general(
@@ -125,8 +139,6 @@
     rows_end = seg_size // pack * rank
     load_ref[rows_end : rows_end + 16, :] = away.astype(bf16)
 
-    copies[1].wait()
-    copies[2].wait()
     blocks = []
     for group in range(seg_size // pack):
         rows = []
@@ -343,6 +355,7 @@
     cluster_total = seg_size * blk_count
     pack = LEAF // columns
     skel_rows = seg_size // pack * rank
+    other = shifted(mine, "rhs", 1)
     own_list, load = pl.pallas_call(
         functools.partial(list_kernel, seg_size),
         out_shape=[
@@ -374,8 +387,7 @@
         compiler_params=PARAMS,
         cost_estimate=cost(0.7),
     )(points)
-    target_rows, later_charges, later_load = lax.optimization_barrier((target_rows, mine, load))
-    other = shifted(later_charges, "rhs", 1)
+    target_rows, later_load = lax.optimization_barrier((target_rows, load))
     narrow = blk_count == 4 and cluster_total <= 256
     if narrow:
         loads = [load, crossed(later_load, -1), shifted(later_load, "blk", 2), first_load]

time: 27.3 us -> 27.1 us (level)
  waiting for transfers between devices: 3.23 us -> 5.26 us
  starting transfers between devices: 9.24 us -> 7.87 us
  Pallas kernels: 13.6 us -> 12.8 us
    ppermute x3, waiting for transfers between devices: 1.47 us -> 3.96 us  [crossed(): return lax.ppermute(block, ('blk', 'rhs'), pairs)]
    ppermute x3, starting transfers between devices: 7.52 us -> 6.24 us  [crossed(): return lax.ppermute(block, ('blk', 'rhs'), pairs)]
    pallas_call x2, Pallas kernels: 7.47 us -> 6.88 us  [near_sum(): pl.pallas_call(functools.partial(near_kernel, base), out_shape=jax.ShapeD...]
    ppermute x3, waiting for transfers between devices: 1.76 us -> 1.3 us  [shifted(): lax.ppermute(block, axis, [(i, (i + shift) % count) for i in range(count)])]
    pallas_call x1, Pallas kernels: 2.8 us -> 2.52 us  [on_device(): pl.pallas_call(functools.partial(list_kernel, seg_size), out_shape=[jax.S...]
  transfers between devices with their start and end apart: 6 -> 6, of which waited for: 4 -> 3; matrix products, arithmetic and copies ran while one was open for 1% -> 1% of each run, Pallas kernels for 40% -> 47%
where the time goes in v8:
time: 27.1 us; the launch traced here: 27 us
  Pallas kernels  12.8 us (47%)
  starting transfers between devices  7.87 us (29%)
  waiting for transfers between devices  5.26 us (19%)
  other arithmetic  0.78 us (3%)
    pallas_call x2, Pallas kernels, near_sum(): pl.pallas_call(functools.partial(near_kernel, base), out_shape=jax.ShapeD...  6.88 us
    ppermute x3, starting transfers between devices, crossed(): return lax.ppermute(block, ('blk', 'rhs'), pairs)  6.24 us
    ppermute x3, waiting for transfers between devices, crossed(): return lax.ppermute(block, ('blk', 'rhs'), pairs)  3.96 us
    pallas_call x1, Pallas kernels, on_device(): pl.pallas_call(functools.partial(far_kernel_phased, seg_size), out_shape=...  2.65 us
    pallas_call x1, Pallas kernels, on_device(): pl.pallas_call(functools.partial(list_kernel, seg_size), out_shape=[jax.S...  2.52 us
    ppermute x3, starting transfers between devices, shifted(): lax.ppermute(block, axis, [(i, (i + shift) % count) for i in range(count)])  1.63 us
    ppermute x3, waiting for transfers between devices, shifted(): lax.ppermute(block, axis, [(i, (i + shift) % count) for i in range(count)])  1.3 us
    pallas_call x1, Pallas kernels, on_device(): pl.pallas_call(functools.partial(feature_kernel, seg_size, own_clusters),...  0.72 us
  transfers between devices with their start and end apart: 6, of which 3 were waited for; matrix products, arithmetic and copies ran while one was open for 1% of the time, Pallas kernels for 47%

profile of v8, /device:TPU:0, one launch (start us, length us, event | category | flops | bytes accessed | tf_op | source)
XLA Modules:
  0.0 27.0 jit_solution(18057829303186390248)
XLA Ops:
  0.0 0.5 %collective-permute-start.1 = (bf16[32,4096]{1,0:T(8,128)(2,1)}, bf16[32,4096]{1,0:T(8,128)(2,1)S(1)}, u32[]{:S(2)}, u32[]{:S(2)}) collective-permute-start(bf16[32,4096]{1,0:T(8,128)(2,1)} %bitcast.3), channel_id=1, source_target_pairs={{0,1},{1,0},{2,3},{3,2},{4,5},{5,4},{6,7},{7,6},{8,9},{9,8},{10,11... | collective-permute-start | bytes 786440 | tf_op jit(solution)/shard_map/ppermute | solution.py:32
  0.5 2.5 %shard_map.64 = (s32[8,128]{1,0:T(8,128)}, bf16[272,128]{1,0:T(8,128)(2,1)}) custom-call(s32[16,27]{1,0:T(8,128)} %near_hbm.1, bf16[32,4096]{1,0:T(8,128)(2,1)} %basis_ref.1, bf16[32,4096]{1,0:T(8,128)(2,1)} %bitcast.4), custom_call_target="tpu_custom_call" | custom-call | flops 3000000000 | tf_op jit(solution)/shard_map/pallas_call | solution.py:359
  3.1 2.7 %collective-permute-start = (bf16[272,128]{1,0:T(8,128)(2,1)}, bf16[272,128]{1,0:T(8,128)(2,1)S(1)}, u32[]{:S(2)}, u32[]{:S(2)}) collective-permute-start(bf16[272,128]{1,0:T(8,128)(2,1)} %get-tuple-element.32.refs_0_), channel_id=1, source_target_pairs={{0,4},{1,13},{4,8},{5,1},{8,12},{9,5},{12,0},{13,9},{2,6},{3,15},{... | collective-permute-start | bytes 208904 | tf_op jit(solution)/shard_map/ppermute | solution.py:41
  5.7 0.7 %shard_map.65 = (bf16[33,48,128]{2,1,0:T(8,128)(2,1)S(1)}, bf16[32,128,48]{2,1,0:T(8,128)(2,1)S(1)}) custom-call(f32[3,16384]{1,0:T(4,128)S(1)} %copy-done.4), custom_call_target="tpu_custom_call" | custom-call | flops 700000000 | tf_op jit(solution)/shard_map/pallas_call | solution.py:379
  6.5 2.1 %collective-permute-start.2 = (bf16[272,128]{1,0:T(8,128)(2,1)}, bf16[272,128]{1,0:T(8,128)(2,1)S(1)}, u32[]{:S(2)}, u32[]{:S(2)}) collective-permute-start(bf16[272,128]{1,0:T(8,128)(2,1)} %get-tuple-element.32.refs_0_), channel_id=1, source_target_pairs={{0,12},{1,5},{4,0},{5,9},{8,4},{9,13},{12,8},{13,1},{2,14},{3,7},{... | collective-permute-start | bytes 208904 | tf_op jit(solution)/shard_map/ppermute | solution.py:41
  8.6 1.0 %collective-permute-start.3 = (bf16[272,128]{1,0:T(8,128)(2,1)}, bf16[272,128]{1,0:T(8,128)(2,1)S(1)}, u32[]{:S(2)}, u32[]{:S(2)}) collective-permute-start(bf16[272,128]{1,0:T(8,128)(2,1)} %get-tuple-element.32.refs_0_), channel_id=1, source_target_pairs={{0,8},{4,12},{8,0},{12,4},{1,9},{5,13},{9,1},{13,5},{2,10},{6,14},... | collective-permute-start | bytes 208904 | tf_op jit(solution)/shard_map/ppermute | solution.py:32
  9.6 0.1 constant_dynamic-slice_fusion
  9.6 0.1 copy.8
  9.7 1.3 %collective-permute-done.refs_3_ = bf16[272,128]{1,0:T(8,128)(2,1)S(1)} collective-permute-done((bf16[272,128]{1,0:T(8,128)(2,1)}, bf16[272,128]{1,0:T(8,128)(2,1)S(1)}, u32[]{:S(2)}, u32[]{:S(2)}) %collective-permute-start) | collective-permute-done | bytes 69664 | tf_op jit(solution)/shard_map/ppermute | solution.py:41
  11.1 0.0 collective-permute-done.1.other_ref
  11.1 4.6 %shard_map.66 = bf16[64,2048]{1,0:T(8,128)(2,1)S(1)} custom-call(s32[8,128]{1,0:T(8,128)S(1)} %fusion.9.list_ref, bf16[33,48,128]{2,1,0:T(8,128)(2,1)S(1)} %get-tuple-element.26.target_ref, bf16[32,128,48]{2,1,0:T(8,128)(2,1)S(1)} %get-tuple-element.27.source_ref, bf16[32,4096]{1,0:T(8,128)(2,1)S(1)} %bitcast.5, ...), custom_call_target="tpu_custom_call" | custom-call | flops 20000000000 | tf_op jit(solution)/shard_map/pallas_call | solution.py:268
  15.7 0.0 copy-start.1
  15.7 0.0 copy-start.2
  15.7 0.0 copy-start.3
  15.7 1.5 %collective-permute-start.4 = (bf16[64,2048]{1,0:T(8,128)(2,1)S(1)}, bf16[64,2048]{1,0:T(8,128)(2,1)S(1)}, u32[]{:S(2)}, u32[]{:S(2)}) collective-permute-start(bf16[64,2048]{1,0:T(8,128)(2,1)S(1)} %shard_map.66), channel_id=1, source_target_pairs={{0,12},{1,5},{4,0},{5,9},{8,4},{9,13},{12,8},{13,1},{2,14},{3,7},{... | collective-permute-start | bytes 786440 | tf_op jit(solution)/shard_map/ppermute | solution.py:41
  17.2 2.3 %shard_map.67 = f32[64,2048]{1,0:T(8,128)S(1)} custom-call(s32[8,128]{1,0:T(8,128)S(1)} %copy-done.6, bf16[33,48,128]{2,1,0:T(8,128)(2,1)S(1)} %get-tuple-element.26.target_ref, bf16[32,128,48]{2,1,0:T(8,128)(2,1)S(1)} %get-tuple-element.27.source_ref, bf16[32,4096]{1,0:T(8,128)(2,1)S(1)} %bitcast.6, bf16[32,4096]{1,0:T(8,128)(2,1)S(1)} %collective-permute-done.1.other_ref), custom_call_target="tpu_custom_call" | custom-call | flops 20000000000 | tf_op jit(solution)/shard_map/pallas_call | solution.py:268
  19.5 0.0 collective-permute-done.2.refs_1_
  19.5 0.0 collective-permute-done.3.refs_2_
  19.5 0.0 copy-done.1
  19.5 2.6 %shard_map.68 = f32[32,2048]{1,0:T(8,128)S(1)} custom-call(s32[16,32]{1,0:T(8,128)S(1)} %fusion.7.far_ref, bf16[16,32,32,32]{3,2,1,0:T(8,128)(2,1)S(1)} %copy-done.1, bf16[32,4096]{1,0:T(8,128)(2,1)S(1)} %copy-done.2, bf16[272,128]{1,0:T(8,128)(2,1)S(1)} %copy-done.3, bf16[272,128]{1,0:T(8,128)(2,1)S(1)} %collective-permute-done.2.refs_1_, ...), custom_call_target="tpu_custom_call" | custom-call | flops 10000000 | tf_op jit(solution)/shard_map/pallas_call | solution.py:414
  22.2 2.6 %collective-permute-done.4 = bf16[64,2048]{1,0:T(8,128)(2,1)S(1)} collective-permute-done((bf16[64,2048]{1,0:T(8,128)(2,1)S(1)}, bf16[64,2048]{1,0:T(8,128)(2,1)S(1)}, u32[]{:S(2)}, u32[]{:S(2)}) %collective-permute-start.4) | collective-permute-done | bytes 262176 | tf_op jit(solution)/shard_map/ppermute | solution.py:41
  24.9 0.1 collective-permute-start.5
  25.0 1.3 %collective-permute-done.5 = bf16[32,2048]{1,0:T(8,128)(2,1)S(1)} collective-permute-done((bf16[32,2048]{1,0:T(8,128)(2,1)S(1)}, bf16[32,2048]{1,0:T(8,128)(2,1)S(1)}, u32[]{:S(2)}, u32[]{:S(2)}) %collective-permute-start.5) | collective-permute-done | bytes 131104 | tf_op jit(solution)/shard_map/ppermute | solution.py:32
  26.3 0.7 %fusion.2 = bf16[2048,32]{0,1:T(8,128)(2,1)} fusion(f32[32,2048]{1,0:T(8,128)S(1)} %shard_map.68, bf16[32,2048]{1,0:T(8,128)(2,1)S(1)} %collective-permute-done.5, f32[64,2048]{1,0:T(8,128)S(1)} %convert_add_fusion), kind=kLoop, calls=%fused_computation.5 | loop fusion | flops 262144 | bytes 786432 | tf_op jit(solution)/shard_map/transpose | solution.py:440
  (15 shorter events, 0.1 us)
Async XLA Ops:
  0.0 9.6 %copy-start = (s32[128,32]{0,1:T(8,128)S(1)}, s32[128,32]{0,1:T(8,128)}, u32[]{:S(2)}) copy-start(s32[128,32]{0,1:T(8,128)} %param.11) | copy-start | bytes 49156
  0.0 5.7 %copy-start.4 = (f32[3,16384]{1,0:T(4,128)S(1)}, f32[3,16384]{1,0:T(4,128)}, u32[]{:S(2)}) copy-start(f32[3,16384]{1,0:T(4,128)} %points_ref) | copy-start | bytes 589828
  0.0 11.1 %copy-start.5 = (bf16[4096,32]{0,1:T(8,128)(2,1)S(1)}, bf16[4096,32]{0,1:T(8,128)(2,1)}, u32[]{:S(2)}) copy-start(bf16[4096,32]{0,1:T(8,128)(2,1)} %param.7) | copy-start | bytes 786436
  0.0 11.1 %collective-permute-start.1 = (bf16[32,4096]{1,0:T(8,128)(2,1)}, bf16[32,4096]{1,0:T(8,128)(2,1)S(1)}, u32[]{:S(2)}, u32[]{:S(2)}) collective-permute-start(bf16[32,4096]{1,0:T(8,128)(2,1)} %bitcast.3), channel_id=1, source_target_pairs={{0,1},{1,0},{2,3},{3,2},{4,5},{5,4},{6,7},{7,6},{8,9},{9,8},{10,11... | collective-permute-start | bytes 786440 | tf_op jit(solution)/shard_map/ppermute | solution.py:32
  3.1 8.0 %collective-permute-start = (bf16[272,128]{1,0:T(8,128)(2,1)}, bf16[272,128]{1,0:T(8,128)(2,1)S(1)}, u32[]{:S(2)}, u32[]{:S(2)}) collective-permute-start(bf16[272,128]{1,0:T(8,128)(2,1)} %get-tuple-element.32.refs_0_), channel_id=1, source_target_pairs={{0,4},{1,13},{4,8},{5,1},{8,12},{9,5},{12,0},{13,9},{2,6},{3,15},{... | collective-permute-start | bytes 208904 | tf_op jit(solution)/shard_map/ppermute | solution.py:41
  6.5 13.0 %collective-permute-start.2 = (bf16[272,128]{1,0:T(8,128)(2,1)}, bf16[272,128]{1,0:T(8,128)(2,1)S(1)}, u32[]{:S(2)}, u32[]{:S(2)}) collective-permute-start(bf16[272,128]{1,0:T(8,128)(2,1)} %get-tuple-element.32.refs_0_), channel_id=1, source_target_pairs={{0,12},{1,5},{4,0},{5,9},{8,4},{9,13},{12,8},{13,1},{2,14},{3,7},{... | collective-permute-start | bytes 208904 | tf_op jit(solution)/shard_map/ppermute | solution.py:41
  8.6 10.9 %collective-permute-start.3 = (bf16[272,128]{1,0:T(8,128)(2,1)}, bf16[272,128]{1,0:T(8,128)(2,1)S(1)}, u32[]{:S(2)}, u32[]{:S(2)}) collective-permute-start(bf16[272,128]{1,0:T(8,128)(2,1)} %get-tuple-element.32.refs_0_), channel_id=1, source_target_pairs={{0,8},{4,12},{8,0},{12,4},{1,9},{5,13},{9,1},{13,5},{2,10},{6,14},... | collective-permute-start | bytes 208904 | tf_op jit(solution)/shard_map/ppermute | solution.py:32
  11.1 6.1 %copy-start.6 = (s32[8,128]{1,0:T(8,128)S(1)}, s32[8,128]{1,0:T(8,128)}, u32[]{:S(2)}) copy-start(s32[8,128]{1,0:T(8,128)} %get-tuple-element.29.list_ref) | copy-start | bytes 12292
  15.7 3.8 %copy-start.1 = (bf16[16,32,32,32]{3,2,1,0:T(8,128)(2,1)S(1)}, bf16[16,32,32,32]{3,2,1,0:T(8,128)(2,1)}, u32[]{:S(2)}) copy-start(bf16[16,32,32,32]{3,2,1,0:T(8,128)(2,1)} %couplings_ref.1) | copy-start | bytes 3145732
  15.7 3.8 %copy-start.2 = (bf16[32,4096]{1,0:T(8,128)(2,1)S(1)}, bf16[32,4096]{1,0:T(8,128)(2,1)}, u32[]{:S(2)}) copy-start(bf16[32,4096]{1,0:T(8,128)(2,1)} %basis_ref.1) | copy-start | bytes 786436
  15.7 3.8 %copy-start.3 = (bf16[272,128]{1,0:T(8,128)(2,1)S(1)}, bf16[272,128]{1,0:T(8,128)(2,1)}, u32[]{:S(2)}) copy-start(bf16[272,128]{1,0:T(8,128)(2,1)} %get-tuple-element.32.refs_0_) | copy-start | bytes 208900
  15.7 9.1 %collective-permute-start.4 = (bf16[64,2048]{1,0:T(8,128)(2,1)S(1)}, bf16[64,2048]{1,0:T(8,128)(2,1)S(1)}, u32[]{:S(2)}, u32[]{:S(2)}) collective-permute-start(bf16[64,2048]{1,0:T(8,128)(2,1)S(1)} %shard_map.66), channel_id=1, source_target_pairs={{0,12},{1,5},{4,0},{5,9},{8,4},{9,13},{12,8},{13,1},{2,14},{3,7},{... | collective-permute-start | bytes 786440 | tf_op jit(solution)/shard_map/ppermute | solution.py:41
  24.9 1.4 %collective-permute-start.5 = (bf16[32,2048]{1,0:T(8,128)(2,1)S(1)}, bf16[32,2048]{1,0:T(8,128)(2,1)S(1)}, u32[]{:S(2)}, u32[]{:S(2)}) collective-permute-start(bf16[32,2048]{1,0:T(8,128)(2,1)S(1)} %slice.39), channel_id=1, source_target_pairs={{0,1},{1,0},{2,3},{3,2},{4,5},{5,4},{6,7},{7,6},{8,9},{9,8},{10,11... | collective-permute-start | bytes 393224 | tf_op jit(solution)/shard_map/ppermute | solution.py:32

commit v9 on v8

--- a/solution.py
+++ b/solution.py
@@ -103,13 +103,14 @@
     leaving = jnp.where(half == 0, jnp.where(is_next, 1, 0), jnp.where(is_prev, 1, 0))
     masks = (is_own, leaving == 1)
     place = jnp.zeros((lines, LEAF), f32)
-    totals = []
+    totals, middles = [], []
     for mask in masks:
         within = jnp.dot(ones(mask), earlier, preferred_element_type=f32)
         count = jnp.dot(ones(mask), whole, preferred_element_type=f32)
         start = jnp.dot(above, count.astype(bf16), preferred_element_type=f32)
         place = jnp.where(mask, start + within, place)
         totals.append(start[lines - 1 :, :] + count[lines - 1 :, :])
+        middles.append(start[lines // 2 : lines // 2 + 1, :])
     place = place.astype(jnp.int32)
     target = target.astype(f32)
     left, right = [], []
@@ -132,9 +133,12 @@
     last = row * LEAF + iota((8, LEAF), 1) == 8 * LEAF - 1
     own = lists[:8] + 256.0 * lists[8:16]
     own_ref[...] = jnp.where(last, totals[0], own).astype(jnp.int32)
-    high = jnp.floor(totals[1] * (1.0 / 256.0))
+    prior = row * LEAF + iota((8, LEAF), 1) == 8 * LEAF - 2
+    length = jnp.where(prior, middles[1], totals[1])
+    high = jnp.floor(length * (1.0 / 256.0))
+    ends = jnp.logical_or(last, prior)
     away = jnp.concatenate(
-        [jnp.where(last, totals[1] - 256.0 * high, lists[16:24]), jnp.where(last, high, lists[24:32])], axis=0
+        [jnp.where(ends, length - 256.0 * high, lists[16:24]), jnp.where(ends, high, lists[24:32])], axis=0
     )
     rows_end = seg_size // pack * rank
     load_ref[rows_end : rows_end + 16, :] = away.astype(bf16)
@@ -216,17 +220,19 @@
     lax.fori_loop(0, seg_size // 8, some_sources, 0)
 
 
-def near_kernel(base, list_ref, target_ref, source_ref, mine_ref, other_ref, out_ref, total, even, odd):
+def near_kernel(base, part, list_ref, target_ref, source_ref, mine_ref, other_ref, out_ref, total, even, odd):
     targets = total.shape[0] - 1
     blank = target_ref.shape[0] - 1
-    length = list_ref[7, LEAF - 1]
-    batches = lax.div(length + (BATCH - 1), BATCH)
+    skipped = targets if part == 1 else 0
+    begin = list_ref[7, LEAF - 2] if part == 1 else 0
+    end = list_ref[7, LEAF - 2] if part == 0 else list_ref[7, LEAF - 1]
+    batches = lax.div(end - begin + (BATCH - 1), BATCH)
     total[...] = jnp.zeros_like(total)
 
     def pair(batch, u):
-        at = batch * BATCH + u
+        at = begin + batch * BATCH + u
         code = list_ref[lax.shift_right_logical(at, 7), lax.bitwise_and(at, 127)]
-        code = jnp.where(at < length, code, targets * 256)
+        code = jnp.where(at < end, code, (skipped + targets) * 256)
         return lax.shift_right_logical(code, 8), lax.bitwise_and(code, 255)
 
     def make(batch, slot):
@@ -242,7 +248,7 @@
             charges = jnp.concatenate([mine_ref[:, cluster(source)], other_ref[:, cluster(source)]], axis=0)
             sums.append((target, jnp.dot(charges, slot[u], preferred_element_type=f32)))
         for target, value in sums:
-            total[target] += value
+            total[target - skipped] += value
 
     make(0, even)
 
@@ -263,10 +269,10 @@
         out_ref[:, i * LEAF : (i + 1) * LEAF] = total[i].astype(out_ref.dtype)
 
 
-def near_sum(base, targets, pairs, target_rows, source_rows, mine, other, dtype):
+def near_sum(base, part, microseconds, targets, pairs, target_rows, source_rows, mine, other, dtype):
     columns = 2 * mine.shape[0]
     return pl.pallas_call(
-        functools.partial(near_kernel, base),
+        functools.partial(near_kernel, base, part),
         out_shape=jax.ShapeDtypeStruct((columns, targets * LEAF), dtype),
         in_specs=[SMEM] + [VMEM] * 4,
         out_specs=VMEM,
@@ -276,7 +282,7 @@
             pltpu.VMEM((BATCH, LEAF, LEAF), bf16),
         ],
         compiler_params=PARAMS,
-        cost_estimate=cost(20.0),
+        cost_estimate=cost(microseconds),
     )(pairs, target_rows, source_rows, mine, other)
 
 
@@ -396,10 +402,14 @@
     args = (target_rows, source_rows, mine, other)
     codes = first_load[skel_rows:].astype(jnp.int32)
     pairs = codes[:8] + 256 * codes[8:]
-    partial = near_sum(0, own_clusters, pairs, *args, bf16)
-    partial, own_list = lax.optimization_barrier((partial, own_list))
-    returned = crossed(partial, -1)
-    own_near = near_sum(own_clusters, own_clusters, own_list, *args, f32)
+    low = near_sum(0, 0, 20.0, own_clusters // 2, pairs, *args, bf16)
+    low, pairs = lax.optimization_barrier((low, pairs))
+    low_back = crossed(low, -1)
+    high = near_sum(0, 1, 20.0, own_clusters // 2, pairs, *args, bf16)
+    high, own_list = lax.optimization_barrier((high, own_list))
+    high_back = crossed(high, -1)
+    low_back, high, own_list = lax.optimization_barrier((low_back, high, own_list))
+    own_near = near_sum(own_clusters, None, 20.0, own_clusters, own_list, *args, f32)
     own_near, loads = lax.optimization_barrier((own_near, loads))
 
     blk = lax.axis_index("blk")
@@ -434,8 +444,8 @@
             compiler_params=PARAMS,
         )(entries, couplings, basis, *loads)
 
-    far, returned = lax.optimization_barrier((far, returned))
-    near = own_near + returned.astype(f32)
+    far, low_back, high_back = lax.optimization_barrier((far, low_back, high_back))
+    near = own_near + jnp.concatenate([low_back, high_back], axis=1).astype(f32)
     got = shifted(near[columns:].astype(bf16), "rhs", 1)
     return (near[:columns] + got.astype(f32) + far).astype(bf16).T
 

time: 27.1 us -> 28.1 us (1.037)
  waiting for transfers between devices: 5.26 us -> 3.71 us
  Pallas kernels: 12.8 us -> 14.2 us
  starting transfers between devices: 7.87 us -> 8.82 us
    ppermute x3 -> x4, waiting for transfers between devices: 3.96 us -> 2.37 us  [crossed(): return lax.ppermute(block, ('blk', 'rhs'), pairs)]
    pallas_call x2 -> x3, Pallas kernels: 6.88 us -> 8.36 us  [near_sum(): pl.pallas_call(functools.partial(near_kernel, base, part), out_shape=jax....]
    ppermute x3 -> x4, starting transfers between devices: 6.24 us -> 7.24 us  [crossed(): return lax.ppermute(block, ('blk', 'rhs'), pairs)]
  transfers between devices with their start and end apart: 6 -> 7, of which waited for: 3 -> 3; matrix products, arithmetic and copies ran while one was open for 1% -> 1% of each run, Pallas kernels for 47% -> 51%
where the time goes in v9:
time: 28.1 us; the launch traced here: 27.9 us
  Pallas kernels  14.2 us (51%)
  starting transfers between devices  8.82 us (31%)
  waiting for transfers between devices  3.71 us (13%)
  other arithmetic  0.79 us (3%)
    pallas_call x3, Pallas kernels, near_sum(): pl.pallas_call(functools.partial(near_kernel, base, part), out_shape=jax....  8.36 us
    ppermute x4, starting transfers between devices, crossed(): return lax.ppermute(block, ('blk', 'rhs'), pairs)  7.24 us
    pallas_call x1, Pallas kernels, on_device(): pl.pallas_call(functools.partial(far_kernel_phased, seg_size), out_shape=...  2.63 us
    pallas_call x1, Pallas kernels, on_device(): pl.pallas_call(functools.partial(list_kernel, seg_size), out_shape=[jax.S...  2.52 us
    ppermute x4, waiting for transfers between devices, crossed(): return lax.ppermute(block, ('blk', 'rhs'), pairs)  2.37 us
    ppermute x3, starting transfers between devices, shifted(): lax.ppermute(block, axis, [(i, (i + shift) % count) for i in range(count)])  1.57 us
    ppermute x3, waiting for transfers between devices, shifted(): lax.ppermute(block, axis, [(i, (i + shift) % count) for i in range(count)])  1.34 us
    pallas_call x1, Pallas kernels, on_device(): pl.pallas_call(functools.partial(feature_kernel, seg_size, own_clusters),...  0.72 us
  transfers between devices with their start and end apart: 7, of which 3 were waited for; matrix products, arithmetic and copies ran while one was open for 1% of the time, Pallas kernels for 51%

profile of v9, /device:TPU:0, one launch (start us, length us, event | category | flops | bytes accessed | tf_op | source)
XLA Modules:
  0.0 27.9 jit_solution(4401196794606664307)
XLA Ops:
  0.0 0.5 %collective-permute-start.1 = (bf16[32,4096]{1,0:T(8,128)(2,1)}, bf16[32,4096]{1,0:T(8,128)(2,1)S(1)}, u32[]{:S(2)}, u32[]{:S(2)}) collective-permute-start(bf16[32,4096]{1,0:T(8,128)(2,1)} %bitcast.3), channel_id=1, source_target_pairs={{0,1},{1,0},{2,3},{3,2},{4,5},{5,4},{6,7},{7,6},{8,9},{9,8},{10,11... | collective-permute-start | bytes 786440 | tf_op jit(solution)/shard_map/ppermute | solution.py:32
  0.5 2.5 %shard_map.64 = (s32[8,128]{1,0:T(8,128)}, bf16[272,128]{1,0:T(8,128)(2,1)}) custom-call(s32[16,27]{1,0:T(8,128)} %near_hbm.1, bf16[32,4096]{1,0:T(8,128)(2,1)} %basis_ref.1, bf16[32,4096]{1,0:T(8,128)(2,1)} %bitcast.4), custom_call_target="tpu_custom_call" | custom-call | flops 3000000000 | tf_op jit(solution)/shard_map/pallas_call | solution.py:365
  3.1 2.7 %collective-permute-start = (bf16[272,128]{1,0:T(8,128)(2,1)}, bf16[272,128]{1,0:T(8,128)(2,1)S(1)}, u32[]{:S(2)}, u32[]{:S(2)}) collective-permute-start(bf16[272,128]{1,0:T(8,128)(2,1)} %get-tuple-element.41.refs_0_), channel_id=1, source_target_pairs={{0,4},{1,13},{4,8},{5,1},{8,12},{9,5},{12,0},{13,9},{2,6},{3,15},{... | collective-permute-start | bytes 208904 | tf_op jit(solution)/shard_map/ppermute | solution.py:41
  5.7 0.7 %shard_map.65 = (bf16[33,48,128]{2,1,0:T(8,128)(2,1)S(1)}, bf16[32,128,48]{2,1,0:T(8,128)(2,1)S(1)}) custom-call(f32[3,16384]{1,0:T(4,128)S(1)} %copy-done.4), custom_call_target="tpu_custom_call" | custom-call | flops 700000000 | tf_op jit(solution)/shard_map/pallas_call | solution.py:385
  6.5 2.1 %collective-permute-start.3 = (bf16[272,128]{1,0:T(8,128)(2,1)}, bf16[272,128]{1,0:T(8,128)(2,1)S(1)}, u32[]{:S(2)}, u32[]{:S(2)}) collective-permute-start(bf16[272,128]{1,0:T(8,128)(2,1)} %get-tuple-element.41.refs_0_), channel_id=1, source_target_pairs={{0,12},{1,5},{4,0},{5,9},{8,4},{9,13},{12,8},{13,1},{2,14},{3,7},{... | collective-permute-start | bytes 208904 | tf_op jit(solution)/shard_map/ppermute | solution.py:41
  8.6 1.0 %collective-permute-start.4 = (bf16[272,128]{1,0:T(8,128)(2,1)}, bf16[272,128]{1,0:T(8,128)(2,1)S(1)}, u32[]{:S(2)}, u32[]{:S(2)}) collective-permute-start(bf16[272,128]{1,0:T(8,128)(2,1)} %get-tuple-element.41.refs_0_), channel_id=1, source_target_pairs={{0,8},{4,12},{8,0},{12,4},{1,9},{5,13},{9,1},{13,5},{2,10},{6,14},... | collective-permute-start | bytes 208904 | tf_op jit(solution)/shard_map/ppermute | solution.py:32
  9.6 0.1 constant_dynamic-slice_fusion
  9.6 0.1 copy.8
  9.7 1.3 %collective-permute-done.refs_3_ = bf16[272,128]{1,0:T(8,128)(2,1)S(1)} collective-permute-done((bf16[272,128]{1,0:T(8,128)(2,1)}, bf16[272,128]{1,0:T(8,128)(2,1)S(1)}, u32[]{:S(2)}, u32[]{:S(2)}) %collective-permute-start) | collective-permute-done | bytes 69664 | tf_op jit(solution)/shard_map/ppermute | solution.py:41
  11.1 0.0 collective-permute-done.1.other_ref
  11.1 2.6 %shard_map.66 = bf16[64,1024]{1,0:T(8,128)(2,1)S(1)} custom-call(s32[8,128]{1,0:T(8,128)S(1)} %fusion.9.list_ref, bf16[33,48,128]{2,1,0:T(8,128)(2,1)S(1)} %get-tuple-element.31.target_ref, bf16[32,128,48]{2,1,0:T(8,128)(2,1)S(1)} %get-tuple-element.32.source_ref, bf16[32,4096]{1,0:T(8,128)(2,1)S(1)} %bitcast.5, ...), custom_call_target="tpu_custom_call" | custom-call | flops 20000000000 | tf_op jit(solution)/shard_map/pallas_call | solution.py:274
  13.7 1.9 %collective-permute-start.2 = (bf16[64,1024]{1,0:T(8,128)(2,1)S(1)}, bf16[64,1024]{1,0:T(8,128)(2,1)S(1)}, u32[]{:S(2)}, u32[]{:S(2)}) collective-permute-start(bf16[64,1024]{1,0:T(8,128)(2,1)S(1)} %shard_map.66), channel_id=1, source_target_pairs={{0,12},{1,5},{4,0},{5,9},{8,4},{9,13},{12,8},{13,1},{2,14},{3,7},{... | collective-permute-start | bytes 393224 | tf_op jit(solution)/shard_map/ppermute | solution.py:41
  15.6 2.9 %shard_map.67 = bf16[64,1024]{1,0:T(8,128)(2,1)S(1)} custom-call(s32[8,128]{1,0:T(8,128)S(1)} %fusion.9.list_ref, bf16[33,48,128]{2,1,0:T(8,128)(2,1)S(1)} %get-tuple-element.31.target_ref, bf16[32,128,48]{2,1,0:T(8,128)(2,1)S(1)} %get-tuple-element.32.source_ref, bf16[32,4096]{1,0:T(8,128)(2,1)S(1)} %bitcast.6, ...), custom_call_target="tpu_custom_call" | custom-call | flops 20000000000 | tf_op jit(solution)/shard_map/pallas_call | solution.py:274
  18.5 0.0 copy-start.1
  18.5 0.0 copy-start.2
  18.5 0.0 copy-start.3
  18.5 0.5 %collective-permute-start.5 = (bf16[64,1024]{1,0:T(8,128)(2,1)S(1)}, bf16[64,1024]{1,0:T(8,128)(2,1)S(1)}, u32[]{:S(2)}, u32[]{:S(2)}) collective-permute-start(bf16[64,1024]{1,0:T(8,128)(2,1)S(1)} %shard_map.67), channel_id=1, source_target_pairs={{0,12},{1,5},{4,0},{5,9},{8,4},{9,13},{12,8},{13,1},{2,14},{3,7},{... | collective-permute-start | bytes 393224 | tf_op jit(solution)/shard_map/ppermute | solution.py:41
  19.1 1.1 %collective-permute-done.2 = bf16[64,1024]{1,0:T(8,128)(2,1)S(1)} collective-permute-done((bf16[64,1024]{1,0:T(8,128)(2,1)S(1)}, bf16[64,1024]{1,0:T(8,128)(2,1)S(1)}, u32[]{:S(2)}, u32[]{:S(2)}) %collective-permute-start.2) | collective-permute-done | bytes 131104 | tf_op jit(solution)/shard_map/ppermute | solution.py:41
  20.1 2.9 %shard_map.68 = f32[64,2048]{1,0:T(8,128)S(1)} custom-call(s32[8,128]{1,0:T(8,128)S(1)} %copy-done.6, bf16[33,48,128]{2,1,0:T(8,128)(2,1)S(1)} %get-tuple-element.31.target_ref, bf16[32,128,48]{2,1,0:T(8,128)(2,1)S(1)} %get-tuple-element.32.source_ref, bf16[32,4096]{1,0:T(8,128)(2,1)S(1)} %bitcast.7, bf16[32,4096]{1,0:T(8,128)(2,1)S(1)} %collective-permute-done.1.other_ref), custom_call_target="tpu_custom_call" | custom-call | flops 20000000000 | tf_op jit(solution)/shard_map/pallas_call | solution.py:274
  23.0 0.0 collective-permute-done.3.refs_1_
  23.1 2.6 %shard_map.69 = f32[32,2048]{1,0:T(8,128)S(1)} custom-call(s32[16,32]{1,0:T(8,128)S(1)} %fusion.7.far_ref, bf16[16,32,32,32]{3,2,1,0:T(8,128)(2,1)S(1)} %copy-done.1, bf16[32,4096]{1,0:T(8,128)(2,1)S(1)} %copy-done.2, bf16[272,128]{1,0:T(8,128)(2,1)S(1)} %copy-done.3, bf16[272,128]{1,0:T(8,128)(2,1)S(1)} %collective-permute-done.3.refs_1_, ...), custom_call_target="tpu_custom_call" | custom-call | flops 10000000 | tf_op jit(solution)/shard_map/pallas_call | solution.py:424
  25.8 0.1 collective-permute-start.6
  25.9 1.3 %collective-permute-done.6 = bf16[32,2048]{1,0:T(8,128)(2,1)S(1)} collective-permute-done((bf16[32,2048]{1,0:T(8,128)(2,1)S(1)}, bf16[32,2048]{1,0:T(8,128)(2,1)S(1)}, u32[]{:S(2)}, u32[]{:S(2)}) %collective-permute-start.6) | collective-permute-done | bytes 131104 | tf_op jit(solution)/shard_map/ppermute | solution.py:32
  27.2 0.7 %fusion.2 = bf16[2048,32]{0,1:T(8,128)(2,1)} fusion(f32[32,2048]{1,0:T(8,128)S(1)} %shard_map.69, bf16[32,2048]{1,0:T(8,128)(2,1)S(1)} %collective-permute-done.6, f32[64,2048]{1,0:T(8,128)S(1)} %convert_add_fusion), kind=kLoop, calls=%fused_computation.5 | loop fusion | flops 262144 | bytes 786432 | tf_op jit(solution)/shard_map/transpose | solution.py:450
  (18 shorter events, 0.1 us)
Async XLA Ops:
  0.0 9.6 %copy-start = (s32[128,32]{0,1:T(8,128)S(1)}, s32[128,32]{0,1:T(8,128)}, u32[]{:S(2)}) copy-start(s32[128,32]{0,1:T(8,128)} %param.11) | copy-start | bytes 49156
  0.0 5.7 %copy-start.4 = (f32[3,16384]{1,0:T(4,128)S(1)}, f32[3,16384]{1,0:T(4,128)}, u32[]{:S(2)}) copy-start(f32[3,16384]{1,0:T(4,128)} %points_ref) | copy-start | bytes 589828
  0.0 11.1 %copy-start.5 = (bf16[4096,32]{0,1:T(8,128)(2,1)S(1)}, bf16[4096,32]{0,1:T(8,128)(2,1)}, u32[]{:S(2)}) copy-start(bf16[4096,32]{0,1:T(8,128)(2,1)} %param.7) | copy-start | bytes 786436
  0.0 11.1 %collective-permute-start.1 = (bf16[32,4096]{1,0:T(8,128)(2,1)}, bf16[32,4096]{1,0:T(8,128)(2,1)S(1)}, u32[]{:S(2)}, u32[]{:S(2)}) collective-permute-start(bf16[32,4096]{1,0:T(8,128)(2,1)} %bitcast.3), channel_id=1, source_target_pairs={{0,1},{1,0},{2,3},{3,2},{4,5},{5,4},{6,7},{7,6},{8,9},{9,8},{10,11... | collective-permute-start | bytes 786440 | tf_op jit(solution)/shard_map/ppermute | solution.py:32
  3.1 8.0 %collective-permute-start = (bf16[272,128]{1,0:T(8,128)(2,1)}, bf16[272,128]{1,0:T(8,128)(2,1)S(1)}, u32[]{:S(2)}, u32[]{:S(2)}) collective-permute-start(bf16[272,128]{1,0:T(8,128)(2,1)} %get-tuple-element.41.refs_0_), channel_id=1, source_target_pairs={{0,4},{1,13},{4,8},{5,1},{8,12},{9,5},{12,0},{13,9},{2,6},{3,15},{... | collective-permute-start | bytes 208904 | tf_op jit(solution)/shard_map/ppermute | solution.py:41
  6.5 16.5 %collective-permute-start.3 = (bf16[272,128]{1,0:T(8,128)(2,1)}, bf16[272,128]{1,0:T(8,128)(2,1)S(1)}, u32[]{:S(2)}, u32[]{:S(2)}) collective-permute-start(bf16[272,128]{1,0:T(8,128)(2,1)} %get-tuple-element.41.refs_0_), channel_id=1, source_target_pairs={{0,12},{1,5},{4,0},{5,9},{8,4},{9,13},{12,8},{13,1},{2,14},{3,7},{... | collective-permute-start | bytes 208904 | tf_op jit(solution)/shard_map/ppermute | solution.py:41
  8.6 14.4 %collective-permute-start.4 = (bf16[272,128]{1,0:T(8,128)(2,1)}, bf16[272,128]{1,0:T(8,128)(2,1)S(1)}, u32[]{:S(2)}, u32[]{:S(2)}) collective-permute-start(bf16[272,128]{1,0:T(8,128)(2,1)} %get-tuple-element.41.refs_0_), channel_id=1, source_target_pairs={{0,8},{4,12},{8,0},{12,4},{1,9},{5,13},{9,1},{13,5},{2,10},{6,14},... | collective-permute-start | bytes 208904 | tf_op jit(solution)/shard_map/ppermute | solution.py:32
  13.7 6.4 %copy-start.6 = (s32[8,128]{1,0:T(8,128)S(1)}, s32[8,128]{1,0:T(8,128)}, u32[]{:S(2)}) copy-start(s32[8,128]{1,0:T(8,128)} %get-tuple-element.38.list_ref) | copy-start | bytes 12292
  13.7 6.4 %collective-permute-start.2 = (bf16[64,1024]{1,0:T(8,128)(2,1)S(1)}, bf16[64,1024]{1,0:T(8,128)(2,1)S(1)}, u32[]{:S(2)}, u32[]{:S(2)}) collective-permute-start(bf16[64,1024]{1,0:T(8,128)(2,1)S(1)} %shard_map.66), channel_id=1, source_target_pairs={{0,12},{1,5},{4,0},{5,9},{8,4},{9,13},{12,8},{13,1},{2,14},{3,7},{... | collective-permute-start | bytes 393224 | tf_op jit(solution)/shard_map/ppermute | solution.py:41
  18.5 4.5 %copy-start.1 = (bf16[16,32,32,32]{3,2,1,0:T(8,128)(2,1)S(1)}, bf16[16,32,32,32]{3,2,1,0:T(8,128)(2,1)}, u32[]{:S(2)}) copy-start(bf16[16,32,32,32]{3,2,1,0:T(8,128)(2,1)} %couplings_ref.1) | copy-start | bytes 3145732
  18.5 4.5 %copy-start.2 = (bf16[32,4096]{1,0:T(8,128)(2,1)S(1)}, bf16[32,4096]{1,0:T(8,128)(2,1)}, u32[]{:S(2)}) copy-start(bf16[32,4096]{1,0:T(8,128)(2,1)} %basis_ref.1) | copy-start | bytes 786436
  18.5 4.5 %copy-start.3 = (bf16[272,128]{1,0:T(8,128)(2,1)S(1)}, bf16[272,128]{1,0:T(8,128)(2,1)}, u32[]{:S(2)}) copy-start(bf16[272,128]{1,0:T(8,128)(2,1)} %get-tuple-element.41.refs_0_) | copy-start | bytes 208900
  18.5 7.2 %collective-permute-start.5 = (bf16[64,1024]{1,0:T(8,128)(2,1)S(1)}, bf16[64,1024]{1,0:T(8,128)(2,1)S(1)}, u32[]{:S(2)}, u32[]{:S(2)}) collective-permute-start(bf16[64,1024]{1,0:T(8,128)(2,1)S(1)} %shard_map.67), channel_id=1, source_target_pairs={{0,12},{1,5},{4,0},{5,9},{8,4},{9,13},{12,8},{13,1},{2,14},{3,7},{... | collective-permute-start | bytes 393224 | tf_op jit(solution)/shard_map/ppermute | solution.py:41
  25.8 1.4 %collective-permute-start.6 = (bf16[32,2048]{1,0:T(8,128)(2,1)S(1)}, bf16[32,2048]{1,0:T(8,128)(2,1)S(1)}, u32[]{:S(2)}, u32[]{:S(2)}) collective-permute-start(bf16[32,2048]{1,0:T(8,128)(2,1)S(1)} %slice.39), channel_id=1, source_target_pairs={{0,1},{1,0},{2,3},{3,2},{4,5},{5,4},{6,7},{7,6},{8,9},{9,8},{10,11... | collective-permute-start | bytes 393224 | tf_op jit(solution)/shard_map/ppermute | solution.py:32

commit v10 on v9

--- a/solution.py
+++ b/solution.py
@@ -408,9 +408,8 @@
     high = near_sum(0, 1, 20.0, own_clusters // 2, pairs, *args, bf16)
     high, own_list = lax.optimization_barrier((high, own_list))
     high_back = crossed(high, -1)
-    low_back, high, own_list = lax.optimization_barrier((low_back, high, own_list))
-    own_near = near_sum(own_clusters, None, 20.0, own_clusters, own_list, *args, f32)
-    own_near, loads = lax.optimization_barrier((own_near, loads))
+    own_near = near_sum(own_clusters, None, 0.5, own_clusters, own_list, *args, f32)
+    own_near, loads, low_back = lax.optimization_barrier((own_near, loads, low_back))
 
     blk = lax.axis_index("blk")
     first = blk * seg_size + lax.axis_index("leaf") * own_clusters
@@ -432,7 +431,7 @@
                 pltpu.VMEM((own_clusters, rank, columns), bf16),
             ],
             compiler_params=PARAMS,
-            cost_estimate=cost(0.01),
+            cost_estimate=cost(20.0),
         )(entries, couplings, basis, *loads)
     else:
         far = pl.pallas_call(

time: 28.1 us -> 26.9 us (0.957)
  waiting for transfers between devices: 3.71 us -> 2.66 us
  Pallas kernels: 14.2 us -> 13.6 us
  starting transfers between devices: 8.82 us -> 9.19 us
    ppermute x4, waiting for transfers between devices: 2.37 us -> 1.32 us  [crossed(): return lax.ppermute(block, ('blk', 'rhs'), pairs)]
    pallas_call x3, Pallas kernels: 8.36 us -> 7.73 us  [near_sum(): pl.pallas_call(functools.partial(near_kernel, base, part), out_shape=jax....]
    ppermute x4, starting transfers between devices: 7.24 us -> 7.62 us  [crossed(): return lax.ppermute(block, ('blk', 'rhs'), pairs)]
  transfers between devices with their start and end apart: 7 -> 7, of which waited for: 3 -> 2; matrix products, arithmetic and copies ran while one was open for 1% -> 1% of each run, Pallas kernels for 51% -> 51%
where the time goes in v10:
time: 26.9 us; the launch traced here: 26.6 us
  Pallas kernels  13.6 us (51%)
  starting transfers between devices  9.19 us (34%)
  waiting for transfers between devices  2.66 us (10%)
  other arithmetic  0.77 us (3%)
    pallas_call x3, Pallas kernels, near_sum(): pl.pallas_call(functools.partial(near_kernel, base, part), out_shape=jax....  7.73 us
    ppermute x4, starting transfers between devices, crossed(): return lax.ppermute(block, ('blk', 'rhs'), pairs)  7.62 us
    pallas_call x1, Pallas kernels, on_device(): pl.pallas_call(functools.partial(far_kernel_phased, seg_size), out_shape=...  2.65 us
    pallas_call x1, Pallas kernels, on_device(): pl.pallas_call(functools.partial(list_kernel, seg_size), out_shape=[jax.S...  2.52 us
    ppermute x3, starting transfers between devices, shifted(): lax.ppermute(block, axis, [(i, (i + shift) % count) for i in range(count)])  1.57 us
    ppermute x3, waiting for transfers between devices, shifted(): lax.ppermute(block, axis, [(i, (i + shift) % count) for i in range(count)])  1.34 us
    ppermute x4, waiting for transfers between devices, crossed(): return lax.ppermute(block, ('blk', 'rhs'), pairs)  1.32 us
    pallas_call x1, Pallas kernels, on_device(): pl.pallas_call(functools.partial(feature_kernel, seg_size, own_clusters),...  0.72 us
  transfers between devices with their start and end apart: 7, of which 2 were waited for; matrix products, arithmetic and copies ran while one was open for 1% of the time, Pallas kernels for 51%

profile of v10, /device:TPU:0, one launch (start us, length us, event | category | flops | bytes accessed | tf_op | source)
XLA Modules:
  0.0 26.6 jit_solution(6441858593232753265)
XLA Ops:
  0.0 0.5 %collective-permute-start.1 = (bf16[32,4096]{1,0:T(8,128)(2,1)}, bf16[32,4096]{1,0:T(8,128)(2,1)S(1)}, u32[]{:S(2)}, u32[]{:S(2)}) collective-permute-start(bf16[32,4096]{1,0:T(8,128)(2,1)} %bitcast.3), channel_id=1, source_target_pairs={{0,1},{1,0},{2,3},{3,2},{4,5},{5,4},{6,7},{7,6},{8,9},{9,8},{10,11... | collective-permute-start | bytes 786440 | tf_op jit(solution)/shard_map/ppermute | solution.py:32
  0.5 2.5 %shard_map.64 = (s32[8,128]{1,0:T(8,128)}, bf16[272,128]{1,0:T(8,128)(2,1)}) custom-call(s32[16,27]{1,0:T(8,128)} %near_hbm.1, bf16[32,4096]{1,0:T(8,128)(2,1)} %basis_ref.1, bf16[32,4096]{1,0:T(8,128)(2,1)} %bitcast.4), custom_call_target="tpu_custom_call" | custom-call | flops 3000000000 | tf_op jit(solution)/shard_map/pallas_call | solution.py:365
  3.1 2.7 %collective-permute-start = (bf16[272,128]{1,0:T(8,128)(2,1)}, bf16[272,128]{1,0:T(8,128)(2,1)S(1)}, u32[]{:S(2)}, u32[]{:S(2)}) collective-permute-start(bf16[272,128]{1,0:T(8,128)(2,1)} %get-tuple-element.38.refs_0_), channel_id=1, source_target_pairs={{0,4},{1,13},{4,8},{5,1},{8,12},{9,5},{12,0},{13,9},{2,6},{3,15},{... | collective-permute-start | bytes 208904 | tf_op jit(solution)/shard_map/ppermute | solution.py:41
  5.7 0.7 %shard_map.65 = (bf16[33,48,128]{2,1,0:T(8,128)(2,1)S(1)}, bf16[32,128,48]{2,1,0:T(8,128)(2,1)S(1)}) custom-call(f32[3,16384]{1,0:T(4,128)S(1)} %copy-done.4), custom_call_target="tpu_custom_call" | custom-call | flops 700000000 | tf_op jit(solution)/shard_map/pallas_call | solution.py:385
  6.5 2.1 %collective-permute-start.2 = (bf16[272,128]{1,0:T(8,128)(2,1)}, bf16[272,128]{1,0:T(8,128)(2,1)S(1)}, u32[]{:S(2)}, u32[]{:S(2)}) collective-permute-start(bf16[272,128]{1,0:T(8,128)(2,1)} %get-tuple-element.38.refs_0_), channel_id=1, source_target_pairs={{0,12},{1,5},{4,0},{5,9},{8,4},{9,13},{12,8},{13,1},{2,14},{3,7},{... | collective-permute-start | bytes 208904 | tf_op jit(solution)/shard_map/ppermute | solution.py:41
  8.6 1.0 %collective-permute-start.3 = (bf16[272,128]{1,0:T(8,128)(2,1)}, bf16[272,128]{1,0:T(8,128)(2,1)S(1)}, u32[]{:S(2)}, u32[]{:S(2)}) collective-permute-start(bf16[272,128]{1,0:T(8,128)(2,1)} %get-tuple-element.38.refs_0_), channel_id=1, source_target_pairs={{0,8},{4,12},{8,0},{12,4},{1,9},{5,13},{9,1},{13,5},{2,10},{6,14},... | collective-permute-start | bytes 208904 | tf_op jit(solution)/shard_map/ppermute | solution.py:32
  9.6 0.1 constant_dynamic-slice_fusion
  9.6 0.1 copy.8
  9.7 1.3 %collective-permute-done.refs_3_ = bf16[272,128]{1,0:T(8,128)(2,1)S(1)} collective-permute-done((bf16[272,128]{1,0:T(8,128)(2,1)}, bf16[272,128]{1,0:T(8,128)(2,1)S(1)}, u32[]{:S(2)}, u32[]{:S(2)}) %collective-permute-start) | collective-permute-done | bytes 69664 | tf_op jit(solution)/shard_map/ppermute | solution.py:41
  11.1 0.0 collective-permute-done.1.other_ref
  11.1 2.8 %shard_map.66 = bf16[64,1024]{1,0:T(8,128)(2,1)S(1)} custom-call(s32[8,128]{1,0:T(8,128)S(1)} %fusion.9.list_ref, bf16[33,48,128]{2,1,0:T(8,128)(2,1)S(1)} %get-tuple-element.30.target_ref, bf16[32,128,48]{2,1,0:T(8,128)(2,1)S(1)} %get-tuple-element.31.source_ref, bf16[32,4096]{1,0:T(8,128)(2,1)S(1)} %bitcast.5, ...), custom_call_target="tpu_custom_call" | custom-call | flops 20000000000 | tf_op jit(solution)/shard_map/pallas_call | solution.py:274
  13.9 0.0 copy-start.3
  13.9 0.0 copy-start.5
  13.9 0.0 copy-start.6
  14.0 1.5 %collective-permute-start.4 = (bf16[64,1024]{1,0:T(8,128)(2,1)S(1)}, bf16[64,1024]{1,0:T(8,128)(2,1)S(1)}, u32[]{:S(2)}, u32[]{:S(2)}) collective-permute-start(bf16[64,1024]{1,0:T(8,128)(2,1)S(1)} %shard_map.66), channel_id=1, source_target_pairs={{0,12},{1,5},{4,0},{5,9},{8,4},{9,13},{12,8},{13,1},{2,14},{3,7},{... | collective-permute-start | bytes 393224 | tf_op jit(solution)/shard_map/ppermute | solution.py:41
  15.4 2.3 %shard_map.67 = bf16[64,1024]{1,0:T(8,128)(2,1)S(1)} custom-call(s32[8,128]{1,0:T(8,128)S(1)} %fusion.9.list_ref, bf16[33,48,128]{2,1,0:T(8,128)(2,1)S(1)} %get-tuple-element.30.target_ref, bf16[32,128,48]{2,1,0:T(8,128)(2,1)S(1)} %get-tuple-element.31.source_ref, bf16[32,4096]{1,0:T(8,128)(2,1)S(1)} %bitcast.6, ...), custom_call_target="tpu_custom_call" | custom-call | flops 20000000000 | tf_op jit(solution)/shard_map/pallas_call | solution.py:274
  17.7 1.4 %collective-permute-start.5 = (bf16[64,1024]{1,0:T(8,128)(2,1)S(1)}, bf16[64,1024]{1,0:T(8,128)(2,1)S(1)}, u32[]{:S(2)}, u32[]{:S(2)}) collective-permute-start(bf16[64,1024]{1,0:T(8,128)(2,1)S(1)} %shard_map.67), channel_id=1, source_target_pairs={{0,12},{1,5},{4,0},{5,9},{8,4},{9,13},{12,8},{13,1},{2,14},{3,7},{... | collective-permute-start | bytes 393224 | tf_op jit(solution)/shard_map/ppermute | solution.py:41
  19.1 2.6 %shard_map.68 = f32[64,2048]{1,0:T(8,128)S(1)} custom-call(s32[8,128]{1,0:T(8,128)S(1)} %copy-done.2, bf16[33,48,128]{2,1,0:T(8,128)(2,1)S(1)} %get-tuple-element.30.target_ref, bf16[32,128,48]{2,1,0:T(8,128)(2,1)S(1)} %get-tuple-element.31.source_ref, bf16[32,4096]{1,0:T(8,128)(2,1)S(1)} %bitcast.7, bf16[32,4096]{1,0:T(8,128)(2,1)S(1)} %collective-permute-done.1.other_ref), custom_call_target="tpu_custom_call" | custom-call | flops 500000000 | tf_op jit(solution)/shard_map/pallas_call | solution.py:274
  21.7 0.0 collective-permute-done.3.refs_2_
  21.7 0.0 collective-permute-done.4
  21.8 2.6 %shard_map.69 = f32[32,2048]{1,0:T(8,128)S(1)} custom-call(s32[16,32]{1,0:T(8,128)S(1)} %fusion.7.far_ref, bf16[16,32,32,32]{3,2,1,0:T(8,128)(2,1)S(1)} %copy-done.3, bf16[32,4096]{1,0:T(8,128)(2,1)S(1)} %copy-done.5, bf16[272,128]{1,0:T(8,128)(2,1)S(1)} %copy-done.6, bf16[272,128]{1,0:T(8,128)(2,1)S(1)} %collective-permute-done.2.refs_1_, ...), custom_call_target="tpu_custom_call" | custom-call | flops 20000000000 | tf_op jit(solution)/shard_map/pallas_call | solution.py:423
  24.5 0.1 collective-permute-start.6
  24.6 1.3 %collective-permute-done.6 = bf16[32,2048]{1,0:T(8,128)(2,1)S(1)} collective-permute-done((bf16[32,2048]{1,0:T(8,128)(2,1)S(1)}, bf16[32,2048]{1,0:T(8,128)(2,1)S(1)}, u32[]{:S(2)}, u32[]{:S(2)}) %collective-permute-start.6) | collective-permute-done | bytes 131104 | tf_op jit(solution)/shard_map/ppermute | solution.py:32
  25.9 0.7 %fusion.2 = bf16[2048,32]{0,1:T(8,128)(2,1)} fusion(f32[32,2048]{1,0:T(8,128)S(1)} %shard_map.69, bf16[32,2048]{1,0:T(8,128)(2,1)S(1)} %collective-permute-done.6, f32[64,2048]{1,0:T(8,128)S(1)} %convert_add_fusion), kind=kLoop, calls=%fused_computation.5 | loop fusion | flops 262144 | bytes 786432 | tf_op jit(solution)/shard_map/transpose | solution.py:449
  (18 shorter events, 0.1 us)
Async XLA Ops:
  0.0 9.6 %copy-start = (s32[128,32]{0,1:T(8,128)S(1)}, s32[128,32]{0,1:T(8,128)}, u32[]{:S(2)}) copy-start(s32[128,32]{0,1:T(8,128)} %param.11) | copy-start | bytes 49156
  0.0 5.7 %copy-start.4 = (f32[3,16384]{1,0:T(4,128)S(1)}, f32[3,16384]{1,0:T(4,128)}, u32[]{:S(2)}) copy-start(f32[3,16384]{1,0:T(4,128)} %points_ref) | copy-start | bytes 589828
  0.0 11.1 %copy-start.1 = (bf16[4096,32]{0,1:T(8,128)(2,1)S(1)}, bf16[4096,32]{0,1:T(8,128)(2,1)}, u32[]{:S(2)}) copy-start(bf16[4096,32]{0,1:T(8,128)(2,1)} %param.7) | copy-start | bytes 786436
  0.0 11.1 %collective-permute-start.1 = (bf16[32,4096]{1,0:T(8,128)(2,1)}, bf16[32,4096]{1,0:T(8,128)(2,1)S(1)}, u32[]{:S(2)}, u32[]{:S(2)}) collective-permute-start(bf16[32,4096]{1,0:T(8,128)(2,1)} %bitcast.3), channel_id=1, source_target_pairs={{0,1},{1,0},{2,3},{3,2},{4,5},{5,4},{6,7},{7,6},{8,9},{9,8},{10,11... | collective-permute-start | bytes 786440 | tf_op jit(solution)/shard_map/ppermute | solution.py:32
  3.1 8.0 %collective-permute-start = (bf16[272,128]{1,0:T(8,128)(2,1)}, bf16[272,128]{1,0:T(8,128)(2,1)S(1)}, u32[]{:S(2)}, u32[]{:S(2)}) collective-permute-start(bf16[272,128]{1,0:T(8,128)(2,1)} %get-tuple-element.38.refs_0_), channel_id=1, source_target_pairs={{0,4},{1,13},{4,8},{5,1},{8,12},{9,5},{12,0},{13,9},{2,6},{3,15},{... | collective-permute-start | bytes 208904 | tf_op jit(solution)/shard_map/ppermute | solution.py:41
  6.5 15.2 %collective-permute-start.2 = (bf16[272,128]{1,0:T(8,128)(2,1)}, bf16[272,128]{1,0:T(8,128)(2,1)S(1)}, u32[]{:S(2)}, u32[]{:S(2)}) collective-permute-start(bf16[272,128]{1,0:T(8,128)(2,1)} %get-tuple-element.38.refs_0_), channel_id=1, source_target_pairs={{0,12},{1,5},{4,0},{5,9},{8,4},{9,13},{12,8},{13,1},{2,14},{3,7},{... | collective-permute-start | bytes 208904 | tf_op jit(solution)/shard_map/ppermute | solution.py:41
  8.6 13.1 %collective-permute-start.3 = (bf16[272,128]{1,0:T(8,128)(2,1)}, bf16[272,128]{1,0:T(8,128)(2,1)S(1)}, u32[]{:S(2)}, u32[]{:S(2)}) collective-permute-start(bf16[272,128]{1,0:T(8,128)(2,1)} %get-tuple-element.38.refs_0_), channel_id=1, source_target_pairs={{0,8},{4,12},{8,0},{12,4},{1,9},{5,13},{9,1},{13,5},{2,10},{6,14},... | collective-permute-start | bytes 208904 | tf_op jit(solution)/shard_map/ppermute | solution.py:32
  13.9 5.2 %copy-start.2 = (s32[8,128]{1,0:T(8,128)S(1)}, s32[8,128]{1,0:T(8,128)}, u32[]{:S(2)}) copy-start(s32[8,128]{1,0:T(8,128)} %get-tuple-element.34.list_ref) | copy-start | bytes 12292
  13.9 7.8 %copy-start.3 = (bf16[16,32,32,32]{3,2,1,0:T(8,128)(2,1)S(1)}, bf16[16,32,32,32]{3,2,1,0:T(8,128)(2,1)}, u32[]{:S(2)}) copy-start(bf16[16,32,32,32]{3,2,1,0:T(8,128)(2,1)} %couplings_ref.1) | copy-start | bytes 3145732
  13.9 7.8 %copy-start.5 = (bf16[32,4096]{1,0:T(8,128)(2,1)S(1)}, bf16[32,4096]{1,0:T(8,128)(2,1)}, u32[]{:S(2)}) copy-start(bf16[32,4096]{1,0:T(8,128)(2,1)} %basis_ref.1) | copy-start | bytes 786436
  13.9 7.8 %copy-start.6 = (bf16[272,128]{1,0:T(8,128)(2,1)S(1)}, bf16[272,128]{1,0:T(8,128)(2,1)}, u32[]{:S(2)}) copy-start(bf16[272,128]{1,0:T(8,128)(2,1)} %get-tuple-element.38.refs_0_) | copy-start | bytes 208900
  14.0 7.8 %collective-permute-start.4 = (bf16[64,1024]{1,0:T(8,128)(2,1)S(1)}, bf16[64,1024]{1,0:T(8,128)(2,1)S(1)}, u32[]{:S(2)}, u32[]{:S(2)}) collective-permute-start(bf16[64,1024]{1,0:T(8,128)(2,1)S(1)} %shard_map.66), channel_id=1, source_target_pairs={{0,12},{1,5},{4,0},{5,9},{8,4},{9,13},{12,8},{13,1},{2,14},{3,7},{... | collective-permute-start | bytes 393224 | tf_op jit(solution)/shard_map/ppermute | solution.py:41
  17.7 6.7 %collective-permute-start.5 = (bf16[64,1024]{1,0:T(8,128)(2,1)S(1)}, bf16[64,1024]{1,0:T(8,128)(2,1)S(1)}, u32[]{:S(2)}, u32[]{:S(2)}) collective-permute-start(bf16[64,1024]{1,0:T(8,128)(2,1)S(1)} %shard_map.67), channel_id=1, source_target_pairs={{0,12},{1,5},{4,0},{5,9},{8,4},{9,13},{12,8},{13,1},{2,14},{3,7},{... | collective-permute-start | bytes 393224 | tf_op jit(solution)/shard_map/ppermute | solution.py:41
  24.5 1.4 %collective-permute-start.6 = (bf16[32,2048]{1,0:T(8,128)(2,1)S(1)}, bf16[32,2048]{1,0:T(8,128)(2,1)S(1)}, u32[]{:S(2)}, u32[]{:S(2)}) collective-permute-start(bf16[32,2048]{1,0:T(8,128)(2,1)S(1)} %slice.39), channel_id=1, source_target_pairs={{0,1},{1,0},{2,3},{3,2},{4,5},{5,4},{6,7},{7,6},{8,9},{9,8},{10,11... | collective-permute-start | bytes 393224 | tf_op jit(solution)/shard_map/ppermute | solution.py:32

commit v11 on v10

--- a/solution.py
+++ b/solution.py
@@ -393,23 +393,22 @@
         compiler_params=PARAMS,
         cost_estimate=cost(0.7),
     )(points)
-    target_rows, later_load = lax.optimization_barrier((target_rows, load))
+    args = (target_rows, source_rows, mine, other)
+    own_near = near_sum(own_clusters, None, 2.6, own_clusters, own_list, *args, f32)
+    own_near, first_load = lax.optimization_barrier((own_near, first_load))
+    codes = first_load[skel_rows:].astype(jnp.int32)
+    pairs = codes[:8] + 256 * codes[8:]
+    low = near_sum(0, 0, 20.0, own_clusters // 2, pairs, *args, bf16)
+    low, pairs, later_load = lax.optimization_barrier((low, pairs, load))
+    low_back = crossed(low, -1)
     narrow = blk_count == 4 and cluster_total <= 256
     if narrow:
         loads = [load, crossed(later_load, -1), shifted(later_load, "blk", 2), first_load]
     else:
         loads = [lax.all_gather(later_load[:skel_rows], "blk", axis=0, tiled=True)]
-    args = (target_rows, source_rows, mine, other)
-    codes = first_load[skel_rows:].astype(jnp.int32)
-    pairs = codes[:8] + 256 * codes[8:]
-    low = near_sum(0, 0, 20.0, own_clusters // 2, pairs, *args, bf16)
-    low, pairs = lax.optimization_barrier((low, pairs))
-    low_back = crossed(low, -1)
     high = near_sum(0, 1, 20.0, own_clusters // 2, pairs, *args, bf16)
-    high, own_list = lax.optimization_barrier((high, own_list))
     high_back = crossed(high, -1)
-    own_near = near_sum(own_clusters, None, 0.5, own_clusters, own_list, *args, f32)
-    own_near, loads, low_back = lax.optimization_barrier((own_near, loads, low_back))
+    _, loads, low_back = lax.optimization_barrier((high, loads, low_back))
 
     blk = lax.axis_index("blk")
     first = blk * seg_size + lax.axis_index("leaf") * own_clusters

time: 26.9 us -> 29.6 us (1.10); the launches traced: 26.6 us -> 29.7 us
  waiting for transfers between devices: 2.66 us -> 5.23 us
  local copies, waits for them, and re-layouts: 0.19 us -> 0.85 us
  starting transfers between devices: 9.19 us -> 8.75 us
  Pallas kernels: 13.6 us -> 14 us
    ppermute x4, waiting for transfers between devices: 1.32 us -> 4.24 us  [crossed(): return lax.ppermute(block, ('blk', 'rhs'), pairs)]
    ppermute x4, starting transfers between devices: 7.62 us -> 5.42 us  [crossed(): return lax.ppermute(block, ('blk', 'rhs'), pairs)]
    ppermute x3, starting transfers between devices: 1.57 us -> 3.33 us  [shifted(): lax.ppermute(block, axis, [(i, (i + shift) % count) for i in range(count)])]
    unnamed x15, local copies, waits for them, and re-layouts: 0.1 us -> 0.77 us
    pallas_call x3, Pallas kernels: 7.73 us -> 8.1 us  [near_sum(): pl.pallas_call(functools.partial(near_kernel, base, part), out_shape=jax....]
    ppermute x3, waiting for transfers between devices: 1.34 us -> 0.99 us  [shifted(): lax.ppermute(block, axis, [(i, (i + shift) % count) for i in range(count)])]
  transfers between devices with their start and end apart: 7 -> 7, of which waited for: 2 -> 4; matrix products, arithmetic and copies ran while one was open for 1% -> 1% of each run, Pallas kernels for 51% -> 37%
where the time goes in v11:
time: 29.6 us; the launch traced here: 29.7 us
  Pallas kernels  14 us (47%)
  starting transfers between devices  8.75 us (30%)
  waiting for transfers between devices  5.23 us (18%)
  local copies, waits for them, and re-layouts  0.85 us (3%)
  other arithmetic  0.79 us (3%)
    pallas_call x3, Pallas kernels, near_sum(): pl.pallas_call(functools.partial(near_kernel, base, part), out_shape=jax....  8.1 us
    ppermute x4, starting transfers between devices, crossed(): return lax.ppermute(block, ('blk', 'rhs'), pairs)  5.42 us
    ppermute x4, waiting for transfers between devices, crossed(): return lax.ppermute(block, ('blk', 'rhs'), pairs)  4.24 us
    ppermute x3, starting transfers between devices, shifted(): lax.ppermute(block, axis, [(i, (i + shift) % count) for i in range(count)])  3.33 us
    pallas_call x1, Pallas kernels, on_device(): pl.pallas_call(functools.partial(far_kernel_phased, seg_size), out_shape=...  2.62 us
    pallas_call x1, Pallas kernels, on_device(): pl.pallas_call(functools.partial(list_kernel, seg_size), out_shape=[jax.S...  2.52 us
    ppermute x3, waiting for transfers between devices, shifted(): lax.ppermute(block, axis, [(i, (i + shift) % count) for i in range(count)])  0.99 us
    unnamed x15, local copies, waits for them, and re-layouts  0.77 us
  transfers between devices with their start and end apart: 7, of which 4 were waited for; matrix products, arithmetic and copies ran while one was open for 1% of the time, Pallas kernels for 37%

profile of v11, /device:TPU:0, one launch (start us, length us, event | category | flops | bytes accessed | tf_op | source)
XLA Modules:
  0.0 29.7 jit_solution(10929034209025662808)
XLA Ops:
  0.0 0.5 %collective-permute-start = (bf16[32,4096]{1,0:T(8,128)(2,1)}, bf16[32,4096]{1,0:T(8,128)(2,1)S(1)}, u32[]{:S(2)}, u32[]{:S(2)}) collective-permute-start(bf16[32,4096]{1,0:T(8,128)(2,1)} %bitcast.3), channel_id=1, source_target_pairs={{0,1},{1,0},{2,3},{3,2},{4,5},{5,4},{6,7},{7,6},{8,9},{9,8},{10,11... | collective-permute-start | bytes 786440 | tf_op jit(solution)/shard_map/ppermute | solution.py:32
  0.5 2.5 %shard_map.64 = (s32[8,128]{1,0:T(8,128)}, bf16[272,128]{1,0:T(8,128)(2,1)}) custom-call(s32[16,27]{1,0:T(8,128)} %near_hbm.1, bf16[32,4096]{1,0:T(8,128)(2,1)} %basis_ref.1, bf16[32,4096]{1,0:T(8,128)(2,1)} %bitcast.4), custom_call_target="tpu_custom_call" | custom-call | flops 3000000000 | tf_op jit(solution)/shard_map/pallas_call | solution.py:365
  3.1 2.7 %collective-permute-start.1 = (bf16[272,128]{1,0:T(8,128)(2,1)}, bf16[272,128]{1,0:T(8,128)(2,1)S(1)}, u32[]{:S(2)}, u32[]{:S(2)}) collective-permute-start(bf16[272,128]{1,0:T(8,128)(2,1)} %get-tuple-element.35.refs_0_), channel_id=1, source_target_pairs={{0,4},{1,13},{4,8},{5,1},{8,12},{9,5},{12,0},{13,9},{2,6},{3,15},{... | collective-permute-start | bytes 208904 | tf_op jit(solution)/shard_map/ppermute | solution.py:41
  5.8 0.1 constant_dynamic-slice_fusion
  5.8 0.1 copy.8
  5.9 0.7 %shard_map.65 = (bf16[33,48,128]{2,1,0:T(8,128)(2,1)S(1)}, bf16[32,128,48]{2,1,0:T(8,128)(2,1)S(1)}) custom-call(f32[3,16384]{1,0:T(4,128)S(1)} %copy-done.2), custom_call_target="tpu_custom_call" | custom-call | flops 700000000 | tf_op jit(solution)/shard_map/pallas_call | solution.py:385
  6.7 0.7 %copy-done.6 = s32[8,128]{1,0:T(8,128)S(1)} copy-done((s32[8,128]{1,0:T(8,128)S(1)}, s32[8,128]{1,0:T(8,128)}, u32[]{:S(2)}) %copy-start.6) | copy-done | bytes 4120
  7.4 2.6 %shard_map.66 = f32[64,2048]{1,0:T(8,128)S(1)} custom-call(s32[8,128]{1,0:T(8,128)S(1)} %copy-done.6, bf16[33,48,128]{2,1,0:T(8,128)(2,1)S(1)} %get-tuple-element.27.target_ref, bf16[32,128,48]{2,1,0:T(8,128)(2,1)S(1)} %get-tuple-element.28.source_ref, bf16[32,4096]{1,0:T(8,128)(2,1)S(1)} %bitcast.5, bf16[32,4096]{1,0:T(8,128)(2,1)S(1)} %collective-permute-done.other_ref), custom_call_target="tpu_custom_call" | custom-call | flops 2600000000 | tf_op jit(solution)/shard_map/pallas_call | solution.py:274
  10.0 0.9 %collective-permute-done.1.refs_3_ = bf16[272,128]{1,0:T(8,128)(2,1)S(1)} collective-permute-done((bf16[272,128]{1,0:T(8,128)(2,1)}, bf16[272,128]{1,0:T(8,128)(2,1)S(1)}, u32[]{:S(2)}, u32[]{:S(2)}) %collective-permute-start.1) | collective-permute-done | bytes 69664 | tf_op jit(solution)/shard_map/ppermute | solution.py:41
  11.0 2.8 %shard_map.67 = bf16[64,1024]{1,0:T(8,128)(2,1)S(1)} custom-call(s32[8,128]{1,0:T(8,128)S(1)} %fusion.9.list_ref, bf16[33,48,128]{2,1,0:T(8,128)(2,1)S(1)} %get-tuple-element.27.target_ref, bf16[32,128,48]{2,1,0:T(8,128)(2,1)S(1)} %get-tuple-element.28.source_ref, bf16[32,4096]{1,0:T(8,128)(2,1)S(1)} %bitcast.6, ...), custom_call_target="tpu_custom_call" | custom-call | flops 20000000000 | tf_op jit(solution)/shard_map/pallas_call | solution.py:274
  13.8 0.0 copy-start.1
  13.8 0.0 copy-start.4
  13.8 2.0 %collective-permute-start.3 = (bf16[272,128]{1,0:T(8,128)(2,1)S(1)}, bf16[272,128]{1,0:T(8,128)(2,1)S(1)}, u32[]{:S(2)}, u32[]{:S(2)}) collective-permute-start(bf16[272,128]{1,0:T(8,128)(2,1)S(1)} %copy-done.5), channel_id=1, source_target_pairs={{0,8},{4,12},{8,0},{12,4},{1,9},{5,13},{9,1},{13,5},{2,10},{6,14},... | collective-permute-start | bytes 208904 | tf_op jit(solution)/shard_map/ppermute | solution.py:32
  15.8 0.5 %collective-permute-start.2 = (bf16[272,128]{1,0:T(8,128)(2,1)S(1)}, bf16[272,128]{1,0:T(8,128)(2,1)S(1)}, u32[]{:S(2)}, u32[]{:S(2)}) collective-permute-start(bf16[272,128]{1,0:T(8,128)(2,1)S(1)} %copy-done.5), channel_id=1, source_target_pairs={{0,12},{1,5},{4,0},{5,9},{8,4},{9,13},{12,8},{13,1},{2,14},{3,7},{... | collective-permute-start | bytes 208904 | tf_op jit(solution)/shard_map/ppermute | solution.py:41
  16.4 1.9 %collective-permute-start.4 = (bf16[64,1024]{1,0:T(8,128)(2,1)S(1)}, bf16[64,1024]{1,0:T(8,128)(2,1)S(1)}, u32[]{:S(2)}, u32[]{:S(2)}) collective-permute-start(bf16[64,1024]{1,0:T(8,128)(2,1)S(1)} %shard_map.67), channel_id=1, source_target_pairs={{0,12},{1,5},{4,0},{5,9},{8,4},{9,13},{12,8},{13,1},{2,14},{3,7},{... | collective-permute-start | bytes 393224 | tf_op jit(solution)/shard_map/ppermute | solution.py:41
  18.3 2.6 %shard_map.68 = bf16[64,1024]{1,0:T(8,128)(2,1)S(1)} custom-call(s32[8,128]{1,0:T(8,128)S(1)} %fusion.9.list_ref, bf16[33,48,128]{2,1,0:T(8,128)(2,1)S(1)} %get-tuple-element.27.target_ref, bf16[32,128,48]{2,1,0:T(8,128)(2,1)S(1)} %get-tuple-element.28.source_ref, bf16[32,4096]{1,0:T(8,128)(2,1)S(1)} %bitcast.7, ...), custom_call_target="tpu_custom_call" | custom-call | flops 20000000000 | tf_op jit(solution)/shard_map/pallas_call | solution.py:274
  20.9 0.3 collective-permute-start.5
  21.2 0.8 %collective-permute-done.2.refs_1_ = bf16[272,128]{1,0:T(8,128)(2,1)S(1)} collective-permute-done((bf16[272,128]{1,0:T(8,128)(2,1)S(1)}, bf16[272,128]{1,0:T(8,128)(2,1)S(1)}, u32[]{:S(2)}, u32[]{:S(2)}) %collective-permute-start.2) | collective-permute-done | bytes 69664 | tf_op jit(solution)/shard_map/ppermute | solution.py:41
  22.0 2.5 %collective-permute-done.4 = bf16[64,1024]{1,0:T(8,128)(2,1)S(1)} collective-permute-done((bf16[64,1024]{1,0:T(8,128)(2,1)S(1)}, bf16[64,1024]{1,0:T(8,128)(2,1)S(1)}, u32[]{:S(2)}, u32[]{:S(2)}) %collective-permute-start.4) | collective-permute-done | bytes 131104 | tf_op jit(solution)/shard_map/ppermute | solution.py:41
  24.5 2.6 %shard_map.69 = f32[32,2048]{1,0:T(8,128)S(1)} custom-call(s32[16,32]{1,0:T(8,128)S(1)} %fusion.7.far_ref, bf16[16,32,32,32]{3,2,1,0:T(8,128)(2,1)S(1)} %copy-done.1, bf16[32,4096]{1,0:T(8,128)(2,1)S(1)} %copy-done.4, bf16[272,128]{1,0:T(8,128)(2,1)S(1)} %copy-done.5, bf16[272,128]{1,0:T(8,128)(2,1)S(1)} %collective-permute-done.2.refs_1_, ...), custom_call_target="tpu_custom_call" | custom-call | flops 20000000000 | tf_op jit(solution)/shard_map/pallas_call | solution.py:422
  27.1 0.1 convert_add_fusion
  27.2 0.8 %collective-permute-start.6 = (bf16[32,2048]{1,0:T(8,128)(2,1)S(1)}, bf16[32,2048]{1,0:T(8,128)(2,1)S(1)}, u32[]{:S(2)}, u32[]{:S(2)}) collective-permute-start(bf16[32,2048]{1,0:T(8,128)(2,1)S(1)} %slice.38), channel_id=1, source_target_pairs={{0,1},{1,0},{2,3},{3,2},{4,5},{5,4},{6,7},{7,6},{8,9},{9,8},{10,11... | collective-permute-start | bytes 393224 | tf_op jit(solution)/shard_map/ppermute | solution.py:32
  28.0 1.0 %collective-permute-done.6 = bf16[32,2048]{1,0:T(8,128)(2,1)S(1)} collective-permute-done((bf16[32,2048]{1,0:T(8,128)(2,1)S(1)}, bf16[32,2048]{1,0:T(8,128)(2,1)S(1)}, u32[]{:S(2)}, u32[]{:S(2)}) %collective-permute-start.6) | collective-permute-done | bytes 131104 | tf_op jit(solution)/shard_map/ppermute | solution.py:32
  29.0 0.7 %fusion.2 = bf16[2048,32]{0,1:T(8,128)(2,1)} fusion(f32[32,2048]{1,0:T(8,128)S(1)} %shard_map.69, bf16[32,2048]{1,0:T(8,128)(2,1)S(1)} %collective-permute-done.6, f32[64,2048]{1,0:T(8,128)S(1)} %convert_add_fusion), kind=kLoop, calls=%fused_computation.5 | loop fusion | flops 262144 | bytes 786432 | tf_op jit(solution)/shard_map/transpose | solution.py:448
  (18 shorter events, 0.1 us)
Async XLA Ops:
  0.0 5.8 %copy-start = (s32[128,32]{0,1:T(8,128)S(1)}, s32[128,32]{0,1:T(8,128)}, u32[]{:S(2)}) copy-start(s32[128,32]{0,1:T(8,128)} %param.11) | copy-start | bytes 49156
  0.0 5.9 %copy-start.2 = (f32[3,16384]{1,0:T(4,128)S(1)}, f32[3,16384]{1,0:T(4,128)}, u32[]{:S(2)}) copy-start(f32[3,16384]{1,0:T(4,128)} %points_ref) | copy-start | bytes 589828
  0.0 6.7 %copy-start.3 = (bf16[4096,32]{0,1:T(8,128)(2,1)S(1)}, bf16[4096,32]{0,1:T(8,128)(2,1)}, u32[]{:S(2)}) copy-start(bf16[4096,32]{0,1:T(8,128)(2,1)} %param.7) | copy-start | bytes 786436
  0.0 6.7 %collective-permute-start = (bf16[32,4096]{1,0:T(8,128)(2,1)}, bf16[32,4096]{1,0:T(8,128)(2,1)S(1)}, u32[]{:S(2)}, u32[]{:S(2)}) collective-permute-start(bf16[32,4096]{1,0:T(8,128)(2,1)} %bitcast.3), channel_id=1, source_target_pairs={{0,1},{1,0},{2,3},{3,2},{4,5},{5,4},{6,7},{7,6},{8,9},{9,8},{10,11... | collective-permute-start | bytes 786440 | tf_op jit(solution)/shard_map/ppermute | solution.py:32
  3.1 7.9 %collective-permute-start.1 = (bf16[272,128]{1,0:T(8,128)(2,1)}, bf16[272,128]{1,0:T(8,128)(2,1)S(1)}, u32[]{:S(2)}, u32[]{:S(2)}) collective-permute-start(bf16[272,128]{1,0:T(8,128)(2,1)} %get-tuple-element.35.refs_0_), channel_id=1, source_target_pairs={{0,4},{1,13},{4,8},{5,1},{8,12},{9,5},{12,0},{13,9},{2,6},{3,15},{... | collective-permute-start | bytes 208904 | tf_op jit(solution)/shard_map/ppermute | solution.py:41
  6.7 0.7 %copy-start.6 = (s32[8,128]{1,0:T(8,128)S(1)}, s32[8,128]{1,0:T(8,128)}, u32[]{:S(2)}) copy-start(s32[8,128]{1,0:T(8,128)} %get-tuple-element.24.list_ref) | copy-start | bytes 12292
  11.0 2.9 %copy-start.5 = (bf16[272,128]{1,0:T(8,128)(2,1)S(1)}, bf16[272,128]{1,0:T(8,128)(2,1)}, u32[]{:S(2)}) copy-start(bf16[272,128]{1,0:T(8,128)(2,1)} %get-tuple-element.35.refs_0_) | copy-start | bytes 208900
  13.8 10.7 %copy-start.1 = (bf16[16,32,32,32]{3,2,1,0:T(8,128)(2,1)S(1)}, bf16[16,32,32,32]{3,2,1,0:T(8,128)(2,1)}, u32[]{:S(2)}) copy-start(bf16[16,32,32,32]{3,2,1,0:T(8,128)(2,1)} %couplings_ref.1) | copy-start | bytes 3145732
  13.8 10.7 %copy-start.4 = (bf16[32,4096]{1,0:T(8,128)(2,1)S(1)}, bf16[32,4096]{1,0:T(8,128)(2,1)}, u32[]{:S(2)}) copy-start(bf16[32,4096]{1,0:T(8,128)(2,1)} %basis_ref.1) | copy-start | bytes 786436
  13.8 7.4 %collective-permute-start.3 = (bf16[272,128]{1,0:T(8,128)(2,1)S(1)}, bf16[272,128]{1,0:T(8,128)(2,1)S(1)}, u32[]{:S(2)}, u32[]{:S(2)}) collective-permute-start(bf16[272,128]{1,0:T(8,128)(2,1)S(1)} %copy-done.5), channel_id=1, source_target_pairs={{0,8},{4,12},{8,0},{12,4},{1,9},{5,13},{9,1},{13,5},{2,10},{6,14},... | collective-permute-start | bytes 208904 | tf_op jit(solution)/shard_map/ppermute | solution.py:32
  15.8 6.2 %collective-permute-start.2 = (bf16[272,128]{1,0:T(8,128)(2,1)S(1)}, bf16[272,128]{1,0:T(8,128)(2,1)S(1)}, u32[]{:S(2)}, u32[]{:S(2)}) collective-permute-start(bf16[272,128]{1,0:T(8,128)(2,1)S(1)} %copy-done.5), channel_id=1, source_target_pairs={{0,12},{1,5},{4,0},{5,9},{8,4},{9,13},{12,8},{13,1},{2,14},{3,7},{... | collective-permute-start | bytes 208904 | tf_op jit(solution)/shard_map/ppermute | solution.py:41
  16.4 8.1 %collective-permute-start.4 = (bf16[64,1024]{1,0:T(8,128)(2,1)S(1)}, bf16[64,1024]{1,0:T(8,128)(2,1)S(1)}, u32[]{:S(2)}, u32[]{:S(2)}) collective-permute-start(bf16[64,1024]{1,0:T(8,128)(2,1)S(1)} %shard_map.67), channel_id=1, source_target_pairs={{0,12},{1,5},{4,0},{5,9},{8,4},{9,13},{12,8},{13,1},{2,14},{3,7},{... | collective-permute-start | bytes 393224 | tf_op jit(solution)/shard_map/ppermute | solution.py:41
  20.9 6.2 %collective-permute-start.5 = (bf16[64,1024]{1,0:T(8,128)(2,1)S(1)}, bf16[64,1024]{1,0:T(8,128)(2,1)S(1)}, u32[]{:S(2)}, u32[]{:S(2)}) collective-permute-start(bf16[64,1024]{1,0:T(8,128)(2,1)S(1)} %shard_map.68), channel_id=1, source_target_pairs={{0,12},{1,5},{4,0},{5,9},{8,4},{9,13},{12,8},{13,1},{2,14},{3,7},{... | collective-permute-start | bytes 393224 | tf_op jit(solution)/shard_map/ppermute | solution.py:41
  27.2 1.8 %collective-permute-start.6 = (bf16[32,2048]{1,0:T(8,128)(2,1)S(1)}, bf16[32,2048]{1,0:T(8,128)(2,1)S(1)}, u32[]{:S(2)}, u32[]{:S(2)}) collective-permute-start(bf16[32,2048]{1,0:T(8,128)(2,1)S(1)} %slice.38), channel_id=1, source_target_pairs={{0,1},{1,0},{2,3},{3,2},{4,5},{5,4},{6,7},{7,6},{8,9},{9,8},{10,11... | collective-permute-start | bytes 393224 | tf_op jit(solution)/shard_map/ppermute | solution.py:32

commit v12 on v10

--- a/solution.py
+++ b/solution.py
@@ -143,23 +143,18 @@
     rows_end = seg_size // pack * rank
     load_ref[rows_end : rows_end + 16, :] = away.astype(bf16)
 
-    blocks = []
-    for group in range(seg_size // pack):
-        rows = []
-        for i in range(pack):
-            at = (group * pack + i) * LEAF
-            parts = [jnp.zeros((columns, LEAF), bf16)] * pack
-            parts[i] = charges_ref[:, at : at + LEAF]
-            rows.append(jnp.concatenate(parts, axis=1))
-        at = group * pack * LEAF
-        blocks.append(
+    singles = []
+    for index in range(seg_size):
+        at = index * LEAF
+        singles.append(
             lax.dot_general(
-                basis_ref[:, at : at + pack * LEAF],
-                jnp.concatenate(rows, axis=0),
+                basis_ref[:, at : at + LEAF],
+                charges_ref[:, at : at + LEAF],
                 (((1,), (1,)), ((), ())),
                 preferred_element_type=f32,
             )
         )
+    blocks = [jnp.concatenate(singles[i : i + pack], axis=1) for i in range(0, seg_size, pack)]
     for group, block in enumerate(blocks):
         load_ref[group * rank : (group + 1) * rank, :] = block.astype(bf16)
 

time: 26.9 us -> 27.1 us (level)
  Pallas kernels: 13.6 us -> 14.2 us
  starting transfers between devices: 9.19 us -> 8.83 us
    pallas_call x3, Pallas kernels: 7.73 us -> 8.32 us  [near_sum(): pl.pallas_call(functools.partial(near_kernel, base, part), out_shape=jax....]
    ppermute x4, starting transfers between devices: 7.62 us -> 7.25 us  [crossed(): return lax.ppermute(block, ('blk', 'rhs'), pairs)]
  transfers between devices with their start and end apart: 7 -> 7, of which waited for: 2 -> 2; matrix products, arithmetic and copies ran while one was open for 1% -> 1% of each run, Pallas kernels for 51% -> 53%
where the time goes in v12:
time: 27.1 us; the launch traced here: 26.8 us
  Pallas kernels  14.2 us (52%)
  starting transfers between devices  8.83 us (33%)
  waiting for transfers between devices  2.66 us (10%)
  other arithmetic  0.77 us (3%)
    pallas_call x3, Pallas kernels, near_sum(): pl.pallas_call(functools.partial(near_kernel, base, part), out_shape=jax....  8.32 us
    ppermute x4, starting transfers between devices, crossed(): return lax.ppermute(block, ('blk', 'rhs'), pairs)  7.25 us
    pallas_call x1, Pallas kernels, on_device(): pl.pallas_call(functools.partial(far_kernel_phased, seg_size), out_shape=...  2.65 us
    pallas_call x1, Pallas kernels, on_device(): pl.pallas_call(functools.partial(list_kernel, seg_size), out_shape=[jax.S...  2.51 us
    ppermute x3, starting transfers between devices, shifted(): lax.ppermute(block, axis, [(i, (i + shift) % count) for i in range(count)])  1.57 us
    ppermute x3, waiting for transfers between devices, shifted(): lax.ppermute(block, axis, [(i, (i + shift) % count) for i in range(count)])  1.34 us
    ppermute x4, waiting for transfers between devices, crossed(): return lax.ppermute(block, ('blk', 'rhs'), pairs)  1.32 us
    pallas_call x1, Pallas kernels, on_device(): pl.pallas_call(functools.partial(feature_kernel, seg_size, own_clusters),...  0.72 us
  transfers between devices with their start and end apart: 7, of which 2 were waited for; matrix products, arithmetic and copies ran while one was open for 1% of the time, Pallas kernels for 53%

profile of v12, /device:TPU:0, one launch (start us, length us, event | category | flops | bytes accessed | tf_op | source)
XLA Modules:
  0.0 26.8 jit_solution(13397944723667606607)
XLA Ops:
  0.0 0.5 %collective-permute-start.1 = (bf16[32,4096]{1,0:T(8,128)(2,1)}, bf16[32,4096]{1,0:T(8,128)(2,1)S(1)}, u32[]{:S(2)}, u32[]{:S(2)}) collective-permute-start(bf16[32,4096]{1,0:T(8,128)(2,1)} %bitcast.3), channel_id=1, source_target_pairs={{0,1},{1,0},{2,3},{3,2},{4,5},{5,4},{6,7},{7,6},{8,9},{9,8},{10,11... | collective-permute-start | bytes 786440 | tf_op jit(solution)/shard_map/ppermute | solution.py:32
  0.5 2.5 %shard_map.64 = (s32[8,128]{1,0:T(8,128)}, bf16[272,128]{1,0:T(8,128)(2,1)}) custom-call(s32[16,27]{1,0:T(8,128)} %near_hbm.1, bf16[32,4096]{1,0:T(8,128)(2,1)} %basis_ref.1, bf16[32,4096]{1,0:T(8,128)(2,1)} %bitcast.4), custom_call_target="tpu_custom_call" | custom-call | flops 3000000000 | tf_op jit(solution)/shard_map/pallas_call | solution.py:360
  3.1 2.7 %collective-permute-start = (bf16[272,128]{1,0:T(8,128)(2,1)}, bf16[272,128]{1,0:T(8,128)(2,1)S(1)}, u32[]{:S(2)}, u32[]{:S(2)}) collective-permute-start(bf16[272,128]{1,0:T(8,128)(2,1)} %get-tuple-element.38.refs_0_), channel_id=1, source_target_pairs={{0,4},{1,13},{4,8},{5,1},{8,12},{9,5},{12,0},{13,9},{2,6},{3,15},{... | collective-permute-start | bytes 208904 | tf_op jit(solution)/shard_map/ppermute | solution.py:41
  5.7 0.7 %shard_map.65 = (bf16[33,48,128]{2,1,0:T(8,128)(2,1)S(1)}, bf16[32,128,48]{2,1,0:T(8,128)(2,1)S(1)}) custom-call(f32[3,16384]{1,0:T(4,128)S(1)} %copy-done.4), custom_call_target="tpu_custom_call" | custom-call | flops 700000000 | tf_op jit(solution)/shard_map/pallas_call | solution.py:380
  6.5 2.1 %collective-permute-start.2 = (bf16[272,128]{1,0:T(8,128)(2,1)}, bf16[272,128]{1,0:T(8,128)(2,1)S(1)}, u32[]{:S(2)}, u32[]{:S(2)}) collective-permute-start(bf16[272,128]{1,0:T(8,128)(2,1)} %get-tuple-element.38.refs_0_), channel_id=1, source_target_pairs={{0,12},{1,5},{4,0},{5,9},{8,4},{9,13},{12,8},{13,1},{2,14},{3,7},{... | collective-permute-start | bytes 208904 | tf_op jit(solution)/shard_map/ppermute | solution.py:41
  8.6 1.0 %collective-permute-start.3 = (bf16[272,128]{1,0:T(8,128)(2,1)}, bf16[272,128]{1,0:T(8,128)(2,1)S(1)}, u32[]{:S(2)}, u32[]{:S(2)}) collective-permute-start(bf16[272,128]{1,0:T(8,128)(2,1)} %get-tuple-element.38.refs_0_), channel_id=1, source_target_pairs={{0,8},{4,12},{8,0},{12,4},{1,9},{5,13},{9,1},{13,5},{2,10},{6,14},... | collective-permute-start | bytes 208904 | tf_op jit(solution)/shard_map/ppermute | solution.py:32
  9.6 0.1 constant_dynamic-slice_fusion
  9.6 0.1 copy.8
  9.7 1.3 %collective-permute-done.refs_3_ = bf16[272,128]{1,0:T(8,128)(2,1)S(1)} collective-permute-done((bf16[272,128]{1,0:T(8,128)(2,1)}, bf16[272,128]{1,0:T(8,128)(2,1)S(1)}, u32[]{:S(2)}, u32[]{:S(2)}) %collective-permute-start) | collective-permute-done | bytes 69664 | tf_op jit(solution)/shard_map/ppermute | solution.py:41
  11.1 0.0 collective-permute-done.1.other_ref
  11.1 2.8 %shard_map.66 = bf16[64,1024]{1,0:T(8,128)(2,1)S(1)} custom-call(s32[8,128]{1,0:T(8,128)S(1)} %fusion.9.list_ref, bf16[33,48,128]{2,1,0:T(8,128)(2,1)S(1)} %get-tuple-element.30.target_ref, bf16[32,128,48]{2,1,0:T(8,128)(2,1)S(1)} %get-tuple-element.31.source_ref, bf16[32,4096]{1,0:T(8,128)(2,1)S(1)} %bitcast.5, ...), custom_call_target="tpu_custom_call" | custom-call | flops 20000000000 | tf_op jit(solution)/shard_map/pallas_call | solution.py:269
  13.9 0.0 copy-start.3
  13.9 0.0 copy-start.5
  13.9 0.0 copy-start.6
  14.0 1.4 %collective-permute-start.4 = (bf16[64,1024]{1,0:T(8,128)(2,1)S(1)}, bf16[64,1024]{1,0:T(8,128)(2,1)S(1)}, u32[]{:S(2)}, u32[]{:S(2)}) collective-permute-start(bf16[64,1024]{1,0:T(8,128)(2,1)S(1)} %shard_map.66), channel_id=1, source_target_pairs={{0,12},{1,5},{4,0},{5,9},{8,4},{9,13},{12,8},{13,1},{2,14},{3,7},{... | collective-permute-start | bytes 393224 | tf_op jit(solution)/shard_map/ppermute | solution.py:41
  15.4 2.6 %shard_map.67 = bf16[64,1024]{1,0:T(8,128)(2,1)S(1)} custom-call(s32[8,128]{1,0:T(8,128)S(1)} %fusion.9.list_ref, bf16[33,48,128]{2,1,0:T(8,128)(2,1)S(1)} %get-tuple-element.30.target_ref, bf16[32,128,48]{2,1,0:T(8,128)(2,1)S(1)} %get-tuple-element.31.source_ref, bf16[32,4096]{1,0:T(8,128)(2,1)S(1)} %bitcast.6, ...), custom_call_target="tpu_custom_call" | custom-call | flops 20000000000 | tf_op jit(solution)/shard_map/pallas_call | solution.py:269
  18.0 1.0 %collective-permute-start.5 = (bf16[64,1024]{1,0:T(8,128)(2,1)S(1)}, bf16[64,1024]{1,0:T(8,128)(2,1)S(1)}, u32[]{:S(2)}, u32[]{:S(2)}) collective-permute-start(bf16[64,1024]{1,0:T(8,128)(2,1)S(1)} %shard_map.67), channel_id=1, source_target_pairs={{0,12},{1,5},{4,0},{5,9},{8,4},{9,13},{12,8},{13,1},{2,14},{3,7},{... | collective-permute-start | bytes 393224 | tf_op jit(solution)/shard_map/ppermute | solution.py:41
  19.1 2.9 %shard_map.68 = f32[64,2048]{1,0:T(8,128)S(1)} custom-call(s32[8,128]{1,0:T(8,128)S(1)} %copy-done.2, bf16[33,48,128]{2,1,0:T(8,128)(2,1)S(1)} %get-tuple-element.30.target_ref, bf16[32,128,48]{2,1,0:T(8,128)(2,1)S(1)} %get-tuple-element.31.source_ref, bf16[32,4096]{1,0:T(8,128)(2,1)S(1)} %bitcast.7, bf16[32,4096]{1,0:T(8,128)(2,1)S(1)} %collective-permute-done.1.other_ref), custom_call_target="tpu_custom_call" | custom-call | flops 500000000 | tf_op jit(solution)/shard_map/pallas_call | solution.py:269
  21.9 0.0 collective-permute-done.2.refs_1_
  21.9 0.0 collective-permute-done.4
  22.0 2.6 %shard_map.69 = f32[32,2048]{1,0:T(8,128)S(1)} custom-call(s32[16,32]{1,0:T(8,128)S(1)} %fusion.7.far_ref, bf16[16,32,32,32]{3,2,1,0:T(8,128)(2,1)S(1)} %copy-done.3, bf16[32,4096]{1,0:T(8,128)(2,1)S(1)} %copy-done.5, bf16[272,128]{1,0:T(8,128)(2,1)S(1)} %copy-done.6, bf16[272,128]{1,0:T(8,128)(2,1)S(1)} %collective-permute-done.2.refs_1_, ...), custom_call_target="tpu_custom_call" | custom-call | flops 20000000000 | tf_op jit(solution)/shard_map/pallas_call | solution.py:418
  24.7 0.1 collective-permute-start.6
  24.8 1.3 %collective-permute-done.6 = bf16[32,2048]{1,0:T(8,128)(2,1)S(1)} collective-permute-done((bf16[32,2048]{1,0:T(8,128)(2,1)S(1)}, bf16[32,2048]{1,0:T(8,128)(2,1)S(1)}, u32[]{:S(2)}, u32[]{:S(2)}) %collective-permute-start.6) | collective-permute-done | bytes 131104 | tf_op jit(solution)/shard_map/ppermute | solution.py:32
  26.1 0.7 %fusion.2 = bf16[2048,32]{0,1:T(8,128)(2,1)} fusion(f32[32,2048]{1,0:T(8,128)S(1)} %shard_map.69, bf16[32,2048]{1,0:T(8,128)(2,1)S(1)} %collective-permute-done.6, f32[64,2048]{1,0:T(8,128)S(1)} %convert_add_fusion), kind=kLoop, calls=%fused_computation.5 | loop fusion | flops 262144 | bytes 786432 | tf_op jit(solution)/shard_map/transpose | solution.py:444
  (18 shorter events, 0.1 us)
Async XLA Ops:
  0.0 9.6 %copy-start = (s32[128,32]{0,1:T(8,128)S(1)}, s32[128,32]{0,1:T(8,128)}, u32[]{:S(2)}) copy-start(s32[128,32]{0,1:T(8,128)} %param.11) | copy-start | bytes 49156
  0.0 5.7 %copy-start.4 = (f32[3,16384]{1,0:T(4,128)S(1)}, f32[3,16384]{1,0:T(4,128)}, u32[]{:S(2)}) copy-start(f32[3,16384]{1,0:T(4,128)} %points_ref) | copy-start | bytes 589828
  0.0 11.1 %copy-start.1 = (bf16[4096,32]{0,1:T(8,128)(2,1)S(1)}, bf16[4096,32]{0,1:T(8,128)(2,1)}, u32[]{:S(2)}) copy-start(bf16[4096,32]{0,1:T(8,128)(2,1)} %param.7) | copy-start | bytes 786436
  0.0 11.0 %collective-permute-start.1 = (bf16[32,4096]{1,0:T(8,128)(2,1)}, bf16[32,4096]{1,0:T(8,128)(2,1)S(1)}, u32[]{:S(2)}, u32[]{:S(2)}) collective-permute-start(bf16[32,4096]{1,0:T(8,128)(2,1)} %bitcast.3), channel_id=1, source_target_pairs={{0,1},{1,0},{2,3},{3,2},{4,5},{5,4},{6,7},{7,6},{8,9},{9,8},{10,11... | collective-permute-start | bytes 786440 | tf_op jit(solution)/shard_map/ppermute | solution.py:32
  3.1 8.0 %collective-permute-start = (bf16[272,128]{1,0:T(8,128)(2,1)}, bf16[272,128]{1,0:T(8,128)(2,1)S(1)}, u32[]{:S(2)}, u32[]{:S(2)}) collective-permute-start(bf16[272,128]{1,0:T(8,128)(2,1)} %get-tuple-element.38.refs_0_), channel_id=1, source_target_pairs={{0,4},{1,13},{4,8},{5,1},{8,12},{9,5},{12,0},{13,9},{2,6},{3,15},{... | collective-permute-start | bytes 208904 | tf_op jit(solution)/shard_map/ppermute | solution.py:41
  6.5 15.5 %collective-permute-start.2 = (bf16[272,128]{1,0:T(8,128)(2,1)}, bf16[272,128]{1,0:T(8,128)(2,1)S(1)}, u32[]{:S(2)}, u32[]{:S(2)}) collective-permute-start(bf16[272,128]{1,0:T(8,128)(2,1)} %get-tuple-element.38.refs_0_), channel_id=1, source_target_pairs={{0,12},{1,5},{4,0},{5,9},{8,4},{9,13},{12,8},{13,1},{2,14},{3,7},{... | collective-permute-start | bytes 208904 | tf_op jit(solution)/shard_map/ppermute | solution.py:41
  8.6 13.4 %collective-permute-start.3 = (bf16[272,128]{1,0:T(8,128)(2,1)}, bf16[272,128]{1,0:T(8,128)(2,1)S(1)}, u32[]{:S(2)}, u32[]{:S(2)}) collective-permute-start(bf16[272,128]{1,0:T(8,128)(2,1)} %get-tuple-element.38.refs_0_), channel_id=1, source_target_pairs={{0,8},{4,12},{8,0},{12,4},{1,9},{5,13},{9,1},{13,5},{2,10},{6,14},... | collective-permute-start | bytes 208904 | tf_op jit(solution)/shard_map/ppermute | solution.py:32
  13.9 5.1 %copy-start.2 = (s32[8,128]{1,0:T(8,128)S(1)}, s32[8,128]{1,0:T(8,128)}, u32[]{:S(2)}) copy-start(s32[8,128]{1,0:T(8,128)} %get-tuple-element.34.list_ref) | copy-start | bytes 12292
  13.9 8.0 %copy-start.3 = (bf16[16,32,32,32]{3,2,1,0:T(8,128)(2,1)S(1)}, bf16[16,32,32,32]{3,2,1,0:T(8,128)(2,1)}, u32[]{:S(2)}) copy-start(bf16[16,32,32,32]{3,2,1,0:T(8,128)(2,1)} %couplings_ref.1) | copy-start | bytes 3145732
  13.9 8.0 %copy-start.5 = (bf16[32,4096]{1,0:T(8,128)(2,1)S(1)}, bf16[32,4096]{1,0:T(8,128)(2,1)}, u32[]{:S(2)}) copy-start(bf16[32,4096]{1,0:T(8,128)(2,1)} %basis_ref.1) | copy-start | bytes 786436
  13.9 8.0 %copy-start.6 = (bf16[272,128]{1,0:T(8,128)(2,1)S(1)}, bf16[272,128]{1,0:T(8,128)(2,1)}, u32[]{:S(2)}) copy-start(bf16[272,128]{1,0:T(8,128)(2,1)} %get-tuple-element.38.refs_0_) | copy-start | bytes 208900
  14.0 8.0 %collective-permute-start.4 = (bf16[64,1024]{1,0:T(8,128)(2,1)S(1)}, bf16[64,1024]{1,0:T(8,128)(2,1)S(1)}, u32[]{:S(2)}, u32[]{:S(2)}) collective-permute-start(bf16[64,1024]{1,0:T(8,128)(2,1)S(1)} %shard_map.66), channel_id=1, source_target_pairs={{0,12},{1,5},{4,0},{5,9},{8,4},{9,13},{12,8},{13,1},{2,14},{3,7},{... | collective-permute-start | bytes 393224 | tf_op jit(solution)/shard_map/ppermute | solution.py:41
  18.0 6.6 %collective-permute-start.5 = (bf16[64,1024]{1,0:T(8,128)(2,1)S(1)}, bf16[64,1024]{1,0:T(8,128)(2,1)S(1)}, u32[]{:S(2)}, u32[]{:S(2)}) collective-permute-start(bf16[64,1024]{1,0:T(8,128)(2,1)S(1)} %shard_map.67), channel_id=1, source_target_pairs={{0,12},{1,5},{4,0},{5,9},{8,4},{9,13},{12,8},{13,1},{2,14},{3,7},{... | collective-permute-start | bytes 393224 | tf_op jit(solution)/shard_map/ppermute | solution.py:41
  24.7 1.4 %collective-permute-start.6 = (bf16[32,2048]{1,0:T(8,128)(2,1)S(1)}, bf16[32,2048]{1,0:T(8,128)(2,1)S(1)}, u32[]{:S(2)}, u32[]{:S(2)}) collective-permute-start(bf16[32,2048]{1,0:T(8,128)(2,1)S(1)} %slice.39), channel_id=1, source_target_pairs={{0,1},{1,0},{2,3},{3,2},{4,5},{5,4},{6,7},{7,6},{8,9},{9,8},{10,11... | collective-permute-start | bytes 393224 | tf_op jit(solution)/shard_map/ppermute | solution.py:32

commit v13 on v12

--- a/solution.py
+++ b/solution.py
@@ -8,7 +8,7 @@
 from jax.sharding import PartitionSpec as P
 
 LEAF = 128
-BATCH = 12
+BATCH = 16
 DEPTH = 48
 
 kernel_scale = 0.0625 / (4.0 * 3.141592653589793)

time: 27.1 us -> 26.8 us (0.989); the launches traced: 26.8 us -> 27.1 us
  waiting for transfers between devices: 2.66 us -> 3.64 us
  starting transfers between devices: 8.83 us -> 8.17 us
    ppermute x4, waiting for transfers between devices: 1.32 us -> 2.3 us  [crossed(): return lax.ppermute(block, ('blk', 'rhs'), pairs)]
    ppermute x4, starting transfers between devices: 7.25 us -> 6.6 us  [crossed(): return lax.ppermute(block, ('blk', 'rhs'), pairs)]
  transfers between devices with their start and end apart: 7 -> 7, of which waited for: 2 -> 3; matrix products, arithmetic and copies ran while one was open for 1% -> 1% of each run, Pallas kernels for 53% -> 52%
where the time goes in v13:
time: 26.8 us; the launch traced here: 27.1 us
  Pallas kernels  14.1 us (53%)
  starting transfers between devices  8.17 us (30%)
  waiting for transfers between devices  3.64 us (14%)
  other arithmetic  0.77 us (3%)
    pallas_call x3, Pallas kernels, near_sum(): pl.pallas_call(functools.partial(near_kernel, base, part), out_shape=jax....  8.29 us
    ppermute x4, starting transfers between devices, crossed(): return lax.ppermute(block, ('blk', 'rhs'), pairs)  6.6 us
    pallas_call x1, Pallas kernels, on_device(): pl.pallas_call(functools.partial(far_kernel_phased, seg_size), out_shape=...  2.62 us
    pallas_call x1, Pallas kernels, on_device(): pl.pallas_call(functools.partial(list_kernel, seg_size), out_shape=[jax.S...  2.51 us
    ppermute x4, waiting for transfers between devices, crossed(): return lax.ppermute(block, ('blk', 'rhs'), pairs)  2.3 us
    ppermute x3, starting transfers between devices, shifted(): lax.ppermute(block, axis, [(i, (i + shift) % count) for i in range(count)])  1.57 us
    ppermute x3, waiting for transfers between devices, shifted(): lax.ppermute(block, axis, [(i, (i + shift) % count) for i in range(count)])  1.34 us
    pallas_call x1, Pallas kernels, on_device(): pl.pallas_call(functools.partial(feature_kernel, seg_size, own_clusters),...  0.72 us
  transfers between devices with their start and end apart: 7, of which 3 were waited for; matrix products, arithmetic and copies ran while one was open for 1% of the time, Pallas kernels for 52%

profile of v13, /device:TPU:0, one launch (start us, length us, event | category | flops | bytes accessed | tf_op | source)
XLA Modules:
  0.0 27.1 jit_solution(6541833072077856241)
XLA Ops:
  0.0 0.5 %collective-permute-start.1 = (bf16[32,4096]{1,0:T(8,128)(2,1)}, bf16[32,4096]{1,0:T(8,128)(2,1)S(1)}, u32[]{:S(2)}, u32[]{:S(2)}) collective-permute-start(bf16[32,4096]{1,0:T(8,128)(2,1)} %bitcast.3), channel_id=1, source_target_pairs={{0,1},{1,0},{2,3},{3,2},{4,5},{5,4},{6,7},{7,6},{8,9},{9,8},{10,11... | collective-permute-start | bytes 786440 | tf_op jit(solution)/shard_map/ppermute | solution.py:32
  0.5 2.5 %shard_map.64 = (s32[8,128]{1,0:T(8,128)}, bf16[272,128]{1,0:T(8,128)(2,1)}) custom-call(s32[16,27]{1,0:T(8,128)} %near_hbm.1, bf16[32,4096]{1,0:T(8,128)(2,1)} %basis_ref.1, bf16[32,4096]{1,0:T(8,128)(2,1)} %bitcast.4), custom_call_target="tpu_custom_call" | custom-call | flops 3000000000 | tf_op jit(solution)/shard_map/pallas_call | solution.py:360
  3.1 2.7 %collective-permute-start = (bf16[272,128]{1,0:T(8,128)(2,1)}, bf16[272,128]{1,0:T(8,128)(2,1)S(1)}, u32[]{:S(2)}, u32[]{:S(2)}) collective-permute-start(bf16[272,128]{1,0:T(8,128)(2,1)} %get-tuple-element.38.refs_0_), channel_id=1, source_target_pairs={{0,4},{1,13},{4,8},{5,1},{8,12},{9,5},{12,0},{13,9},{2,6},{3,15},{... | collective-permute-start | bytes 208904 | tf_op jit(solution)/shard_map/ppermute | solution.py:41
  5.7 0.7 %shard_map.65 = (bf16[33,48,128]{2,1,0:T(8,128)(2,1)S(1)}, bf16[32,128,48]{2,1,0:T(8,128)(2,1)S(1)}) custom-call(f32[3,16384]{1,0:T(4,128)S(1)} %copy-done.4), custom_call_target="tpu_custom_call" | custom-call | flops 700000000 | tf_op jit(solution)/shard_map/pallas_call | solution.py:380
  6.5 2.1 %collective-permute-start.2 = (bf16[272,128]{1,0:T(8,128)(2,1)}, bf16[272,128]{1,0:T(8,128)(2,1)S(1)}, u32[]{:S(2)}, u32[]{:S(2)}) collective-permute-start(bf16[272,128]{1,0:T(8,128)(2,1)} %get-tuple-element.38.refs_0_), channel_id=1, source_target_pairs={{0,12},{1,5},{4,0},{5,9},{8,4},{9,13},{12,8},{13,1},{2,14},{3,7},{... | collective-permute-start | bytes 208904 | tf_op jit(solution)/shard_map/ppermute | solution.py:41
  8.6 1.0 %collective-permute-start.3 = (bf16[272,128]{1,0:T(8,128)(2,1)}, bf16[272,128]{1,0:T(8,128)(2,1)S(1)}, u32[]{:S(2)}, u32[]{:S(2)}) collective-permute-start(bf16[272,128]{1,0:T(8,128)(2,1)} %get-tuple-element.38.refs_0_), channel_id=1, source_target_pairs={{0,8},{4,12},{8,0},{12,4},{1,9},{5,13},{9,1},{13,5},{2,10},{6,14},... | collective-permute-start | bytes 208904 | tf_op jit(solution)/shard_map/ppermute | solution.py:32
  9.6 0.1 constant_dynamic-slice_fusion
  9.6 0.1 copy.8
  9.7 1.3 %collective-permute-done.refs_3_ = bf16[272,128]{1,0:T(8,128)(2,1)S(1)} collective-permute-done((bf16[272,128]{1,0:T(8,128)(2,1)}, bf16[272,128]{1,0:T(8,128)(2,1)S(1)}, u32[]{:S(2)}, u32[]{:S(2)}) %collective-permute-start) | collective-permute-done | bytes 69664 | tf_op jit(solution)/shard_map/ppermute | solution.py:41
  11.1 0.0 collective-permute-done.1.other_ref
  11.1 2.6 %shard_map.66 = bf16[64,1024]{1,0:T(8,128)(2,1)S(1)} custom-call(s32[8,128]{1,0:T(8,128)S(1)} %fusion.9.list_ref, bf16[33,48,128]{2,1,0:T(8,128)(2,1)S(1)} %get-tuple-element.30.target_ref, bf16[32,128,48]{2,1,0:T(8,128)(2,1)S(1)} %get-tuple-element.31.source_ref, bf16[32,4096]{1,0:T(8,128)(2,1)S(1)} %bitcast.5, ...), custom_call_target="tpu_custom_call" | custom-call | flops 20000000000 | tf_op jit(solution)/shard_map/pallas_call | solution.py:269
  13.7 0.0 copy-start.3
  13.7 0.0 copy-start.5
  13.7 0.0 copy-start.6
  13.7 1.7 %collective-permute-start.4 = (bf16[64,1024]{1,0:T(8,128)(2,1)S(1)}, bf16[64,1024]{1,0:T(8,128)(2,1)S(1)}, u32[]{:S(2)}, u32[]{:S(2)}) collective-permute-start(bf16[64,1024]{1,0:T(8,128)(2,1)S(1)} %shard_map.66), channel_id=1, source_target_pairs={{0,12},{1,5},{4,0},{5,9},{8,4},{9,13},{12,8},{13,1},{2,14},{3,7},{... | collective-permute-start | bytes 393224 | tf_op jit(solution)/shard_map/ppermute | solution.py:41
  15.4 3.1 %shard_map.67 = bf16[64,1024]{1,0:T(8,128)(2,1)S(1)} custom-call(s32[8,128]{1,0:T(8,128)S(1)} %fusion.9.list_ref, bf16[33,48,128]{2,1,0:T(8,128)(2,1)S(1)} %get-tuple-element.30.target_ref, bf16[32,128,48]{2,1,0:T(8,128)(2,1)S(1)} %get-tuple-element.31.source_ref, bf16[32,4096]{1,0:T(8,128)(2,1)S(1)} %bitcast.6, ...), custom_call_target="tpu_custom_call" | custom-call | flops 20000000000 | tf_op jit(solution)/shard_map/pallas_call | solution.py:269
  18.5 0.1 collective-permute-start.5
  18.6 2.6 %shard_map.68 = f32[64,2048]{1,0:T(8,128)S(1)} custom-call(s32[8,128]{1,0:T(8,128)S(1)} %copy-done.2, bf16[33,48,128]{2,1,0:T(8,128)(2,1)S(1)} %get-tuple-element.30.target_ref, bf16[32,128,48]{2,1,0:T(8,128)(2,1)S(1)} %get-tuple-element.31.source_ref, bf16[32,4096]{1,0:T(8,128)(2,1)S(1)} %bitcast.7, bf16[32,4096]{1,0:T(8,128)(2,1)S(1)} %collective-permute-done.1.other_ref), custom_call_target="tpu_custom_call" | custom-call | flops 500000000 | tf_op jit(solution)/shard_map/pallas_call | solution.py:269
  21.2 0.0 collective-permute-done.2.refs_1_
  21.3 2.6 %shard_map.69 = f32[32,2048]{1,0:T(8,128)S(1)} custom-call(s32[16,32]{1,0:T(8,128)S(1)} %fusion.7.far_ref, bf16[16,32,32,32]{3,2,1,0:T(8,128)(2,1)S(1)} %copy-done.3, bf16[32,4096]{1,0:T(8,128)(2,1)S(1)} %copy-done.5, bf16[272,128]{1,0:T(8,128)(2,1)S(1)} %copy-done.6, bf16[272,128]{1,0:T(8,128)(2,1)S(1)} %collective-permute-done.2.refs_1_, ...), custom_call_target="tpu_custom_call" | custom-call | flops 20000000000 | tf_op jit(solution)/shard_map/pallas_call | solution.py:418
  23.9 1.0 %collective-permute-done.5 = bf16[64,1024]{1,0:T(8,128)(2,1)S(1)} collective-permute-done((bf16[64,1024]{1,0:T(8,128)(2,1)S(1)}, bf16[64,1024]{1,0:T(8,128)(2,1)S(1)}, u32[]{:S(2)}, u32[]{:S(2)}) %collective-permute-start.5) | collective-permute-done | bytes 131104 | tf_op jit(solution)/shard_map/ppermute | solution.py:41
  25.0 0.1 collective-permute-start.6
  25.0 1.3 %collective-permute-done.6 = bf16[32,2048]{1,0:T(8,128)(2,1)S(1)} collective-permute-done((bf16[32,2048]{1,0:T(8,128)(2,1)S(1)}, bf16[32,2048]{1,0:T(8,128)(2,1)S(1)}, u32[]{:S(2)}, u32[]{:S(2)}) %collective-permute-start.6) | collective-permute-done | bytes 131104 | tf_op jit(solution)/shard_map/ppermute | solution.py:32
  26.4 0.7 %fusion.2 = bf16[2048,32]{0,1:T(8,128)(2,1)} fusion(f32[32,2048]{1,0:T(8,128)S(1)} %shard_map.69, bf16[32,2048]{1,0:T(8,128)(2,1)S(1)} %collective-permute-done.6, f32[64,2048]{1,0:T(8,128)S(1)} %convert_add_fusion), kind=kLoop, calls=%fused_computation.5 | loop fusion | flops 262144 | bytes 786432 | tf_op jit(solution)/shard_map/transpose | solution.py:444
  (18 shorter events, 0.1 us)
Async XLA Ops:
  0.0 9.6 %copy-start = (s32[128,32]{0,1:T(8,128)S(1)}, s32[128,32]{0,1:T(8,128)}, u32[]{:S(2)}) copy-start(s32[128,32]{0,1:T(8,128)} %param.11) | copy-start | bytes 49156
  0.0 5.7 %copy-start.4 = (f32[3,16384]{1,0:T(4,128)S(1)}, f32[3,16384]{1,0:T(4,128)}, u32[]{:S(2)}) copy-start(f32[3,16384]{1,0:T(4,128)} %points_ref) | copy-start | bytes 589828
  0.0 11.1 %copy-start.1 = (bf16[4096,32]{0,1:T(8,128)(2,1)S(1)}, bf16[4096,32]{0,1:T(8,128)(2,1)}, u32[]{:S(2)}) copy-start(bf16[4096,32]{0,1:T(8,128)(2,1)} %param.7) | copy-start | bytes 786436
  0.0 11.0 %collective-permute-start.1 = (bf16[32,4096]{1,0:T(8,128)(2,1)}, bf16[32,4096]{1,0:T(8,128)(2,1)S(1)}, u32[]{:S(2)}, u32[]{:S(2)}) collective-permute-start(bf16[32,4096]{1,0:T(8,128)(2,1)} %bitcast.3), channel_id=1, source_target_pairs={{0,1},{1,0},{2,3},{3,2},{4,5},{5,4},{6,7},{7,6},{8,9},{9,8},{10,11... | collective-permute-start | bytes 786440 | tf_op jit(solution)/shard_map/ppermute | solution.py:32
  3.1 8.0 %collective-permute-start = (bf16[272,128]{1,0:T(8,128)(2,1)}, bf16[272,128]{1,0:T(8,128)(2,1)S(1)}, u32[]{:S(2)}, u32[]{:S(2)}) collective-permute-start(bf16[272,128]{1,0:T(8,128)(2,1)} %get-tuple-element.38.refs_0_), channel_id=1, source_target_pairs={{0,4},{1,13},{4,8},{5,1},{8,12},{9,5},{12,0},{13,9},{2,6},{3,15},{... | collective-permute-start | bytes 208904 | tf_op jit(solution)/shard_map/ppermute | solution.py:41
  6.5 14.8 %collective-permute-start.2 = (bf16[272,128]{1,0:T(8,128)(2,1)}, bf16[272,128]{1,0:T(8,128)(2,1)S(1)}, u32[]{:S(2)}, u32[]{:S(2)}) collective-permute-start(bf16[272,128]{1,0:T(8,128)(2,1)} %get-tuple-element.38.refs_0_), channel_id=1, source_target_pairs={{0,12},{1,5},{4,0},{5,9},{8,4},{9,13},{12,8},{13,1},{2,14},{3,7},{... | collective-permute-start | bytes 208904 | tf_op jit(solution)/shard_map/ppermute | solution.py:41
  8.6 12.7 %collective-permute-start.3 = (bf16[272,128]{1,0:T(8,128)(2,1)}, bf16[272,128]{1,0:T(8,128)(2,1)S(1)}, u32[]{:S(2)}, u32[]{:S(2)}) collective-permute-start(bf16[272,128]{1,0:T(8,128)(2,1)} %get-tuple-element.38.refs_0_), channel_id=1, source_target_pairs={{0,8},{4,12},{8,0},{12,4},{1,9},{5,13},{9,1},{13,5},{2,10},{6,14},... | collective-permute-start | bytes 208904 | tf_op jit(solution)/shard_map/ppermute | solution.py:32
  13.7 4.9 %copy-start.2 = (s32[8,128]{1,0:T(8,128)S(1)}, s32[8,128]{1,0:T(8,128)}, u32[]{:S(2)}) copy-start(s32[8,128]{1,0:T(8,128)} %get-tuple-element.34.list_ref) | copy-start | bytes 12292
  13.7 7.6 %copy-start.3 = (bf16[16,32,32,32]{3,2,1,0:T(8,128)(2,1)S(1)}, bf16[16,32,32,32]{3,2,1,0:T(8,128)(2,1)}, u32[]{:S(2)}) copy-start(bf16[16,32,32,32]{3,2,1,0:T(8,128)(2,1)} %couplings_ref.1) | copy-start | bytes 3145732
  13.7 7.6 %copy-start.5 = (bf16[32,4096]{1,0:T(8,128)(2,1)S(1)}, bf16[32,4096]{1,0:T(8,128)(2,1)}, u32[]{:S(2)}) copy-start(bf16[32,4096]{1,0:T(8,128)(2,1)} %basis_ref.1) | copy-start | bytes 786436
  13.7 7.6 %copy-start.6 = (bf16[272,128]{1,0:T(8,128)(2,1)S(1)}, bf16[272,128]{1,0:T(8,128)(2,1)}, u32[]{:S(2)}) copy-start(bf16[272,128]{1,0:T(8,128)(2,1)} %get-tuple-element.38.refs_0_) | copy-start | bytes 208900
  13.7 7.5 %collective-permute-start.4 = (bf16[64,1024]{1,0:T(8,128)(2,1)S(1)}, bf16[64,1024]{1,0:T(8,128)(2,1)S(1)}, u32[]{:S(2)}, u32[]{:S(2)}) collective-permute-start(bf16[64,1024]{1,0:T(8,128)(2,1)S(1)} %shard_map.66), channel_id=1, source_target_pairs={{0,12},{1,5},{4,0},{5,9},{8,4},{9,13},{12,8},{13,1},{2,14},{3,7},{... | collective-permute-start | bytes 393224 | tf_op jit(solution)/shard_map/ppermute | solution.py:41
  18.5 6.4 %collective-permute-start.5 = (bf16[64,1024]{1,0:T(8,128)(2,1)S(1)}, bf16[64,1024]{1,0:T(8,128)(2,1)S(1)}, u32[]{:S(2)}, u32[]{:S(2)}) collective-permute-start(bf16[64,1024]{1,0:T(8,128)(2,1)S(1)} %shard_map.67), channel_id=1, source_target_pairs={{0,12},{1,5},{4,0},{5,9},{8,4},{9,13},{12,8},{13,1},{2,14},{3,7},{... | collective-permute-start | bytes 393224 | tf_op jit(solution)/shard_map/ppermute | solution.py:41
  25.0 1.4 %collective-permute-start.6 = (bf16[32,2048]{1,0:T(8,128)(2,1)S(1)}, bf16[32,2048]{1,0:T(8,128)(2,1)S(1)}, u32[]{:S(2)}, u32[]{:S(2)}) collective-permute-start(bf16[32,2048]{1,0:T(8,128)(2,1)S(1)} %slice.39), channel_id=1, source_target_pairs={{0,1},{1,0},{2,3},{3,2},{4,5},{5,4},{6,7},{7,6},{8,9},{9,8},{10,11... | collective-permute-start | bytes 393224 | tf_op jit(solution)/shard_map/ppermute | solution.py:32

commit v14 on v13

--- a/solution.py
+++ b/solution.py
@@ -80,8 +80,7 @@
     row = iota((8, LEAF), 0)
     lower = iota((LEAF, LEAF), 0)
     filler = jnp.full((1, width - near_count), -1, jnp.int32)
-    for copy in copies:
-        copy.wait()
+    copies[0].wait()
     packed = []
     for line in range(lines):
         pieces = []
@@ -143,6 +142,8 @@
     rows_end = seg_size // pack * rank
     load_ref[rows_end : rows_end + 16, :] = away.astype(bf16)
 
+    copies[1].wait()
+    copies[2].wait()
     singles = []
     for index in range(seg_size):
         at = index * LEAF

time: 26.8 us -> 26.6 us (level); the launches traced: 27.1 us -> 26.5 us
  Pallas kernels: 14.1 us -> 13.6 us
  waiting for transfers between devices: 3.64 us -> 3.19 us
  starting transfers between devices: 8.17 us -> 8.6 us
    ppermute x4, waiting for transfers between devices: 2.3 us -> 1.85 us  [crossed(): return lax.ppermute(block, ('blk', 'rhs'), pairs)]
    ppermute x4, starting transfers between devices: 6.6 us -> 7.03 us  [crossed(): return lax.ppermute(block, ('blk', 'rhs'), pairs)]
    pallas_call x3, Pallas kernels: 8.29 us -> 7.87 us  [near_sum(): pl.pallas_call(functools.partial(near_kernel, base, part), out_shape=jax....]
  transfers between devices with their start and end apart: 7 -> 7, of which waited for: 3 -> 3; matrix products, arithmetic and copies ran while one was open for 1% -> 1% of each run, Pallas kernels for 52% -> 51%
where the time goes in v14:
time: 26.6 us; the launch traced here: 26.5 us
  Pallas kernels  13.6 us (51%)
  starting transfers between devices  8.6 us (32%)
  waiting for transfers between devices  3.19 us (12%)
  other arithmetic  0.77 us (3%)
    pallas_call x3, Pallas kernels, near_sum(): pl.pallas_call(functools.partial(near_kernel, base, part), out_shape=jax....  7.87 us
    ppermute x4, starting transfers between devices, crossed(): return lax.ppermute(block, ('blk', 'rhs'), pairs)  7.03 us
    pallas_call x1, Pallas kernels, on_device(): pl.pallas_call(functools.partial(far_kernel_phased, seg_size), out_shape=...  2.63 us
    pallas_call x1, Pallas kernels, on_device(): pl.pallas_call(functools.partial(list_kernel, seg_size), out_shape=[jax.S...  2.36 us
    ppermute x4, waiting for transfers between devices, crossed(): return lax.ppermute(block, ('blk', 'rhs'), pairs)  1.85 us
    ppermute x3, starting transfers between devices, shifted(): lax.ppermute(block, axis, [(i, (i + shift) % count) for i in range(count)])  1.57 us
    ppermute x3, waiting for transfers between devices, shifted(): lax.ppermute(block, axis, [(i, (i + shift) % count) for i in range(count)])  1.34 us
    pallas_call x1, Pallas kernels, on_device(): pl.pallas_call(functools.partial(feature_kernel, seg_size, own_clusters),...  0.72 us
  transfers between devices with their start and end apart: 7, of which 3 were waited for; matrix products, arithmetic and copies ran while one was open for 1% of the time, Pallas kernels for 51%

profile of v14, /device:TPU:0, one launch (start us, length us, event | category | flops | bytes accessed | tf_op | source)
XLA Modules:
  0.0 26.5 jit_solution(11485758340743811549)
XLA Ops:
  0.0 0.5 %collective-permute-start.1 = (bf16[32,4096]{1,0:T(8,128)(2,1)}, bf16[32,4096]{1,0:T(8,128)(2,1)S(1)}, u32[]{:S(2)}, u32[]{:S(2)}) collective-permute-start(bf16[32,4096]{1,0:T(8,128)(2,1)} %bitcast.3), channel_id=1, source_target_pairs={{0,1},{1,0},{2,3},{3,2},{4,5},{5,4},{6,7},{7,6},{8,9},{9,8},{10,11... | collective-permute-start | bytes 786440 | tf_op jit(solution)/shard_map/ppermute | solution.py:32
  0.5 2.4 %shard_map.64 = (s32[8,128]{1,0:T(8,128)}, bf16[272,128]{1,0:T(8,128)(2,1)}) custom-call(s32[16,27]{1,0:T(8,128)} %near_hbm.1, bf16[32,4096]{1,0:T(8,128)(2,1)} %basis_ref.1, bf16[32,4096]{1,0:T(8,128)(2,1)} %bitcast.4), custom_call_target="tpu_custom_call" | custom-call | flops 3000000000 | tf_op jit(solution)/shard_map/pallas_call | solution.py:361
  2.9 2.7 %collective-permute-start = (bf16[272,128]{1,0:T(8,128)(2,1)}, bf16[272,128]{1,0:T(8,128)(2,1)S(1)}, u32[]{:S(2)}, u32[]{:S(2)}) collective-permute-start(bf16[272,128]{1,0:T(8,128)(2,1)} %get-tuple-element.38.refs_0_), channel_id=1, source_target_pairs={{0,4},{1,13},{4,8},{5,1},{8,12},{9,5},{12,0},{13,9},{2,6},{3,15},{... | collective-permute-start | bytes 208904 | tf_op jit(solution)/shard_map/ppermute | solution.py:41
  5.6 0.7 %shard_map.65 = (bf16[33,48,128]{2,1,0:T(8,128)(2,1)S(1)}, bf16[32,128,48]{2,1,0:T(8,128)(2,1)S(1)}) custom-call(f32[3,16384]{1,0:T(4,128)S(1)} %copy-done.4), custom_call_target="tpu_custom_call" | custom-call | flops 700000000 | tf_op jit(solution)/shard_map/pallas_call | solution.py:381
  6.3 2.1 %collective-permute-start.2 = (bf16[272,128]{1,0:T(8,128)(2,1)}, bf16[272,128]{1,0:T(8,128)(2,1)S(1)}, u32[]{:S(2)}, u32[]{:S(2)}) collective-permute-start(bf16[272,128]{1,0:T(8,128)(2,1)} %get-tuple-element.38.refs_0_), channel_id=1, source_target_pairs={{0,12},{1,5},{4,0},{5,9},{8,4},{9,13},{12,8},{13,1},{2,14},{3,7},{... | collective-permute-start | bytes 208904 | tf_op jit(solution)/shard_map/ppermute | solution.py:41
  8.4 1.0 %collective-permute-start.3 = (bf16[272,128]{1,0:T(8,128)(2,1)}, bf16[272,128]{1,0:T(8,128)(2,1)S(1)}, u32[]{:S(2)}, u32[]{:S(2)}) collective-permute-start(bf16[272,128]{1,0:T(8,128)(2,1)} %get-tuple-element.38.refs_0_), channel_id=1, source_target_pairs={{0,8},{4,12},{8,0},{12,4},{1,9},{5,13},{9,1},{13,5},{2,10},{6,14},... | collective-permute-start | bytes 208904 | tf_op jit(solution)/shard_map/ppermute | solution.py:32
  9.4 0.1 constant_dynamic-slice_fusion
  9.5 0.1 copy.8
  9.6 1.3 %collective-permute-done.refs_3_ = bf16[272,128]{1,0:T(8,128)(2,1)S(1)} collective-permute-done((bf16[272,128]{1,0:T(8,128)(2,1)}, bf16[272,128]{1,0:T(8,128)(2,1)S(1)}, u32[]{:S(2)}, u32[]{:S(2)}) %collective-permute-start) | collective-permute-done | bytes 69664 | tf_op jit(solution)/shard_map/ppermute | solution.py:41
  10.9 0.0 collective-permute-done.1.other_ref
  10.9 2.6 %shard_map.66 = bf16[64,1024]{1,0:T(8,128)(2,1)S(1)} custom-call(s32[8,128]{1,0:T(8,128)S(1)} %fusion.9.list_ref, bf16[33,48,128]{2,1,0:T(8,128)(2,1)S(1)} %get-tuple-element.30.target_ref, bf16[32,128,48]{2,1,0:T(8,128)(2,1)S(1)} %get-tuple-element.31.source_ref, bf16[32,4096]{1,0:T(8,128)(2,1)S(1)} %bitcast.5, ...), custom_call_target="tpu_custom_call" | custom-call | flops 20000000000 | tf_op jit(solution)/shard_map/pallas_call | solution.py:270
  13.5 0.0 copy-start.3
  13.6 0.0 copy-start.5
  13.6 0.0 copy-start.6
  13.6 1.7 %collective-permute-start.4 = (bf16[64,1024]{1,0:T(8,128)(2,1)S(1)}, bf16[64,1024]{1,0:T(8,128)(2,1)S(1)}, u32[]{:S(2)}, u32[]{:S(2)}) collective-permute-start(bf16[64,1024]{1,0:T(8,128)(2,1)S(1)} %shard_map.66), channel_id=1, source_target_pairs={{0,12},{1,5},{4,0},{5,9},{8,4},{9,13},{12,8},{13,1},{2,14},{3,7},{... | collective-permute-start | bytes 393224 | tf_op jit(solution)/shard_map/ppermute | solution.py:41
  15.3 2.6 %shard_map.67 = bf16[64,1024]{1,0:T(8,128)(2,1)S(1)} custom-call(s32[8,128]{1,0:T(8,128)S(1)} %fusion.9.list_ref, bf16[33,48,128]{2,1,0:T(8,128)(2,1)S(1)} %get-tuple-element.30.target_ref, bf16[32,128,48]{2,1,0:T(8,128)(2,1)S(1)} %get-tuple-element.31.source_ref, bf16[32,4096]{1,0:T(8,128)(2,1)S(1)} %bitcast.6, ...), custom_call_target="tpu_custom_call" | custom-call | flops 20000000000 | tf_op jit(solution)/shard_map/pallas_call | solution.py:270
  17.9 0.6 %collective-permute-start.5 = (bf16[64,1024]{1,0:T(8,128)(2,1)S(1)}, bf16[64,1024]{1,0:T(8,128)(2,1)S(1)}, u32[]{:S(2)}, u32[]{:S(2)}) collective-permute-start(bf16[64,1024]{1,0:T(8,128)(2,1)S(1)} %shard_map.67), channel_id=1, source_target_pairs={{0,12},{1,5},{4,0},{5,9},{8,4},{9,13},{12,8},{13,1},{2,14},{3,7},{... | collective-permute-start | bytes 393224 | tf_op jit(solution)/shard_map/ppermute | solution.py:41
  18.4 2.6 %shard_map.68 = f32[64,2048]{1,0:T(8,128)S(1)} custom-call(s32[8,128]{1,0:T(8,128)S(1)} %copy-done.2, bf16[33,48,128]{2,1,0:T(8,128)(2,1)S(1)} %get-tuple-element.30.target_ref, bf16[32,128,48]{2,1,0:T(8,128)(2,1)S(1)} %get-tuple-element.31.source_ref, bf16[32,4096]{1,0:T(8,128)(2,1)S(1)} %bitcast.7, bf16[32,4096]{1,0:T(8,128)(2,1)S(1)} %collective-permute-done.1.other_ref), custom_call_target="tpu_custom_call" | custom-call | flops 500000000 | tf_op jit(solution)/shard_map/pallas_call | solution.py:270
  21.1 0.0 collective-permute-done.2.refs_1_
  21.1 2.6 %shard_map.69 = f32[32,2048]{1,0:T(8,128)S(1)} custom-call(s32[16,32]{1,0:T(8,128)S(1)} %fusion.7.far_ref, bf16[16,32,32,32]{3,2,1,0:T(8,128)(2,1)S(1)} %copy-done.3, bf16[32,4096]{1,0:T(8,128)(2,1)S(1)} %copy-done.5, bf16[272,128]{1,0:T(8,128)(2,1)S(1)} %copy-done.6, bf16[272,128]{1,0:T(8,128)(2,1)S(1)} %collective-permute-done.2.refs_1_, ...), custom_call_target="tpu_custom_call" | custom-call | flops 20000000000 | tf_op jit(solution)/shard_map/pallas_call | solution.py:419
  23.8 0.5 %collective-permute-done.5 = bf16[64,1024]{1,0:T(8,128)(2,1)S(1)} collective-permute-done((bf16[64,1024]{1,0:T(8,128)(2,1)S(1)}, bf16[64,1024]{1,0:T(8,128)(2,1)S(1)}, u32[]{:S(2)}, u32[]{:S(2)}) %collective-permute-start.5) | collective-permute-done | bytes 131104 | tf_op jit(solution)/shard_map/ppermute | solution.py:41
  24.4 0.1 collective-permute-start.6
  24.5 1.3 %collective-permute-done.6 = bf16[32,2048]{1,0:T(8,128)(2,1)S(1)} collective-permute-done((bf16[32,2048]{1,0:T(8,128)(2,1)S(1)}, bf16[32,2048]{1,0:T(8,128)(2,1)S(1)}, u32[]{:S(2)}, u32[]{:S(2)}) %collective-permute-start.6) | collective-permute-done | bytes 131104 | tf_op jit(solution)/shard_map/ppermute | solution.py:32
  25.8 0.7 %fusion.2 = bf16[2048,32]{0,1:T(8,128)(2,1)} fusion(f32[32,2048]{1,0:T(8,128)S(1)} %shard_map.69, bf16[32,2048]{1,0:T(8,128)(2,1)S(1)} %collective-permute-done.6, f32[64,2048]{1,0:T(8,128)S(1)} %convert_add_fusion), kind=kLoop, calls=%fused_computation.5 | loop fusion | flops 262144 | bytes 786432 | tf_op jit(solution)/shard_map/transpose | solution.py:445
  (18 shorter events, 0.1 us)
Async XLA Ops:
  0.0 9.4 %copy-start = (s32[128,32]{0,1:T(8,128)S(1)}, s32[128,32]{0,1:T(8,128)}, u32[]{:S(2)}) copy-start(s32[128,32]{0,1:T(8,128)} %param.11) | copy-start | bytes 49156
  0.0 5.6 %copy-start.4 = (f32[3,16384]{1,0:T(4,128)S(1)}, f32[3,16384]{1,0:T(4,128)}, u32[]{:S(2)}) copy-start(f32[3,16384]{1,0:T(4,128)} %points_ref) | copy-start | bytes 589828
  0.0 10.9 %copy-start.1 = (bf16[4096,32]{0,1:T(8,128)(2,1)S(1)}, bf16[4096,32]{0,1:T(8,128)(2,1)}, u32[]{:S(2)}) copy-start(bf16[4096,32]{0,1:T(8,128)(2,1)} %param.7) | copy-start | bytes 786436
  0.0 10.9 %collective-permute-start.1 = (bf16[32,4096]{1,0:T(8,128)(2,1)}, bf16[32,4096]{1,0:T(8,128)(2,1)S(1)}, u32[]{:S(2)}, u32[]{:S(2)}) collective-permute-start(bf16[32,4096]{1,0:T(8,128)(2,1)} %bitcast.3), channel_id=1, source_target_pairs={{0,1},{1,0},{2,3},{3,2},{4,5},{5,4},{6,7},{7,6},{8,9},{9,8},{10,11... | collective-permute-start | bytes 786440 | tf_op jit(solution)/shard_map/ppermute | solution.py:32
  2.9 8.0 %collective-permute-start = (bf16[272,128]{1,0:T(8,128)(2,1)}, bf16[272,128]{1,0:T(8,128)(2,1)S(1)}, u32[]{:S(2)}, u32[]{:S(2)}) collective-permute-start(bf16[272,128]{1,0:T(8,128)(2,1)} %get-tuple-element.38.refs_0_), channel_id=1, source_target_pairs={{0,4},{1,13},{4,8},{5,1},{8,12},{9,5},{12,0},{13,9},{2,6},{3,15},{... | collective-permute-start | bytes 208904 | tf_op jit(solution)/shard_map/ppermute | solution.py:41
  6.3 14.8 %collective-permute-start.2 = (bf16[272,128]{1,0:T(8,128)(2,1)}, bf16[272,128]{1,0:T(8,128)(2,1)S(1)}, u32[]{:S(2)}, u32[]{:S(2)}) collective-permute-start(bf16[272,128]{1,0:T(8,128)(2,1)} %get-tuple-element.38.refs_0_), channel_id=1, source_target_pairs={{0,12},{1,5},{4,0},{5,9},{8,4},{9,13},{12,8},{13,1},{2,14},{3,7},{... | collective-permute-start | bytes 208904 | tf_op jit(solution)/shard_map/ppermute | solution.py:41
  8.4 12.7 %collective-permute-start.3 = (bf16[272,128]{1,0:T(8,128)(2,1)}, bf16[272,128]{1,0:T(8,128)(2,1)S(1)}, u32[]{:S(2)}, u32[]{:S(2)}) collective-permute-start(bf16[272,128]{1,0:T(8,128)(2,1)} %get-tuple-element.38.refs_0_), channel_id=1, source_target_pairs={{0,8},{4,12},{8,0},{12,4},{1,9},{5,13},{9,1},{13,5},{2,10},{6,14},... | collective-permute-start | bytes 208904 | tf_op jit(solution)/shard_map/ppermute | solution.py:32
  13.5 4.9 %copy-start.2 = (s32[8,128]{1,0:T(8,128)S(1)}, s32[8,128]{1,0:T(8,128)}, u32[]{:S(2)}) copy-start(s32[8,128]{1,0:T(8,128)} %get-tuple-element.34.list_ref) | copy-start | bytes 12292
  13.5 7.6 %copy-start.3 = (bf16[16,32,32,32]{3,2,1,0:T(8,128)(2,1)S(1)}, bf16[16,32,32,32]{3,2,1,0:T(8,128)(2,1)}, u32[]{:S(2)}) copy-start(bf16[16,32,32,32]{3,2,1,0:T(8,128)(2,1)} %couplings_ref.1) | copy-start | bytes 3145732
  13.6 7.6 %copy-start.5 = (bf16[32,4096]{1,0:T(8,128)(2,1)S(1)}, bf16[32,4096]{1,0:T(8,128)(2,1)}, u32[]{:S(2)}) copy-start(bf16[32,4096]{1,0:T(8,128)(2,1)} %basis_ref.1) | copy-start | bytes 786436
  13.6 7.6 %copy-start.6 = (bf16[272,128]{1,0:T(8,128)(2,1)S(1)}, bf16[272,128]{1,0:T(8,128)(2,1)}, u32[]{:S(2)}) copy-start(bf16[272,128]{1,0:T(8,128)(2,1)} %get-tuple-element.38.refs_0_) | copy-start | bytes 208900
  13.6 7.5 %collective-permute-start.4 = (bf16[64,1024]{1,0:T(8,128)(2,1)S(1)}, bf16[64,1024]{1,0:T(8,128)(2,1)S(1)}, u32[]{:S(2)}, u32[]{:S(2)}) collective-permute-start(bf16[64,1024]{1,0:T(8,128)(2,1)S(1)} %shard_map.66), channel_id=1, source_target_pairs={{0,12},{1,5},{4,0},{5,9},{8,4},{9,13},{12,8},{13,1},{2,14},{3,7},{... | collective-permute-start | bytes 393224 | tf_op jit(solution)/shard_map/ppermute | solution.py:41
  17.9 6.4 %collective-permute-start.5 = (bf16[64,1024]{1,0:T(8,128)(2,1)S(1)}, bf16[64,1024]{1,0:T(8,128)(2,1)S(1)}, u32[]{:S(2)}, u32[]{:S(2)}) collective-permute-start(bf16[64,1024]{1,0:T(8,128)(2,1)S(1)} %shard_map.67), channel_id=1, source_target_pairs={{0,12},{1,5},{4,0},{5,9},{8,4},{9,13},{12,8},{13,1},{2,14},{3,7},{... | collective-permute-start | bytes 393224 | tf_op jit(solution)/shard_map/ppermute | solution.py:41
  24.4 1.4 %collective-permute-start.6 = (bf16[32,2048]{1,0:T(8,128)(2,1)S(1)}, bf16[32,2048]{1,0:T(8,128)(2,1)S(1)}, u32[]{:S(2)}, u32[]{:S(2)}) collective-permute-start(bf16[32,2048]{1,0:T(8,128)(2,1)S(1)} %slice.39), channel_id=1, source_target_pairs={{0,1},{1,0},{2,3},{3,2},{4,5},{5,4},{6,7},{7,6},{8,9},{9,8},{10,11... | collective-permute-start | bytes 393224 | tf_op jit(solution)/shard_map/ppermute | solution.py:32

commit v15 on v14

--- a/solution.py
+++ b/solution.py
@@ -8,7 +8,7 @@
 from jax.sharding import PartitionSpec as P
 
 LEAF = 128
-BATCH = 16
+BATCH = 18
 DEPTH = 48
 
 kernel_scale = 0.0625 / (4.0 * 3.141592653589793)

time: 26.6 us -> 26.6 us (level)
  waiting for transfers between devices: 3.19 us -> 2.73 us
  starting transfers between devices: 8.6 us -> 8.89 us
    ppermute x4, waiting for transfers between devices: 1.85 us -> 1.39 us  [crossed(): return lax.ppermute(block, ('blk', 'rhs'), pairs)]
    ppermute x4, starting transfers between devices: 7.03 us -> 7.32 us  [crossed(): return lax.ppermute(block, ('blk', 'rhs'), pairs)]
where the time goes in v15:
time: 26.6 us; the launch traced here: 26.3 us
  Pallas kernels  13.5 us (51%)
  starting transfers between devices  8.89 us (33%)
  waiting for transfers between devices  2.73 us (10%)
  other arithmetic  0.77 us (3%)
    pallas_call x3, Pallas kernels, near_sum(): pl.pallas_call(functools.partial(near_kernel, base, part), out_shape=jax....  7.82 us
    ppermute x4, starting transfers between devices, crossed(): return lax.ppermute(block, ('blk', 'rhs'), pairs)  7.32 us
    pallas_call x1, Pallas kernels, on_device(): pl.pallas_call(functools.partial(far_kernel_phased, seg_size), out_shape=...  2.63 us
    pallas_call x1, Pallas kernels, on_device(): pl.pallas_call(functools.partial(list_kernel, seg_size), out_shape=[jax.S...  2.36 us
    ppermute x3, starting transfers between devices, shifted(): lax.ppermute(block, axis, [(i, (i + shift) % count) for i in range(count)])  1.57 us
    ppermute x4, waiting for transfers between devices, crossed(): return lax.ppermute(block, ('blk', 'rhs'), pairs)  1.39 us
    ppermute x3, waiting for transfers between devices, shifted(): lax.ppermute(block, axis, [(i, (i + shift) % count) for i in range(count)])  1.34 us
    pallas_call x1, Pallas kernels, on_device(): pl.pallas_call(functools.partial(feature_kernel, seg_size, own_clusters),...  0.72 us
  transfers between devices with their start and end apart: 7, of which 3 were waited for; matrix products, arithmetic and copies ran while one was open for 1% of the time, Pallas kernels for 51%

profile of v15, /device:TPU:0, one launch (start us, length us, event | category | flops | bytes accessed | tf_op | source)
XLA Modules:
  0.0 26.3 jit_solution(7062775263319643622)
XLA Ops:
  0.0 0.5 %collective-permute-start.1 = (bf16[32,4096]{1,0:T(8,128)(2,1)}, bf16[32,4096]{1,0:T(8,128)(2,1)S(1)}, u32[]{:S(2)}, u32[]{:S(2)}) collective-permute-start(bf16[32,4096]{1,0:T(8,128)(2,1)} %bitcast.3), channel_id=1, source_target_pairs={{0,1},{1,0},{2,3},{3,2},{4,5},{5,4},{6,7},{7,6},{8,9},{9,8},{10,11... | collective-permute-start | bytes 786440 | tf_op jit(solution)/shard_map/ppermute | solution.py:32
  0.5 2.4 %shard_map.64 = (s32[8,128]{1,0:T(8,128)}, bf16[272,128]{1,0:T(8,128)(2,1)}) custom-call(s32[16,27]{1,0:T(8,128)} %near_hbm.1, bf16[32,4096]{1,0:T(8,128)(2,1)} %basis_ref.1, bf16[32,4096]{1,0:T(8,128)(2,1)} %bitcast.4), custom_call_target="tpu_custom_call" | custom-call | flops 3000000000 | tf_op jit(solution)/shard_map/pallas_call | solution.py:361
  2.9 2.7 %collective-permute-start = (bf16[272,128]{1,0:T(8,128)(2,1)}, bf16[272,128]{1,0:T(8,128)(2,1)S(1)}, u32[]{:S(2)}, u32[]{:S(2)}) collective-permute-start(bf16[272,128]{1,0:T(8,128)(2,1)} %get-tuple-element.38.refs_0_), channel_id=1, source_target_pairs={{0,4},{1,13},{4,8},{5,1},{8,12},{9,5},{12,0},{13,9},{2,6},{3,15},{... | collective-permute-start | bytes 208904 | tf_op jit(solution)/shard_map/ppermute | solution.py:41
  5.6 0.7 %shard_map.65 = (bf16[33,48,128]{2,1,0:T(8,128)(2,1)S(1)}, bf16[32,128,48]{2,1,0:T(8,128)(2,1)S(1)}) custom-call(f32[3,16384]{1,0:T(4,128)S(1)} %copy-done.4), custom_call_target="tpu_custom_call" | custom-call | flops 700000000 | tf_op jit(solution)/shard_map/pallas_call | solution.py:381
  6.3 2.1 %collective-permute-start.2 = (bf16[272,128]{1,0:T(8,128)(2,1)}, bf16[272,128]{1,0:T(8,128)(2,1)S(1)}, u32[]{:S(2)}, u32[]{:S(2)}) collective-permute-start(bf16[272,128]{1,0:T(8,128)(2,1)} %get-tuple-element.38.refs_0_), channel_id=1, source_target_pairs={{0,12},{1,5},{4,0},{5,9},{8,4},{9,13},{12,8},{13,1},{2,14},{3,7},{... | collective-permute-start | bytes 208904 | tf_op jit(solution)/shard_map/ppermute | solution.py:41
  8.4 1.0 %collective-permute-start.3 = (bf16[272,128]{1,0:T(8,128)(2,1)}, bf16[272,128]{1,0:T(8,128)(2,1)S(1)}, u32[]{:S(2)}, u32[]{:S(2)}) collective-permute-start(bf16[272,128]{1,0:T(8,128)(2,1)} %get-tuple-element.38.refs_0_), channel_id=1, source_target_pairs={{0,8},{4,12},{8,0},{12,4},{1,9},{5,13},{9,1},{13,5},{2,10},{6,14},... | collective-permute-start | bytes 208904 | tf_op jit(solution)/shard_map/ppermute | solution.py:32
  9.4 0.1 constant_dynamic-slice_fusion
  9.5 0.1 copy.8
  9.6 1.3 %collective-permute-done.refs_3_ = bf16[272,128]{1,0:T(8,128)(2,1)S(1)} collective-permute-done((bf16[272,128]{1,0:T(8,128)(2,1)}, bf16[272,128]{1,0:T(8,128)(2,1)S(1)}, u32[]{:S(2)}, u32[]{:S(2)}) %collective-permute-start) | collective-permute-done | bytes 69664 | tf_op jit(solution)/shard_map/ppermute | solution.py:41
  10.9 2.5 %shard_map.66 = bf16[64,1024]{1,0:T(8,128)(2,1)S(1)} custom-call(s32[8,128]{1,0:T(8,128)S(1)} %fusion.9.list_ref, bf16[33,48,128]{2,1,0:T(8,128)(2,1)S(1)} %get-tuple-element.30.target_ref, bf16[32,128,48]{2,1,0:T(8,128)(2,1)S(1)} %get-tuple-element.31.source_ref, bf16[32,4096]{1,0:T(8,128)(2,1)S(1)} %bitcast.5, ...), custom_call_target="tpu_custom_call" | custom-call | flops 20000000000 | tf_op jit(solution)/shard_map/pallas_call | solution.py:270
  13.4 0.0 copy-start.3
  13.4 0.0 copy-start.5
  13.5 0.0 copy-start.6
  13.5 1.7 %collective-permute-start.4 = (bf16[64,1024]{1,0:T(8,128)(2,1)S(1)}, bf16[64,1024]{1,0:T(8,128)(2,1)S(1)}, u32[]{:S(2)}, u32[]{:S(2)}) collective-permute-start(bf16[64,1024]{1,0:T(8,128)(2,1)S(1)} %shard_map.66), channel_id=1, source_target_pairs={{0,12},{1,5},{4,0},{5,9},{8,4},{9,13},{12,8},{13,1},{2,14},{3,7},{... | collective-permute-start | bytes 393224 | tf_op jit(solution)/shard_map/ppermute | solution.py:41
  15.1 2.5 %shard_map.67 = bf16[64,1024]{1,0:T(8,128)(2,1)S(1)} custom-call(s32[8,128]{1,0:T(8,128)S(1)} %fusion.9.list_ref, bf16[33,48,128]{2,1,0:T(8,128)(2,1)S(1)} %get-tuple-element.30.target_ref, bf16[32,128,48]{2,1,0:T(8,128)(2,1)S(1)} %get-tuple-element.31.source_ref, bf16[32,4096]{1,0:T(8,128)(2,1)S(1)} %bitcast.6, ...), custom_call_target="tpu_custom_call" | custom-call | flops 20000000000 | tf_op jit(solution)/shard_map/pallas_call | solution.py:270
  17.7 0.8 %collective-permute-start.5 = (bf16[64,1024]{1,0:T(8,128)(2,1)S(1)}, bf16[64,1024]{1,0:T(8,128)(2,1)S(1)}, u32[]{:S(2)}, u32[]{:S(2)}) collective-permute-start(bf16[64,1024]{1,0:T(8,128)(2,1)S(1)} %shard_map.67), channel_id=1, source_target_pairs={{0,12},{1,5},{4,0},{5,9},{8,4},{9,13},{12,8},{13,1},{2,14},{3,7},{... | collective-permute-start | bytes 393224 | tf_op jit(solution)/shard_map/ppermute | solution.py:41
  18.5 2.8 %shard_map.68 = f32[64,2048]{1,0:T(8,128)S(1)} custom-call(s32[8,128]{1,0:T(8,128)S(1)} %copy-done.2, bf16[33,48,128]{2,1,0:T(8,128)(2,1)S(1)} %get-tuple-element.30.target_ref, bf16[32,128,48]{2,1,0:T(8,128)(2,1)S(1)} %get-tuple-element.31.source_ref, bf16[32,4096]{1,0:T(8,128)(2,1)S(1)} %bitcast.7, bf16[32,4096]{1,0:T(8,128)(2,1)S(1)} %collective-permute-done.1.other_ref), custom_call_target="tpu_custom_call" | custom-call | flops 500000000 | tf_op jit(solution)/shard_map/pallas_call | solution.py:270
  21.3 0.0 collective-permute-done.3.refs_2_
  21.4 0.0 collective-permute-done.4
  21.4 2.6 %shard_map.69 = f32[32,2048]{1,0:T(8,128)S(1)} custom-call(s32[16,32]{1,0:T(8,128)S(1)} %fusion.7.far_ref, bf16[16,32,32,32]{3,2,1,0:T(8,128)(2,1)S(1)} %copy-done.3, bf16[32,4096]{1,0:T(8,128)(2,1)S(1)} %copy-done.5, bf16[272,128]{1,0:T(8,128)(2,1)S(1)} %copy-done.6, bf16[272,128]{1,0:T(8,128)(2,1)S(1)} %collective-permute-done.2.refs_1_, ...), custom_call_target="tpu_custom_call" | custom-call | flops 20000000000 | tf_op jit(solution)/shard_map/pallas_call | solution.py:419
  24.0 0.1 collective-permute-done.5
  24.2 0.1 collective-permute-start.6
  24.2 1.3 %collective-permute-done.6 = bf16[32,2048]{1,0:T(8,128)(2,1)S(1)} collective-permute-done((bf16[32,2048]{1,0:T(8,128)(2,1)S(1)}, bf16[32,2048]{1,0:T(8,128)(2,1)S(1)}, u32[]{:S(2)}, u32[]{:S(2)}) %collective-permute-start.6) | collective-permute-done | bytes 131104 | tf_op jit(solution)/shard_map/ppermute | solution.py:32
  25.6 0.7 %fusion.2 = bf16[2048,32]{0,1:T(8,128)(2,1)} fusion(f32[32,2048]{1,0:T(8,128)S(1)} %shard_map.69, bf16[32,2048]{1,0:T(8,128)(2,1)S(1)} %collective-permute-done.6, f32[64,2048]{1,0:T(8,128)S(1)} %convert_add_fusion), kind=kLoop, calls=%fused_computation.5 | loop fusion | flops 262144 | bytes 786432 | tf_op jit(solution)/shard_map/transpose | solution.py:445
  (18 shorter events, 0.1 us)
Async XLA Ops:
  0.0 9.4 %copy-start = (s32[128,32]{0,1:T(8,128)S(1)}, s32[128,32]{0,1:T(8,128)}, u32[]{:S(2)}) copy-start(s32[128,32]{0,1:T(8,128)} %param.11) | copy-start | bytes 49156
  0.0 5.6 %copy-start.4 = (f32[3,16384]{1,0:T(4,128)S(1)}, f32[3,16384]{1,0:T(4,128)}, u32[]{:S(2)}) copy-start(f32[3,16384]{1,0:T(4,128)} %points_ref) | copy-start | bytes 589828
  0.0 10.9 %copy-start.1 = (bf16[4096,32]{0,1:T(8,128)(2,1)S(1)}, bf16[4096,32]{0,1:T(8,128)(2,1)}, u32[]{:S(2)}) copy-start(bf16[4096,32]{0,1:T(8,128)(2,1)} %param.7) | copy-start | bytes 786436
  0.0 10.9 %collective-permute-start.1 = (bf16[32,4096]{1,0:T(8,128)(2,1)}, bf16[32,4096]{1,0:T(8,128)(2,1)S(1)}, u32[]{:S(2)}, u32[]{:S(2)}) collective-permute-start(bf16[32,4096]{1,0:T(8,128)(2,1)} %bitcast.3), channel_id=1, source_target_pairs={{0,1},{1,0},{2,3},{3,2},{4,5},{5,4},{6,7},{7,6},{8,9},{9,8},{10,11... | collective-permute-start | bytes 786440 | tf_op jit(solution)/shard_map/ppermute | solution.py:32
  2.9 8.0 %collective-permute-start = (bf16[272,128]{1,0:T(8,128)(2,1)}, bf16[272,128]{1,0:T(8,128)(2,1)S(1)}, u32[]{:S(2)}, u32[]{:S(2)}) collective-permute-start(bf16[272,128]{1,0:T(8,128)(2,1)} %get-tuple-element.38.refs_0_), channel_id=1, source_target_pairs={{0,4},{1,13},{4,8},{5,1},{8,12},{9,5},{12,0},{13,9},{2,6},{3,15},{... | collective-permute-start | bytes 208904 | tf_op jit(solution)/shard_map/ppermute | solution.py:41
  6.3 15.0 %collective-permute-start.2 = (bf16[272,128]{1,0:T(8,128)(2,1)}, bf16[272,128]{1,0:T(8,128)(2,1)S(1)}, u32[]{:S(2)}, u32[]{:S(2)}) collective-permute-start(bf16[272,128]{1,0:T(8,128)(2,1)} %get-tuple-element.38.refs_0_), channel_id=1, source_target_pairs={{0,12},{1,5},{4,0},{5,9},{8,4},{9,13},{12,8},{13,1},{2,14},{3,7},{... | collective-permute-start | bytes 208904 | tf_op jit(solution)/shard_map/ppermute | solution.py:41
  8.4 12.9 %collective-permute-start.3 = (bf16[272,128]{1,0:T(8,128)(2,1)}, bf16[272,128]{1,0:T(8,128)(2,1)S(1)}, u32[]{:S(2)}, u32[]{:S(2)}) collective-permute-start(bf16[272,128]{1,0:T(8,128)(2,1)} %get-tuple-element.38.refs_0_), channel_id=1, source_target_pairs={{0,8},{4,12},{8,0},{12,4},{1,9},{5,13},{9,1},{13,5},{2,10},{6,14},... | collective-permute-start | bytes 208904 | tf_op jit(solution)/shard_map/ppermute | solution.py:32
  13.4 5.1 %copy-start.2 = (s32[8,128]{1,0:T(8,128)S(1)}, s32[8,128]{1,0:T(8,128)}, u32[]{:S(2)}) copy-start(s32[8,128]{1,0:T(8,128)} %get-tuple-element.34.list_ref) | copy-start | bytes 12292
  13.4 7.9 %copy-start.3 = (bf16[16,32,32,32]{3,2,1,0:T(8,128)(2,1)S(1)}, bf16[16,32,32,32]{3,2,1,0:T(8,128)(2,1)}, u32[]{:S(2)}) copy-start(bf16[16,32,32,32]{3,2,1,0:T(8,128)(2,1)} %couplings_ref.1) | copy-start | bytes 3145732
  13.4 7.9 %copy-start.5 = (bf16[32,4096]{1,0:T(8,128)(2,1)S(1)}, bf16[32,4096]{1,0:T(8,128)(2,1)}, u32[]{:S(2)}) copy-start(bf16[32,4096]{1,0:T(8,128)(2,1)} %basis_ref.1) | copy-start | bytes 786436
  13.5 7.9 %copy-start.6 = (bf16[272,128]{1,0:T(8,128)(2,1)S(1)}, bf16[272,128]{1,0:T(8,128)(2,1)}, u32[]{:S(2)}) copy-start(bf16[272,128]{1,0:T(8,128)(2,1)} %get-tuple-element.38.refs_0_) | copy-start | bytes 208900
  13.5 7.9 %collective-permute-start.4 = (bf16[64,1024]{1,0:T(8,128)(2,1)S(1)}, bf16[64,1024]{1,0:T(8,128)(2,1)S(1)}, u32[]{:S(2)}, u32[]{:S(2)}) collective-permute-start(bf16[64,1024]{1,0:T(8,128)(2,1)S(1)} %shard_map.66), channel_id=1, source_target_pairs={{0,12},{1,5},{4,0},{5,9},{8,4},{9,13},{12,8},{13,1},{2,14},{3,7},{... | collective-permute-start | bytes 393224 | tf_op jit(solution)/shard_map/ppermute | solution.py:41
  17.7 6.4 %collective-permute-start.5 = (bf16[64,1024]{1,0:T(8,128)(2,1)S(1)}, bf16[64,1024]{1,0:T(8,128)(2,1)S(1)}, u32[]{:S(2)}, u32[]{:S(2)}) collective-permute-start(bf16[64,1024]{1,0:T(8,128)(2,1)S(1)} %shard_map.67), channel_id=1, source_target_pairs={{0,12},{1,5},{4,0},{5,9},{8,4},{9,13},{12,8},{13,1},{2,14},{3,7},{... | collective-permute-start | bytes 393224 | tf_op jit(solution)/shard_map/ppermute | solution.py:41
  24.2 1.4 %collective-permute-start.6 = (bf16[32,2048]{1,0:T(8,128)(2,1)S(1)}, bf16[32,2048]{1,0:T(8,128)(2,1)S(1)}, u32[]{:S(2)}, u32[]{:S(2)}) collective-permute-start(bf16[32,2048]{1,0:T(8,128)(2,1)S(1)} %slice.39), channel_id=1, source_target_pairs={{0,1},{1,0},{2,3},{3,2},{4,5},{5,4},{6,7},{7,6},{8,9},{9,8},{10,11... | collective-permute-start | bytes 393224 | tf_op jit(solution)/shard_map/ppermute | solution.py:32
